TPU v7x, 32 devices: a whole 2x2x4 slice. The times are simulated.
32 devices in a mesh: dim: 16 (over z, y, core), row: 2 (over x).
Axes of the slice: x: 2, y: 2, z: 4, core: 2. Of those that a mesh axis runs over, the one named last changes fastest.
Arguments:
- vectors: bfloat16 [3328, 4096], P('row', 'dim'), may hold values from -6 to 6
- blocks: float32 [5, 4096, 128], P(None, 'dim'), may hold values from -0.5 to 0.5
- angles: float32 [5, 4096], P(None, 'dim'), may hold values from -3.140625 to 3.140625
- codes: int32 [3328, 4096], P('row', 'dim'), may hold values from 0 to 15
- scale_index: int32 [3328], P('row'), may hold values from 0 to 15
- scale_table: float32 [16], replicated, may hold values from 0.05 to 0.3
- block_state: float32 [5, 4096, 128], P(None, 'dim'), may hold values from 0.1 to 2
- angle_state: float32 [5, 4096], P(None, 'dim'), may hold values from 0.1 to 2
Outputs:
- step_blocks: float32 [5, 4096, 128], P(None, 'dim')
- new_block_state: float32 [5, 4096, 128], P(None, 'dim')
- step_angles: float32 [5, 4096], P(None, 'dim')
- new_angle_state: float32 [5, 4096], P(None, 'dim')
All inputs are finite; a program needn't handle non-finite values.
Results may differ from a plain program's by a relative error of at most 0.015.
The roundings to bfloat16 on the way count: a program that leaves them out, or rounds other values in their place, can miss the bound.
Values may be sent and summed in bfloat16 or wider, within the bound.
No kernel may reach another device: no remote copies, remote signals or barrier semaphores. Data moves between devices by JAX's collectives and lax.ppermute only.
A program may use at most 128 MiB of HBM per device.

v0:
```python
import math

import jax
import jax.numpy as jnp
from jax import lax
from jax.sharding import PartitionSpec as P

BLOCK = 128
S = 5


def swapped(value, axis, distance):
    mask = 2**distance
    pairs = [(source, source ^ mask) for source in range(lax.axis_size(axis))]
    return lax.ppermute(value, axis, pairs)


def swap_halves(tensor, section):
    layout = tensor.shape
    stride = 2**section
    number = layout[-2]
    parted = tensor.reshape(layout[:-2] + (number // (2 * stride), 2, stride, layout[-1]))
    return jnp.flip(parted, axis=-3).reshape(layout)


def local(vectors, blocks, angles, codes, scale_index, scale_table, block_state, angle_state):
    num_rows = vectors.shape[0]
    width = vectors.shape[1]
    local_blocks = width // BLOCK
    local_bits = local_blocks.bit_length() - 1
    device = lax.axis_index("dim")
    global_ids = device * local_blocks + jnp.arange(local_blocks, dtype=jnp.int32)
    weights = blocks.astype(jnp.bfloat16).reshape(S, local_blocks, BLOCK, BLOCK)
    thetas = angles.reshape(S, local_blocks, BLOCK)
    cosines = jnp.cos(thetas)
    sines = jnp.sin(thetas)
    current = vectors.reshape(num_rows, local_blocks, BLOCK)
    saved = []
    for section in range(S):
        signs = jnp.where(global_ids // 2**section % 2 == 0, 1.0, -1.0).astype(jnp.float32)[:, None]
        mixed = jnp.einsum(
            "rnb,nbc->rnc", current, weights[section], preferred_element_type=jnp.float32
        ).astype(jnp.bfloat16)
        if section < local_bits:
            partner = swap_halves(mixed, section)
        else:
            partner = swapped(mixed, "dim", section - local_bits)
        result = (
            cosines[section] * mixed.astype(jnp.float32)
            + signs * sines[section] * partner.astype(jnp.float32)
        ).astype(jnp.bfloat16)
        saved.append((current, mixed, partner, signs))
        current = result
    levels = (
        scale_index[:, None] == jnp.arange(scale_table.shape[0], dtype=jnp.int32)[None, :]
    ).astype(jnp.float32)
    factor = jnp.sum(levels * scale_table[None, :], axis=1)
    recon = factor[:, None] * (codes.astype(jnp.float32) - 7.5)
    total_rows = num_rows * lax.axis_size("row")
    cotangent = (
        ((current.reshape(num_rows, width).astype(jnp.float32) - recon) / math.sqrt(total_rows))
        .astype(jnp.bfloat16)
        .reshape(num_rows, local_blocks, BLOCK)
    )
    block_grads = [None] * S
    angle_grads = [None] * S
    for section in reversed(range(S)):
        source, mixed, partner, signs = saved[section]
        upstream = cotangent.astype(jnp.float32)
        angle_grad = jnp.sum(
            upstream
            * (
                -sines[section] * mixed.astype(jnp.float32)
                + signs * cosines[section] * partner.astype(jnp.float32)
            ),
            axis=0,
        )
        outgoing = (signs * sines[section] * upstream).astype(jnp.bfloat16)
        if section < local_bits:
            incoming = swap_halves(outgoing, section)
        else:
            incoming = swapped(outgoing, "dim", section - local_bits)
        direction = (cosines[section] * upstream + incoming.astype(jnp.float32)).astype(
            jnp.bfloat16
        )
        block_grad = jnp.einsum(
            "rnb,rnc->nbc", source, direction, preferred_element_type=jnp.float32
        )
        if section > 0:
            cotangent = jnp.einsum(
                "rnc,nbc->rnb", direction, weights[section], preferred_element_type=jnp.float32
            ).astype(jnp.bfloat16)
        block_grad, angle_grad = lax.psum((block_grad, angle_grad), "row")
        block_grads[section] = block_grad
        angle_grads[section] = angle_grad
    grad_blocks = jnp.stack(block_grads).reshape(S, width, BLOCK)
    grad_angles = jnp.stack(angle_grads).reshape(S, width)
    new_block_state = 0.9 * block_state + 0.1 * grad_blocks * grad_blocks
    step_blocks = grad_blocks / jnp.sqrt(new_block_state)
    new_angle_state = 0.9 * angle_state + 0.1 * grad_angles * grad_angles
    step_angles = grad_angles / jnp.sqrt(new_angle_state)
    return (step_blocks, new_block_state, step_angles, new_angle_state)


def solution(mesh):
    in_specs = (
        P("row", "dim"),
        P(None, "dim", None),
        P(None, "dim"),
        P("row", "dim"),
        P("row"),
        P(),
        P(None, "dim", None),
        P(None, "dim"),
    )
    out_specs = (P(None, "dim", None), P(None, "dim", None), P(None, "dim"), P(None, "dim"))
    return jax.shard_map(local, mesh=mesh, in_specs=in_specs, out_specs=out_specs, check_vma=False)
```

profile of v0, /device:TPU:0, one launch (start us, length us, event | category | flops | bytes accessed | tf_op | source)
XLA Modules:
  0.0 249.4 jit_solution(3274056117074677992)
XLA Ops:
  8.1 1.1 convert_element_type.192
  13.9 1.4 collective-permute-done
  15.8 3.0 %collective-permute-start.1 = (bf16[1664,2,128]{2,0,1:T(8,128)(2,1)S(1)}, bf16[1664,2,128]{2,0,1:T(8,128)(2,1)S(1)}, u32[]{:S(2)}, u32[]{:S(2)}) collective-permute-start(bf16[1664,2,128]{2,0,1:T(8,128)(2,1)S(1)} %fusion.10), channel_id=1, source_target_pairs={{0,4},{2,6},{4,0},{6,2},{8,12},{10,14},{12,8},{14,10},{16,20},{18,... | collective-permute-start | bytes 2555912 | tf_op jit(solution)/shard_map/ppermute | solution.py:15
  19.3 18.7 %collective-permute-done.1 = bf16[1664,2,128]{2,0,1:T(8,128)(2,1)S(1)} collective-permute-done((bf16[1664,2,128]{2,0,1:T(8,128)(2,1)S(1)}, bf16[1664,2,128]{2,0,1:T(8,128)(2,1)S(1)}, u32[]{:S(2)}, u32[]{:S(2)}) %collective-permute-start.1) | collective-permute-done | bytes 852000 | tf_op jit(solution)/shard_map/ppermute | solution.py:15
  38.5 1.9 collective-permute-start.2
  41.0 18.0 %collective-permute-done.2 = bf16[1664,2,128]{2,0,1:T(8,128)(2,1)S(1)} collective-permute-done((bf16[1664,2,128]{2,0,1:T(8,128)(2,1)S(1)}, bf16[1664,2,128]{2,0,1:T(8,128)(2,1)S(1)}, u32[]{:S(2)}, u32[]{:S(2)}) %collective-permute-start.2) | collective-permute-done | bytes 852000 | tf_op jit(solution)/shard_map/ppermute | solution.py:15
  59.0 0.9 copy-done.9
  60.5 2.6 %collective-permute-start.3 = (bf16[1664,2,128]{0,2,1:T(8,128)(2,1)S(1)}, bf16[1664,2,128]{0,2,1:T(8,128)(2,1)S(1)}, u32[]{:S(2)}, u32[]{:S(2)}) collective-permute-start(bf16[1664,2,128]{0,2,1:T(8,128)(2,1)S(1)} %fusion.12), channel_id=1, source_target_pairs={{0,16},{2,18},{4,20},{6,22},{8,24},{10,26},{12,28},{14,30},{16,0},... | collective-permute-start | bytes 2555912 | tf_op jit(solution)/shard_map/ppermute | solution.py:15
  63.8 35.5 %collective-permute-done.3 = bf16[1664,2,128]{0,2,1:T(8,128)(2,1)S(1)} collective-permute-done((bf16[1664,2,128]{0,2,1:T(8,128)(2,1)S(1)}, bf16[1664,2,128]{0,2,1:T(8,128)(2,1)S(1)}, u32[]{:S(2)}, u32[]{:S(2)}) %collective-permute-start.3) | collective-permute-done | bytes 852000 | tf_op jit(solution)/shard_map/ppermute | solution.py:15
  100.2 1.4 bitcast_convert_fusion
  101.6 1.8 copy.43
  103.4 3.0 %fusion.38 = f32[1664,256]{1,0:T(8,128)} fusion(f32[1664,256]{1,0:T(8,128)S(1)} %copy.43, s32[1664,256]{1,0:T(8,128)} %param.11, f32[1664]{0:T(1024)S(1)} %select_reduce_fusion), kind=kLoop, calls=%fused_computation.79 | loop fusion | flops 2981888 | bytes 5118464 | tf_op jit(solution)/shard_map/convert_element_type | solution.py:69
  106.4 1.8 copy.44
  108.5 39.3 %collective-permute-done.4 = bf16[1664,2,128]{0,2,1:T(8,128)(2,1)S(1)} collective-permute-done((bf16[1664,2,128]{0,2,1:T(8,128)(2,1)S(1)}, bf16[1664,2,128]{0,2,1:T(8,128)(2,1)S(1)}, u32[]{:S(2)}, u32[]{:S(2)}) %collective-permute-start.4) | collective-permute-done | bytes 852000 | tf_op jit(solution)/shard_map/ppermute | solution.py:15
  149.0 19.7 %collective-permute-done.5 = bf16[1664,2,128]{2,0,1:T(8,128)(2,1)S(1)} collective-permute-done((bf16[1664,2,128]{2,0,1:T(8,128)(2,1)S(1)}, bf16[1664,2,128]{2,0,1:T(8,128)(2,1)S(1)}, u32[]{:S(2)}, u32[]{:S(2)}) %collective-permute-start.5) | collective-permute-done | bytes 852000 | tf_op jit(solution)/shard_map/ppermute | solution.py:15
  170.8 18.8 %collective-permute-done.6 = bf16[1664,2,128]{2,0,1:T(8,128)(2,1)S(1)} collective-permute-done((bf16[1664,2,128]{2,0,1:T(8,128)(2,1)S(1)}, bf16[1664,2,128]{2,0,1:T(8,128)(2,1)S(1)}, u32[]{:S(2)}, u32[]{:S(2)}) %collective-permute-start.6) | collective-permute-done | bytes 852000 | tf_op jit(solution)/shard_map/ppermute | solution.py:15
  191.7 1.2 fusion.42
  192.9 1.2 fusion.45
  194.2 1.2 fusion.48
  195.7 1.0 fusion.63
  196.7 2.0 fusion.17
  198.7 2.2 reshape.277
  201.0 2.9 %fusion.39 = f32[2,128,128]{1,2,0:T(8,128)} fusion(bf16[1664,2,128]{0,2,1:T(8,128)(2,1)S(1)} %bitcast.110, bf16[1664,2,128]{0,2,1:T(8,128)(2,1)} %reshape.277, f32[1664,2,128]{0,2,1:T(8,128)} %get-tuple-element.61, f32[2,128]{1,0:T(2,128)S(1)} %bitcast.134), kind=kOutput, calls=%fused_computation.80 | convolution fusion | flops 110755840 | bytes 3539968 | tf_op jit(solution)/shard_map/rnb,rnc->nbc/dot_general | solution.py:86
  204.0 1.7 fusion.37
  205.7 5.0 %all-reduce = (f32[1,256]{1,0:T(1,128)S(1)}, f32[1,256]{1,0:T(1,128)S(1)}, f32[1,256]{1,0:T(1,128)S(1)}, f32[1,256]{1,0:T(1,128)S(1)}, f32[1,256]{1,0:T(1,128)S(1)}) all-reduce(f32[1,256]{1,0:T(1,128)S(1)} %bitcast.146, f32[1,256]{1,0:T(1,128)S(1)} %bitcast.145, ...), channel_id=1, replica_groups=mesh['dim'=16,'row'=2] {'row'}, use_global_device_ids=true, to_apply=%region_7.8 | all-reduce | flops 1280 | bytes 10240 | tf_op jit(solution)/shard_map/psum | solution.py:93
  211.4 25.4 %all-reduce.4.cloned.1.call-done = (f32[1,256,128]{2,1,0:T(8,128)}, f32[1,256,128]{2,1,0:T(8,128)}, f32[1,256,128]{2,1,0:T(8,128)}, f32[1,256,128]{2,1,0:T(8,128)}, f32[1,256,128]{2,1,0:T(8,128)}) async-done(((f32[1,256,128]{2,1,0:T(8,128)}, f32[1,256,128]{2,1,0:T(8,128)}, f32[1,256,128]{2,1,0:T(8,128)}, f32[1,256,128]{2,1,0:T(8,128)}, f32[1,256,128]{2,1,0:T(8,128)}), (f32[1,256,128]{2,1,0:T(8,128)}, ...) | async-done | bytes 655376 | tf_op jit(solution)/shard_map/psum | solution.py:93
  236.8 0.9 constant_dynamic-update-slice_fusion.4
  237.7 0.9 constant_dynamic-update-slice_fusion.3
  238.6 0.9 constant_dynamic-update-slice_fusion.2
  239.5 0.9 constant_dynamic-update-slice_fusion.1
  240.5 0.9 constant_dynamic-update-slice_fusion
  241.4 1.2 rsqrt_multiply_fusion
  (141 shorter events, 16.2 us)
Async XLA Ops:
  7.2 229.6 %all-reduce.4.cloned.1.call-start = ((), (), s32[]{:S(2)}) async-start(), calls=%async_computation | async-start | bytes 1310720 | tf_op jit(solution)/shard_map/psum | solution.py:93
  10.6 4.7 %copy-start.25 = (f32[1,256]{1,0:T(1,128)}, f32[1,256]{1,0:T(1,128)S(1)}, u32[]{:S(2)}) copy-start(f32[1,256]{1,0:T(1,128)S(1)} %get-tuple-element.34) | copy-start | bytes 3076
  10.6 27.4 %copy-start.27 = (f32[1,256]{1,0:T(1,128)}, f32[1,256]{1,0:T(1,128)S(1)}, u32[]{:S(2)}) copy-start(f32[1,256]{1,0:T(1,128)S(1)} %get-tuple-element.33) | copy-start | bytes 3076
  12.7 25.7 %copy-start.4 = (bf16[1664,2,128]{2,0,1:T(8,128)(2,1)}, bf16[1664,2,128]{2,0,1:T(8,128)(2,1)S(1)}, u32[]{:S(2)}) copy-start(bf16[1664,2,128]{2,0,1:T(8,128)(2,1)S(1)} %fusion.9) | copy-start | bytes 2555908
  12.7 25.2 %copy-start.21 = (bf16[1,256,128]{2,1,0:T(8,128)(2,1)S(1)}, bf16[1,256,128]{2,1,0:T(8,128)(2,1)}, u32[]{:S(2)}) copy-start(bf16[1,256,128]{2,1,0:T(8,128)(2,1)} %get-tuple-element.28) | copy-start | bytes 196612
  12.8 2.5 %collective-permute-start = (bf16[1664,2,128]{2,0,1:T(8,128)(2,1)S(1)}, bf16[1664,2,128]{2,0,1:T(8,128)(2,1)S(1)}, u32[]{:S(2)}, u32[]{:S(2)}) collective-permute-start(bf16[1664,2,128]{2,0,1:T(8,128)(2,1)S(1)} %fusion.9), channel_id=1, source_target_pairs={{0,2},{2,0},{4,6},{6,4},{8,10},{10,8},{12,14},{14,12},{16,18},{18,... | collective-permute-start | bytes 2555912 | tf_op jit(solution)/shard_map/ppermute | solution.py:15
  13.9 24.6 %copy-start.39 = (f32[2,128]{1,0:T(2,128)}, f32[2,128]{1,0:T(2,128)S(1)}, u32[]{:S(2)}) copy-start(f32[2,128]{1,0:T(2,128)S(1)} %get-tuple-element.50) | copy-start | bytes 3076
  15.3 22.7 %copy-start.12 = (bf16[1664,2,128]{2,0,1:T(8,128)(2,1)}, bf16[1664,2,128]{2,0,1:T(8,128)(2,1)S(1)}, u32[]{:S(2)}) copy-start(bf16[1664,2,128]{2,0,1:T(8,128)(2,1)S(1)} %collective-permute-done) | copy-start | bytes 2555908
  15.7 22.2 %copy-start.14 = (bf16[1664,2,128]{2,0,1:T(8,128)(2,1)}, bf16[1664,2,128]{2,0,1:T(8,128)(2,1)S(1)}, u32[]{:S(2)}) copy-start(bf16[1664,2,128]{2,0,1:T(8,128)(2,1)S(1)} %fusion.10) | copy-start | bytes 2555908
  15.8 22.2 %collective-permute-start.1 = (bf16[1664,2,128]{2,0,1:T(8,128)(2,1)S(1)}, bf16[1664,2,128]{2,0,1:T(8,128)(2,1)S(1)}, u32[]{:S(2)}, u32[]{:S(2)}) collective-permute-start(bf16[1664,2,128]{2,0,1:T(8,128)(2,1)S(1)} %fusion.10), channel_id=1, source_target_pairs={{0,4},{2,6},{4,0},{6,2},{8,12},{10,14},{12,8},{14,10},{16,20},{18,... | collective-permute-start | bytes 2555912 | tf_op jit(solution)/shard_map/ppermute | solution.py:15
  19.3 41.2 %copy-start.45 = (f32[2,128]{1,0:T(2,128)}, f32[2,128]{1,0:T(2,128)S(1)}, u32[]{:S(2)}) copy-start(f32[2,128]{1,0:T(2,128)S(1)} %get-tuple-element.48) | copy-start | bytes 3076
  38.0 22.5 %copy-start.16 = (bf16[1664,2,128]{2,0,1:T(8,128)(2,1)}, bf16[1664,2,128]{2,0,1:T(8,128)(2,1)S(1)}, u32[]{:S(2)}) copy-start(bf16[1664,2,128]{2,0,1:T(8,128)(2,1)S(1)} %collective-permute-done.1) | copy-start | bytes 2555908
  38.5 60.8 %copy-start.7 = (bf16[1664,2,128]{2,0,1:T(8,128)(2,1)}, bf16[1664,2,128]{2,0,1:T(8,128)(2,1)S(1)}, u32[]{:S(2)}) copy-start(bf16[1664,2,128]{2,0,1:T(8,128)(2,1)S(1)} %fusion.11) | copy-start | bytes 2555908
  38.5 24.6 %copy-start.35 = (s32[1664]{0:T(1024)S(1)}, s32[1664]{0:T(1024)}, u32[]{:S(2)}) copy-start(s32[1664]{0:T(1024)} %param.12) | copy-start | bytes 19972
  38.5 24.6 %copy-start.51 = (f32[16]{0:T(128)S(1)}, f32[16]{0:T(128)}, u32[]{:S(2)}) copy-start(f32[16]{0:T(128)} %param.13) | copy-start | bytes 196
  38.5 20.5 %collective-permute-start.2 = (bf16[1664,2,128]{2,0,1:T(8,128)(2,1)S(1)}, bf16[1664,2,128]{2,0,1:T(8,128)(2,1)S(1)}, u32[]{:S(2)}, u32[]{:S(2)}) collective-permute-start(bf16[1664,2,128]{2,0,1:T(8,128)(2,1)S(1)} %fusion.11), channel_id=1, source_target_pairs={{0,8},{2,10},{4,12},{6,14},{8,0},{10,2},{12,4},{14,6},{16,24},{18,... | collective-permute-start | bytes 2555912 | tf_op jit(solution)/shard_map/ppermute | solution.py:15
  41.0 19.5 %copy-start.29 = (f32[2,128]{1,0:T(2,128)}, f32[2,128]{1,0:T(2,128)S(1)}, u32[]{:S(2)}) copy-start(f32[2,128]{1,0:T(2,128)S(1)} %get-tuple-element.46) | copy-start | bytes 3076
  60.5 38.8 %copy-start.2 = (bf16[1664,2,128]{0,2,1:T(8,128)(2,1)}, bf16[1664,2,128]{0,2,1:T(8,128)(2,1)S(1)}, u32[]{:S(2)}) copy-start(bf16[1664,2,128]{0,2,1:T(8,128)(2,1)S(1)} %fusion.12) | copy-start | bytes 2555908
  60.5 38.8 %collective-permute-start.3 = (bf16[1664,2,128]{0,2,1:T(8,128)(2,1)S(1)}, bf16[1664,2,128]{0,2,1:T(8,128)(2,1)S(1)}, u32[]{:S(2)}, u32[]{:S(2)}) collective-permute-start(bf16[1664,2,128]{0,2,1:T(8,128)(2,1)S(1)} %fusion.12), channel_id=1, source_target_pairs={{0,16},{2,18},{4,20},{6,22},{8,24},{10,26},{12,28},{14,30},{16,0},... | collective-permute-start | bytes 2555912 | tf_op jit(solution)/shard_map/ppermute | solution.py:15
  63.8 35.9 %copy-start.31 = (f32[2,128]{1,0:T(2,128)}, f32[2,128]{1,0:T(2,128)S(1)}, u32[]{:S(2)}) copy-start(f32[2,128]{1,0:T(2,128)S(1)} %get-tuple-element.44) | copy-start | bytes 3076
  108.4 39.8 %copy-start.8 = (bf16[1664,2,128]{2,0,1:T(8,128)(2,1)S(1)}, bf16[1664,2,128]{2,0,1:T(8,128)(2,1)}, u32[]{:S(2)}) copy-start(bf16[1664,2,128]{2,0,1:T(8,128)(2,1)} %copy-done.7) | copy-start | bytes 2555908
  108.4 39.8 %copy-start.10 = (bf16[1664,2,128]{2,0,1:T(8,128)(2,1)S(1)}, bf16[1664,2,128]{2,0,1:T(8,128)(2,1)}, u32[]{:S(2)}) copy-start(bf16[1664,2,128]{2,0,1:T(8,128)(2,1)} %copy-done.9) | copy-start | bytes 2555908
  108.4 39.8 %copy-start.30 = (f32[2,128]{1,0:T(2,128)S(1)}, f32[2,128]{1,0:T(2,128)}, u32[]{:S(2)}) copy-start(f32[2,128]{1,0:T(2,128)} %copy-done.29) | copy-start | bytes 3076
  108.4 39.8 %copy-start.49 = (f32[2,128]{1,0:T(2,128)S(1)}, f32[2,128]{1,0:T(2,128)}, u32[]{:S(2)}) copy-start(f32[2,128]{1,0:T(2,128)} %get-tuple-element.45) | copy-start | bytes 3076
  108.4 39.8 %copy-start.50 = (f32[2,128]{1,0:T(2,128)S(1)}, f32[2,128]{1,0:T(2,128)}, u32[]{:S(2)}) copy-start(f32[2,128]{1,0:T(2,128)} %get-tuple-element.56) | copy-start | bytes 3076
  108.4 39.4 %collective-permute-start.4 = (bf16[1664,2,128]{0,2,1:T(8,128)(2,1)S(1)}, bf16[1664,2,128]{0,2,1:T(8,128)(2,1)S(1)}, u32[]{:S(2)}, u32[]{:S(2)}) collective-permute-start(bf16[1664,2,128]{0,2,1:T(8,128)(2,1)S(1)} %multiply_convert_fusion.4), channel_id=1, source_target_pairs={{0,16},{2,18},{4,20},{6,22},{8,24},{10,26},{12,28},{14,30},{16,0},... | collective-permute-start | bytes 2555912 | tf_op jit(solution)/shard_map/ppermute | solution.py:15
  148.9 19.8 %collective-permute-start.5 = (bf16[1664,2,128]{2,0,1:T(8,128)(2,1)S(1)}, bf16[1664,2,128]{2,0,1:T(8,128)(2,1)S(1)}, u32[]{:S(2)}, u32[]{:S(2)}) collective-permute-start(bf16[1664,2,128]{2,0,1:T(8,128)(2,1)S(1)} %get-tuple-element.19), channel_id=1, source_target_pairs={{0,8},{2,10},{4,12},{6,14},{8,0},{10,2},{12,4},{14,6},{16,24},{18,... | collective-permute-start | bytes 2555912 | tf_op jit(solution)/shard_map/ppermute | solution.py:15
  170.1 19.5 %copy-start.28 = (f32[1,256]{1,0:T(1,128)S(1)}, f32[1,256]{1,0:T(1,128)}, u32[]{:S(2)}) copy-start(f32[1,256]{1,0:T(1,128)} %copy-done.27) | copy-start | bytes 3076
  170.7 18.8 %collective-permute-start.6 = (bf16[1664,2,128]{2,0,1:T(8,128)(2,1)S(1)}, bf16[1664,2,128]{2,0,1:T(8,128)(2,1)S(1)}, u32[]{:S(2)}, u32[]{:S(2)}) collective-permute-start(bf16[1664,2,128]{2,0,1:T(8,128)(2,1)S(1)} %get-tuple-element.21), channel_id=1, source_target_pairs={{0,4},{2,6},{4,0},{6,2},{8,12},{10,14},{12,8},{14,10},{16,20},{18,... | collective-permute-start | bytes 2555912 | tf_op jit(solution)/shard_map/ppermute | solution.py:15
  191.6 3.8 %collective-permute-start.7 = (bf16[1664,2,128]{2,0,1:T(8,128)(2,1)S(1)}, bf16[1664,2,128]{2,0,1:T(8,128)(2,1)S(1)}, u32[]{:S(2)}, u32[]{:S(2)}) collective-permute-start(bf16[1664,2,128]{2,0,1:T(8,128)(2,1)S(1)} %get-tuple-element.23), channel_id=1, source_target_pairs={{0,2},{2,0},{4,6},{6,4},{8,10},{10,8},{12,14},{14,12},{16,18},{18,... | collective-permute-start | bytes 2555912 | tf_op jit(solution)/shard_map/ppermute | solution.py:15
  203.9 6.8 %copy-start.36 = (f32[5,256]{1,0:T(8,128)S(1)}, f32[5,256]{1,0:T(8,128)}, u32[]{:S(2)}) copy-start(f32[5,256]{1,0:T(8,128)} %param.15) | copy-start | bytes 15364
  204.0 37.4 %copy-start.18 = (f32[5,256,128]{2,1,0:T(8,128)S(1)}, f32[5,256,128]{2,1,0:T(8,128)}, u32[]{:S(2)}) copy-start(f32[5,256,128]{2,1,0:T(8,128)} %param.14) | copy-start | bytes 1966084
  (29 other events, 47.6 us)
Sparse Core Ops, SparseCore 0:
  204.0 32.7 all-reduce.3
where the time goes:
time: 250 us; the launch traced here: 249 us
  waiting for transfers between devices  177 us (71%)
  local copies, waits for them, and re-layouts  16.7 us (7%)
  between operations  14.7 us (6%)
  other arithmetic  14.1 us (6%)
  matrix products  14 us (6%)
  starting transfers between devices  8.21 us (3%)
  blocking collectives  5 us (2%)
    ppermute x8, waiting for transfers between devices, swapped(): return lax.ppermute(value, axis, pairs)  151 us
    psum x1, waiting for transfers between devices, local(): block_grad, angle_grad = lax.psum((block_grad, angle_grad), 'row')  25.4 us
    ppermute x8, starting transfers between devices, swapped(): return lax.ppermute(value, axis, pairs)  8.18 us
    unnamed x108, local copies, waits for them, and re-layouts  7.8 us
    dot_general x5, matrix products, local(): jnp.einsum('rnb,rnc->nbc', source, direction, preferred_element_type=jnp....  7.64 us
  transfers between devices with their start and end apart: 9, of which 8 were waited for; matrix products, arithmetic and copies ran while one was open for 3% of the time, Pallas kernels for 0%

commit v1 on v0

v1 whole, which is shorter than its diff:
```python
import math

import jax
import jax.numpy as jnp
from jax import lax
from jax.experimental import pallas as pl
from jax.experimental.pallas import tpu as pltpu
from jax.sharding import PartitionSpec as P

BLOCK = 128
GROUP = 4
EXTRA = 8
TRIG = 16
BF = jnp.bfloat16
F32 = jnp.float32


def swapped(value, axis, mask):
    pairs = [(source, source ^ mask) for source in range(lax.axis_size(axis))]
    return lax.ppermute(value, axis, pairs)


def dot(a, b):
    return lax.dot_general(a, b, (((1,), (0,)), ((), ())), preferred_element_type=F32)


def dot_t(a, b):
    return lax.dot_general(a, b, (((1,), (1,)), ((), ())), preferred_element_type=F32)


def t_dot(a, b):
    return lax.dot_general(a, b, (((0,), (0,)), ((), ())), preferred_element_type=F32)


def tile_of(rows):
    best = 16
    for size in range(16, 257, 16):
        if rows % size == 0:
            best = size
    return best


def call(body, outs, args, specs=None, scratch=(), flops=0):
    whole = [pl.BlockSpec(a.shape, lambda i, n=a.ndim: (0,) * n) for a in args]
    for at, spec in (specs or {}).items():
        whole[at] = spec
    moved = sum(math.prod(a.shape) * a.dtype.itemsize for a in args) + sum(
        math.prod(o.shape) * o.dtype.itemsize for o in outs
    )
    return list(pl.pallas_call(
        body,
        grid=(1,),
        in_specs=whole,
        out_specs=[pl.BlockSpec(o.shape, lambda i, n=len(o.shape): (0,) * n) for o in outs],
        out_shape=outs,
        scratch_shapes=list(scratch),
        compiler_params=pltpu.CompilerParams(vmem_limit_bytes=40 * 2**20),
        cost_estimate=pl.CostEstimate(flops=flops, bytes_accessed=moved, transcendentals=0),
    )(*args))


def shape(dims, dtype=BF):
    return jax.ShapeDtypeStruct(dims, dtype)


SMEM = pl.BlockSpec(memory_space=pltpu.SMEM)


def split3(x):
    hi = x.astype(BF)
    rest = x - hi.astype(F32)
    mid = rest.astype(BF)
    low = (rest - mid.astype(F32)).astype(BF)
    return [hi, mid, low]


def section_spec(s, width, columns):
    return pl.BlockSpec((1, width, columns), lambda i: (s, 0, 0))


def local(vectors, blocks, angles, codes, scale_index, scale_table, block_state, angle_state):
    rows, width = vectors.shape
    sections = blocks.shape[0]
    nb = width // BLOCK
    local_bits = nb.bit_length() - 1
    shift = sections - 2 - local_bits
    quarter = rows // GROUP
    nrow = lax.axis_size("row")
    inv = 1.0 / math.sqrt(rows * nrow)
    tile = tile_of(quarter)
    device = lax.axis_index("dim")
    place = ((device >> shift) % GROUP).astype(jnp.int32)
    place_arr = place.reshape(1)
    last, third = sections - 1, sections - 2

    ids = device * nb + jnp.arange(width, dtype=jnp.int32) // BLOCK
    bits = (ids[None, :] >> jnp.arange(sections, dtype=jnp.int32)[:, None]) & 1
    signs = jnp.where(bits == 0, 1.0, -1.0).astype(F32)
    trig = jnp.concatenate([jnp.cos(angles), signs * jnp.sin(angles)], axis=0)

    def col(c):
        return slice(c * BLOCK, (c + 1) * BLOCK)

    def cs(ref, s, c):
        return ref[s : s + 1, col(c)], ref[sections + s : sections + s + 1, col(c)]

    def first_body(u_ref, w_ref, trig_ref, *outs):
        saved, sent = outs[:-1], outs[-1]
        weights = [
            [w_ref[s, col(c), :].astype(BF) for c in range(nb)] for s in range(local_bits + 1)
        ]
        for r in range(0, rows, tile):
            at = pl.ds(r, tile)
            u = [u_ref[at, col(c)] for c in range(nb)]
            for s in range(local_bits):
                v = [dot(u[c], weights[s][c]).astype(BF) for c in range(nb)]
                for c in range(nb):
                    saved[2 * s][at, col(c)] = v[c]
                for c in range(nb):
                    co, si = cs(trig_ref, s, c)
                    u[c] = (co * v[c].astype(F32) + si * v[c ^ (1 << s)].astype(F32)).astype(BF)
                    saved[2 * s + 1][at, col(c)] = u[c]
            for c in range(nb):
                sent[at, col(c)] = dot(u[c], weights[local_bits][c]).astype(BF)

    firsts = call(
        first_body,
        [shape((rows, width))] * (2 * local_bits + 1),
        [vectors, blocks, trig],
        flops=rows * width * BLOCK * 4,
    )
    v0s, u0s = firsts[:-1:2], [vectors] + list(firsts[1:-1:2])
    v_first = firsts[-1]

    def pack_body(place_ref, index_ref, table_ref, codes_ref, w_ref, trig_ref, *outs):
        z = place_ref[0]
        w = w_ref[0].astype(BF)
        lines = []
        for s in (third, last):
            lines += split3(trig_ref[s : s + 1, :]) + split3(
                trig_ref[sections + s : sections + s + 1, :]
            )
        lines.append(jnp.zeros((TRIG - len(lines), width), BF))
        for m in range(GROUP):
            q = jnp.bitwise_xor(z, m)
            start = pl.multiple_of(q * quarter, 16)
            for r in range(0, quarter, tile):
                outs[m][r : r + tile, :] = (
                    codes_ref[pl.ds(start + r, tile), :].astype(F32).astype(BF)
                )
            for c in range(nb):
                outs[m][quarter : quarter + BLOCK, col(c)] = w[col(c), :]
            outs[m][quarter + BLOCK :, :] = jnp.concatenate(
                [x.astype(F32) for x in lines], axis=0
            ).astype(BF)
        levels = table_ref.shape[0]
        index = index_ref[pl.ds(z, 1), :]
        onehot = jnp.where(
            lax.broadcasted_iota(jnp.int32, (levels, quarter), 0) == index, 1.0, 0.0
        ).astype(BF)
        total = jnp.zeros((quarter, BLOCK), F32)
        for part in split3(jnp.broadcast_to(table_ref[...], (levels, BLOCK))):
            total = total + t_dot(onehot, part)
        outs[GROUP][...] = total

    packed = call(
        pack_body,
        [shape((quarter + BLOCK + TRIG, width))] * GROUP + [shape((quarter, BLOCK), F32)],
        [
            place_arr,
            scale_index.reshape(GROUP, quarter),
            scale_table.reshape(-1, 1),
            codes,
            blocks,
            trig,
        ],
        specs={0: SMEM, 4: section_spec(last, width, BLOCK)},
        flops=quarter * BLOCK * 100,
    )
    factor = packed[GROUP]
    packs = [packed[0]] + [swapped(packed[m], "dim", m << shift) for m in range(1, GROUP)]

    chunks = list(range(nb))

    def column(c):
        return pl.BlockSpec((rows, BLOCK), lambda i: (0, c))

    def wspec(s, c):
        return pl.BlockSpec((1, BLOCK, BLOCK), lambda i: (s, c, 0))

    product = rows * BLOCK * BLOCK * 2
    other_first = swapped(v_first, "dim", 1)
    saves = {c: {} for c in chunks}

    def middle(c, s, v, other, wide, quarters):
        def body(place_ref, v_ref, o_ref, w_ref, trig_ref, u_out, *outs):
            co, si = cs(trig_ref, s, c)
            w = w_ref[0].astype(BF)
            z = place_ref[0]

            def step(rd, write):
                u = (co * v_ref[rd, :].astype(F32) + si * o_ref[rd, :].astype(F32)).astype(BF)
                u_out[rd, :] = u
                write(dot(u, w).astype(BF))

            if not quarters:
                for r in range(0, rows, tile):

                    def write(x, r=r):
                        outs[0][r : r + tile, :] = x

                    step(pl.ds(r, tile), write)
            else:
                for m in range(GROUP):
                    start = pl.multiple_of(jnp.bitwise_xor(z, m) * quarter, 16)
                    for r in range(0, quarter, tile):

                        def write(x, r=r, m=m):
                            outs[m][r : r + tile, :] = x

                        step(pl.ds(start + r, tile), write)

        outs = [shape((rows, BLOCK))]
        outs += [shape((quarter, BLOCK))] * GROUP if quarters else [shape((rows, BLOCK))]
        specs = {0: SMEM, 3: wspec(s + 1, c)}
        if wide:
            specs.update({1: column(c), 2: column(c)})
        return call(
            body, outs, [place_arr, v, other, blocks, trig], specs=specs, flops=product
        )

    middles = list(range(local_bits, third))
    state = {c: (v_first, other_first) for c in chunks}
    for s in middles:
        for c in chunks:
            v, other = state[c]
            out = middle(c, s, v, other, s == local_bits, s + 1 == third)
            saves[c][s] = (v, other, out[0])
            if s + 1 < third:
                state[c] = (out[1], swapped(out[1], "dim", 1 << (s + 1 - local_bits)))
            else:
                state[c] = [out[1]] + [
                    swapped(out[1 + m], "dim", m << shift) for m in range(1, GROUP)
                ]

    def group_stage(c):
        def body(*refs):
            a_refs, p_refs = refs[:GROUP], refs[GROUP : 2 * GROUP]
            f_ref = refs[2 * GROUP]
            outs, grad = refs[2 * GROUP + 1 : 3 * GROUP + 1], refs[3 * GROUP + 1]
            coef, w = [], []
            for m in range(GROUP):
                t = p_refs[m][quarter + BLOCK :, :].astype(F32)
                coef.append([t[3 * k : 3 * k + 1] + t[3 * k + 1 : 3 * k + 2] + t[3 * k + 2 : 3 * k + 3] for k in range(4)])
                w.append(p_refs[m][quarter : quarter + BLOCK, :])
            gw = [jnp.zeros((BLOCK, BLOCK), F32)] * GROUP
            ga = [[jnp.zeros((1, BLOCK), F32)] * GROUP for _ in range(2)]
            every = range(GROUP)
            for r in range(0, quarter, tile):
                at = pl.ds(r, tile)
                a = [a_refs[m][at, :].astype(F32) for m in every]
                u = [(coef[m][0] * a[m] + coef[m][1] * a[m ^ 1]).astype(BF) for m in every]
                v = [dot(u[m], w[m]).astype(BF).astype(F32) for m in every]
                f = f_ref[at, :]
                g = []
                for m in every:
                    end = (coef[m][2] * v[m] + coef[m][3] * v[m ^ 2]).astype(BF).astype(F32)
                    recon = f * (p_refs[m][at, :].astype(F32) - 7.5)
                    g.append(((end - recon) * inv).astype(BF).astype(F32))
                for m in every:
                    ga[0][m] = ga[0][m] + jnp.sum(
                        g[m] * (coef[m][2] * v[m ^ 2] - coef[m][3] * v[m]), axis=0, keepdims=True
                    )
                q = [(coef[m][3] * g[m]).astype(BF).astype(F32) for m in every]
                dv = [(coef[m][2] * g[m] + q[m ^ 2]).astype(BF) for m in every]
                g = []
                for m in every:
                    gw[m] = gw[m] + t_dot(u[m], dv[m])
                    g.append(dot_t(dv[m], w[m]).astype(BF).astype(F32))
                for m in every:
                    ga[1][m] = ga[1][m] + jnp.sum(
                        g[m] * (coef[m][0] * a[m ^ 1] - coef[m][1] * a[m]), axis=0, keepdims=True
                    )
                q = [(coef[m][1] * g[m]).astype(BF).astype(F32) for m in every]
                for m in every:
                    outs[m][at, :] = (coef[m][0] * g[m] + q[m ^ 1]).astype(BF)
            for m in every:
                grad[m, :BLOCK, :] = gw[m]
                grad[m, BLOCK:, :] = jnp.concatenate(
                    [ga[0][m], ga[1][m], jnp.zeros((EXTRA - 2, BLOCK), F32)], axis=0
                )

        high = quarter + BLOCK + TRIG
        specs = {
            GROUP + m: pl.BlockSpec((high, BLOCK), lambda i: (0, c)) for m in range(GROUP)
        }
        return call(
            body,
            [shape((quarter, BLOCK))] * GROUP + [shape((GROUP, BLOCK + EXTRA, BLOCK), F32)],
            state[c] + packs + [factor],
            specs=specs,
            flops=3 * product,
        )

    back, partial = {}, {}
    for c in chunks:
        out = group_stage(c)
        partial[c] = out[GROUP]
        back[c] = [out[0]] + [swapped(out[m], "dim", m << shift) for m in range(1, GROUP)]

    def write_grad(out, gw, ga):
        out[:BLOCK, :] = gw
        out[BLOCK:, :] = jnp.concatenate([ga, jnp.zeros((EXTRA - 1, BLOCK), F32)], axis=0)

    grad_shape = shape((BLOCK + EXTRA, BLOCK), F32)

    def back_quarters(c, s):
        v, other, u = saves[c][s - 1]
        wide = s - 1 == local_bits

        def body(place_ref, *refs):
            d_refs = refs[:GROUP]
            u_ref, v_ref, o_ref, w_ref, trig_ref, g_out, q_out, grad = refs[GROUP:]
            w = w_ref[0].astype(BF)
            co, si = cs(trig_ref, s - 1, c)
            z = place_ref[0]
            gw = jnp.zeros((BLOCK, BLOCK), F32)
            ga = jnp.zeros((1, BLOCK), F32)
            for m in range(GROUP):
                start = pl.multiple_of(jnp.bitwise_xor(z, m) * quarter, 16)
                for r in range(0, quarter, tile):
                    d = d_refs[m][r : r + tile, :]
                    at = pl.ds(start + r, tile)
                    gw = gw + t_dot(u_ref[at, :], d)
                    g16 = dot_t(d, w).astype(BF)
                    g = g16.astype(F32)
                    g_out[at, :] = g16
                    ga = ga + jnp.sum(
                        g * (co * o_ref[at, :].astype(F32) - si * v_ref[at, :].astype(F32)),
                        axis=0,
                        keepdims=True,
                    )
                    q_out[at, :] = (si * g).astype(BF)
            write_grad(grad, gw, ga)

        specs = {0: SMEM, GROUP + 4: wspec(s, c)}
        if wide:
            specs.update({GROUP + 2: column(c), GROUP + 3: column(c)})
        return call(
            body,
            [shape((rows, BLOCK)), shape((rows, BLOCK)), grad_shape],
            [place_arr] + back[c] + [u, v, other, blocks, trig],
            specs=specs,
            flops=2 * product,
        )

    def back_middle(c, s, g, incoming):
        v, other, u = saves[c][s - 1]
        wide = s - 1 == local_bits

        def body(g_ref, i_ref, u_ref, v_ref, o_ref, w_ref, trig_ref, g_out, q_out, grad):
            w = w_ref[0].astype(BF)
            here = cs(trig_ref, s, c)[0]
            co, si = cs(trig_ref, s - 1, c)
            gw = jnp.zeros((BLOCK, BLOCK), F32)
            ga = jnp.zeros((1, BLOCK), F32)
            for r in range(0, rows, tile):
                at = pl.ds(r, tile)
                d = (here * g_ref[at, :].astype(F32) + i_ref[at, :].astype(F32)).astype(BF)
                gw = gw + t_dot(u_ref[at, :], d)
                g16 = dot_t(d, w).astype(BF)
                gf = g16.astype(F32)
                g_out[at, :] = g16
                ga = ga + jnp.sum(
                    gf * (co * o_ref[at, :].astype(F32) - si * v_ref[at, :].astype(F32)),
                    axis=0,
                    keepdims=True,
                )
                q_out[at, :] = (si * gf).astype(BF)
            write_grad(grad, gw, ga)

        specs = {5: wspec(s, c)}
        if wide:
            specs.update({3: column(c), 4: column(c)})
        return call(
            body,
            [shape((rows, BLOCK)), shape((rows, BLOCK)), grad_shape],
            [g, incoming, u, v, other, blocks, trig],
            specs=specs,
            flops=2 * product,
        )

    grads = {c: {} for c in chunks}
    flow = {}
    for c in chunks:
        g, q, grads[c][third] = back_quarters(c, third)
        flow[c] = (g, swapped(q, "dim", 1 << (third - 1 - local_bits)))
    for s in reversed(middles[1:]):
        for c in chunks:
            g, q, grads[c][s] = back_middle(c, s, *flow[c])
            flow[c] = (g, swapped(q, "dim", 1 << (s - 1 - local_bits)))

    low = local_bits + 1

    def end_body(*refs):
        g_refs, i_refs = refs[:nb], refs[nb : 2 * nb]
        u_refs = refs[2 * nb : 2 * nb + low]
        v_refs = refs[2 * nb + low : 2 * nb + low + local_bits]
        w_ref, trig_ref, grad = refs[2 * nb + low + local_bits :]
        gw = [[jnp.zeros((BLOCK, BLOCK), F32)] * nb for _ in range(low)]
        ga = [[jnp.zeros((1, BLOCK), F32)] * nb for _ in range(low)]
        w = [[w_ref[s, col(c), :].astype(BF) for c in range(nb)] for s in range(low)]
        for r in range(0, rows, tile):
            at = pl.ds(r, tile)
            d = []
            for c in range(nb):
                here = cs(trig_ref, local_bits, c)[0]
                d.append(
                    (here * g_refs[c][at, :].astype(F32) + i_refs[c][at, :].astype(F32)).astype(BF)
                )
            for s in reversed(range(low)):
                for c in range(nb):
                    gw[s][c] = gw[s][c] + t_dot(u_refs[s][at, col(c)], d[c])
                if s == 0:
                    break
                g = [dot_t(d[c], w[s][c]).astype(BF).astype(F32) for c in range(nb)]
                t = s - 1
                v = [v_refs[t][at, col(c)].astype(F32) for c in range(nb)]
                q = []
                for c in range(nb):
                    co, si = cs(trig_ref, t, c)
                    ga[t][c] = ga[t][c] + jnp.sum(
                        g[c] * (co * v[c ^ (1 << t)] - si * v[c]), axis=0, keepdims=True
                    )
                    q.append((si * g[c]).astype(BF).astype(F32))
                d = [
                    (cs(trig_ref, t, c)[0] * g[c] + q[c ^ (1 << t)]).astype(BF) for c in range(nb)
                ]
        for s in range(low):
            for c in range(nb):
                write_grad(grad.at[s * nb + c], gw[s][c], ga[s][c])

    (ends,) = call(
        end_body,
        [shape((low * nb, BLOCK + EXTRA, BLOCK), F32)],
        [flow[c][0] for c in chunks]
        + [flow[c][1] for c in chunks]
        + u0s
        + v0s
        + [blocks, trig],
        flops=6 * product,
    )

    stacked = jnp.stack([partial[c] for c in chunks], axis=1)
    arrived = [swapped(stacked[m], "dim", m << shift) for m in range(1, GROUP)]
    high = sections - low
    uppers = [(s, c) for s in range(low, third + 1) for c in chunks]

    def upper_body(*refs):
        own, others, rest, out = refs[0], refs[1:GROUP], refs[GROUP:-1], refs[-1]
        for k in range(len(uppers)):
            out[k] = rest[k][...]
        for c in range(nb):
            total = own[0, c]
            for other in others:
                total = total + other[c]
            out[len(uppers) + c] = total

    (upper,) = call(
        upper_body,
        [shape((high * nb, BLOCK + EXTRA, BLOCK), F32)],
        [stacked] + arrived + [grads[c][s] for s, c in uppers],
    )
    if nrow == 2:
        pairs = [(ends, swapped(ends, "row", 1)), (upper, swapped(upper, "row", 1))]
    else:
        pairs = [lax.psum(ends, "row"), lax.psum(upper, "row")]
        pairs = [(p, jnp.zeros_like(p)) for p in pairs]

    def final_body(e0, e1, p0, p1, bs_ref, as_ref, sign_ref, step, new, step_a, new_a):
        def get(s, c):
            k = s * nb + c
            if s < low:
                return e0[k] + e1[k]
            k -= low * nb
            return p0[k] + p1[k]

        for c in range(nb):
            angle = [None] * sections
            for s in range(sections):
                total = get(s, c)
                g = total[:BLOCK, :]
                state_new = 0.9 * bs_ref[s, col(c), :] + 0.1 * g * g
                new[s, col(c), :] = state_new
                step[s, col(c), :] = g * lax.rsqrt(state_new)
                if s == last:
                    angle[last] = total[BLOCK : BLOCK + 1, :]
                    angle[third] = total[BLOCK + 1 : BLOCK + 2, :]
                elif s >= low:
                    angle[s - 1] = total[BLOCK : BLOCK + 1, :]
                elif s < local_bits:
                    angle[s] = total[BLOCK : BLOCK + 1, :]
            g = jnp.concatenate(angle, axis=0) * sign_ref[:, col(c)]
            state_new = 0.9 * as_ref[:, col(c)] + 0.1 * g * g
            new_a[:, col(c)] = state_new
            step_a[:, col(c)] = g * lax.rsqrt(state_new)

    step, new, step_a, new_a = call(
        final_body,
        [shape(block_state.shape, F32)] * 2 + [shape(angle_state.shape, F32)] * 2,
        [*pairs[0], *pairs[1], block_state, angle_state, signs],
    )
    return step, new, step_a, new_a


def solution(mesh):
    in_specs = (
        P("row", "dim"),
        P(None, "dim", None),
        P(None, "dim"),
        P("row", "dim"),
        P("row"),
        P(),
        P(None, "dim", None),
        P(None, "dim"),
    )
    out_specs = (P(None, "dim", None), P(None, "dim", None), P(None, "dim"), P(None, "dim"))
    return jax.shard_map(local, mesh=mesh, in_specs=in_specs, out_specs=out_specs, check_vma=False)
```

time: 250 us -> 133 us (0.53)
  waiting for transfers between devices: 177 us -> 53.7 us
  starting transfers between devices: 8.21 us -> 54.8 us
  Pallas kernels: 0 us -> 15.6 us
  matrix products: 14 us -> 0 us
  between operations: 14.7 us -> 0.87 us
  other arithmetic: 14.1 us -> 0.83 us
  local copies, waits for them, and re-layouts: 16.7 us -> 6.49 us
  blocking collectives: 5 us -> 0 us
    ppermute x8 -> x27, waiting for transfers between devices: 151 us -> 53.7 us  [swapped(): return lax.ppermute(value, axis, pairs)]
    ppermute x8 -> x27, starting transfers between devices: 8.18 us -> 54.8 us  [swapped(): return lax.ppermute(value, axis, pairs)]
    psum x1 -> x0, waiting for transfers between devices: 25.4 us -> none  [local(): block_grad, angle_grad = lax.psum((block_grad, angle_grad), 'row')]
    pallas_call x0 -> x15, Pallas kernels: none -> 15.6 us  [call(): pl.pallas_call(body, grid=(1,), in_specs=whole, out_specs=[pl.BlockSpec(o...]
    dot_general x14 -> x0, matrix products: 14 us -> none  [the longest x5 7.64 us: local(): jnp.einsum('rnb,rnc->nbc', source, direction, preferred_element_type=jnp....]
    convert_element_type x10 -> x0, other arithmetic: 7.38 us -> none  [the longest x1 3.01 us: local(): upstream = cotangent.astype(jnp.float32)]
    psum x1 -> x0, blocking collectives: 5 us -> none  [local(): block_grad, angle_grad = lax.psum((block_grad, angle_grad), 'row')]
    convert_element_type x2 -> x0, local copies, waits for them, and re-layouts: 3.54 us -> none  [the longest x1 1.77 us: local(): upstream = cotangent.astype(jnp.float32)]
  transfers between devices with their start and end apart: 9 -> 27, of which waited for: 8 -> 14; matrix products, arithmetic and copies ran while one was open for 3% -> 0% of each run, Pallas kernels for 0% -> 9%
where the time goes in v1:
time: 133 us; the launch traced here: 132 us
  starting transfers between devices  54.8 us (41%)
  waiting for transfers between devices  53.7 us (40%)
  Pallas kernels  15.6 us (12%)
  local copies, waits for them, and re-layouts  6.49 us (5%)
    ppermute x27, starting transfers between devices, swapped(): return lax.ppermute(value, axis, pairs)  54.8 us
    ppermute x27, waiting for transfers between devices, swapped(): return lax.ppermute(value, axis, pairs)  53.7 us
    pallas_call x15, Pallas kernels, call(): pl.pallas_call(body, grid=(1,), in_specs=whole, out_specs=[pl.BlockSpec(o...  15.6 us
    unnamed x34, local copies, waits for them, and re-layouts  6.33 us
  transfers between devices with their start and end apart: 27, of which 14 were waited for; matrix products, arithmetic and copies ran while one was open for 0% of the time, Pallas kernels for 9%

profile of v1, /device:TPU:0, one launch (start us, length us, event | category | flops | bytes accessed | tf_op | source)
XLA Modules:
  0.0 132.3 jit_solution(4884355695877828477)
XLA Ops:
  3.7 1.7 %shard_map.111 = (bf16[1664,256]{1,0:T(8,128)(2,1)S(1)}, bf16[1664,256]{1,0:T(8,128)(2,1)S(1)}, bf16[1664,256]{1,0:T(8,128)(2,1)S(1)}) custom-call(bf16[1664,256]{1,0:T(8,128)(2,1)S(1)} %copy-done.2, f32[5,256,128]{2,1,0:T(8,128)S(1)} %copy-done, f32[10,256]{1,0:T(8,128)S(1)} %pad_maximum_fusion.1.trig_ref.refs_8_), custom_call_target="tpu_custom_call" | custom-call | flops 218103808 | bytes 4073472 | tf_op jit(solution)/shard_map/pallas_call | solution.py:50
  7.7 2.0 %collective-permute-done.o_ref = bf16[1664,256]{1,0:T(8,128)(2,1)S(1)} collective-permute-done((bf16[1664,256]{1,0:T(8,128)(2,1)S(1)}, bf16[1664,256]{1,0:T(8,128)(2,1)S(1)}, u32[]{:S(2)}, u32[]{:S(2)}) %collective-permute-start) | collective-permute-done | bytes 852000 | tf_op jit(solution)/shard_map/ppermute | solution.py:20
  10.9 2.9 %collective-permute-start.12 = (bf16[1664,128]{1,0:T(8,128)(2,1)}, bf16[1664,128]{1,0:T(8,128)(2,1)}, u32[]{:S(2)}, u32[]{:S(2)}) collective-permute-start(bf16[1664,128]{1,0:T(8,128)(2,1)} %get-tuple-element.68.v_ref.refs_5_), channel_id=1, source_target_pairs={{0,4},{2,6},{4,0},{6,2},{8,12},{10,14},{12,8},{14,10},{16,20},{18,... | collective-permute-start | bytes 1277960 | tf_op jit(solution)/shard_map/ppermute | solution.py:20
  17.4 1.8 %collective-permute-start.5 = (bf16[560,256]{1,0:T(8,128)(2,1)S(1)}, bf16[560,256]{1,0:T(8,128)(2,1)S(1)}, u32[]{:S(2)}, u32[]{:S(2)}) collective-permute-start(bf16[560,256]{1,0:T(8,128)(2,1)S(1)} %get-tuple-element.55), channel_id=1, source_target_pairs={{0,8},{2,10},{4,12},{6,14},{8,0},{10,2},{12,4},{14,6},{16,24},{18,... | collective-permute-start | bytes 860168 | tf_op jit(solution)/shard_map/ppermute | solution.py:20
  19.2 2.6 %collective-permute-start.6 = (bf16[560,256]{1,0:T(8,128)(2,1)S(1)}, bf16[560,256]{1,0:T(8,128)(2,1)S(1)}, u32[]{:S(2)}, u32[]{:S(2)}) collective-permute-start(bf16[560,256]{1,0:T(8,128)(2,1)S(1)} %get-tuple-element.56), channel_id=1, source_target_pairs={{0,16},{2,18},{4,20},{6,22},{8,24},{10,26},{12,28},{14,30},{16,0},... | collective-permute-start | bytes 860168 | tf_op jit(solution)/shard_map/ppermute | solution.py:20
  21.8 2.9 %collective-permute-done.12.o_ref.refs_6_ = bf16[1664,128]{1,0:T(8,128)(2,1)} collective-permute-done((bf16[1664,128]{1,0:T(8,128)(2,1)}, bf16[1664,128]{1,0:T(8,128)(2,1)}, u32[]{:S(2)}, u32[]{:S(2)}) %collective-permute-start.12) | collective-permute-done | bytes 426016 | tf_op jit(solution)/shard_map/ppermute | solution.py:20
  26.3 2.2 %collective-permute-start.13 = (bf16[416,128]{1,0:T(8,128)(2,1)S(1)}, bf16[416,128]{1,0:T(8,128)(2,1)S(1)}, u32[]{:S(2)}, u32[]{:S(2)}) collective-permute-start(bf16[416,128]{1,0:T(8,128)(2,1)S(1)} %get-tuple-element.70), channel_id=1, source_target_pairs={{0,8},{2,10},{4,12},{6,14},{8,0},{10,2},{12,4},{14,6},{16,24},{18,... | collective-permute-start | bytes 319496 | tf_op jit(solution)/shard_map/ppermute | solution.py:20
  28.5 4.0 %collective-permute-done.5.refs_5_ = bf16[560,256]{1,0:T(8,128)(2,1)S(1)} collective-permute-done((bf16[560,256]{1,0:T(8,128)(2,1)S(1)}, bf16[560,256]{1,0:T(8,128)(2,1)S(1)}, u32[]{:S(2)}, u32[]{:S(2)}) %collective-permute-start.5) | collective-permute-done | bytes 286752 | tf_op jit(solution)/shard_map/ppermute | solution.py:20
  32.4 2.0 %collective-permute-start.14 = (bf16[416,128]{1,0:T(8,128)(2,1)S(1)}, bf16[416,128]{1,0:T(8,128)(2,1)S(1)}, u32[]{:S(2)}, u32[]{:S(2)}) collective-permute-start(bf16[416,128]{1,0:T(8,128)(2,1)S(1)} %get-tuple-element.71), channel_id=1, source_target_pairs={{0,16},{2,18},{4,20},{6,22},{8,24},{10,26},{12,28},{14,30},{16,0},... | collective-permute-start | bytes 319496 | tf_op jit(solution)/shard_map/ppermute | solution.py:20
  34.4 2.7 %collective-permute-start.15 = (bf16[416,128]{1,0:T(8,128)(2,1)S(1)}, bf16[416,128]{1,0:T(8,128)(2,1)S(1)}, u32[]{:S(2)}, u32[]{:S(2)}) collective-permute-start(bf16[416,128]{1,0:T(8,128)(2,1)S(1)} %get-tuple-element.72), channel_id=1, source_target_pairs={{0,24},{2,26},{4,28},{6,30},{8,16},{10,18},{12,20},{14,22},{16,8},... | collective-permute-start | bytes 319496 | tf_op jit(solution)/shard_map/ppermute | solution.py:20
  37.5 5.5 %collective-permute-done.6.refs_6_ = bf16[560,256]{1,0:T(8,128)(2,1)S(1)} collective-permute-done((bf16[560,256]{1,0:T(8,128)(2,1)S(1)}, bf16[560,256]{1,0:T(8,128)(2,1)S(1)}, u32[]{:S(2)}, u32[]{:S(2)}) %collective-permute-start.6) | collective-permute-done | bytes 286752 | tf_op jit(solution)/shard_map/ppermute | solution.py:20
  43.0 2.2 %collective-permute-start.2 = (bf16[416,128]{1,0:T(8,128)(2,1)S(1)}, bf16[416,128]{1,0:T(8,128)(2,1)S(1)}, u32[]{:S(2)}, u32[]{:S(2)}) collective-permute-start(bf16[416,128]{1,0:T(8,128)(2,1)S(1)} %get-tuple-element.51), channel_id=1, source_target_pairs={{0,8},{2,10},{4,12},{6,14},{8,0},{10,2},{12,4},{14,6},{16,24},{18,... | collective-permute-start | bytes 319496 | tf_op jit(solution)/shard_map/ppermute | solution.py:20
  45.2 9.3 %collective-permute-start.3 = (bf16[416,128]{1,0:T(8,128)(2,1)S(1)}, bf16[416,128]{1,0:T(8,128)(2,1)S(1)}, u32[]{:S(2)}, u32[]{:S(2)}) collective-permute-start(bf16[416,128]{1,0:T(8,128)(2,1)S(1)} %get-tuple-element.52), channel_id=1, source_target_pairs={{0,16},{2,18},{4,20},{6,22},{8,24},{10,26},{12,28},{14,30},{16,0},... | collective-permute-start | bytes 319496 | tf_op jit(solution)/shard_map/ppermute | solution.py:20
  55.8 1.6 %collective-permute-done.14.refs_2_ = bf16[416,128]{1,0:T(8,128)(2,1)S(1)} collective-permute-done((bf16[416,128]{1,0:T(8,128)(2,1)S(1)}, bf16[416,128]{1,0:T(8,128)(2,1)S(1)}, u32[]{:S(2)}, u32[]{:S(2)}) %collective-permute-start.14) | collective-permute-done | bytes 106528 | tf_op jit(solution)/shard_map/ppermute | solution.py:20
  58.9 6.5 %collective-permute-start.16 = (bf16[416,128]{1,0:T(8,128)(2,1)S(1)}, bf16[416,128]{1,0:T(8,128)(2,1)S(1)}, u32[]{:S(2)}, u32[]{:S(2)}) collective-permute-start(bf16[416,128]{1,0:T(8,128)(2,1)S(1)} %get-tuple-element.74), channel_id=1, source_target_pairs={{0,8},{2,10},{4,12},{6,14},{8,0},{10,2},{12,4},{14,6},{16,24},{18,... | collective-permute-start | bytes 319496 | tf_op jit(solution)/shard_map/ppermute | solution.py:20
  65.4 2.1 %collective-permute-start.17 = (bf16[416,128]{1,0:T(8,128)(2,1)S(1)}, bf16[416,128]{1,0:T(8,128)(2,1)S(1)}, u32[]{:S(2)}, u32[]{:S(2)}) collective-permute-start(bf16[416,128]{1,0:T(8,128)(2,1)S(1)} %get-tuple-element.75), channel_id=1, source_target_pairs={{0,16},{2,18},{4,20},{6,22},{8,24},{10,26},{12,28},{14,30},{16,0},... | collective-permute-start | bytes 319496 | tf_op jit(solution)/shard_map/ppermute | solution.py:20
  71.0 2.4 %collective-permute-start.9 = (bf16[416,128]{1,0:T(8,128)(2,1)S(1)}, bf16[416,128]{1,0:T(8,128)(2,1)S(1)}, u32[]{:S(2)}, u32[]{:S(2)}) collective-permute-start(bf16[416,128]{1,0:T(8,128)(2,1)S(1)} %get-tuple-element.61), channel_id=1, source_target_pairs={{0,16},{2,18},{4,20},{6,22},{8,24},{10,26},{12,28},{14,30},{16,0},... | collective-permute-start | bytes 319496 | tf_op jit(solution)/shard_map/ppermute | solution.py:20
  74.9 2.4 %collective-permute-done.18.refs_3_ = bf16[416,128]{1,0:T(8,128)(2,1)S(1)} collective-permute-done((bf16[416,128]{1,0:T(8,128)(2,1)S(1)}, bf16[416,128]{1,0:T(8,128)(2,1)S(1)}, u32[]{:S(2)}, u32[]{:S(2)}) %collective-permute-start.18) | collective-permute-done | bytes 106528 | tf_op jit(solution)/shard_map/ppermute | solution.py:20
  77.3 1.7 %shard_map.121 = (bf16[1664,128]{1,0:T(8,128)(2,1)S(1)}, bf16[1664,128]{1,0:T(8,128)(2,1)S(1)}, f32[136,128]{1,0:T(8,128)S(1)}) custom-call(s32[1]{0:T(128)} %bitcast.place_ref, bf16[416,128]{1,0:T(8,128)(2,1)S(1)} %get-tuple-element.73.refs_0_, bf16[416,128]{1,0:T(8,128)(2,1)S(1)} %collective-permute-done.16.refs_1_, ...), custom_call_target="tpu_custom_call" | custom-call | flops 109051904 | bytes 3291140 | tf_op jit(solution)/shard_map/pallas_call | solution.py:50
  79.0 1.8 %collective-permute-start.19 = (bf16[1664,128]{1,0:T(8,128)(2,1)S(1)}, bf16[1664,128]{1,0:T(8,128)(2,1)S(1)}, u32[]{:S(2)}, u32[]{:S(2)}) collective-permute-start(bf16[1664,128]{1,0:T(8,128)(2,1)S(1)} %get-tuple-element.79), channel_id=1, source_target_pairs={{0,4},{2,6},{4,0},{6,2},{8,12},{10,14},{12,8},{14,10},{16,20},{18,... | collective-permute-start | bytes 1277960 | tf_op jit(solution)/shard_map/ppermute | solution.py:20
  80.7 1.6 %collective-permute-done.9.refs_2_ = bf16[416,128]{1,0:T(8,128)(2,1)S(1)} collective-permute-done((bf16[416,128]{1,0:T(8,128)(2,1)S(1)}, bf16[416,128]{1,0:T(8,128)(2,1)S(1)}, u32[]{:S(2)}, u32[]{:S(2)}) %collective-permute-start.9) | collective-permute-done | bytes 106528 | tf_op jit(solution)/shard_map/ppermute | solution.py:20
  83.0 1.6 %collective-permute-start.11 = (bf16[1664,128]{1,0:T(8,128)(2,1)S(1)}, bf16[1664,128]{1,0:T(8,128)(2,1)S(1)}, u32[]{:S(2)}, u32[]{:S(2)}) collective-permute-start(bf16[1664,128]{1,0:T(8,128)(2,1)S(1)} %get-tuple-element.65), channel_id=1, source_target_pairs={{0,4},{2,6},{4,0},{6,2},{8,12},{10,14},{12,8},{14,10},{16,20},{18,... | collective-permute-start | bytes 1277960 | tf_op jit(solution)/shard_map/ppermute | solution.py:20
  84.5 5.1 %collective-permute-done.19.i_ref = bf16[1664,128]{1,0:T(8,128)(2,1)S(1)} collective-permute-done((bf16[1664,128]{1,0:T(8,128)(2,1)S(1)}, bf16[1664,128]{1,0:T(8,128)(2,1)S(1)}, u32[]{:S(2)}, u32[]{:S(2)}) %collective-permute-start.19) | collective-permute-done | bytes 426016 | tf_op jit(solution)/shard_map/ppermute | solution.py:20
  90.4 3.9 %collective-permute-done.11.i_ref = bf16[1664,128]{1,0:T(8,128)(2,1)S(1)} collective-permute-done((bf16[1664,128]{1,0:T(8,128)(2,1)S(1)}, bf16[1664,128]{1,0:T(8,128)(2,1)S(1)}, u32[]{:S(2)}, u32[]{:S(2)}) %collective-permute-start.11) | collective-permute-done | bytes 426016 | tf_op jit(solution)/shard_map/ppermute | solution.py:20
  95.0 5.1 %collective-permute-start.25 = (f32[2,136,128]{2,1,0:T(8,128)S(1)}, f32[2,136,128]{2,1,0:T(8,128)S(1)}, u32[]{:S(2)}, u32[]{:S(2)}) collective-permute-start(f32[2,136,128]{2,1,0:T(8,128)S(1)} %get-tuple-element.92), channel_id=1, source_target_pairs={{0,24},{2,26},{4,28},{6,30},{8,16},{10,18},{12,20},{14,22},{16,8},... | collective-permute-start | bytes 417800 | tf_op jit(solution)/shard_map/ppermute | solution.py:20
  100.1 1.9 %collective-permute-start.23 = (f32[2,136,128]{2,1,0:T(8,128)S(1)}, f32[2,136,128]{2,1,0:T(8,128)S(1)}, u32[]{:S(2)}, u32[]{:S(2)}) collective-permute-start(f32[2,136,128]{2,1,0:T(8,128)S(1)} %get-tuple-element.93), channel_id=1, source_target_pairs={{0,8},{2,10},{4,12},{6,14},{8,0},{10,2},{12,4},{14,6},{16,24},{18,... | collective-permute-start | bytes 417800 | tf_op jit(solution)/shard_map/ppermute | solution.py:20
  102.1 2.5 %collective-permute-done.25.refs_3_ = f32[2,136,128]{2,1,0:T(8,128)S(1)} collective-permute-done((f32[2,136,128]{2,1,0:T(8,128)S(1)}, f32[2,136,128]{2,1,0:T(8,128)S(1)}, u32[]{:S(2)}, u32[]{:S(2)}) %collective-permute-start.25) | collective-permute-done | bytes 139296 | tf_op jit(solution)/shard_map/ppermute | solution.py:20
  104.6 2.8 %collective-permute-done.23.refs_1_ = f32[2,136,128]{2,1,0:T(8,128)S(1)} collective-permute-done((f32[2,136,128]{2,1,0:T(8,128)S(1)}, f32[2,136,128]{2,1,0:T(8,128)S(1)}, u32[]{:S(2)}, u32[]{:S(2)}) %collective-permute-start.23) | collective-permute-done | bytes 139296 | tf_op jit(solution)/shard_map/ppermute | solution.py:20
  107.4 5.9 %collective-permute-done.24.refs_2_ = f32[2,136,128]{2,1,0:T(8,128)S(1)} collective-permute-done((f32[2,136,128]{2,1,0:T(8,128)S(1)}, f32[2,136,128]{2,1,0:T(8,128)S(1)}, u32[]{:S(2)}, u32[]{:S(2)}) %collective-permute-start.24) | collective-permute-done | bytes 139296 | tf_op jit(solution)/shard_map/ppermute | solution.py:20
  115.0 2.2 %shard_map.123.e0 = f32[4,136,128]{2,1,0:T(8,128)S(1)} custom-call(bf16[1664,128]{1,0:T(8,128)(2,1)S(1)} %get-tuple-element.67.refs_0_, bf16[1664,128]{1,0:T(8,128)(2,1)S(1)} %get-tuple-element.81.refs_1_, bf16[1664,128]{1,0:T(8,128)(2,1)S(1)} %collective-permute-done.20.refs_2_, bf16[1664,128]{1,0:T(8,128)(2,1)S(1)} %collective-permute-done.21.refs_3_, ...), custom_call_target="tpu_custom_call" | custom-call | flops 327155712 | bytes 5203968 | tf_op jit(solution)/shard_map/pallas_call | solution.py:50
  117.9 8.1 %collective-permute-done.26.p1 = f32[6,136,128]{2,1,0:T(8,128)S(1)} collective-permute-done((f32[6,136,128]{2,1,0:T(8,128)S(1)}, f32[6,136,128]{2,1,0:T(8,128)S(1)}, u32[]{:S(2)}, u32[]{:S(2)}) %collective-permute-start.26) | collective-permute-done | bytes 417824 | tf_op jit(solution)/shard_map/ppermute | solution.py:20
  126.0 5.1 %collective-permute-done.22.e1 = f32[4,136,128]{2,1,0:T(8,128)S(1)} collective-permute-done((f32[4,136,128]{2,1,0:T(8,128)S(1)}, f32[4,136,128]{2,1,0:T(8,128)S(1)}, u32[]{:S(2)}, u32[]{:S(2)}) %collective-permute-start.22) | collective-permute-done | bytes 278560 | tf_op jit(solution)/shard_map/ppermute | solution.py:20
  (78 shorter events, 25.1 us)
Async XLA Ops:
  7.3 2.5 %collective-permute-start = (bf16[1664,256]{1,0:T(8,128)(2,1)S(1)}, bf16[1664,256]{1,0:T(8,128)(2,1)S(1)}, u32[]{:S(2)}, u32[]{:S(2)}) collective-permute-start(bf16[1664,256]{1,0:T(8,128)(2,1)S(1)} %get-tuple-element.48.v_ref), channel_id=1, source_target_pairs={{0,2},{2,0},{4,6},{6,4},{8,10},{10,8},{12,14},{14,12},{16,18},{18,... | collective-permute-start | bytes 2555912 | tf_op jit(solution)/shard_map/ppermute | solution.py:20
  10.9 13.8 %collective-permute-start.12 = (bf16[1664,128]{1,0:T(8,128)(2,1)}, bf16[1664,128]{1,0:T(8,128)(2,1)}, u32[]{:S(2)}, u32[]{:S(2)}) collective-permute-start(bf16[1664,128]{1,0:T(8,128)(2,1)} %get-tuple-element.68.v_ref.refs_5_), channel_id=1, source_target_pairs={{0,4},{2,6},{4,0},{6,2},{8,12},{10,14},{12,8},{14,10},{16,20},{18,... | collective-permute-start | bytes 1277960 | tf_op jit(solution)/shard_map/ppermute | solution.py:20
  15.0 19.4 %collective-permute-start.1 = (bf16[1664,128]{1,0:T(8,128)(2,1)S(1)}, bf16[1664,128]{1,0:T(8,128)(2,1)S(1)}, u32[]{:S(2)}, u32[]{:S(2)}) collective-permute-start(bf16[1664,128]{1,0:T(8,128)(2,1)S(1)} %get-tuple-element.49.v_ref.refs_5_), channel_id=1, source_target_pairs={{0,4},{2,6},{4,0},{6,2},{8,12},{10,14},{12,8},{14,10},{16,20},{18,... | collective-permute-start | bytes 1277960 | tf_op jit(solution)/shard_map/ppermute | solution.py:20
  17.4 15.1 %collective-permute-start.5 = (bf16[560,256]{1,0:T(8,128)(2,1)S(1)}, bf16[560,256]{1,0:T(8,128)(2,1)S(1)}, u32[]{:S(2)}, u32[]{:S(2)}) collective-permute-start(bf16[560,256]{1,0:T(8,128)(2,1)S(1)} %get-tuple-element.55), channel_id=1, source_target_pairs={{0,8},{2,10},{4,12},{6,14},{8,0},{10,2},{12,4},{14,6},{16,24},{18,... | collective-permute-start | bytes 860168 | tf_op jit(solution)/shard_map/ppermute | solution.py:20
  19.2 23.8 %collective-permute-start.6 = (bf16[560,256]{1,0:T(8,128)(2,1)S(1)}, bf16[560,256]{1,0:T(8,128)(2,1)S(1)}, u32[]{:S(2)}, u32[]{:S(2)}) collective-permute-start(bf16[560,256]{1,0:T(8,128)(2,1)S(1)} %get-tuple-element.56), channel_id=1, source_target_pairs={{0,16},{2,18},{4,20},{6,22},{8,24},{10,26},{12,28},{14,30},{16,0},... | collective-permute-start | bytes 860168 | tf_op jit(solution)/shard_map/ppermute | solution.py:20
  21.8 23.4 %collective-permute-start.7 = (bf16[560,256]{1,0:T(8,128)(2,1)S(1)}, bf16[560,256]{1,0:T(8,128)(2,1)S(1)}, u32[]{:S(2)}, u32[]{:S(2)}) collective-permute-start(bf16[560,256]{1,0:T(8,128)(2,1)S(1)} %get-tuple-element.57), channel_id=1, source_target_pairs={{0,24},{2,26},{4,28},{6,30},{8,16},{10,18},{12,20},{14,22},{16,8},... | collective-permute-start | bytes 860168 | tf_op jit(solution)/shard_map/ppermute | solution.py:20
  26.3 28.2 %collective-permute-start.13 = (bf16[416,128]{1,0:T(8,128)(2,1)S(1)}, bf16[416,128]{1,0:T(8,128)(2,1)S(1)}, u32[]{:S(2)}, u32[]{:S(2)}) collective-permute-start(bf16[416,128]{1,0:T(8,128)(2,1)S(1)} %get-tuple-element.70), channel_id=1, source_target_pairs={{0,8},{2,10},{4,12},{6,14},{8,0},{10,2},{12,4},{14,6},{16,24},{18,... | collective-permute-start | bytes 319496 | tf_op jit(solution)/shard_map/ppermute | solution.py:20
  32.4 25.0 %collective-permute-start.14 = (bf16[416,128]{1,0:T(8,128)(2,1)S(1)}, bf16[416,128]{1,0:T(8,128)(2,1)S(1)}, u32[]{:S(2)}, u32[]{:S(2)}) collective-permute-start(bf16[416,128]{1,0:T(8,128)(2,1)S(1)} %get-tuple-element.71), channel_id=1, source_target_pairs={{0,16},{2,18},{4,20},{6,22},{8,24},{10,26},{12,28},{14,30},{16,0},... | collective-permute-start | bytes 319496 | tf_op jit(solution)/shard_map/ppermute | solution.py:20
  34.4 23.1 %collective-permute-start.15 = (bf16[416,128]{1,0:T(8,128)(2,1)S(1)}, bf16[416,128]{1,0:T(8,128)(2,1)S(1)}, u32[]{:S(2)}, u32[]{:S(2)}) collective-permute-start(bf16[416,128]{1,0:T(8,128)(2,1)S(1)} %get-tuple-element.72), channel_id=1, source_target_pairs={{0,24},{2,26},{4,28},{6,30},{8,16},{10,18},{12,20},{14,22},{16,8},... | collective-permute-start | bytes 319496 | tf_op jit(solution)/shard_map/ppermute | solution.py:20
  43.0 24.5 %collective-permute-start.2 = (bf16[416,128]{1,0:T(8,128)(2,1)S(1)}, bf16[416,128]{1,0:T(8,128)(2,1)S(1)}, u32[]{:S(2)}, u32[]{:S(2)}) collective-permute-start(bf16[416,128]{1,0:T(8,128)(2,1)S(1)} %get-tuple-element.51), channel_id=1, source_target_pairs={{0,8},{2,10},{4,12},{6,14},{8,0},{10,2},{12,4},{14,6},{16,24},{18,... | collective-permute-start | bytes 319496 | tf_op jit(solution)/shard_map/ppermute | solution.py:20
  45.2 23.7 %collective-permute-start.3 = (bf16[416,128]{1,0:T(8,128)(2,1)S(1)}, bf16[416,128]{1,0:T(8,128)(2,1)S(1)}, u32[]{:S(2)}, u32[]{:S(2)}) collective-permute-start(bf16[416,128]{1,0:T(8,128)(2,1)S(1)} %get-tuple-element.52), channel_id=1, source_target_pairs={{0,16},{2,18},{4,20},{6,22},{8,24},{10,26},{12,28},{14,30},{16,0},... | collective-permute-start | bytes 319496 | tf_op jit(solution)/shard_map/ppermute | solution.py:20
  54.5 14.4 %collective-permute-start.4 = (bf16[416,128]{1,0:T(8,128)(2,1)S(1)}, bf16[416,128]{1,0:T(8,128)(2,1)S(1)}, u32[]{:S(2)}, u32[]{:S(2)}) collective-permute-start(bf16[416,128]{1,0:T(8,128)(2,1)S(1)} %get-tuple-element.53), channel_id=1, source_target_pairs={{0,24},{2,26},{4,28},{6,30},{8,16},{10,18},{12,20},{14,22},{16,8},... | collective-permute-start | bytes 319496 | tf_op jit(solution)/shard_map/ppermute | solution.py:20
  58.9 14.5 %collective-permute-start.16 = (bf16[416,128]{1,0:T(8,128)(2,1)S(1)}, bf16[416,128]{1,0:T(8,128)(2,1)S(1)}, u32[]{:S(2)}, u32[]{:S(2)}) collective-permute-start(bf16[416,128]{1,0:T(8,128)(2,1)S(1)} %get-tuple-element.74), channel_id=1, source_target_pairs={{0,8},{2,10},{4,12},{6,14},{8,0},{10,2},{12,4},{14,6},{16,24},{18,... | collective-permute-start | bytes 319496 | tf_op jit(solution)/shard_map/ppermute | solution.py:20
  65.4 9.5 %collective-permute-start.17 = (bf16[416,128]{1,0:T(8,128)(2,1)S(1)}, bf16[416,128]{1,0:T(8,128)(2,1)S(1)}, u32[]{:S(2)}, u32[]{:S(2)}) collective-permute-start(bf16[416,128]{1,0:T(8,128)(2,1)S(1)} %get-tuple-element.75), channel_id=1, source_target_pairs={{0,16},{2,18},{4,20},{6,22},{8,24},{10,26},{12,28},{14,30},{16,0},... | collective-permute-start | bytes 319496 | tf_op jit(solution)/shard_map/ppermute | solution.py:20
  67.5 9.7 %collective-permute-start.18 = (bf16[416,128]{1,0:T(8,128)(2,1)S(1)}, bf16[416,128]{1,0:T(8,128)(2,1)S(1)}, u32[]{:S(2)}, u32[]{:S(2)}) collective-permute-start(bf16[416,128]{1,0:T(8,128)(2,1)S(1)} %get-tuple-element.76), channel_id=1, source_target_pairs={{0,24},{2,26},{4,28},{6,30},{8,16},{10,18},{12,20},{14,22},{16,8},... | collective-permute-start | bytes 319496 | tf_op jit(solution)/shard_map/ppermute | solution.py:20
  70.4 10.3 %collective-permute-start.8 = (bf16[416,128]{1,0:T(8,128)(2,1)S(1)}, bf16[416,128]{1,0:T(8,128)(2,1)S(1)}, u32[]{:S(2)}, u32[]{:S(2)}) collective-permute-start(bf16[416,128]{1,0:T(8,128)(2,1)S(1)} %get-tuple-element.60), channel_id=1, source_target_pairs={{0,8},{2,10},{4,12},{6,14},{8,0},{10,2},{12,4},{14,6},{16,24},{18,... | collective-permute-start | bytes 319496 | tf_op jit(solution)/shard_map/ppermute | solution.py:20
  71.0 11.4 %collective-permute-start.9 = (bf16[416,128]{1,0:T(8,128)(2,1)S(1)}, bf16[416,128]{1,0:T(8,128)(2,1)S(1)}, u32[]{:S(2)}, u32[]{:S(2)}) collective-permute-start(bf16[416,128]{1,0:T(8,128)(2,1)S(1)} %get-tuple-element.61), channel_id=1, source_target_pairs={{0,16},{2,18},{4,20},{6,22},{8,24},{10,26},{12,28},{14,30},{16,0},... | collective-permute-start | bytes 319496 | tf_op jit(solution)/shard_map/ppermute | solution.py:20
  73.5 8.9 %collective-permute-start.10 = (bf16[416,128]{1,0:T(8,128)(2,1)S(1)}, bf16[416,128]{1,0:T(8,128)(2,1)S(1)}, u32[]{:S(2)}, u32[]{:S(2)}) collective-permute-start(bf16[416,128]{1,0:T(8,128)(2,1)S(1)} %get-tuple-element.62), channel_id=1, source_target_pairs={{0,24},{2,26},{4,28},{6,30},{8,16},{10,18},{12,20},{14,22},{16,8},... | collective-permute-start | bytes 319496 | tf_op jit(solution)/shard_map/ppermute | solution.py:20
  79.0 10.7 %collective-permute-start.19 = (bf16[1664,128]{1,0:T(8,128)(2,1)S(1)}, bf16[1664,128]{1,0:T(8,128)(2,1)S(1)}, u32[]{:S(2)}, u32[]{:S(2)}) collective-permute-start(bf16[1664,128]{1,0:T(8,128)(2,1)S(1)} %get-tuple-element.79), channel_id=1, source_target_pairs={{0,4},{2,6},{4,0},{6,2},{8,12},{10,14},{12,8},{14,10},{16,20},{18,... | collective-permute-start | bytes 1277960 | tf_op jit(solution)/shard_map/ppermute | solution.py:20
  83.0 11.3 %collective-permute-start.11 = (bf16[1664,128]{1,0:T(8,128)(2,1)S(1)}, bf16[1664,128]{1,0:T(8,128)(2,1)S(1)}, u32[]{:S(2)}, u32[]{:S(2)}) collective-permute-start(bf16[1664,128]{1,0:T(8,128)(2,1)S(1)} %get-tuple-element.65), channel_id=1, source_target_pairs={{0,4},{2,6},{4,0},{6,2},{8,12},{10,14},{12,8},{14,10},{16,20},{18,... | collective-permute-start | bytes 1277960 | tf_op jit(solution)/shard_map/ppermute | solution.py:20
  90.3 24.7 %collective-permute-start.21 = (bf16[1664,128]{1,0:T(8,128)(2,1)S(1)}, bf16[1664,128]{1,0:T(8,128)(2,1)S(1)}, u32[]{:S(2)}, u32[]{:S(2)}) collective-permute-start(bf16[1664,128]{1,0:T(8,128)(2,1)S(1)} %get-tuple-element.83), channel_id=1, source_target_pairs={{0,2},{2,0},{4,6},{6,4},{8,10},{10,8},{12,14},{14,12},{16,18},{18,... | collective-permute-start | bytes 1277960 | tf_op jit(solution)/shard_map/ppermute | solution.py:20
  94.9 20.1 %collective-permute-start.20 = (bf16[1664,128]{1,0:T(8,128)(2,1)S(1)}, bf16[1664,128]{1,0:T(8,128)(2,1)S(1)}, u32[]{:S(2)}, u32[]{:S(2)}) collective-permute-start(bf16[1664,128]{1,0:T(8,128)(2,1)S(1)} %get-tuple-element.82), channel_id=1, source_target_pairs={{0,2},{2,0},{4,6},{6,4},{8,10},{10,8},{12,14},{14,12},{16,18},{18,... | collective-permute-start | bytes 1277960 | tf_op jit(solution)/shard_map/ppermute | solution.py:20
  95.0 20.0 %copy-start.3 = (bf16[1664,256]{1,0:T(8,128)(2,1)S(1)}, bf16[1664,256]{1,0:T(8,128)(2,1)}, u32[]{:S(2)}) copy-start(bf16[1664,256]{1,0:T(8,128)(2,1)} %refs_4_.1) | copy-start | bytes 2555908
  95.0 20.0 %copy-start.6 = (bf16[1664,256]{1,0:T(8,128)(2,1)S(1)}, bf16[1664,256]{1,0:T(8,128)(2,1)}, u32[]{:S(2)}) copy-start(bf16[1664,256]{1,0:T(8,128)(2,1)} %copy-done.5) | copy-start | bytes 2555908
  95.0 20.0 %copy-start.8 = (bf16[1664,256]{1,0:T(8,128)(2,1)S(1)}, bf16[1664,256]{1,0:T(8,128)(2,1)}, u32[]{:S(2)}) copy-start(bf16[1664,256]{1,0:T(8,128)(2,1)} %copy-done.7) | copy-start | bytes 2555908
  95.0 9.6 %collective-permute-start.25 = (f32[2,136,128]{2,1,0:T(8,128)S(1)}, f32[2,136,128]{2,1,0:T(8,128)S(1)}, u32[]{:S(2)}, u32[]{:S(2)}) collective-permute-start(f32[2,136,128]{2,1,0:T(8,128)S(1)} %get-tuple-element.92), channel_id=1, source_target_pairs={{0,24},{2,26},{4,28},{6,30},{8,16},{10,18},{12,20},{14,22},{16,8},... | collective-permute-start | bytes 417800 | tf_op jit(solution)/shard_map/ppermute | solution.py:20
  100.1 7.3 %collective-permute-start.23 = (f32[2,136,128]{2,1,0:T(8,128)S(1)}, f32[2,136,128]{2,1,0:T(8,128)S(1)}, u32[]{:S(2)}, u32[]{:S(2)}) collective-permute-start(f32[2,136,128]{2,1,0:T(8,128)S(1)} %get-tuple-element.93), channel_id=1, source_target_pairs={{0,8},{2,10},{4,12},{6,14},{8,0},{10,2},{12,4},{14,6},{16,24},{18,... | collective-permute-start | bytes 417800 | tf_op jit(solution)/shard_map/ppermute | solution.py:20
  102.1 11.3 %collective-permute-start.24 = (f32[2,136,128]{2,1,0:T(8,128)S(1)}, f32[2,136,128]{2,1,0:T(8,128)S(1)}, u32[]{:S(2)}, u32[]{:S(2)}) collective-permute-start(f32[2,136,128]{2,1,0:T(8,128)S(1)} %get-tuple-element.94), channel_id=1, source_target_pairs={{0,16},{2,18},{4,20},{6,22},{8,24},{10,26},{12,28},{14,30},{16,0},... | collective-permute-start | bytes 417800 | tf_op jit(solution)/shard_map/ppermute | solution.py:20
  113.4 12.6 %collective-permute-start.26 = (f32[6,136,128]{2,1,0:T(8,128)S(1)}, f32[6,136,128]{2,1,0:T(8,128)S(1)}, u32[]{:S(2)}, u32[]{:S(2)}) collective-permute-start(f32[6,136,128]{2,1,0:T(8,128)S(1)} %shard_map.124.p0), channel_id=1, source_target_pairs={{0,1},{1,0},{2,3},{3,2},{4,5},{5,4},{6,7},{7,6},{8,9},{9,8},{10,11... | collective-permute-start | bytes 1253384 | tf_op jit(solution)/shard_map/ppermute | solution.py:20
  115.0 16.1 %copy-start.9 = (f32[5,256,128]{2,1,0:T(8,128)S(1)}, f32[5,256,128]{2,1,0:T(8,128)}, u32[]{:S(2)}) copy-start(f32[5,256,128]{2,1,0:T(8,128)} %bs_ref.1) | copy-start | bytes 1966084
  115.0 16.1 %copy-start.14 = (f32[5,256]{1,0:T(8,128)S(1)}, f32[5,256]{1,0:T(8,128)}, u32[]{:S(2)}) copy-start(f32[5,256]{1,0:T(8,128)} %as_ref.1) | copy-start | bytes 15364
  117.3 13.8 %collective-permute-start.22 = (f32[4,136,128]{2,1,0:T(8,128)S(1)}, f32[4,136,128]{2,1,0:T(8,128)S(1)}, u32[]{:S(2)}, u32[]{:S(2)}) collective-permute-start(f32[4,136,128]{2,1,0:T(8,128)S(1)} %shard_map.123.e0), channel_id=1, source_target_pairs={{0,1},{1,0},{2,3},{3,2},{4,5},{5,4},{6,7},{7,6},{8,9},{9,8},{10,11... | collective-permute-start | bytes 835592 | tf_op jit(solution)/shard_map/ppermute | solution.py:20
  (12 other events, 39.9 us)

commit v2 on v1

v2 whole, which is shorter than its diff:
```python
import math

import jax
import jax.numpy as jnp
from jax import lax
from jax.experimental import pallas as pl
from jax.experimental.pallas import tpu as pltpu
from jax.sharding import PartitionSpec as P

BLOCK = 128
GROUP = 4
EXTRA = 16
TRIG = 16
OPEN_LIMIT = 60
BF = jnp.bfloat16
F32 = jnp.float32


def swapped(value, axis, mask):
    pairs = [(source, source ^ mask) for source in range(lax.axis_size(axis))]
    return lax.ppermute(value, axis, pairs)


def dot(a, b):
    return lax.dot_general(a, b, (((1,), (0,)), ((), ())), preferred_element_type=F32)


def dot_t(a, b):
    return lax.dot_general(a, b, (((1,), (1,)), ((), ())), preferred_element_type=F32)


def t_dot(a, b):
    return lax.dot_general(a, b, (((0,), (0,)), ((), ())), preferred_element_type=F32)


def tile_of(rows):
    best = 16
    for size in range(16, 257, 16):
        if rows % size == 0:
            best = size
    return best


def call(name, body, outs, args, specs=None, scratch=(), flops=0, out_specs=None, limit=16):
    whole = [pl.BlockSpec(a.shape, lambda i, n=a.ndim: (0,) * n) for a in args]
    for at, spec in (specs or {}).items():
        whole[at] = spec
    moved = sum(math.prod(a.shape) * a.dtype.itemsize for a in args) + sum(
        math.prod(o.shape) * o.dtype.itemsize for o in outs
    )
    return list(
        pl.pallas_call(
            body,
            grid=(1,),
            in_specs=whole,
            out_specs=out_specs
            or [pl.BlockSpec(o.shape, lambda i, n=len(o.shape): (0,) * n) for o in outs],
            out_shape=outs,
            scratch_shapes=list(scratch),
            compiler_params=pltpu.CompilerParams(vmem_limit_bytes=limit * 2**20),
            cost_estimate=pl.CostEstimate(flops=flops*100, bytes_accessed=moved*20, transcendentals=0),
            name=name,
        )(*args)
    )


def shape(dims, dtype=BF):
    return jax.ShapeDtypeStruct(dims, dtype)


SMEM = pl.BlockSpec(memory_space=pltpu.SMEM)
HBM = pl.BlockSpec(memory_space=pltpu.HBM)


def split3(x):
    hi = x.astype(BF)
    rest = x - hi.astype(F32)
    mid = rest.astype(BF)
    low = (rest - mid.astype(F32)).astype(BF)
    return [hi, mid, low]


def stack_lines(lines, height):
    lines = [x.astype(F32) for x in lines]
    lines.append(jnp.zeros((height - len(lines), lines[0].shape[1]), F32))
    return jnp.concatenate(lines, axis=0)


def pack_grad(matrix, lines):
    parts = []
    for line in lines:
        parts += split3(line)[:2]
    return matrix.astype(BF), stack_lines(parts, EXTRA).astype(BF)


def unpack_line(tile, k):
    return tile[2 * k : 2 * k + 1] + tile[2 * k + 1 : 2 * k + 2]


def local(vectors, blocks, angles, codes, scale_index, scale_table, block_state, angle_state):
    rows, width = vectors.shape
    sections = blocks.shape[0]
    nb = width // BLOCK
    chunks = list(range(nb))
    local_bits = nb.bit_length() - 1
    shift = sections - 2 - local_bits
    quarter = rows // GROUP
    nrow = lax.axis_size("row")
    inv = 1.0 / math.sqrt(rows * nrow)
    tile = tile_of(quarter)
    device = lax.axis_index("dim")
    place_arr = ((device >> shift) & (GROUP - 1)).astype(jnp.int32).reshape(1)
    last, third = sections - 1, sections - 2
    product = rows * BLOCK * BLOCK * 2
    grad_rows = BLOCK + EXTRA

    ids = device * nb + jnp.arange(width, dtype=jnp.int32) // BLOCK
    bits = (ids[None, :] >> jnp.arange(sections, dtype=jnp.int32)[:, None]) & 1
    signs = jnp.where(bits == 0, 1.0, -1.0).astype(F32)

    def col(c):
        return slice(c * BLOCK, (c + 1) * BLOCK)

    def cs(ref, s, c):
        return ref[s : s + 1, col(c)], ref[sections + s : sections + s + 1, col(c)]

    def quarter_at(z, m):
        return pl.multiple_of(jnp.bitwise_xor(z, m) * quarter, 16)

    order = [2, 3, 1, 0]
    early = local_bits + 1
    high = quarter + BLOCK + TRIG

    def forward(u, weights, trig_ref):
        steps = []
        for s in range(local_bits):
            v = [dot(u[c], weights[s][c]).astype(BF) for c in chunks]
            steps.append((u, v))
            turned = []
            for c in chunks:
                co, si = cs(trig_ref, s, c)
                turned.append(
                    (co * v[c].astype(F32) + si * v[c ^ (1 << s)].astype(F32)).astype(BF)
                )
            u = turned
        return steps, u

    def open_body(place_ref, u_hbm, w_hbm, codes_hbm, angle_ref, sign_ref, *rest):
        p_hbm, v_hbm, wb_hbm, trig_out = rest[:GROUP], *rest[GROUP : GROUP + 3]
        u_held, w_held, c_held, p_held, v_held, wb_held = rest[GROUP + 3 : GROUP + 9]
        u_sems, w_sems, c_sems, p_sems, v_sems, wb_sem = rest[GROUP + 9 :]
        z = place_ref[0]

        def part(m):
            return pl.ds(m * quarter, quarter)

        w_in = [
            pltpu.make_async_copy(w_hbm.at[s], w_held.at[s], w_sems.at[s]) for s in range(sections)
        ]
        u_in = [
            pltpu.make_async_copy(u_hbm.at[part(m)], u_held.at[part(m)], u_sems.at[m])
            for m in range(GROUP)
        ]
        c_in = [
            pltpu.make_async_copy(
                codes_hbm.at[pl.ds(quarter_at(z, m), quarter)], c_held.at[m], c_sems.at[m]
            )
            for m in range(GROUP)
        ]
        p_out = [pltpu.make_async_copy(p_held.at[m], p_hbm[m], p_sems.at[m]) for m in range(GROUP)]
        v_out = [
            pltpu.make_async_copy(v_held.at[part(m)], v_hbm.at[part(m)], v_sems.at[m])
            for m in range(GROUP)
        ]
        wb_out = pltpu.make_async_copy(wb_held, wb_hbm, wb_sem)
        for copy in w_in[:early] + u_in + w_in[early:]:
            copy.start()
        for m in order:
            c_in[m].start()
        angle = angle_ref[...]
        co, si = jnp.cos(angle), sign_ref[...] * jnp.sin(angle)
        trig_out[...] = jnp.concatenate([co, si], axis=0)
        for s in range(early):
            w_in[s].wait()
            wb_held[s] = w_held[s].astype(BF)
        weights = [[wb_held[s, col(c), :] for c in chunks] for s in range(early)]
        for m in range(GROUP):
            u_in[m].wait()
            for r in range(m * quarter, (m + 1) * quarter, tile):
                at = pl.ds(r, tile)
                u = forward([u_held[at, col(c)] for c in chunks], weights, trig_out)[1]
                for c in chunks:
                    v_held[at, col(c)] = dot(u[c], weights[local_bits][c]).astype(BF)
            v_out[m].start()
        for s in range(early, sections):
            w_in[s].wait()
            wb_held[s] = w_held[s].astype(BF)
        wb_out.start()
        lines = []
        for s in (third, last):
            lines += split3(co[s : s + 1]) + split3(si[s : s + 1])
        lines = stack_lines(lines, TRIG).astype(BF)
        for m in order:
            p_held[m, quarter + BLOCK :, :] = lines
            for c in chunks:
                p_held[m, quarter : quarter + BLOCK, col(c)] = wb_held[last, col(c), :]
            c_in[m].wait()
            for r in range(0, quarter, tile):
                at = pl.ds(r, tile)
                p_held[m, at, :] = c_held[m, at, :].astype(F32).astype(BF)
            p_out[m].start()
        for copy in v_out + [wb_out] + p_out:
            copy.wait()

    opened = call(
        "open",
        open_body,
        [shape((high, width))] * GROUP
        + [shape((rows, width)), shape(blocks.shape), shape((2 * sections, width), F32)],
        [place_arr, vectors, blocks, codes, angles, signs],
        specs={0: SMEM, 1: HBM, 2: HBM, 3: HBM},
        out_specs=[HBM] * (GROUP + 2) + [pl.BlockSpec((2 * sections, width), lambda i: (0, 0))],
        scratch=[
            pltpu.VMEM((rows, width), BF),
            pltpu.VMEM(blocks.shape, F32),
            pltpu.VMEM((GROUP, quarter, width), jnp.int32),
            pltpu.VMEM((GROUP, high, width), BF),
            pltpu.VMEM((rows, width), BF),
            pltpu.VMEM(blocks.shape, BF),
            pltpu.SemaphoreType.DMA((GROUP,)),
            pltpu.SemaphoreType.DMA((sections,)),
            pltpu.SemaphoreType.DMA((GROUP,)),
            pltpu.SemaphoreType.DMA((GROUP,)),
            pltpu.SemaphoreType.DMA((GROUP,)),
            pltpu.SemaphoreType.DMA,
        ],
        flops=rows * width * BLOCK * 4,
        limit=OPEN_LIMIT,
    )
    packed, v_first, wb, trig = opened[:GROUP], *opened[GROUP:]
    other_first = swapped(v_first, "dim", 1)
    packs = {m: swapped(packed[m], "dim", m << shift) for m in order[:-1]}
    packs[0] = packed[0]

    def scale_body(place_ref, table_ref, index_ref, out):
        index = index_ref[pl.ds(place_ref[0], 1), :]
        values = jnp.zeros(index.shape, F32)
        for level in range(table_ref.shape[0]):
            values = jnp.where(index == level, table_ref[level], values)
        parts = stack_lines(split3(values), 16).astype(BF)
        out[...] = t_dot(parts, jnp.ones((16, BLOCK), BF))

    (factor,) = call(
        "scales",
        scale_body,
        [shape((quarter, BLOCK), F32)],
        [place_arr, scale_table, scale_index.reshape(GROUP, quarter)],
        specs={0: SMEM, 1: SMEM},
    )

    saves = {c: {} for c in chunks}

    def middle(c, s, v, other, quarters):
        wide = v.shape[1] != BLOCK
        cols = col(c) if wide else slice(None)

        def body(place_ref, v_ref, o_ref, w_ref, trig_ref, *outs):
            co, si = cs(trig_ref, s, c)
            w = w_ref[s + 1, col(c), :]
            z = place_ref[0]
            for m in range(GROUP):
                start = quarter_at(z, m) if quarters else m * quarter
                for r in range(0, quarter, tile):
                    at = pl.ds(start + r, tile)
                    u = (
                        co * v_ref[at, cols].astype(F32) + si * o_ref[at, cols].astype(F32)
                    ).astype(BF)
                    v_new = dot(u, w).astype(BF)
                    if quarters:
                        outs[m][r : r + tile, :] = v_new
                    else:
                        outs[0][at, :] = v_new

        outs = [shape((quarter, BLOCK))] * GROUP if quarters else [shape((rows, BLOCK))]
        return call(
            f"forward{s + 1}_chunk{c}",
            body,
            outs,
            [place_arr, v, other, wb, trig],
            specs={0: SMEM},
            flops=product,
        )

    middles = list(range(local_bits, third))
    state = {c: (v_first, other_first) for c in chunks}
    for s in middles:
        for c in chunks:
            v, other = state[c]
            out = middle(c, s, v, other, s + 1 == third)
            saves[c][s] = (v, other)
            if s + 1 < third:
                state[c] = (out[0], swapped(out[0], "dim", 1 << (s + 1 - local_bits)))
            else:
                got = {m: swapped(out[m], "dim", m << shift) for m in order[:-1]}
                got[0] = out[0]
                state[c] = [got[m] for m in range(GROUP)]

    def group_stage(c, earlier):
        final = c == chunks[-1]

        def body(*refs):
            a_refs, p_refs = refs[:GROUP], refs[GROUP : 2 * GROUP]
            f_ref = refs[2 * GROUP]
            e_refs = refs[2 * GROUP + 1 : 2 * GROUP + 1 + len(earlier)]
            refs = refs[2 * GROUP + 1 + len(earlier) :]
            outs, grad_refs = refs[:GROUP], refs[GROUP:]
            coef, w = [], []
            for m in range(GROUP):
                t = p_refs[m][quarter + BLOCK :, col(c)].astype(F32)
                coef.append(
                    [t[3 * k : 3 * k + 1] + t[3 * k + 1 : 3 * k + 2] + t[3 * k + 2 : 3 * k + 3] for k in range(4)]
                )
                w.append(p_refs[m][quarter : quarter + BLOCK, col(c)])
            gw = [jnp.zeros((BLOCK, BLOCK), F32)] * GROUP
            ga = [[jnp.zeros((1, BLOCK), F32)] * GROUP for _ in range(2)]
            every = range(GROUP)
            for r in range(0, quarter, tile):
                at = pl.ds(r, tile)
                a = [a_refs[m][at, :].astype(F32) for m in every]
                u = [(coef[m][0] * a[m] + coef[m][1] * a[m ^ 1]).astype(BF) for m in every]
                v = [dot(u[m], w[m]).astype(BF).astype(F32) for m in every]
                f = f_ref[at, :]
                g = []
                for m in every:
                    end = (coef[m][2] * v[m] + coef[m][3] * v[m ^ 2]).astype(BF).astype(F32)
                    recon = f * (p_refs[m][at, col(c)].astype(F32) - 7.5)
                    g.append(((end - recon) * inv).astype(BF).astype(F32))
                for m in every:
                    ga[0][m] = ga[0][m] + jnp.sum(
                        g[m] * (coef[m][2] * v[m ^ 2] - coef[m][3] * v[m]), axis=0, keepdims=True
                    )
                q = [(coef[m][3] * g[m]).astype(BF).astype(F32) for m in every]
                dv = [(coef[m][2] * g[m] + q[m ^ 2]).astype(BF) for m in every]
                g = []
                for m in every:
                    gw[m] = gw[m] + t_dot(u[m], dv[m])
                    g.append(dot_t(dv[m], w[m]).astype(BF).astype(F32))
                for m in every:
                    ga[1][m] = ga[1][m] + jnp.sum(
                        g[m] * (coef[m][0] * a[m ^ 1] - coef[m][1] * a[m]), axis=0, keepdims=True
                    )
                q = [(coef[m][1] * g[m]).astype(BF).astype(F32) for m in every]
                for m in every:
                    outs[m][at, :] = (coef[m][0] * g[m] + q[m ^ 1]).astype(BF)
            for m in every:
                if final:
                    out = grad_refs[m]
                    if m:
                        for k in range(len(earlier)):
                            for h in range(0, grad_rows, 16):
                                out[k, h : h + 16, :] = e_refs[k][m, h : h + 16, :]
                    out = out.at[c] if m else out
                else:
                    out = grad_refs[0].at[m]
                matrix, lines = pack_grad(gw[m], [ga[0][m], ga[1][m]])
                out[:BLOCK, :] = matrix
                out[BLOCK:, :] = lines

        grads = (
            [shape((grad_rows, BLOCK))] + [shape((nb, grad_rows, BLOCK))] * (GROUP - 1)
            if final
            else [shape((GROUP, grad_rows, BLOCK))]
        )
        return call(
            f"group_chunk{c}",
            body,
            [shape((quarter, BLOCK))] * GROUP + grads,
            state[c] + [packs[m] for m in range(GROUP)] + [factor] + earlier,
            flops=3 * product,
        )

    returned, partial = {}, []
    for c in chunks:
        out = group_stage(c, list(partial))
        returned[c] = {m: swapped(out[m], "dim", m << shift) for m in order[:-1]}
        returned[c][0] = out[0]
        partial.append(out[GROUP])
    sums = out[GROUP + 1 :]

    def write_grad(out, gw, ga):
        out[:BLOCK, :] = gw
        out[BLOCK:, :] = stack_lines([ga], EXTRA)

    grad_shape = shape((grad_rows, BLOCK), F32)

    def back(c, s, load, v, other, w_ref, trig_ref, spans, g_out, q_out, grad):
        cols = col(c) if v.shape[1] != BLOCK else slice(None)
        w = w_ref[s, col(c), :]
        co, si = cs(trig_ref, s - 1, c)
        gw = jnp.zeros((BLOCK, BLOCK), F32)
        ga = jnp.zeros((1, BLOCK), F32)
        for m, start in enumerate(spans):
            for r in range(0, quarter, tile):
                at = pl.ds(start + r, tile)
                d = load(m, r, at)
                mine, theirs = v[at, cols].astype(F32), other[at, cols].astype(F32)
                gw = gw + t_dot((co * mine + si * theirs).astype(BF), d)
                g16 = dot_t(d, w).astype(BF)
                g = g16.astype(F32)
                g_out[at, :] = g16
                ga = ga + jnp.sum(g * (co * theirs - si * mine), axis=0, keepdims=True)
                q_out[at, :] = (si * g).astype(BF)
        write_grad(grad, gw, ga)

    def back_quarters(c, s):
        v, other = saves[c][s - 1]

        def body(place_ref, *refs):
            d_refs = refs[:GROUP]
            v_ref, o_ref, w_ref, trig_ref, g_out, q_out, grad = refs[GROUP:]
            spans = [quarter_at(place_ref[0], m) for m in range(GROUP)]

            def load(m, r, at):
                return d_refs[m][r : r + tile, :]

            back(c, s, load, v_ref, o_ref, w_ref, trig_ref, spans, g_out, q_out, grad)

        return call(
            f"backward{s}_chunk{c}",
            body,
            [shape((rows, BLOCK)), shape((rows, BLOCK)), grad_shape],
            [place_arr] + [returned[c][m] for m in range(GROUP)] + [v, other, wb, trig],
            specs={0: SMEM},
            flops=2 * product,
        )

    uppers = [(s, c) for s in range(early, third + 1) for c in chunks]
    upper_shape = shape(((sections - early) * nb, grad_rows, BLOCK))

    def gather_uppers(owns, others, given, out):
        for k, grad in enumerate(given):
            matrix, lines = pack_grad(grad[:BLOCK, :], [grad[BLOCK : BLOCK + 1, :]])
            out[k, :BLOCK, :] = matrix
            out[k, BLOCK:, :] = lines
        for c in chunks:
            own = owns[c] if c == chunks[-1] else owns[c].at[0]
            total = own[:BLOCK, :].astype(F32)
            tail = own[BLOCK:, :].astype(F32)
            for other in others:
                total = total + other[c, :BLOCK, :].astype(F32)
                tail = tail + other[c, BLOCK:, :].astype(F32)
            matrix, lines = pack_grad(total, [unpack_line(tail, 0), unpack_line(tail, 1)])
            out[len(uppers) + c, :BLOCK, :] = matrix
            out[len(uppers) + c, BLOCK:, :] = lines

    def back_middle(c, s, g, incoming, gathered=()):
        v, other = saves[c][s - 1]
        given = []
        if gathered:
            given = [grads[e][t] for t, e in uppers if (t, e) != (s, c)]

        def body(g_ref, i_ref, v_ref, o_ref, w_ref, trig_ref, *refs):
            owns, others = refs[:nb], refs[nb : nb + GROUP - 1]
            done, refs = refs[: len(gathered) + len(given)], refs[len(gathered) + len(given) :]
            g_out, q_out, grad = refs[:3]
            here = cs(trig_ref, s, c)[0]
            spans = [m * quarter for m in range(GROUP)]

            def load(m, r, at):
                return (here * g_ref[at, :].astype(F32) + i_ref[at, :].astype(F32)).astype(BF)

            back(c, s, load, v_ref, o_ref, w_ref, trig_ref, spans, g_out, q_out, grad)
            if gathered:
                held = list(done[len(gathered) :])
                held.insert(uppers.index((s, c)), grad)
                gather_uppers(owns, others, held, refs[3])

        return call(
            f"backward{s}_chunk{c}",
            body,
            [shape((rows, BLOCK)), shape((rows, BLOCK)), grad_shape]
            + ([upper_shape] if gathered else []),
            [g, incoming, v, other, wb, trig, *gathered, *given],
            flops=2 * product,
        )

    grads = {c: {} for c in chunks}
    flow = {}
    for c in chunks:
        g, q, grads[c][third] = back_quarters(c, third)
        flow[c] = (g, swapped(q, "dim", 1 << (third - 1 - local_bits)))
    sums, q = lax.optimization_barrier((sums, q))
    arrived = [swapped(sums[m - 1], "dim", m << shift) for m in order[:-1]]
    for s in reversed(middles[1:]):
        for c in chunks:
            ending = s == middles[1] and c == chunks[-1]
            out = back_middle(c, s, *flow[c], gathered=partial + arrived if ending else ())
            g, q, grads[c][s] = out[:3]
            flow[c] = (g, swapped(q, "dim", 1 << (s - 1 - local_bits)))
    upper = out[3]

    def end_body(*refs):
        g_refs, i_refs = refs[:nb], refs[nb : 2 * nb]
        u_ref, w_ref, trig_ref, grad = refs[2 * nb :]
        gw = [[jnp.zeros((BLOCK, BLOCK), F32)] * nb for _ in range(early)]
        ga = [[jnp.zeros((1, BLOCK), F32)] * nb for _ in range(early)]
        w = [[w_ref[s, col(c), :] for c in chunks] for s in range(early)]
        for r in range(0, rows, tile):
            at = pl.ds(r, tile)
            steps, u = forward([u_ref[at, col(c)] for c in chunks], w, trig_ref)
            inputs = [u for u, _ in steps] + [u]
            d = []
            for c in chunks:
                here = cs(trig_ref, local_bits, c)[0]
                d.append(
                    (here * g_refs[c][at, :].astype(F32) + i_refs[c][at, :].astype(F32)).astype(BF)
                )
            for s in reversed(range(early)):
                for c in chunks:
                    gw[s][c] = gw[s][c] + t_dot(inputs[s][c], d[c])
                if s == 0:
                    break
                g = [dot_t(d[c], w[s][c]).astype(BF).astype(F32) for c in chunks]
                t = s - 1
                v = [x.astype(F32) for x in steps[t][1]]
                q = []
                for c in chunks:
                    co, si = cs(trig_ref, t, c)
                    ga[t][c] = ga[t][c] + jnp.sum(
                        g[c] * (co * v[c ^ (1 << t)] - si * v[c]), axis=0, keepdims=True
                    )
                    q.append((si * g[c]).astype(BF).astype(F32))
                d = [
                    (cs(trig_ref, t, c)[0] * g[c] + q[c ^ (1 << t)]).astype(BF) for c in chunks
                ]
        for s in range(early):
            for c in chunks:
                matrix, lines = pack_grad(gw[s][c], [ga[s][c]])
                grad[s * nb + c, :BLOCK, :] = matrix
                grad[s * nb + c, BLOCK:, :] = lines

    (ends,) = call(
        "end",
        end_body,
        [shape((early * nb, grad_rows, BLOCK))],
        [flow[c][0] for c in chunks]
        + [flow[c][1] for c in chunks]
        + [vectors, wb, trig],
        flops=6 * product,
    )

    if nrow == 2:
        pairs = [(ends, swapped(ends, "row", 1)), (upper, swapped(upper, "row", 1))]
    else:
        pairs = [lax.psum(ends.astype(F32), "row"), lax.psum(upper.astype(F32), "row")]
        pairs = [(p, jnp.zeros_like(p)) for p in pairs]

    def final_body(e0, e1, p0, p1, bs_ref, as_ref, sign_ref, step, new, step_a, new_a):
        def get(s, c):
            k = s * nb + c
            a, b = (e0, e1) if s < early else (p0, p1)
            k = k if s < early else k - early * nb
            matrix = a[k, :BLOCK, :].astype(F32) + b[k, :BLOCK, :].astype(F32)
            return matrix, a[k, BLOCK:, :].astype(F32) + b[k, BLOCK:, :].astype(F32)

        for c in chunks:
            angle = [None] * sections
            for s in range(sections):
                g, lines = get(s, c)
                state_new = 0.9 * bs_ref[s, col(c), :] + 0.1 * g * g
                new[s, col(c), :] = state_new
                step[s, col(c), :] = g * lax.rsqrt(state_new)
                if s == last:
                    angle[last], angle[third] = unpack_line(lines, 0), unpack_line(lines, 1)
                elif s >= early:
                    angle[s - 1] = unpack_line(lines, 0)
                elif s < local_bits:
                    angle[s] = unpack_line(lines, 0)
            g = jnp.concatenate(angle, axis=0) * sign_ref[:, col(c)]
            state_new = 0.9 * as_ref[:, col(c)] + 0.1 * g * g
            new_a[:, col(c)] = state_new
            step_a[:, col(c)] = g * lax.rsqrt(state_new)

    step, new, step_a, new_a = call(
        "final",
        final_body,
        [shape(block_state.shape, F32)] * 2 + [shape(angle_state.shape, F32)] * 2,
        [*pairs[0], *pairs[1], block_state, angle_state, signs],
    )
    return step, new, step_a, new_a


def solution(mesh):
    in_specs = (
        P("row", "dim"),
        P(None, "dim", None),
        P(None, "dim"),
        P("row", "dim"),
        P("row"),
        P(),
        P(None, "dim", None),
        P(None, "dim"),
    )
    out_specs = (P(None, "dim", None), P(None, "dim", None), P(None, "dim"), P(None, "dim"))
    return jax.shard_map(local, mesh=mesh, in_specs=in_specs, out_specs=out_specs, check_vma=False)
```

time: 133 us -> 104 us (0.78)
  the two profiles are of different devices: /device:TPU:0 before, /device:TPU:20 now
where the time goes in v2:
time: 104 us
  waiting for transfers between devices  50.8 us (49%)
  starting transfers between devices  28.9 us (28%)
  Pallas kernels  19.6 us (19%)
  local copies, waits for them, and re-layouts  2.96 us (3%)
    ppermute x27, waiting for transfers between devices, swapped(): return lax.ppermute(value, axis, pairs)  50.8 us
    ppermute x27, starting transfers between devices, swapped(): return lax.ppermute(value, axis, pairs)  28.9 us
    pallas_call x14, Pallas kernels, call(): pl.pallas_call(body, grid=(1,), in_specs=whole, out_specs=out_specs or [p...  19.6 us
    unnamed x26, local copies, waits for them, and re-layouts  2.88 us
  transfers between devices with their start and end apart: 27, of which 13 were waited for; matrix products, arithmetic and copies ran while one was open for 0% of the time, Pallas kernels for 12%

profile of v2, /device:TPU:20, one launch (start us, length us, event | category | flops | bytes accessed | tf_op | source)
XLA Modules:
  0.0 103.7 jit_solution(18415450532077213367)
XLA Ops:
  1.3 6.0 %open.1 = (bf16[560,256]{1,0:T(8,128)(2,1)}, bf16[560,256]{1,0:T(8,128)(2,1)}, bf16[560,256]{1,0:T(8,128)(2,1)}, bf16[560,256]{1,0:T(8,128)(2,1)}, bf16[1664,256...) custom-call(s32[1]{0:T(128)} %bitcast.place_ref, bf16[1664,256]{1,0:T(8,128)(2,1)} %refs_4_.1, ...), custom_call_target="tpu_custom_call" | custom-call | flops 21810380800 | bytes 111165520 | tf_op jit(solution)/shard_map/open/pallas_call | solution.py:52
  7.3 1.6 %collective-permute-start.5 = (bf16[560,256]{1,0:T(8,128)(2,1)}, bf16[560,256]{1,0:T(8,128)(2,1)S(1)}, u32[]{:S(2)}, u32[]{:S(2)}) collective-permute-start(bf16[560,256]{1,0:T(8,128)(2,1)} %get-tuple-element.55), channel_id=1, source_target_pairs={{0,8},{2,10},{4,12},{6,14},{8,0},{10,2},{12,4},{14,6},{16,24},{18,... | collective-permute-start | bytes 860168 | tf_op jit(solution)/shard_map/ppermute | solution.py:21
  9.3 1.6 %collective-permute-start.7 = (bf16[560,256]{1,0:T(8,128)(2,1)}, bf16[560,256]{1,0:T(8,128)(2,1)S(1)}, u32[]{:S(2)}, u32[]{:S(2)}) collective-permute-start(bf16[560,256]{1,0:T(8,128)(2,1)} %get-tuple-element.57), channel_id=1, source_target_pairs={{0,24},{2,26},{4,28},{6,30},{8,16},{10,18},{12,20},{14,22},{16,8},... | collective-permute-start | bytes 860168 | tf_op jit(solution)/shard_map/ppermute | solution.py:21
  11.8 1.1 %copy-done.5 = bf16[1664,256]{1,0:T(8,128)(2,1)S(1)} copy-done((bf16[1664,256]{1,0:T(8,128)(2,1)S(1)}, bf16[1664,256]{1,0:T(8,128)(2,1)}, u32[]{:S(2)}) %copy-start.5) | copy-done | bytes 851992
  16.0 1.6 %collective-permute-start.12 = (bf16[1664,128]{1,0:T(8,128)(2,1)S(1)}, bf16[1664,128]{1,0:T(8,128)(2,1)S(1)}, u32[]{:S(2)}, u32[]{:S(2)}) collective-permute-start(bf16[1664,128]{1,0:T(8,128)(2,1)S(1)} %forward2_chunk1.1.v_ref.refs_4_), channel_id=1, source_target_pairs={{0,4},{2,6},{4,0},{6,2},{8,12},{10,14},{12,8},{14,10},{16,20},{18,... | collective-permute-start | bytes 1277960 | tf_op jit(solution)/shard_map/ppermute | solution.py:21
  17.6 10.3 %collective-permute-done.1.o_ref.refs_5_ = bf16[1664,128]{1,0:T(8,128)(2,1)S(1)} collective-permute-done((bf16[1664,128]{1,0:T(8,128)(2,1)S(1)}, bf16[1664,128]{1,0:T(8,128)(2,1)S(1)}, u32[]{:S(2)}, u32[]{:S(2)}) %collective-permute-start.1) | collective-permute-done | bytes 426016 | tf_op jit(solution)/shard_map/ppermute | solution.py:21
  28.2 2.5 %collective-permute-start.2 = (bf16[416,128]{1,0:T(8,128)(2,1)S(1)}, bf16[416,128]{1,0:T(8,128)(2,1)S(1)}, u32[]{:S(2)}, u32[]{:S(2)}) collective-permute-start(bf16[416,128]{1,0:T(8,128)(2,1)S(1)} %get-tuple-element.51), channel_id=1, source_target_pairs={{0,8},{2,10},{4,12},{6,14},{8,0},{10,2},{12,4},{14,6},{16,24},{18,... | collective-permute-start | bytes 319496 | tf_op jit(solution)/shard_map/ppermute | solution.py:21
  30.7 4.8 %collective-permute-done.12.o_ref.refs_5_ = bf16[1664,128]{1,0:T(8,128)(2,1)S(1)} collective-permute-done((bf16[1664,128]{1,0:T(8,128)(2,1)S(1)}, bf16[1664,128]{1,0:T(8,128)(2,1)S(1)}, u32[]{:S(2)}, u32[]{:S(2)}) %collective-permute-start.12) | collective-permute-done | bytes 426016 | tf_op jit(solution)/shard_map/ppermute | solution.py:21
  36.4 2.4 %collective-permute-start.13 = (bf16[416,128]{1,0:T(8,128)(2,1)S(1)}, bf16[416,128]{1,0:T(8,128)(2,1)S(1)}, u32[]{:S(2)}, u32[]{:S(2)}) collective-permute-start(bf16[416,128]{1,0:T(8,128)(2,1)S(1)} %get-tuple-element.66), channel_id=1, source_target_pairs={{0,8},{2,10},{4,12},{6,14},{8,0},{10,2},{12,4},{14,6},{16,24},{18,... | collective-permute-start | bytes 319496 | tf_op jit(solution)/shard_map/ppermute | solution.py:21
  39.5 1.4 %collective-permute-start.14 = (bf16[416,128]{1,0:T(8,128)(2,1)S(1)}, bf16[416,128]{1,0:T(8,128)(2,1)S(1)}, u32[]{:S(2)}, u32[]{:S(2)}) collective-permute-start(bf16[416,128]{1,0:T(8,128)(2,1)S(1)} %get-tuple-element.67), channel_id=1, source_target_pairs={{0,16},{2,18},{4,20},{6,22},{8,24},{10,26},{12,28},{14,30},{16,0},... | collective-permute-start | bytes 319496 | tf_op jit(solution)/shard_map/ppermute | solution.py:21
  41.5 5.2 %collective-permute-done.3.refs_2_ = bf16[416,128]{1,0:T(8,128)(2,1)S(1)} collective-permute-done((bf16[416,128]{1,0:T(8,128)(2,1)S(1)}, bf16[416,128]{1,0:T(8,128)(2,1)S(1)}, u32[]{:S(2)}, u32[]{:S(2)}) %collective-permute-start.3) | collective-permute-done | bytes 106528 | tf_op jit(solution)/shard_map/ppermute | solution.py:21
  46.7 4.2 %collective-permute-done.4.refs_3_ = bf16[416,128]{1,0:T(8,128)(2,1)S(1)} collective-permute-done((bf16[416,128]{1,0:T(8,128)(2,1)S(1)}, bf16[416,128]{1,0:T(8,128)(2,1)S(1)}, u32[]{:S(2)}, u32[]{:S(2)}) %collective-permute-start.4) | collective-permute-done | bytes 106528 | tf_op jit(solution)/shard_map/ppermute | solution.py:21
  51.0 1.4 %group_chunk0.1 = (bf16[416,128]{1,0:T(8,128)(2,1)S(1)}, bf16[416,128]{1,0:T(8,128)(2,1)S(1)}, bf16[416,128]{1,0:T(8,128)(2,1)S(1)}, bf16[416,128]{1,0:T(8,128)(2,1)S(1)}, bf16[4,144,128]{2,1,0:T(8,128)(2,1)S(1)}) custom-call(bf16[416,128]{1,0:T(8,128)(2,1)S(1)} %get-tuple-element.50.refs_0_, bf16[416,128]{1,0:T(8,128)(2,1)S(1)} %collective-permute-done.2.refs_1_, ...), custom_call_target="tpu_custom_call" | custom-call | flops 16357785600 | bytes 47185920 | tf_op jit(solution)/shard_map/group_chunk0/pallas_call | solution.py:52
  52.5 2.0 %collective-permute-start.9 = (bf16[416,128]{1,0:T(8,128)(2,1)S(1)}, bf16[416,128]{1,0:T(8,128)(2,1)S(1)}, u32[]{:S(2)}, u32[]{:S(2)}) collective-permute-start(bf16[416,128]{1,0:T(8,128)(2,1)S(1)} %get-tuple-element.60), channel_id=1, source_target_pairs={{0,16},{2,18},{4,20},{6,22},{8,24},{10,26},{12,28},{14,30},{16,0},... | collective-permute-start | bytes 319496 | tf_op jit(solution)/shard_map/ppermute | solution.py:21
  54.5 1.5 %collective-permute-start.10 = (bf16[416,128]{1,0:T(8,128)(2,1)S(1)}, bf16[416,128]{1,0:T(8,128)(2,1)S(1)}, u32[]{:S(2)}, u32[]{:S(2)}) collective-permute-start(bf16[416,128]{1,0:T(8,128)(2,1)S(1)} %get-tuple-element.61), channel_id=1, source_target_pairs={{0,24},{2,26},{4,28},{6,30},{8,16},{10,18},{12,20},{14,22},{16,8},... | collective-permute-start | bytes 319496 | tf_op jit(solution)/shard_map/ppermute | solution.py:21
  56.0 1.4 %group_chunk1.1 = (bf16[416,128]{1,0:T(8,128)(2,1)S(1)}, bf16[416,128]{1,0:T(8,128)(2,1)S(1)}, bf16[416,128]{1,0:T(8,128)(2,1)S(1)}, bf16[416,128]{1,0:T(8,128)(...) custom-call(bf16[416,128]{1,0:T(8,128)(2,1)S(1)} %get-tuple-element., ...), custom_call_target="tpu_custom_call" | custom-call | flops 16357785600 | bytes 52346880 | tf_op jit(solution)/shard_map/group_chunk1/pallas_call | solution.py:52
  57.4 1.0 %collective-permute-start.16 = (bf16[416,128]{1,0:T(8,128)(2,1)S(1)}, bf16[416,128]{1,0:T(8,128)(2,1)S(1)}, u32[]{:S(2)}, u32[]{:S(2)}) collective-permute-start(bf16[416,128]{1,0:T(8,128)(2,1)S(1)} %get-tuple-element.71), channel_id=1, source_target_pairs={{0,8},{2,10},{4,12},{6,14},{8,0},{10,2},{12,4},{14,6},{16,24},{18,... | collective-permute-start | bytes 319496 | tf_op jit(solution)/shard_map/ppermute | solution.py:21
  58.4 1.0 collective-permute-start.17
  59.5 1.5 %collective-permute-start.18 = (bf16[416,128]{1,0:T(8,128)(2,1)S(1)}, bf16[416,128]{1,0:T(8,128)(2,1)S(1)}, u32[]{:S(2)}, u32[]{:S(2)}) collective-permute-start(bf16[416,128]{1,0:T(8,128)(2,1)S(1)} %get-tuple-element.73), channel_id=1, source_target_pairs={{0,24},{2,26},{4,28},{6,30},{8,16},{10,18},{12,20},{14,22},{16,8},... | collective-permute-start | bytes 319496 | tf_op jit(solution)/shard_map/ppermute | solution.py:21
  61.0 1.1 %collective-permute-done.9.refs_2_ = bf16[416,128]{1,0:T(8,128)(2,1)S(1)} collective-permute-done((bf16[416,128]{1,0:T(8,128)(2,1)S(1)}, bf16[416,128]{1,0:T(8,128)(2,1)S(1)}, u32[]{:S(2)}, u32[]{:S(2)}) %collective-permute-start.9) | collective-permute-done | bytes 106528 | tf_op jit(solution)/shard_map/ppermute | solution.py:21
  62.0 7.2 %collective-permute-done.10.refs_3_ = bf16[416,128]{1,0:T(8,128)(2,1)S(1)} collective-permute-done((bf16[416,128]{1,0:T(8,128)(2,1)S(1)}, bf16[416,128]{1,0:T(8,128)(2,1)S(1)}, u32[]{:S(2)}, u32[]{:S(2)}) %collective-permute-start.10) | collective-permute-done | bytes 106528 | tf_op jit(solution)/shard_map/ppermute | solution.py:21
  70.4 2.6 %collective-permute-done.18.refs_3_ = bf16[416,128]{1,0:T(8,128)(2,1)S(1)} collective-permute-done((bf16[416,128]{1,0:T(8,128)(2,1)S(1)}, bf16[416,128]{1,0:T(8,128)(2,1)S(1)}, u32[]{:S(2)}, u32[]{:S(2)}) %collective-permute-start.18) | collective-permute-done | bytes 106528 | tf_op jit(solution)/shard_map/ppermute | solution.py:21
  74.5 1.1 %collective-permute-start.21 = (bf16[2,144,128]{2,1,0:T(8,128)(2,1)S(1)}, bf16[2,144,128]{2,1,0:T(8,128)(2,1)S(1)}, u32[]{:S(2)}, u32[]{:S(2)}) collective-permute-start(bf16[2,144,128]{2,1,0:T(8,128)(2,1)S(1)} %get-tuple-element.81), channel_id=1, source_target_pairs={{0,24},{2,26},{4,28},{6,30},{8,16},{10,18},{12,20},{14,22},{16,8},... | collective-permute-start | bytes 221192 | tf_op jit(solution)/shard_map/ppermute | solution.py:21
  75.6 3.0 %collective-permute-start.22 = (bf16[2,144,128]{2,1,0:T(8,128)(2,1)S(1)}, bf16[2,144,128]{2,1,0:T(8,128)(2,1)S(1)}, u32[]{:S(2)}, u32[]{:S(2)}) collective-permute-start(bf16[2,144,128]{2,1,0:T(8,128)(2,1)S(1)} %get-tuple-element.82), channel_id=1, source_target_pairs={{0,8},{2,10},{4,12},{6,14},{8,0},{10,2},{12,4},{14,6},{16,24},{18,... | collective-permute-start | bytes 221192 | tf_op jit(solution)/shard_map/ppermute | solution.py:21
  78.6 4.0 %collective-permute-done.11.i_ref = bf16[1664,128]{1,0:T(8,128)(2,1)S(1)} collective-permute-done((bf16[1664,128]{1,0:T(8,128)(2,1)S(1)}, bf16[1664,128]{1,0:T(8,128)(2,1)S(1)}, u32[]{:S(2)}, u32[]{:S(2)}) %collective-permute-start.11) | collective-permute-done | bytes 426016 | tf_op jit(solution)/shard_map/ppermute | solution.py:21
  83.4 5.9 %collective-permute-done.19.i_ref = bf16[1664,128]{1,0:T(8,128)(2,1)S(1)} collective-permute-done((bf16[1664,128]{1,0:T(8,128)(2,1)S(1)}, bf16[1664,128]{1,0:T(8,128)(2,1)S(1)}, u32[]{:S(2)}, u32[]{:S(2)}) %collective-permute-start.19) | collective-permute-done | bytes 426016 | tf_op jit(solution)/shard_map/ppermute | solution.py:21
  89.3 1.3 %backward2_chunk1.1 = (bf16[1664,128]{1,0:T(8,128)(2,1)S(1)}, bf16[1664,128]{1,0:T(8,128)(2,1)S(1)}, f32[144,128]{1,0:T(8,128)}, bf16[6,144,128]{2,1,0:T(8,128)(2,1)S(1)}) custom-call(bf16[1664,128]{1,0:T(8,128)(2,1)S(1)} %get-tuple-element.74.g_ref, bf16[1664,128]{1,0:T(8,128)(2,1)S(1)} %collective-permute-done.19.i_ref, bf16[1664,256]{1,0:T(8,128)(2,1)S(1)} %copy-done.6, ...), custom_call_target="tpu_custom_call" | custom-call | flops 10905190400 | bytes 93347840 | tf_op jit(solution)/shard_map/backward2_chunk1/pallas_call | solution.py:52
  90.6 1.5 %collective-permute-start.26 = (bf16[6,144,128]{2,1,0:T(8,128)(2,1)S(1)}, bf16[6,144,128]{2,1,0:T(8,128)(2,1)S(1)}, u32[]{:S(2)}, u32[]{:S(2)}) collective-permute-start(bf16[6,144,128]{2,1,0:T(8,128)(2,1)S(1)} %get-tuple-element.89.p0), channel_id=1, source_target_pairs={{0,1},{1,0},{2,3},{3,2},{4,5},{5,4},{6,7},{7,6},{8,9},{9,8},{10,11... | collective-permute-start | bytes 663560 | tf_op jit(solution)/shard_map/ppermute | solution.py:21
  92.4 4.0 %end.1.e0 = bf16[4,144,128]{2,1,0:T(8,128)(2,1)S(1)} custom-call(bf16[1664,128]{1,0:T(8,128)(2,1)S(1)} %get-tuple-element.64.refs_0_, bf16[1664,128]{1,0:T(8,128)(2,1)S(1)} %get-tuple-element.86.refs_1_, bf16[1664,128]{1,0:T(8,128)(2,1)S(1)} %collective-permute-done.23.refs_2_, bf16[1664,128]{1,0:T(8,128)(2,1)S(1)} %collective-permute-done.24.refs_3_, ...), custom_call_target="tpu_custom_call" | custom-call | flops 32715571200 | bytes 60825600 | tf_op jit(solution)/shard_map/end/pallas_call | solution.py:52
  96.5 1.6 %collective-permute-start.25 = (bf16[4,144,128]{2,1,0:T(8,128)(2,1)S(1)}, bf16[4,144,128]{2,1,0:T(8,128)(2,1)S(1)}, u32[]{:S(2)}, u32[]{:S(2)}) collective-permute-start(bf16[4,144,128]{2,1,0:T(8,128)(2,1)S(1)} %end.1.e0), channel_id=1, source_target_pairs={{0,1},{1,0},{2,3},{3,2},{4,5},{5,4},{6,7},{7,6},{8,9},{9,8},{10,11... | collective-permute-start | bytes 442376 | tf_op jit(solution)/shard_map/ppermute | solution.py:21
  98.5 3.9 %collective-permute-done.25.e1 = bf16[4,144,128]{2,1,0:T(8,128)(2,1)S(1)} collective-permute-done((bf16[4,144,128]{2,1,0:T(8,128)(2,1)S(1)}, bf16[4,144,128]{2,1,0:T(8,128)(2,1)S(1)}, u32[]{:S(2)}, u32[]{:S(2)}) %collective-permute-start.25) | collective-permute-done | bytes 147488 | tf_op jit(solution)/shard_map/ppermute | solution.py:21
  102.4 1.2 %final.1 = (f32[5,256,128]{2,1,0:T(8,128)}, f32[5,256,128]{2,1,0:T(8,128)}, f32[5,256]{1,0:T(8,128)}, f32[5,256]{1,0:T(8,128)}) custom-call(bf16[4,144,128]{2,1,0:T(8,128)(2,1)S(1)} %end.1.e0, bf16[4,144,128]{2,1,0:T(8,128)(2,1)S(1)} %collective-permute-done.25.e1, bf16[6,144,128]{2,1,0:T(8,128)(2,1)S(1)} %get-tuple-element.89.p0, ...), custom_call_target="tpu_custom_call" | custom-call | bytes 54476800 | tf_op jit(solution)/shard_map/final/pallas_call | solution.py:52
  (65 shorter events, 11.7 us)
Async XLA Ops:
  7.2 4.5 %collective-permute-start = (bf16[1664,256]{1,0:T(8,128)(2,1)}, bf16[1664,256]{1,0:T(8,128)(2,1)S(1)}, u32[]{:S(2)}, u32[]{:S(2)}) collective-permute-start(bf16[1664,256]{1,0:T(8,128)(2,1)} %get-tuple-element.47.v_ref), channel_id=1, source_target_pairs={{0,2},{2,0},{4,6},{6,4},{8,10},{10,8},{12,14},{14,12},{16,18},{18,... | collective-permute-start | bytes 2555912 | tf_op jit(solution)/shard_map/ppermute | solution.py:21
  7.3 23.4 %collective-permute-start.5 = (bf16[560,256]{1,0:T(8,128)(2,1)}, bf16[560,256]{1,0:T(8,128)(2,1)S(1)}, u32[]{:S(2)}, u32[]{:S(2)}) collective-permute-start(bf16[560,256]{1,0:T(8,128)(2,1)} %get-tuple-element.55), channel_id=1, source_target_pairs={{0,8},{2,10},{4,12},{6,14},{8,0},{10,2},{12,4},{14,6},{16,24},{18,... | collective-permute-start | bytes 860168 | tf_op jit(solution)/shard_map/ppermute | solution.py:21
  9.0 27.4 %collective-permute-start.6 = (bf16[560,256]{1,0:T(8,128)(2,1)}, bf16[560,256]{1,0:T(8,128)(2,1)S(1)}, u32[]{:S(2)}, u32[]{:S(2)}) collective-permute-start(bf16[560,256]{1,0:T(8,128)(2,1)} %get-tuple-element.56), channel_id=1, source_target_pairs={{0,16},{2,18},{4,20},{6,22},{8,24},{10,26},{12,28},{14,30},{16,0},... | collective-permute-start | bytes 860168 | tf_op jit(solution)/shard_map/ppermute | solution.py:21
  9.3 30.2 %collective-permute-start.7 = (bf16[560,256]{1,0:T(8,128)(2,1)}, bf16[560,256]{1,0:T(8,128)(2,1)S(1)}, u32[]{:S(2)}, u32[]{:S(2)}) collective-permute-start(bf16[560,256]{1,0:T(8,128)(2,1)} %get-tuple-element.57), channel_id=1, source_target_pairs={{0,24},{2,26},{4,28},{6,30},{8,16},{10,18},{12,20},{14,22},{16,8},... | collective-permute-start | bytes 860168 | tf_op jit(solution)/shard_map/ppermute | solution.py:21
  15.0 12.8 %copy-start.8 = (bf16[5,256,128]{2,1,0:T(8,128)(2,1)S(1)}, bf16[5,256,128]{2,1,0:T(8,128)(2,1)}, u32[]{:S(2)}) copy-start(bf16[5,256,128]{2,1,0:T(8,128)(2,1)} %get-tuple-element.48.w_ref.refs_6_.refs_5_) | copy-start | bytes 983044
  15.0 12.8 %collective-permute-start.1 = (bf16[1664,128]{1,0:T(8,128)(2,1)S(1)}, bf16[1664,128]{1,0:T(8,128)(2,1)S(1)}, u32[]{:S(2)}, u32[]{:S(2)}) collective-permute-start(bf16[1664,128]{1,0:T(8,128)(2,1)S(1)} %forward2_chunk0.1.v_ref.refs_4_), channel_id=1, source_target_pairs={{0,4},{2,6},{4,0},{6,2},{8,12},{10,14},{12,8},{14,10},{16,20},{18,... | collective-permute-start | bytes 1277960 | tf_op jit(solution)/shard_map/ppermute | solution.py:21
  16.0 19.6 %collective-permute-start.12 = (bf16[1664,128]{1,0:T(8,128)(2,1)S(1)}, bf16[1664,128]{1,0:T(8,128)(2,1)S(1)}, u32[]{:S(2)}, u32[]{:S(2)}) collective-permute-start(bf16[1664,128]{1,0:T(8,128)(2,1)S(1)} %forward2_chunk1.1.v_ref.refs_4_), channel_id=1, source_target_pairs={{0,4},{2,6},{4,0},{6,2},{8,12},{10,14},{12,8},{14,10},{16,20},{18,... | collective-permute-start | bytes 1277960 | tf_op jit(solution)/shard_map/ppermute | solution.py:21
  28.2 12.7 %collective-permute-start.2 = (bf16[416,128]{1,0:T(8,128)(2,1)S(1)}, bf16[416,128]{1,0:T(8,128)(2,1)S(1)}, u32[]{:S(2)}, u32[]{:S(2)}) collective-permute-start(bf16[416,128]{1,0:T(8,128)(2,1)S(1)} %get-tuple-element.51), channel_id=1, source_target_pairs={{0,8},{2,10},{4,12},{6,14},{8,0},{10,2},{12,4},{14,6},{16,24},{18,... | collective-permute-start | bytes 319496 | tf_op jit(solution)/shard_map/ppermute | solution.py:21
  30.7 16.0 %collective-permute-start.3 = (bf16[416,128]{1,0:T(8,128)(2,1)S(1)}, bf16[416,128]{1,0:T(8,128)(2,1)S(1)}, u32[]{:S(2)}, u32[]{:S(2)}) collective-permute-start(bf16[416,128]{1,0:T(8,128)(2,1)S(1)} %get-tuple-element.52), channel_id=1, source_target_pairs={{0,16},{2,18},{4,20},{6,22},{8,24},{10,26},{12,28},{14,30},{16,0},... | collective-permute-start | bytes 319496 | tf_op jit(solution)/shard_map/ppermute | solution.py:21
  35.5 15.4 %copy-start.9 = (bf16[560,256]{1,0:T(8,128)(2,1)S(1)}, bf16[560,256]{1,0:T(8,128)(2,1)}, u32[]{:S(2)}) copy-start(bf16[560,256]{1,0:T(8,128)(2,1)} %get-tuple-element.54.refs_4_) | copy-start | bytes 860164
  35.5 15.4 %collective-permute-start.4 = (bf16[416,128]{1,0:T(8,128)(2,1)S(1)}, bf16[416,128]{1,0:T(8,128)(2,1)S(1)}, u32[]{:S(2)}, u32[]{:S(2)}) collective-permute-start(bf16[416,128]{1,0:T(8,128)(2,1)S(1)} %get-tuple-element.53), channel_id=1, source_target_pairs={{0,24},{2,26},{4,28},{6,30},{8,16},{10,18},{12,20},{14,22},{16,8},... | collective-permute-start | bytes 319496 | tf_op jit(solution)/shard_map/ppermute | solution.py:21
  36.4 18.1 %collective-permute-start.13 = (bf16[416,128]{1,0:T(8,128)(2,1)S(1)}, bf16[416,128]{1,0:T(8,128)(2,1)S(1)}, u32[]{:S(2)}, u32[]{:S(2)}) collective-permute-start(bf16[416,128]{1,0:T(8,128)(2,1)S(1)} %get-tuple-element.66), channel_id=1, source_target_pairs={{0,8},{2,10},{4,12},{6,14},{8,0},{10,2},{12,4},{14,6},{16,24},{18,... | collective-permute-start | bytes 319496 | tf_op jit(solution)/shard_map/ppermute | solution.py:21
  39.5 16.5 %collective-permute-start.14 = (bf16[416,128]{1,0:T(8,128)(2,1)S(1)}, bf16[416,128]{1,0:T(8,128)(2,1)S(1)}, u32[]{:S(2)}, u32[]{:S(2)}) collective-permute-start(bf16[416,128]{1,0:T(8,128)(2,1)S(1)} %get-tuple-element.67), channel_id=1, source_target_pairs={{0,16},{2,18},{4,20},{6,22},{8,24},{10,26},{12,28},{14,30},{16,0},... | collective-permute-start | bytes 319496 | tf_op jit(solution)/shard_map/ppermute | solution.py:21
  40.9 15.0 %collective-permute-start.15 = (bf16[416,128]{1,0:T(8,128)(2,1)S(1)}, bf16[416,128]{1,0:T(8,128)(2,1)S(1)}, u32[]{:S(2)}, u32[]{:S(2)}) collective-permute-start(bf16[416,128]{1,0:T(8,128)(2,1)S(1)} %get-tuple-element.68), channel_id=1, source_target_pairs={{0,24},{2,26},{4,28},{6,30},{8,16},{10,18},{12,20},{14,22},{16,8},... | collective-permute-start | bytes 319496 | tf_op jit(solution)/shard_map/ppermute | solution.py:21
  52.4 7.1 %collective-permute-start.8 = (bf16[416,128]{1,0:T(8,128)(2,1)S(1)}, bf16[416,128]{1,0:T(8,128)(2,1)S(1)}, u32[]{:S(2)}, u32[]{:S(2)}) collective-permute-start(bf16[416,128]{1,0:T(8,128)(2,1)S(1)} %get-tuple-element.59), channel_id=1, source_target_pairs={{0,8},{2,10},{4,12},{6,14},{8,0},{10,2},{12,4},{14,6},{16,24},{18,... | collective-permute-start | bytes 319496 | tf_op jit(solution)/shard_map/ppermute | solution.py:21
  52.5 9.5 %collective-permute-start.9 = (bf16[416,128]{1,0:T(8,128)(2,1)S(1)}, bf16[416,128]{1,0:T(8,128)(2,1)S(1)}, u32[]{:S(2)}, u32[]{:S(2)}) collective-permute-start(bf16[416,128]{1,0:T(8,128)(2,1)S(1)} %get-tuple-element.60), channel_id=1, source_target_pairs={{0,16},{2,18},{4,20},{6,22},{8,24},{10,26},{12,28},{14,30},{16,0},... | collective-permute-start | bytes 319496 | tf_op jit(solution)/shard_map/ppermute | solution.py:21
  54.5 14.7 %collective-permute-start.10 = (bf16[416,128]{1,0:T(8,128)(2,1)S(1)}, bf16[416,128]{1,0:T(8,128)(2,1)S(1)}, u32[]{:S(2)}, u32[]{:S(2)}) collective-permute-start(bf16[416,128]{1,0:T(8,128)(2,1)S(1)} %get-tuple-element.61), channel_id=1, source_target_pairs={{0,24},{2,26},{4,28},{6,30},{8,16},{10,18},{12,20},{14,22},{16,8},... | collective-permute-start | bytes 319496 | tf_op jit(solution)/shard_map/ppermute | solution.py:21
  57.4 13.0 %collective-permute-start.16 = (bf16[416,128]{1,0:T(8,128)(2,1)S(1)}, bf16[416,128]{1,0:T(8,128)(2,1)S(1)}, u32[]{:S(2)}, u32[]{:S(2)}) collective-permute-start(bf16[416,128]{1,0:T(8,128)(2,1)S(1)} %get-tuple-element.71), channel_id=1, source_target_pairs={{0,8},{2,10},{4,12},{6,14},{8,0},{10,2},{12,4},{14,6},{16,24},{18,... | collective-permute-start | bytes 319496 | tf_op jit(solution)/shard_map/ppermute | solution.py:21
  58.4 12.0 %collective-permute-start.17 = (bf16[416,128]{1,0:T(8,128)(2,1)S(1)}, bf16[416,128]{1,0:T(8,128)(2,1)S(1)}, u32[]{:S(2)}, u32[]{:S(2)}) collective-permute-start(bf16[416,128]{1,0:T(8,128)(2,1)S(1)} %get-tuple-element.72), channel_id=1, source_target_pairs={{0,16},{2,18},{4,20},{6,22},{8,24},{10,26},{12,28},{14,30},{16,0},... | collective-permute-start | bytes 319496 | tf_op jit(solution)/shard_map/ppermute | solution.py:21
  59.5 13.5 %collective-permute-start.18 = (bf16[416,128]{1,0:T(8,128)(2,1)S(1)}, bf16[416,128]{1,0:T(8,128)(2,1)S(1)}, u32[]{:S(2)}, u32[]{:S(2)}) collective-permute-start(bf16[416,128]{1,0:T(8,128)(2,1)S(1)} %get-tuple-element.73), channel_id=1, source_target_pairs={{0,24},{2,26},{4,28},{6,30},{8,16},{10,18},{12,20},{14,22},{16,8},... | collective-permute-start | bytes 319496 | tf_op jit(solution)/shard_map/ppermute | solution.py:21
  69.8 12.8 %collective-permute-start.11 = (bf16[1664,128]{1,0:T(8,128)(2,1)S(1)}, bf16[1664,128]{1,0:T(8,128)(2,1)S(1)}, u32[]{:S(2)}, u32[]{:S(2)}) collective-permute-start(bf16[1664,128]{1,0:T(8,128)(2,1)S(1)} %get-tuple-element.63), channel_id=1, source_target_pairs={{0,4},{2,6},{4,0},{6,2},{8,12},{10,14},{12,8},{14,10},{16,20},{18,... | collective-permute-start | bytes 1277960 | tf_op jit(solution)/shard_map/ppermute | solution.py:21
  73.6 15.7 %collective-permute-start.19 = (bf16[1664,128]{1,0:T(8,128)(2,1)S(1)}, bf16[1664,128]{1,0:T(8,128)(2,1)S(1)}, u32[]{:S(2)}, u32[]{:S(2)}) collective-permute-start(bf16[1664,128]{1,0:T(8,128)(2,1)S(1)} %get-tuple-element.75), channel_id=1, source_target_pairs={{0,4},{2,6},{4,0},{6,2},{8,12},{10,14},{12,8},{14,10},{16,20},{18,... | collective-permute-start | bytes 1277960 | tf_op jit(solution)/shard_map/ppermute | solution.py:21
  74.2 9.2 %collective-permute-start.20 = (bf16[2,144,128]{2,1,0:T(8,128)(2,1)S(1)}, bf16[2,144,128]{2,1,0:T(8,128)(2,1)S(1)}, u32[]{:S(2)}, u32[]{:S(2)}) collective-permute-start(bf16[2,144,128]{2,1,0:T(8,128)(2,1)S(1)} %get-tuple-element.80), channel_id=1, source_target_pairs={{0,16},{2,18},{4,20},{6,22},{8,24},{10,26},{12,28},{14,30},{16,0},... | collective-permute-start | bytes 221192 | tf_op jit(solution)/shard_map/ppermute | solution.py:21
  74.5 8.9 %collective-permute-start.21 = (bf16[2,144,128]{2,1,0:T(8,128)(2,1)S(1)}, bf16[2,144,128]{2,1,0:T(8,128)(2,1)S(1)}, u32[]{:S(2)}, u32[]{:S(2)}) collective-permute-start(bf16[2,144,128]{2,1,0:T(8,128)(2,1)S(1)} %get-tuple-element.81), channel_id=1, source_target_pairs={{0,24},{2,26},{4,28},{6,30},{8,16},{10,18},{12,20},{14,22},{16,8},... | collective-permute-start | bytes 221192 | tf_op jit(solution)/shard_map/ppermute | solution.py:21
  75.6 7.8 %collective-permute-start.22 = (bf16[2,144,128]{2,1,0:T(8,128)(2,1)S(1)}, bf16[2,144,128]{2,1,0:T(8,128)(2,1)S(1)}, u32[]{:S(2)}, u32[]{:S(2)}) collective-permute-start(bf16[2,144,128]{2,1,0:T(8,128)(2,1)S(1)} %get-tuple-element.82), channel_id=1, source_target_pairs={{0,8},{2,10},{4,12},{6,14},{8,0},{10,2},{12,4},{14,6},{16,24},{18,... | collective-permute-start | bytes 221192 | tf_op jit(solution)/shard_map/ppermute | solution.py:21
  83.3 8.8 %collective-permute-start.23 = (bf16[1664,128]{1,0:T(8,128)(2,1)S(1)}, bf16[1664,128]{1,0:T(8,128)(2,1)S(1)}, u32[]{:S(2)}, u32[]{:S(2)}) collective-permute-start(bf16[1664,128]{1,0:T(8,128)(2,1)S(1)} %get-tuple-element.87), channel_id=1, source_target_pairs={{0,2},{2,0},{4,6},{6,4},{8,10},{10,8},{12,14},{14,12},{16,18},{18,... | collective-permute-start | bytes 1277960 | tf_op jit(solution)/shard_map/ppermute | solution.py:21
  90.6 1.8 %collective-permute-start.24 = (bf16[1664,128]{1,0:T(8,128)(2,1)S(1)}, bf16[1664,128]{1,0:T(8,128)(2,1)S(1)}, u32[]{:S(2)}, u32[]{:S(2)}) collective-permute-start(bf16[1664,128]{1,0:T(8,128)(2,1)S(1)} %get-tuple-element.88), channel_id=1, source_target_pairs={{0,2},{2,0},{4,6},{6,4},{8,10},{10,8},{12,14},{14,12},{16,18},{18,... | collective-permute-start | bytes 1277960 | tf_op jit(solution)/shard_map/ppermute | solution.py:21
  90.6 7.8 %collective-permute-start.26 = (bf16[6,144,128]{2,1,0:T(8,128)(2,1)S(1)}, bf16[6,144,128]{2,1,0:T(8,128)(2,1)S(1)}, u32[]{:S(2)}, u32[]{:S(2)}) collective-permute-start(bf16[6,144,128]{2,1,0:T(8,128)(2,1)S(1)} %get-tuple-element.89.p0), channel_id=1, source_target_pairs={{0,1},{1,0},{2,3},{3,2},{4,5},{5,4},{6,7},{7,6},{8,9},{9,8},{10,11... | collective-permute-start | bytes 663560 | tf_op jit(solution)/shard_map/ppermute | solution.py:21
  92.4 10.0 %copy-start = (f32[5,256,128]{2,1,0:T(8,128)S(1)}, f32[5,256,128]{2,1,0:T(8,128)}, u32[]{:S(2)}) copy-start(f32[5,256,128]{2,1,0:T(8,128)} %bs_ref.1) | copy-start | bytes 1966084
  92.4 10.0 %copy-start.1 = (f32[5,256]{1,0:T(8,128)S(1)}, f32[5,256]{1,0:T(8,128)}, u32[]{:S(2)}) copy-start(f32[5,256]{1,0:T(8,128)} %fusion.sign_ref) | copy-start | bytes 15364
  92.4 10.0 %copy-start.2 = (f32[5,256]{1,0:T(8,128)S(1)}, f32[5,256]{1,0:T(8,128)}, u32[]{:S(2)}) copy-start(f32[5,256]{1,0:T(8,128)} %as_ref.1) | copy-start | bytes 15364
  96.5 6.0 %collective-permute-start.25 = (bf16[4,144,128]{2,1,0:T(8,128)(2,1)S(1)}, bf16[4,144,128]{2,1,0:T(8,128)(2,1)S(1)}, u32[]{:S(2)}, u32[]{:S(2)}) collective-permute-start(bf16[4,144,128]{2,1,0:T(8,128)(2,1)S(1)} %end.1.e0), channel_id=1, source_target_pairs={{0,1},{1,0},{2,3},{3,2},{4,5},{5,4},{6,7},{7,6},{8,9},{9,8},{10,11... | collective-permute-start | bytes 442376 | tf_op jit(solution)/shard_map/ppermute | solution.py:21
  (8 other events, 35.9 us)

commit v3 on v2

--- a/solution.py
+++ b/solution.py
@@ -11,7 +11,7 @@
 GROUP = 4
 EXTRA = 16
 TRIG = 16
-OPEN_LIMIT = 60
+OPEN_LIMIT = 58
 BF = jnp.bfloat16
 F32 = jnp.float32
 
@@ -109,14 +109,16 @@
     inv = 1.0 / math.sqrt(rows * nrow)
     tile = tile_of(quarter)
     device = lax.axis_index("dim")
-    place_arr = ((device >> shift) & (GROUP - 1)).astype(jnp.int32).reshape(1)
+    place_arr = device.astype(jnp.int32).reshape(1)
     last, third = sections - 1, sections - 2
     product = rows * BLOCK * BLOCK * 2
     grad_rows = BLOCK + EXTRA
 
-    ids = device * nb + jnp.arange(width, dtype=jnp.int32) // BLOCK
-    bits = (ids[None, :] >> jnp.arange(sections, dtype=jnp.int32)[:, None]) & 1
-    signs = jnp.where(bits == 0, 1.0, -1.0).astype(F32)
+    def signs(place_ref):
+        dims = (sections, width)
+        ids = place_ref[0] * nb + lax.broadcasted_iota(jnp.int32, dims, 1) // BLOCK
+        bits = lax.shift_right_logical(ids, lax.broadcasted_iota(jnp.int32, dims, 0)) & 1
+        return 1.0 - 2.0 * bits.astype(F32)
 
     def col(c):
         return slice(c * BLOCK, (c + 1) * BLOCK)
@@ -124,12 +126,19 @@
     def cs(ref, s, c):
         return ref[s : s + 1, col(c)], ref[sections + s : sections + s + 1, col(c)]
 
+    def place_of(place_ref):
+        return lax.shift_right_logical(place_ref[0], shift) & (GROUP - 1)
+
     def quarter_at(z, m):
         return pl.multiple_of(jnp.bitwise_xor(z, m) * quarter, 16)
 
     order = [2, 3, 1, 0]
     early = local_bits + 1
-    high = quarter + BLOCK + TRIG
+    base = quarter + TRIG
+    highs = [base + (0 if m == GROUP - 1 else BLOCK) for m in range(GROUP)]
+
+    def placed(refs):
+        return [refs[order.index(m)] for m in range(GROUP)]
 
     def forward(u, weights, trig_ref):
         steps = []
@@ -145,105 +154,84 @@
             u = turned
         return steps, u
 
-    def open_body(place_ref, u_hbm, w_hbm, codes_hbm, angle_ref, sign_ref, *rest):
-        p_hbm, v_hbm, wb_hbm, trig_out = rest[:GROUP], *rest[GROUP : GROUP + 3]
-        u_held, w_held, c_held, p_held, v_held, wb_held = rest[GROUP + 3 : GROUP + 9]
-        u_sems, w_sems, c_sems, p_sems, v_sems, wb_sem = rest[GROUP + 9 :]
-        z = place_ref[0]
-
-        def part(m):
-            return pl.ds(m * quarter, quarter)
-
-        w_in = [
-            pltpu.make_async_copy(w_hbm.at[s], w_held.at[s], w_sems.at[s]) for s in range(sections)
-        ]
-        u_in = [
-            pltpu.make_async_copy(u_hbm.at[part(m)], u_held.at[part(m)], u_sems.at[m])
-            for m in range(GROUP)
-        ]
+    def pack_body(place_ref, w_hbm, codes_hbm, angle_hbm, *rest):
+        p_out, trig_out = rest[:GROUP], rest[GROUP]
+        w_held, c_held, a_held, w_sem, c_sems, a_sem = rest[GROUP + 1 :]
+        z = place_of(place_ref)
+        a_in = pltpu.make_async_copy(angle_hbm, a_held, a_sem)
+        w_in = pltpu.make_async_copy(w_hbm.at[last], w_held, w_sem)
         c_in = [
             pltpu.make_async_copy(
                 codes_hbm.at[pl.ds(quarter_at(z, m), quarter)], c_held.at[m], c_sems.at[m]
             )
             for m in range(GROUP)
         ]
-        p_out = [pltpu.make_async_copy(p_held.at[m], p_hbm[m], p_sems.at[m]) for m in range(GROUP)]
-        v_out = [
-            pltpu.make_async_copy(v_held.at[part(m)], v_hbm.at[part(m)], v_sems.at[m])
-            for m in range(GROUP)
-        ]
-        wb_out = pltpu.make_async_copy(wb_held, wb_hbm, wb_sem)
-        for copy in w_in[:early] + u_in + w_in[early:]:
-            copy.start()
+        a_in.start()
+        w_in.start()
         for m in order:
             c_in[m].start()
-        angle = angle_ref[...]
-        co, si = jnp.cos(angle), sign_ref[...] * jnp.sin(angle)
+        a_in.wait()
+        angle = a_held[...]
+        co, si = jnp.cos(angle), signs(place_ref) * jnp.sin(angle)
         trig_out[...] = jnp.concatenate([co, si], axis=0)
-        for s in range(early):
-            w_in[s].wait()
-            wb_held[s] = w_held[s].astype(BF)
-        weights = [[wb_held[s, col(c), :] for c in chunks] for s in range(early)]
-        for m in range(GROUP):
-            u_in[m].wait()
-            for r in range(m * quarter, (m + 1) * quarter, tile):
-                at = pl.ds(r, tile)
-                u = forward([u_held[at, col(c)] for c in chunks], weights, trig_out)[1]
-                for c in chunks:
-                    v_held[at, col(c)] = dot(u[c], weights[local_bits][c]).astype(BF)
-            v_out[m].start()
-        for s in range(early, sections):
-            w_in[s].wait()
-            wb_held[s] = w_held[s].astype(BF)
-        wb_out.start()
         lines = []
         for s in (third, last):
             lines += split3(co[s : s + 1]) + split3(si[s : s + 1])
         lines = stack_lines(lines, TRIG).astype(BF)
+        w_in.wait()
         for m in order:
-            p_held[m, quarter + BLOCK :, :] = lines
-            for c in chunks:
-                p_held[m, quarter : quarter + BLOCK, col(c)] = wb_held[last, col(c), :]
+            p_out[m][quarter:base, :] = lines
+            if highs[m] > base:
+                for c in chunks:
+                    p_out[m][base:, col(c)] = w_held[col(c), :].astype(BF)
             c_in[m].wait()
             for r in range(0, quarter, tile):
                 at = pl.ds(r, tile)
-                p_held[m, at, :] = c_held[m, at, :].astype(F32).astype(BF)
-            p_out[m].start()
-        for copy in v_out + [wb_out] + p_out:
-            copy.wait()
-
-    opened = call(
-        "open",
-        open_body,
-        [shape((high, width))] * GROUP
-        + [shape((rows, width)), shape(blocks.shape), shape((2 * sections, width), F32)],
-        [place_arr, vectors, blocks, codes, angles, signs],
+                p_out[m][at, :] = c_held[m, at, :].astype(F32).astype(BF)
+
+    packed = call(
+        "pack",
+        pack_body,
+        [shape((high, width)) for high in highs] + [shape((2 * sections, width), F32)],
+        [place_arr, blocks, codes, angles],
         specs={0: SMEM, 1: HBM, 2: HBM, 3: HBM},
-        out_specs=[HBM] * (GROUP + 2) + [pl.BlockSpec((2 * sections, width), lambda i: (0, 0))],
         scratch=[
-            pltpu.VMEM((rows, width), BF),
-            pltpu.VMEM(blocks.shape, F32),
+            pltpu.VMEM((width, BLOCK), F32),
             pltpu.VMEM((GROUP, quarter, width), jnp.int32),
-            pltpu.VMEM((GROUP, high, width), BF),
-            pltpu.VMEM((rows, width), BF),
-            pltpu.VMEM(blocks.shape, BF),
-            pltpu.SemaphoreType.DMA((GROUP,)),
-            pltpu.SemaphoreType.DMA((sections,)),
-            pltpu.SemaphoreType.DMA((GROUP,)),
-            pltpu.SemaphoreType.DMA((GROUP,)),
+            pltpu.VMEM(angles.shape, F32),
+            pltpu.SemaphoreType.DMA,
             pltpu.SemaphoreType.DMA((GROUP,)),
             pltpu.SemaphoreType.DMA,
         ],
-        flops=rows * width * BLOCK * 4,
         limit=OPEN_LIMIT,
     )
-    packed, v_first, wb, trig = opened[:GROUP], *opened[GROUP:]
-    other_first = swapped(v_first, "dim", 1)
+    trig = packed.pop()
     packs = {m: swapped(packed[m], "dim", m << shift) for m in order[:-1]}
     packs[0] = packed[0]
 
+    def first_body(u_ref, w_ref, trig_ref, v_out, wb_out):
+        for s in range(early):
+            wb_out[s] = w_ref[s].astype(BF)
+        weights = [[wb_out[s, col(c), :] for c in chunks] for s in range(early)]
+        for r in range(0, rows, tile):
+            at = pl.ds(r, tile)
+            u = forward([u_ref[at, col(c)] for c in chunks], weights, trig_ref)[1]
+            for c in chunks:
+                v_out[at, col(c)] = dot(u[c], weights[local_bits][c]).astype(BF)
+        for s in range(early, sections):
+            wb_out[s] = w_ref[s].astype(BF)
+
+    v_first, wb = call(
+        "first",
+        first_body,
+        [shape((rows, width)), shape(blocks.shape)],
+        [vectors, blocks, trig],
+        flops=rows * width * BLOCK * 4,
+    )
+    other_first = swapped(v_first, "dim", 1)
+
     def scale_body(place_ref, table_ref, index_ref, out):
-        index = index_ref[pl.ds(place_ref[0], 1), :]
+        index = index_ref[pl.ds(place_of(place_ref), 1), :]
         values = jnp.zeros(index.shape, F32)
         for level in range(table_ref.shape[0]):
             values = jnp.where(index == level, table_ref[level], values)
@@ -267,7 +255,7 @@
         def body(place_ref, v_ref, o_ref, w_ref, trig_ref, *outs):
             co, si = cs(trig_ref, s, c)
             w = w_ref[s + 1, col(c), :]
-            z = place_ref[0]
+            z = place_of(place_ref)
             for m in range(GROUP):
                 start = quarter_at(z, m) if quarters else m * quarter
                 for r in range(0, quarter, tile):
@@ -291,36 +279,54 @@
             flops=product,
         )
 
+    def with_weights(mine):
+        def body(m_ref, p_ref, out):
+            for r in range(0, quarter, tile):
+                at = pl.ds(r, tile)
+                out[at, :] = m_ref[at, :]
+            for c in chunks:
+                out[quarter + c * BLOCK : quarter + (c + 1) * BLOCK, :] = p_ref[base:, col(c)]
+
+        return call(
+            "near", body, [shape((quarter + nb * BLOCK, BLOCK))], [mine, packs[GROUP - 2]]
+        )[0]
+
     middles = list(range(local_bits, third))
     state = {c: (v_first, other_first) for c in chunks}
     for s in middles:
         for c in chunks:
             v, other = state[c]
+            if s + 1 == third and c == chunks[0]:
+                other, packs[1] = lax.optimization_barrier((other, packs[1]))
             out = middle(c, s, v, other, s + 1 == third)
             saves[c][s] = (v, other)
             if s + 1 < third:
                 state[c] = (out[0], swapped(out[0], "dim", 1 << (s + 1 - local_bits)))
             else:
+                if c == chunks[0]:
+                    out[1] = with_weights(out[1])
                 got = {m: swapped(out[m], "dim", m << shift) for m in order[:-1]}
                 got[0] = out[0]
-                state[c] = [got[m] for m in range(GROUP)]
+                state[c] = [got[m] for m in order]
+                if c == chunks[0]:
+                    relayed = got[1]
 
     def group_stage(c, earlier):
         final = c == chunks[-1]
 
         def body(*refs):
-            a_refs, p_refs = refs[:GROUP], refs[GROUP : 2 * GROUP]
-            f_ref = refs[2 * GROUP]
-            e_refs = refs[2 * GROUP + 1 : 2 * GROUP + 1 + len(earlier)]
-            refs = refs[2 * GROUP + 1 + len(earlier) :]
+            a_refs, p_refs = placed(refs[:GROUP]), placed(refs[GROUP : 2 * GROUP])
+            f_ref, far_ref = refs[2 * GROUP], refs[2 * GROUP + 1]
+            e_refs = refs[2 * GROUP + 2 : 2 * GROUP + 2 + len(earlier)]
+            refs = refs[2 * GROUP + 2 + len(earlier) :]
             outs, grad_refs = refs[:GROUP], refs[GROUP:]
             coef, w = [], []
             for m in range(GROUP):
-                t = p_refs[m][quarter + BLOCK :, col(c)].astype(F32)
+                t = p_refs[m][quarter:base, col(c)].astype(F32)
                 coef.append(
                     [t[3 * k : 3 * k + 1] + t[3 * k + 1 : 3 * k + 2] + t[3 * k + 2 : 3 * k + 3] for k in range(4)]
                 )
-                w.append(p_refs[m][quarter : quarter + BLOCK, col(c)])
+                w.append(p_refs[m][base:, col(c)] if highs[m] > base else far_ref[quarter + c * BLOCK : quarter + (c + 1) * BLOCK, :])
             gw = [jnp.zeros((BLOCK, BLOCK), F32)] * GROUP
             ga = [[jnp.zeros((1, BLOCK), F32)] * GROUP for _ in range(2)]
             every = range(GROUP)
@@ -375,13 +381,15 @@
             f"group_chunk{c}",
             body,
             [shape((quarter, BLOCK))] * GROUP + grads,
-            state[c] + [packs[m] for m in range(GROUP)] + [factor] + earlier,
+            state[c] + [packs[m] for m in order] + [factor, relayed] + earlier,
             flops=3 * product,
         )
 
     returned, partial = {}, []
     for c in chunks:
         out = group_stage(c, list(partial))
+        if c > 0:
+            out[2], out[3], _ = lax.optimization_barrier((out[2], out[3], returned[c - 1][2]))
         returned[c] = {m: swapped(out[m], "dim", m << shift) for m in order[:-1]}
         returned[c][0] = out[0]
         partial.append(out[GROUP])
@@ -416,9 +424,9 @@
         v, other = saves[c][s - 1]
 
         def body(place_ref, *refs):
-            d_refs = refs[:GROUP]
+            d_refs = placed(refs[:GROUP])
             v_ref, o_ref, w_ref, trig_ref, g_out, q_out, grad = refs[GROUP:]
-            spans = [quarter_at(place_ref[0], m) for m in range(GROUP)]
+            spans = [quarter_at(place_of(place_ref), m) for m in range(GROUP)]
 
             def load(m, r, at):
                 return d_refs[m][r : r + tile, :]
@@ -429,7 +437,7 @@
             f"backward{s}_chunk{c}",
             body,
             [shape((rows, BLOCK)), shape((rows, BLOCK)), grad_shape],
-            [place_arr] + [returned[c][m] for m in range(GROUP)] + [v, other, wb, trig],
+            [place_arr] + [returned[c][m] for m in order] + [v, other, wb, trig],
             specs={0: SMEM},
             flops=2 * product,
         )
@@ -501,8 +509,7 @@
 
     def end_body(*refs):
         g_refs, i_refs = refs[:nb], refs[nb : 2 * nb]
-        u_ref, w_ref, trig_ref, grad = refs[2 * nb :]
-        gw = [[jnp.zeros((BLOCK, BLOCK), F32)] * nb for _ in range(early)]
+        u_ref, w_ref, trig_ref, grad, u_held, d_held = refs[2 * nb :]
         ga = [[jnp.zeros((1, BLOCK), F32)] * nb for _ in range(early)]
         w = [[w_ref[s, col(c), :] for c in chunks] for s in range(early)]
         for r in range(0, rows, tile):
@@ -517,7 +524,9 @@
                 )
             for s in reversed(range(early)):
                 for c in chunks:
-                    gw[s][c] = gw[s][c] + t_dot(inputs[s][c], d[c])
+                    d_held[s, at, col(c)] = d[c]
+                    if s:
+                        u_held[s - 1, at, col(c)] = inputs[s][c]
                 if s == 0:
                     break
                 g = [dot_t(d[c], w[s][c]).astype(BF).astype(F32) for c in chunks]
@@ -535,7 +544,8 @@
                 ]
         for s in range(early):
             for c in chunks:
-                matrix, lines = pack_grad(gw[s][c], [ga[s][c]])
+                left = u_held[s - 1, :, col(c)] if s else u_ref[:, col(c)]
+                matrix, lines = pack_grad(t_dot(left, d_held[s, :, col(c)]), [ga[s][c]])
                 grad[s * nb + c, :BLOCK, :] = matrix
                 grad[s * nb + c, BLOCK:, :] = lines
 
@@ -546,6 +556,7 @@
         [flow[c][0] for c in chunks]
         + [flow[c][1] for c in chunks]
         + [vectors, wb, trig],
+        scratch=[pltpu.VMEM((local_bits, rows, width), BF), pltpu.VMEM((early, rows, width), BF)],
         flops=6 * product,
     )
 
@@ -555,7 +566,7 @@
         pairs = [lax.psum(ends.astype(F32), "row"), lax.psum(upper.astype(F32), "row")]
         pairs = [(p, jnp.zeros_like(p)) for p in pairs]
 
-    def final_body(e0, e1, p0, p1, bs_ref, as_ref, sign_ref, step, new, step_a, new_a):
+    def final_body(place_ref, e0, e1, p0, p1, bs_ref, as_ref, step, new, step_a, new_a):
         def get(s, c):
             k = s * nb + c
             a, b = (e0, e1) if s < early else (p0, p1)
@@ -563,6 +574,7 @@
             matrix = a[k, :BLOCK, :].astype(F32) + b[k, :BLOCK, :].astype(F32)
             return matrix, a[k, BLOCK:, :].astype(F32) + b[k, BLOCK:, :].astype(F32)
 
+        sign = signs(place_ref)
         for c in chunks:
             angle = [None] * sections
             for s in range(sections):
@@ -576,7 +588,7 @@
                     angle[s - 1] = unpack_line(lines, 0)
                 elif s < local_bits:
                     angle[s] = unpack_line(lines, 0)
-            g = jnp.concatenate(angle, axis=0) * sign_ref[:, col(c)]
+            g = jnp.concatenate(angle, axis=0) * sign[:, col(c)]
             state_new = 0.9 * as_ref[:, col(c)] + 0.1 * g * g
             new_a[:, col(c)] = state_new
             step_a[:, col(c)] = g * lax.rsqrt(state_new)
@@ -585,7 +597,8 @@
         "final",
         final_body,
         [shape(block_state.shape, F32)] * 2 + [shape(angle_state.shape, F32)] * 2,
-        [*pairs[0], *pairs[1], block_state, angle_state, signs],
+        [place_arr, *pairs[0], *pairs[1], block_state, angle_state],
+        specs={0: SMEM},
     )
     return step, new, step_a, new_a
 

time: 104 us -> 96.3 us (0.926)
  the two profiles are of different devices: /device:TPU:20 before, /device:TPU:0 now
where the time goes in v3:
time: 96.3 us; the launch traced here: 94.7 us
  waiting for transfers between devices  39.3 us (41%)
  starting transfers between devices  33.9 us (35%)
  Pallas kernels  18.1 us (19%)
  local copies, waits for them, and re-layouts  2.52 us (3%)
    ppermute x27, waiting for transfers between devices, swapped(): return lax.ppermute(value, axis, pairs)  39.3 us
    ppermute x27, starting transfers between devices, swapped(): return lax.ppermute(value, axis, pairs)  33.9 us
    pallas_call x16, Pallas kernels, call(): pl.pallas_call(body, grid=(1,), in_specs=whole, out_specs=out_specs or [p...  18.1 us
    unnamed x24, local copies, waits for them, and re-layouts  2.44 us
  transfers between devices with their start and end apart: 27, of which 14 were waited for; matrix products, arithmetic and copies ran while one was open for 0% of the time, Pallas kernels for 13%

profile of v3, /device:TPU:0, one launch (start us, length us, event | category | flops | bytes accessed | tf_op | source)
XLA Modules:
  0.0 94.7 jit_solution(13364636365286338346)
XLA Ops:
  0.7 2.6 %pack.1 = (bf16[560,256]{1,0:T(8,128)(2,1)}, bf16[560,256]{1,0:T(8,128)(2,1)}, bf16[560,256]{1,0:T(8,128)(2,1)}, bf16[432,256]{1,0:T(8,128)(2,1)}, f32[10,256]{1,0:T(8,128)}) custom-call(s32[1]{0:T(128)} %bitcast.place_ref, f32[5,256,128]{2,1,0:T(8,128)} %w_ref.1, s32[1664,256]{1,0:T(8,128)} %codes_hbm.1, f32[5,256]{1,0:T(8,128)} %angle_hbm.1), custom_call_target="tpu_custom_call" | custom-call | bytes 69120080 | tf_op jit(solution)/shard_map/pack/pallas_call | solution.py:52
  4.0 1.8 %first.1 = (bf16[1664,256]{1,0:T(8,128)(2,1)S(1)}, bf16[5,256,128]{2,1,0:T(8,128)(2,1)S(1)}) custom-call(bf16[1664,256]{1,0:T(8,128)(2,1)S(1)} %copy-done.4, f32[5,256,128]{2,1,0:T(8,128)S(1)} %copy-done.1, f32[10,256]{1,0:T(8,128)S(1)} %copy-done.6), custom_call_target="tpu_custom_call" | custom-call | flops 21810380800 | bytes 53944320 | tf_op jit(solution)/shard_map/first/pallas_call | solution.py:52
  7.0 4.6 %collective-permute-start.7 = (bf16[432,256]{1,0:T(8,128)(2,1)}, bf16[432,256]{1,0:T(8,128)(2,1)}, u32[]{:S(2)}, u32[]{:S(2)}) collective-permute-start(bf16[432,256]{1,0:T(8,128)(2,1)} %get-tuple-element.61), channel_id=1, source_target_pairs={{0,24},{2,26},{4,28},{6,30},{8,16},{10,18},{12,20},{14,22},{16,8},... | collective-permute-start | bytes 663560 | tf_op jit(solution)/shard_map/ppermute | solution.py:21
  13.1 1.0 %copy-done.9 = bf16[5,256,128]{2,1,0:T(8,128)(2,1)S(1)} copy-done((bf16[5,256,128]{2,1,0:T(8,128)(2,1)S(1)}, bf16[5,256,128]{2,1,0:T(8,128)(2,1)}, u32[]{:S(2)}) %copy-start.9) | copy-done | bytes 327704
  14.5 1.8 %collective-permute-start.1 = (bf16[1664,128]{1,0:T(8,128)(2,1)S(1)}, bf16[1664,128]{1,0:T(8,128)(2,1)S(1)}, u32[]{:S(2)}, u32[]{:S(2)}) collective-permute-start(bf16[1664,128]{1,0:T(8,128)(2,1)S(1)} %forward2_chunk0.1.v_ref.refs_4_), channel_id=1, source_target_pairs={{0,4},{2,6},{4,0},{6,2},{8,12},{10,14},{12,8},{14,10},{16,20},{18,... | collective-permute-start | bytes 1277960 | tf_op jit(solution)/shard_map/ppermute | solution.py:21
  17.0 9.6 %collective-permute-done.2.refs_6_ = bf16[560,256]{1,0:T(8,128)(2,1)S(1)} collective-permute-done((bf16[560,256]{1,0:T(8,128)(2,1)}, bf16[560,256]{1,0:T(8,128)(2,1)S(1)}, u32[]{:S(2)}, u32[]{:S(2)}) %collective-permute-start.2) | collective-permute-done | bytes 286752 | tf_op jit(solution)/shard_map/ppermute | solution.py:21
  27.6 2.4 %collective-permute-start.3 = (bf16[416,128]{1,0:T(8,128)(2,1)S(1)}, bf16[416,128]{1,0:T(8,128)(2,1)S(1)}, u32[]{:S(2)}, u32[]{:S(2)}) collective-permute-start(bf16[416,128]{1,0:T(8,128)(2,1)S(1)} %get-tuple-element.56), channel_id=1, source_target_pairs={{0,16},{2,18},{4,20},{6,22},{8,24},{10,26},{12,28},{14,30},{16,0},... | collective-permute-start | bytes 319496 | tf_op jit(solution)/shard_map/ppermute | solution.py:21
  30.0 1.6 %collective-permute-start.4 = (bf16[416,128]{1,0:T(8,128)(2,1)S(1)}, bf16[416,128]{1,0:T(8,128)(2,1)S(1)}, u32[]{:S(2)}, u32[]{:S(2)}) collective-permute-start(bf16[416,128]{1,0:T(8,128)(2,1)S(1)} %get-tuple-element.57), channel_id=1, source_target_pairs={{0,24},{2,26},{4,28},{6,30},{8,16},{10,18},{12,20},{14,22},{16,8},... | collective-permute-start | bytes 319496 | tf_op jit(solution)/shard_map/ppermute | solution.py:21
  31.6 7.5 %collective-permute-done.5.p_ref.refs_4_ = bf16[560,256]{1,0:T(8,128)(2,1)S(1)} collective-permute-done((bf16[560,256]{1,0:T(8,128)(2,1)}, bf16[560,256]{1,0:T(8,128)(2,1)S(1)}, u32[]{:S(2)}, u32[]{:S(2)}) %collective-permute-start.5) | collective-permute-done | bytes 286752 | tf_op jit(solution)/shard_map/ppermute | solution.py:21
  39.6 3.1 %collective-permute-start.13 = (bf16[416,128]{1,0:T(8,128)(2,1)S(1)}, bf16[416,128]{1,0:T(8,128)(2,1)S(1)}, u32[]{:S(2)}, u32[]{:S(2)}) collective-permute-start(bf16[416,128]{1,0:T(8,128)(2,1)S(1)} %get-tuple-element.71), channel_id=1, source_target_pairs={{0,16},{2,18},{4,20},{6,22},{8,24},{10,26},{12,28},{14,30},{16,0},... | collective-permute-start | bytes 319496 | tf_op jit(solution)/shard_map/ppermute | solution.py:21
  42.7 1.4 %collective-permute-start.14 = (bf16[416,128]{1,0:T(8,128)(2,1)S(1)}, bf16[416,128]{1,0:T(8,128)(2,1)S(1)}, u32[]{:S(2)}, u32[]{:S(2)}) collective-permute-start(bf16[416,128]{1,0:T(8,128)(2,1)S(1)} %get-tuple-element.72), channel_id=1, source_target_pairs={{0,24},{2,26},{4,28},{6,30},{8,16},{10,18},{12,20},{14,22},{16,8},... | collective-permute-start | bytes 319496 | tf_op jit(solution)/shard_map/ppermute | solution.py:21
  44.1 5.0 %collective-permute-done.6.refs_2_.refs_9_ = bf16[672,128]{1,0:T(8,128)(2,1)S(1)} collective-permute-done((bf16[672,128]{1,0:T(8,128)(2,1)S(1)}, bf16[672,128]{1,0:T(8,128)(2,1)S(1)}, u32[]{:S(2)}, u32[]{:S(2)}) %collective-permute-start.6) | collective-permute-done | bytes 172064 | tf_op jit(solution)/shard_map/ppermute | solution.py:21
  49.1 2.4 %group_chunk0.1 = (bf16[416,128]{1,0:T(8,128)(2,1)S(1)}, bf16[416,128]{1,0:T(8,128)(2,1)S(1)}, bf16[416,128]{1,0:T(8,128)(2,1)S(1)}, bf16[416,128]{1,0:T(8,128)(2,1)S(1)}, bf16[4,144,128]{2,1,0:T(8,128)(2,1)S(1)}) custom-call(bf16[416,128]{1,0:T(8,128)(2,1)S(1)} %collective-permute-done.3.refs_0_, bf16[416,128]{1,0:T(8,128)(2,1)S(1)} %collective-permute-done.4.refs_1_, ...), custom_call_target="tpu_custom_call" | custom-call | flops 16357785600 | bytes 50626560 | tf_op jit(solution)/shard_map/group_chunk0/pallas_call | solution.py:52
  51.5 3.2 %collective-permute-start.9 = (bf16[416,128]{1,0:T(8,128)(2,1)S(1)}, bf16[416,128]{1,0:T(8,128)(2,1)S(1)}, u32[]{:S(2)}, u32[]{:S(2)}) collective-permute-start(bf16[416,128]{1,0:T(8,128)(2,1)S(1)} %get-tuple-element.65), channel_id=1, source_target_pairs={{0,24},{2,26},{4,28},{6,30},{8,16},{10,18},{12,20},{14,22},{16,8},... | collective-permute-start | bytes 319496 | tf_op jit(solution)/shard_map/ppermute | solution.py:21
  55.2 2.4 %group_chunk1.1 = (bf16[416,128]{1,0:T(8,128)(2,1)S(1)}, bf16[416,128]{1,0:T(8,128)(2,1)S(1)}, bf16[416,128]{1,0:T(8,128)(2,1)S(1)}, bf16[416,128]{1,0:T(8,128)(...) custom-call(bf16[416,128]{1,0:T(8,128)(2,1)S(1)} %collective-permute, ...), custom_call_target="tpu_custom_call" | custom-call | flops 16357785600 | bytes 54476800 | tf_op jit(solution)/shard_map/group_chunk1/pallas_call | solution.py:52
  57.6 1.6 %collective-permute-start.18 = (bf16[416,128]{1,0:T(8,128)(2,1)S(1)}, bf16[416,128]{1,0:T(8,128)(2,1)S(1)}, u32[]{:S(2)}, u32[]{:S(2)}) collective-permute-start(bf16[416,128]{1,0:T(8,128)(2,1)S(1)} %get-tuple-element.80), channel_id=1, source_target_pairs={{0,8},{2,10},{4,12},{6,14},{8,0},{10,2},{12,4},{14,6},{16,24},{18,... | collective-permute-start | bytes 319496 | tf_op jit(solution)/shard_map/ppermute | solution.py:21
  59.2 1.4 %collective-permute-done.8.refs_0_ = bf16[416,128]{1,0:T(8,128)(2,1)S(1)} collective-permute-done((bf16[416,128]{1,0:T(8,128)(2,1)S(1)}, bf16[416,128]{1,0:T(8,128)(2,1)S(1)}, u32[]{:S(2)}, u32[]{:S(2)}) %collective-permute-start.8) | collective-permute-done | bytes 106528 | tf_op jit(solution)/shard_map/ppermute | solution.py:21
  61.1 1.4 %collective-permute-start.17 = (bf16[416,128]{1,0:T(8,128)(2,1)S(1)}, bf16[416,128]{1,0:T(8,128)(2,1)S(1)}, u32[]{:S(2)}, u32[]{:S(2)}) collective-permute-start(bf16[416,128]{1,0:T(8,128)(2,1)S(1)} %get-tuple-element.79), channel_id=1, source_target_pairs={{0,24},{2,26},{4,28},{6,30},{8,16},{10,18},{12,20},{14,22},{16,8},... | collective-permute-start | bytes 319496 | tf_op jit(solution)/shard_map/ppermute | solution.py:21
  63.2 1.6 %collective-permute-start.11 = (bf16[1664,128]{1,0:T(8,128)(2,1)S(1)}, bf16[1664,128]{1,0:T(8,128)(2,1)S(1)}, u32[]{:S(2)}, u32[]{:S(2)}) collective-permute-start(bf16[1664,128]{1,0:T(8,128)(2,1)S(1)} %get-tuple-element.69), channel_id=1, source_target_pairs={{0,4},{2,6},{4,0},{6,2},{8,12},{10,14},{12,8},{14,10},{16,20},{18,... | collective-permute-start | bytes 1277960 | tf_op jit(solution)/shard_map/ppermute | solution.py:21
  64.8 4.7 %collective-permute-done.16.refs_0_ = bf16[416,128]{1,0:T(8,128)(2,1)S(1)} collective-permute-done((bf16[416,128]{1,0:T(8,128)(2,1)S(1)}, bf16[416,128]{1,0:T(8,128)(2,1)S(1)}, u32[]{:S(2)}, u32[]{:S(2)}) %collective-permute-start.16) | collective-permute-done | bytes 106528 | tf_op jit(solution)/shard_map/ppermute | solution.py:21
  70.1 1.6 %collective-permute-start.19 = (bf16[1664,128]{1,0:T(8,128)(2,1)S(1)}, bf16[1664,128]{1,0:T(8,128)(2,1)S(1)}, u32[]{:S(2)}, u32[]{:S(2)}) collective-permute-start(bf16[1664,128]{1,0:T(8,128)(2,1)S(1)} %get-tuple-element.83), channel_id=1, source_target_pairs={{0,4},{2,6},{4,0},{6,2},{8,12},{10,14},{12,8},{14,10},{16,20},{18,... | collective-permute-start | bytes 1277960 | tf_op jit(solution)/shard_map/ppermute | solution.py:21
  71.7 2.7 %collective-permute-start.20 = (bf16[2,144,128]{2,1,0:T(8,128)(2,1)S(1)}, bf16[2,144,128]{2,1,0:T(8,128)(2,1)S(1)}, u32[]{:S(2)}, u32[]{:S(2)}) collective-permute-start(bf16[2,144,128]{2,1,0:T(8,128)(2,1)S(1)} %get-tuple-element.88), channel_id=1, source_target_pairs={{0,16},{2,18},{4,20},{6,22},{8,24},{10,26},{12,28},{14,30},{16,0},... | collective-permute-start | bytes 221192 | tf_op jit(solution)/shard_map/ppermute | solution.py:21
  74.4 1.4 %collective-permute-start.21 = (bf16[2,144,128]{2,1,0:T(8,128)(2,1)S(1)}, bf16[2,144,128]{2,1,0:T(8,128)(2,1)S(1)}, u32[]{:S(2)}, u32[]{:S(2)}) collective-permute-start(bf16[2,144,128]{2,1,0:T(8,128)(2,1)S(1)} %get-tuple-element.89), channel_id=1, source_target_pairs={{0,24},{2,26},{4,28},{6,30},{8,16},{10,18},{12,20},{14,22},{16,8},... | collective-permute-start | bytes 221192 | tf_op jit(solution)/shard_map/ppermute | solution.py:21
  76.7 2.3 %collective-permute-done.20.refs_2_ = bf16[2,144,128]{2,1,0:T(8,128)(2,1)S(1)} collective-permute-done((bf16[2,144,128]{2,1,0:T(8,128)(2,1)S(1)}, bf16[2,144,128]{2,1,0:T(8,128)(2,1)S(1)}, u32[]{:S(2)}, u32[]{:S(2)}) %collective-permute-start.20) | collective-permute-done | bytes 73760 | tf_op jit(solution)/shard_map/ppermute | solution.py:21
  79.0 1.7 %collective-permute-done.21.refs_3_ = bf16[2,144,128]{2,1,0:T(8,128)(2,1)S(1)} collective-permute-done((bf16[2,144,128]{2,1,0:T(8,128)(2,1)S(1)}, bf16[2,144,128]{2,1,0:T(8,128)(2,1)S(1)}, u32[]{:S(2)}, u32[]{:S(2)}) %collective-permute-start.21) | collective-permute-done | bytes 73760 | tf_op jit(solution)/shard_map/ppermute | solution.py:21
  81.1 1.3 %backward2_chunk1.1 = (bf16[1664,128]{1,0:T(8,128)(2,1)S(1)}, bf16[1664,128]{1,0:T(8,128)(2,1)S(1)}, f32[144,128]{1,0:T(8,128)}, bf16[6,144,128]{2,1,0:T(8,128)(2,1)S(1)}) custom-call(bf16[1664,128]{1,0:T(8,128)(2,1)S(1)} %get-tuple-element.82.g_ref, bf16[1664,128]{1,0:T(8,128)(2,1)S(1)} %collective-permute-done.19.i_ref, ...), custom_call_target="tpu_custom_call" | custom-call | flops 10905190400 | bytes 93347840 | tf_op jit(solution)/shard_map/backward2_chunk1/pallas_call | solution.py:52
  82.4 1.5 %collective-permute-start.26 = (bf16[6,144,128]{2,1,0:T(8,128)(2,1)S(1)}, bf16[6,144,128]{2,1,0:T(8,128)(2,1)S(1)}, u32[]{:S(2)}, u32[]{:S(2)}) collective-permute-start(bf16[6,144,128]{2,1,0:T(8,128)(2,1)S(1)} %get-tuple-element.97.p0), channel_id=1, source_target_pairs={{0,1},{1,0},{2,3},{3,2},{4,5},{5,4},{6,7},{7,6},{8,9},{9,8},{10,11... | collective-permute-start | bytes 663560 | tf_op jit(solution)/shard_map/ppermute | solution.py:21
  84.2 2.1 %end.1.e0 = bf16[4,144,128]{2,1,0:T(8,128)(2,1)S(1)} custom-call(bf16[1664,128]{1,0:T(8,128)(2,1)S(1)} %get-tuple-element.70.refs_0_, bf16[1664,128]{1,0:T(8,128)(2,1)S(1)} %get-tuple-element.94.refs_1_, bf16[1664,128]{1,0:T(8,128)(2,1)S(1)} %collective-permute-done.23.refs_2_, bf16[1664,128]{1,0:T(8,128)(2,1)S(1)} %collective-permute-done.24.refs_3_, ...), custom_call_target="tpu_custom_call" | custom-call | flops 32715571200 | bytes 60825600 | tf_op jit(solution)/shard_map/end/pallas_call | solution.py:52
  86.4 1.6 %collective-permute-start.25 = (bf16[4,144,128]{2,1,0:T(8,128)(2,1)S(1)}, bf16[4,144,128]{2,1,0:T(8,128)(2,1)S(1)}, u32[]{:S(2)}, u32[]{:S(2)}) collective-permute-start(bf16[4,144,128]{2,1,0:T(8,128)(2,1)S(1)} %end.1.e0), channel_id=1, source_target_pairs={{0,1},{1,0},{2,3},{3,2},{4,5},{5,4},{6,7},{7,6},{8,9},{9,8},{10,11... | collective-permute-start | bytes 442376 | tf_op jit(solution)/shard_map/ppermute | solution.py:21
  87.9 2.8 %collective-permute-done.26.p1 = bf16[6,144,128]{2,1,0:T(8,128)(2,1)S(1)} collective-permute-done((bf16[6,144,128]{2,1,0:T(8,128)(2,1)S(1)}, bf16[6,144,128]{2,1,0:T(8,128)(2,1)S(1)}, u32[]{:S(2)}, u32[]{:S(2)}) %collective-permute-start.26) | collective-permute-done | bytes 221216 | tf_op jit(solution)/shard_map/ppermute | solution.py:21
  90.7 2.8 %collective-permute-done.25.e1 = bf16[4,144,128]{2,1,0:T(8,128)(2,1)S(1)} collective-permute-done((bf16[4,144,128]{2,1,0:T(8,128)(2,1)S(1)}, bf16[4,144,128]{2,1,0:T(8,128)(2,1)S(1)}, u32[]{:S(2)}, u32[]{:S(2)}) %collective-permute-start.25) | collective-permute-done | bytes 147488 | tf_op jit(solution)/shard_map/ppermute | solution.py:21
  93.4 1.2 %final.1 = (f32[5,256,128]{2,1,0:T(8,128)}, f32[5,256,128]{2,1,0:T(8,128)}, f32[5,256]{1,0:T(8,128)}, f32[5,256]{1,0:T(8,128)}) custom-call(s32[1]{0:T(128)} %bitcast.place_ref, bf16[4,144,128]{2,1,0:T(8,128)(2,1)S(1)} %end.1.e0, bf16[4,144,128]{2,1,0:T(8,128)(2,1)S(1)} %collective-permute-done.25.e1, bf16[6,144,128]{2,1,0:T(8,128)(2,1)S(1)} %get-tuple-element.97.p0, ...), custom_call_target="tpu_custom_call" | custom-call | bytes 54374480 | tf_op jit(solution)/shard_map/final/pallas_call | solution.py:52
  (63 shorter events, 9.9 us)
Async XLA Ops:
  4.0 9.1 %copy-start.7 = (f32[10,256]{1,0:T(8,128)S(1)}, f32[10,256]{1,0:T(8,128)}, u32[]{:S(2)}) copy-start(f32[10,256]{1,0:T(8,128)} %get-tuple-element.51.trig_ref.refs_7_.refs_6_) | copy-start | bytes 30724
  6.6 6.5 %collective-permute-start = (bf16[1664,256]{1,0:T(8,128)(2,1)S(1)}, bf16[1664,256]{1,0:T(8,128)(2,1)S(1)}, u32[]{:S(2)}, u32[]{:S(2)}) collective-permute-start(bf16[1664,256]{1,0:T(8,128)(2,1)S(1)} %get-tuple-element.52.v_ref), channel_id=1, source_target_pairs={{0,2},{2,0},{4,6},{6,4},{8,10},{10,8},{12,14},{14,12},{16,18},{18,... | collective-permute-start | bytes 2555912 | tf_op jit(solution)/shard_map/ppermute | solution.py:21
  7.0 35.7 %collective-permute-start.7 = (bf16[432,256]{1,0:T(8,128)(2,1)}, bf16[432,256]{1,0:T(8,128)(2,1)}, u32[]{:S(2)}, u32[]{:S(2)}) collective-permute-start(bf16[432,256]{1,0:T(8,128)(2,1)} %get-tuple-element.61), channel_id=1, source_target_pairs={{0,24},{2,26},{4,28},{6,30},{8,16},{10,18},{12,20},{14,22},{16,8},... | collective-permute-start | bytes 663560 | tf_op jit(solution)/shard_map/ppermute | solution.py:21
  11.6 15.0 %collective-permute-start.2 = (bf16[560,256]{1,0:T(8,128)(2,1)}, bf16[560,256]{1,0:T(8,128)(2,1)S(1)}, u32[]{:S(2)}, u32[]{:S(2)}) collective-permute-start(bf16[560,256]{1,0:T(8,128)(2,1)} %get-tuple-element.54), channel_id=1, source_target_pairs={{0,8},{2,10},{4,12},{6,14},{8,0},{10,2},{12,4},{14,6},{16,24},{18,... | collective-permute-start | bytes 860168 | tf_op jit(solution)/shard_map/ppermute | solution.py:21
  11.6 27.5 %collective-permute-start.5 = (bf16[560,256]{1,0:T(8,128)(2,1)}, bf16[560,256]{1,0:T(8,128)(2,1)S(1)}, u32[]{:S(2)}, u32[]{:S(2)}) collective-permute-start(bf16[560,256]{1,0:T(8,128)(2,1)} %get-tuple-element.59), channel_id=1, source_target_pairs={{0,16},{2,18},{4,20},{6,22},{8,24},{10,26},{12,28},{14,30},{16,0},... | collective-permute-start | bytes 860168 | tf_op jit(solution)/shard_map/ppermute | solution.py:21
  14.5 12.8 %collective-permute-start.1 = (bf16[1664,128]{1,0:T(8,128)(2,1)S(1)}, bf16[1664,128]{1,0:T(8,128)(2,1)S(1)}, u32[]{:S(2)}, u32[]{:S(2)}) collective-permute-start(bf16[1664,128]{1,0:T(8,128)(2,1)S(1)} %forward2_chunk0.1.v_ref.refs_4_), channel_id=1, source_target_pairs={{0,4},{2,6},{4,0},{6,2},{8,12},{10,14},{12,8},{14,10},{16,20},{18,... | collective-permute-start | bytes 1277960 | tf_op jit(solution)/shard_map/ppermute | solution.py:21
  16.6 22.6 %copy-start.10 = (bf16[5,256,128]{2,1,0:T(8,128)(2,1)S(1)}, bf16[5,256,128]{2,1,0:T(8,128)(2,1)}, u32[]{:S(2)}) copy-start(bf16[5,256,128]{2,1,0:T(8,128)(2,1)} %copy-done.8) | copy-start | bytes 983044
  16.7 22.6 %collective-permute-start.12 = (bf16[1664,128]{1,0:T(8,128)(2,1)S(1)}, bf16[1664,128]{1,0:T(8,128)(2,1)S(1)}, u32[]{:S(2)}, u32[]{:S(2)}) collective-permute-start(bf16[1664,128]{1,0:T(8,128)(2,1)S(1)} %forward2_chunk1.1.v_ref.refs_4_), channel_id=1, source_target_pairs={{0,4},{2,6},{4,0},{6,2},{8,12},{10,14},{12,8},{14,10},{16,20},{18,... | collective-permute-start | bytes 1277960 | tf_op jit(solution)/shard_map/ppermute | solution.py:21
  27.6 16.5 %collective-permute-start.3 = (bf16[416,128]{1,0:T(8,128)(2,1)S(1)}, bf16[416,128]{1,0:T(8,128)(2,1)S(1)}, u32[]{:S(2)}, u32[]{:S(2)}) collective-permute-start(bf16[416,128]{1,0:T(8,128)(2,1)S(1)} %get-tuple-element.56), channel_id=1, source_target_pairs={{0,16},{2,18},{4,20},{6,22},{8,24},{10,26},{12,28},{14,30},{16,0},... | collective-permute-start | bytes 319496 | tf_op jit(solution)/shard_map/ppermute | solution.py:21
  30.0 14.0 %collective-permute-start.4 = (bf16[416,128]{1,0:T(8,128)(2,1)S(1)}, bf16[416,128]{1,0:T(8,128)(2,1)S(1)}, u32[]{:S(2)}, u32[]{:S(2)}) collective-permute-start(bf16[416,128]{1,0:T(8,128)(2,1)S(1)} %get-tuple-element.57), channel_id=1, source_target_pairs={{0,24},{2,26},{4,28},{6,30},{8,16},{10,18},{12,20},{14,22},{16,8},... | collective-permute-start | bytes 319496 | tf_op jit(solution)/shard_map/ppermute | solution.py:21
  39.1 9.9 %copy-start.5 = (bf16[560,256]{1,0:T(8,128)(2,1)S(1)}, bf16[560,256]{1,0:T(8,128)(2,1)}, u32[]{:S(2)}) copy-start(bf16[560,256]{1,0:T(8,128)(2,1)} %get-tuple-element.63.refs_7_) | copy-start | bytes 860164
  39.1 9.9 %collective-permute-start.6 = (bf16[672,128]{1,0:T(8,128)(2,1)S(1)}, bf16[672,128]{1,0:T(8,128)(2,1)S(1)}, u32[]{:S(2)}, u32[]{:S(2)}) collective-permute-start(bf16[672,128]{1,0:T(8,128)(2,1)S(1)} %near.1), channel_id=1, source_target_pairs={{0,8},{2,10},{4,12},{6,14},{8,0},{10,2},{12,4},{14,6},{16,24},{18,... | collective-permute-start | bytes 516104 | tf_op jit(solution)/shard_map/ppermute | solution.py:21
  39.6 15.1 %collective-permute-start.13 = (bf16[416,128]{1,0:T(8,128)(2,1)S(1)}, bf16[416,128]{1,0:T(8,128)(2,1)S(1)}, u32[]{:S(2)}, u32[]{:S(2)}) collective-permute-start(bf16[416,128]{1,0:T(8,128)(2,1)S(1)} %get-tuple-element.71), channel_id=1, source_target_pairs={{0,16},{2,18},{4,20},{6,22},{8,24},{10,26},{12,28},{14,30},{16,0},... | collective-permute-start | bytes 319496 | tf_op jit(solution)/shard_map/ppermute | solution.py:21
  42.7 12.5 %collective-permute-start.14 = (bf16[416,128]{1,0:T(8,128)(2,1)S(1)}, bf16[416,128]{1,0:T(8,128)(2,1)S(1)}, u32[]{:S(2)}, u32[]{:S(2)}) collective-permute-start(bf16[416,128]{1,0:T(8,128)(2,1)S(1)} %get-tuple-element.72), channel_id=1, source_target_pairs={{0,24},{2,26},{4,28},{6,30},{8,16},{10,18},{12,20},{14,22},{16,8},... | collective-permute-start | bytes 319496 | tf_op jit(solution)/shard_map/ppermute | solution.py:21
  44.0 11.2 %collective-permute-start.15 = (bf16[416,128]{1,0:T(8,128)(2,1)S(1)}, bf16[416,128]{1,0:T(8,128)(2,1)S(1)}, u32[]{:S(2)}, u32[]{:S(2)}) collective-permute-start(bf16[416,128]{1,0:T(8,128)(2,1)S(1)} %get-tuple-element.73), channel_id=1, source_target_pairs={{0,8},{2,10},{4,12},{6,14},{8,0},{10,2},{12,4},{14,6},{16,24},{18,... | collective-permute-start | bytes 319496 | tf_op jit(solution)/shard_map/ppermute | solution.py:21
  51.4 9.2 %collective-permute-start.8 = (bf16[416,128]{1,0:T(8,128)(2,1)S(1)}, bf16[416,128]{1,0:T(8,128)(2,1)S(1)}, u32[]{:S(2)}, u32[]{:S(2)}) collective-permute-start(bf16[416,128]{1,0:T(8,128)(2,1)S(1)} %get-tuple-element.64), channel_id=1, source_target_pairs={{0,16},{2,18},{4,20},{6,22},{8,24},{10,26},{12,28},{14,30},{16,0},... | collective-permute-start | bytes 319496 | tf_op jit(solution)/shard_map/ppermute | solution.py:21
  51.5 11.1 %collective-permute-start.9 = (bf16[416,128]{1,0:T(8,128)(2,1)S(1)}, bf16[416,128]{1,0:T(8,128)(2,1)S(1)}, u32[]{:S(2)}, u32[]{:S(2)}) collective-permute-start(bf16[416,128]{1,0:T(8,128)(2,1)S(1)} %get-tuple-element.65), channel_id=1, source_target_pairs={{0,24},{2,26},{4,28},{6,30},{8,16},{10,18},{12,20},{14,22},{16,8},... | collective-permute-start | bytes 319496 | tf_op jit(solution)/shard_map/ppermute | solution.py:21
  54.7 7.9 %collective-permute-start.10 = (bf16[416,128]{1,0:T(8,128)(2,1)S(1)}, bf16[416,128]{1,0:T(8,128)(2,1)S(1)}, u32[]{:S(2)}, u32[]{:S(2)}) collective-permute-start(bf16[416,128]{1,0:T(8,128)(2,1)S(1)} %get-tuple-element.66), channel_id=1, source_target_pairs={{0,8},{2,10},{4,12},{6,14},{8,0},{10,2},{12,4},{14,6},{16,24},{18,... | collective-permute-start | bytes 319496 | tf_op jit(solution)/shard_map/ppermute | solution.py:21
  57.6 7.2 %collective-permute-start.18 = (bf16[416,128]{1,0:T(8,128)(2,1)S(1)}, bf16[416,128]{1,0:T(8,128)(2,1)S(1)}, u32[]{:S(2)}, u32[]{:S(2)}) collective-permute-start(bf16[416,128]{1,0:T(8,128)(2,1)S(1)} %get-tuple-element.80), channel_id=1, source_target_pairs={{0,8},{2,10},{4,12},{6,14},{8,0},{10,2},{12,4},{14,6},{16,24},{18,... | collective-permute-start | bytes 319496 | tf_op jit(solution)/shard_map/ppermute | solution.py:21
  60.6 8.9 %collective-permute-start.16 = (bf16[416,128]{1,0:T(8,128)(2,1)S(1)}, bf16[416,128]{1,0:T(8,128)(2,1)S(1)}, u32[]{:S(2)}, u32[]{:S(2)}) collective-permute-start(bf16[416,128]{1,0:T(8,128)(2,1)S(1)} %get-tuple-element.78), channel_id=1, source_target_pairs={{0,16},{2,18},{4,20},{6,22},{8,24},{10,26},{12,28},{14,30},{16,0},... | collective-permute-start | bytes 319496 | tf_op jit(solution)/shard_map/ppermute | solution.py:21
  61.1 8.4 %collective-permute-start.17 = (bf16[416,128]{1,0:T(8,128)(2,1)S(1)}, bf16[416,128]{1,0:T(8,128)(2,1)S(1)}, u32[]{:S(2)}, u32[]{:S(2)}) collective-permute-start(bf16[416,128]{1,0:T(8,128)(2,1)S(1)} %get-tuple-element.79), channel_id=1, source_target_pairs={{0,24},{2,26},{4,28},{6,30},{8,16},{10,18},{12,20},{14,22},{16,8},... | collective-permute-start | bytes 319496 | tf_op jit(solution)/shard_map/ppermute | solution.py:21
  63.2 12.8 %collective-permute-start.11 = (bf16[1664,128]{1,0:T(8,128)(2,1)S(1)}, bf16[1664,128]{1,0:T(8,128)(2,1)S(1)}, u32[]{:S(2)}, u32[]{:S(2)}) collective-permute-start(bf16[1664,128]{1,0:T(8,128)(2,1)S(1)} %get-tuple-element.69), channel_id=1, source_target_pairs={{0,4},{2,6},{4,0},{6,2},{8,12},{10,14},{12,8},{14,10},{16,20},{18,... | collective-permute-start | bytes 1277960 | tf_op jit(solution)/shard_map/ppermute | solution.py:21
  70.1 11.0 %collective-permute-start.19 = (bf16[1664,128]{1,0:T(8,128)(2,1)S(1)}, bf16[1664,128]{1,0:T(8,128)(2,1)S(1)}, u32[]{:S(2)}, u32[]{:S(2)}) collective-permute-start(bf16[1664,128]{1,0:T(8,128)(2,1)S(1)} %get-tuple-element.83), channel_id=1, source_target_pairs={{0,4},{2,6},{4,0},{6,2},{8,12},{10,14},{12,8},{14,10},{16,20},{18,... | collective-permute-start | bytes 1277960 | tf_op jit(solution)/shard_map/ppermute | solution.py:21
  71.7 7.3 %collective-permute-start.20 = (bf16[2,144,128]{2,1,0:T(8,128)(2,1)S(1)}, bf16[2,144,128]{2,1,0:T(8,128)(2,1)S(1)}, u32[]{:S(2)}, u32[]{:S(2)}) collective-permute-start(bf16[2,144,128]{2,1,0:T(8,128)(2,1)S(1)} %get-tuple-element.88), channel_id=1, source_target_pairs={{0,16},{2,18},{4,20},{6,22},{8,24},{10,26},{12,28},{14,30},{16,0},... | collective-permute-start | bytes 221192 | tf_op jit(solution)/shard_map/ppermute | solution.py:21
  74.4 6.3 %collective-permute-start.21 = (bf16[2,144,128]{2,1,0:T(8,128)(2,1)S(1)}, bf16[2,144,128]{2,1,0:T(8,128)(2,1)S(1)}, u32[]{:S(2)}, u32[]{:S(2)}) collective-permute-start(bf16[2,144,128]{2,1,0:T(8,128)(2,1)S(1)} %get-tuple-element.89), channel_id=1, source_target_pairs={{0,24},{2,26},{4,28},{6,30},{8,16},{10,18},{12,20},{14,22},{16,8},... | collective-permute-start | bytes 221192 | tf_op jit(solution)/shard_map/ppermute | solution.py:21
  75.8 5.1 %collective-permute-start.22 = (bf16[2,144,128]{2,1,0:T(8,128)(2,1)S(1)}, bf16[2,144,128]{2,1,0:T(8,128)(2,1)S(1)}, u32[]{:S(2)}, u32[]{:S(2)}) collective-permute-start(bf16[2,144,128]{2,1,0:T(8,128)(2,1)S(1)} %get-tuple-element.90), channel_id=1, source_target_pairs={{0,8},{2,10},{4,12},{6,14},{8,0},{10,2},{12,4},{14,6},{16,24},{18,... | collective-permute-start | bytes 221192 | tf_op jit(solution)/shard_map/ppermute | solution.py:21
  76.6 7.3 %collective-permute-start.23 = (bf16[1664,128]{1,0:T(8,128)(2,1)S(1)}, bf16[1664,128]{1,0:T(8,128)(2,1)S(1)}, u32[]{:S(2)}, u32[]{:S(2)}) collective-permute-start(bf16[1664,128]{1,0:T(8,128)(2,1)S(1)} %get-tuple-element.95), channel_id=1, source_target_pairs={{0,2},{2,0},{4,6},{6,4},{8,10},{10,8},{12,14},{14,12},{16,18},{18,... | collective-permute-start | bytes 1277960 | tf_op jit(solution)/shard_map/ppermute | solution.py:21
  82.4 1.8 %collective-permute-start.24 = (bf16[1664,128]{1,0:T(8,128)(2,1)S(1)}, bf16[1664,128]{1,0:T(8,128)(2,1)S(1)}, u32[]{:S(2)}, u32[]{:S(2)}) collective-permute-start(bf16[1664,128]{1,0:T(8,128)(2,1)S(1)} %get-tuple-element.96), channel_id=1, source_target_pairs={{0,2},{2,0},{4,6},{6,4},{8,10},{10,8},{12,14},{14,12},{16,18},{18,... | collective-permute-start | bytes 1277960 | tf_op jit(solution)/shard_map/ppermute | solution.py:21
  82.4 8.2 %collective-permute-start.26 = (bf16[6,144,128]{2,1,0:T(8,128)(2,1)S(1)}, bf16[6,144,128]{2,1,0:T(8,128)(2,1)S(1)}, u32[]{:S(2)}, u32[]{:S(2)}) collective-permute-start(bf16[6,144,128]{2,1,0:T(8,128)(2,1)S(1)} %get-tuple-element.97.p0), channel_id=1, source_target_pairs={{0,1},{1,0},{2,3},{3,2},{4,5},{5,4},{6,7},{7,6},{8,9},{9,8},{10,11... | collective-permute-start | bytes 663560 | tf_op jit(solution)/shard_map/ppermute | solution.py:21
  84.2 9.2 %copy-start = (f32[5,256,128]{2,1,0:T(8,128)S(1)}, f32[5,256,128]{2,1,0:T(8,128)}, u32[]{:S(2)}) copy-start(f32[5,256,128]{2,1,0:T(8,128)} %bs_ref.1) | copy-start | bytes 1966084
  84.2 9.2 %copy-start.2 = (f32[5,256]{1,0:T(8,128)S(1)}, f32[5,256]{1,0:T(8,128)}, u32[]{:S(2)}) copy-start(f32[5,256]{1,0:T(8,128)} %as_ref.1) | copy-start | bytes 15364
  86.4 7.1 %collective-permute-start.25 = (bf16[4,144,128]{2,1,0:T(8,128)(2,1)S(1)}, bf16[4,144,128]{2,1,0:T(8,128)(2,1)S(1)}, u32[]{:S(2)}, u32[]{:S(2)}) collective-permute-start(bf16[4,144,128]{2,1,0:T(8,128)(2,1)S(1)} %end.1.e0), channel_id=1, source_target_pairs={{0,1},{1,0},{2,3},{3,2},{4,5},{5,4},{6,7},{7,6},{8,9},{9,8},{10,11... | collective-permute-start | bytes 442376 | tf_op jit(solution)/shard_map/ppermute | solution.py:21
  (7 other events, 24.2 us)

commit v4 on v3

--- a/solution.py
+++ b/solution.py
@@ -41,7 +41,7 @@
     return best
 
 
-def call(name, body, outs, args, specs=None, scratch=(), flops=0, out_specs=None, limit=16):
+def call(name, body, outs, args, specs=None, scratch=(), flops=0, weight=1, limit=16):
     whole = [pl.BlockSpec(a.shape, lambda i, n=a.ndim: (0,) * n) for a in args]
     for at, spec in (specs or {}).items():
         whole[at] = spec
@@ -53,12 +53,13 @@
             body,
             grid=(1,),
             in_specs=whole,
-            out_specs=out_specs
-            or [pl.BlockSpec(o.shape, lambda i, n=len(o.shape): (0,) * n) for o in outs],
+            out_specs=[pl.BlockSpec(o.shape, lambda i, n=len(o.shape): (0,) * n) for o in outs],
             out_shape=outs,
             scratch_shapes=list(scratch),
             compiler_params=pltpu.CompilerParams(vmem_limit_bytes=limit * 2**20),
-            cost_estimate=pl.CostEstimate(flops=flops*100, bytes_accessed=moved*20, transcendentals=0),
+            cost_estimate=pl.CostEstimate(
+                flops=int(flops * weight * 100), bytes_accessed=int(moved * weight * 20), transcendentals=0
+            ),
             name=name,
         )(*args)
     )
@@ -209,28 +210,26 @@
     packs = {m: swapped(packed[m], "dim", m << shift) for m in order[:-1]}
     packs[0] = packed[0]
 
-    def first_body(u_ref, w_ref, trig_ref, v_out, wb_out):
-        for s in range(early):
-            wb_out[s] = w_ref[s].astype(BF)
-        weights = [[wb_out[s, col(c), :] for c in chunks] for s in range(early)]
+    def first_body(u_ref, w_ref, trig_ref, v_out):
+        weights = [[w_ref[s, col(c), :].astype(BF) for c in chunks] for s in range(early)]
         for r in range(0, rows, tile):
             at = pl.ds(r, tile)
             u = forward([u_ref[at, col(c)] for c in chunks], weights, trig_ref)[1]
             for c in chunks:
                 v_out[at, col(c)] = dot(u[c], weights[local_bits][c]).astype(BF)
-        for s in range(early, sections):
-            wb_out[s] = w_ref[s].astype(BF)
-
-    v_first, wb = call(
+
+    (v_first,) = call(
         "first",
         first_body,
-        [shape((rows, width)), shape(blocks.shape)],
+        [shape((rows, width))],
         [vectors, blocks, trig],
         flops=rows * width * BLOCK * 4,
     )
     other_first = swapped(v_first, "dim", 1)
 
-    def scale_body(place_ref, table_ref, index_ref, out):
+    def scale_body(place_ref, table_ref, index_ref, w_ref, out, wb_out):
+        for s in range(sections):
+            wb_out[s] = w_ref[s].astype(BF)
         index = index_ref[pl.ds(place_of(place_ref), 1), :]
         values = jnp.zeros(index.shape, F32)
         for level in range(table_ref.shape[0]):
@@ -238,11 +237,11 @@
         parts = stack_lines(split3(values), 16).astype(BF)
         out[...] = t_dot(parts, jnp.ones((16, BLOCK), BF))
 
-    (factor,) = call(
+    factor, wb = call(
         "scales",
         scale_body,
-        [shape((quarter, BLOCK), F32)],
-        [place_arr, scale_table, scale_index.reshape(GROUP, quarter)],
+        [shape((quarter, BLOCK), F32), shape(blocks.shape)],
+        [place_arr, scale_table, scale_index.reshape(GROUP, quarter), blocks],
         specs={0: SMEM, 1: SMEM},
     )
 
@@ -401,7 +400,7 @@
 
     grad_shape = shape((grad_rows, BLOCK), F32)
 
-    def back(c, s, load, v, other, w_ref, trig_ref, spans, g_out, q_out, grad):
+    def back(c, s, load, v, other, w_ref, trig_ref, spans, g_out, q_out, grad, packing=False):
         cols = col(c) if v.shape[1] != BLOCK else slice(None)
         w = w_ref[s, col(c), :]
         co, si = cs(trig_ref, s - 1, c)
@@ -418,7 +417,10 @@
                 g_out[at, :] = g16
                 ga = ga + jnp.sum(g * (co * theirs - si * mine), axis=0, keepdims=True)
                 q_out[at, :] = (si * g).astype(BF)
-        write_grad(grad, gw, ga)
+        if packing:
+            grad[:BLOCK, :], grad[BLOCK:, :] = pack_grad(gw, [ga])
+        else:
+            write_grad(grad, gw, ga)
 
     def back_quarters(c, s):
         v, other = saves[c][s - 1]
@@ -443,13 +445,14 @@
         )
 
     uppers = [(s, c) for s in range(early, third + 1) for c in chunks]
-    upper_shape = shape(((sections - early) * nb, grad_rows, BLOCK))
+    upper_shape = shape(((sections - early) * nb - 1, grad_rows, BLOCK))
 
     def gather_uppers(owns, others, given, out):
         for k, grad in enumerate(given):
             matrix, lines = pack_grad(grad[:BLOCK, :], [grad[BLOCK : BLOCK + 1, :]])
             out[k, :BLOCK, :] = matrix
             out[k, BLOCK:, :] = lines
+        base_at = len(uppers) - 1
         for c in chunks:
             own = owns[c] if c == chunks[-1] else owns[c].at[0]
             total = own[:BLOCK, :].astype(F32)
@@ -458,37 +461,31 @@
                 total = total + other[c, :BLOCK, :].astype(F32)
                 tail = tail + other[c, BLOCK:, :].astype(F32)
             matrix, lines = pack_grad(total, [unpack_line(tail, 0), unpack_line(tail, 1)])
-            out[len(uppers) + c, :BLOCK, :] = matrix
-            out[len(uppers) + c, BLOCK:, :] = lines
-
-    def back_middle(c, s, g, incoming, gathered=()):
+            out[base_at + c, :BLOCK, :] = matrix
+            out[base_at + c, BLOCK:, :] = lines
+
+    def upper_body(*refs):
+        owns, others = refs[:nb], refs[nb : nb + GROUP - 1]
+        gather_uppers(owns, others, refs[nb + GROUP - 1 : -1], refs[-1])
+
+    def back_middle(c, s, g, incoming, ending):
         v, other = saves[c][s - 1]
-        given = []
-        if gathered:
-            given = [grads[e][t] for t, e in uppers if (t, e) != (s, c)]
-
-        def body(g_ref, i_ref, v_ref, o_ref, w_ref, trig_ref, *refs):
-            owns, others = refs[:nb], refs[nb : nb + GROUP - 1]
-            done, refs = refs[: len(gathered) + len(given)], refs[len(gathered) + len(given) :]
-            g_out, q_out, grad = refs[:3]
+
+        def body(g_ref, i_ref, v_ref, o_ref, w_ref, trig_ref, g_out, q_out, grad):
             here = cs(trig_ref, s, c)[0]
             spans = [m * quarter for m in range(GROUP)]
 
             def load(m, r, at):
                 return (here * g_ref[at, :].astype(F32) + i_ref[at, :].astype(F32)).astype(BF)
 
-            back(c, s, load, v_ref, o_ref, w_ref, trig_ref, spans, g_out, q_out, grad)
-            if gathered:
-                held = list(done[len(gathered) :])
-                held.insert(uppers.index((s, c)), grad)
-                gather_uppers(owns, others, held, refs[3])
+            back(c, s, load, v_ref, o_ref, w_ref, trig_ref, spans, g_out, q_out, grad, ending)
 
         return call(
             f"backward{s}_chunk{c}",
             body,
-            [shape((rows, BLOCK)), shape((rows, BLOCK)), grad_shape]
-            + ([upper_shape] if gathered else []),
-            [g, incoming, v, other, wb, trig, *gathered, *given],
+            [shape((rows, BLOCK)), shape((rows, BLOCK))]
+            + [shape((grad_rows, BLOCK)) if ending else grad_shape],
+            [g, incoming, v, other, wb, trig],
             flops=2 * product,
         )
 
@@ -502,14 +499,20 @@
     for s in reversed(middles[1:]):
         for c in chunks:
             ending = s == middles[1] and c == chunks[-1]
-            out = back_middle(c, s, *flow[c], gathered=partial + arrived if ending else ())
-            g, q, grads[c][s] = out[:3]
+            g, incoming = flow[c]
+            if ending:
+                given = [grads[e][t] for t, e in uppers if (t, e) != (s, c)]
+                (upper,) = call("uppers", upper_body, [upper_shape], partial + arrived + given)
+                incoming, upper = lax.optimization_barrier((incoming, upper))
+            g, q, grads[c][s] = back_middle(c, s, g, incoming, ending)
             flow[c] = (g, swapped(q, "dim", 1 << (s - 1 - local_bits)))
-    upper = out[3]
+    late = grads[chunks[-1]][middles[1]]
+    late_at = uppers.index((middles[1], chunks[-1]))
 
     def end_body(*refs):
         g_refs, i_refs = refs[:nb], refs[nb : 2 * nb]
-        u_ref, w_ref, trig_ref, grad, u_held, d_held = refs[2 * nb :]
+        u_ref, w_ref, trig_ref, late_ref, grad, u_held, d_held = refs[2 * nb :]
+        grad[early * nb] = late_ref[...]
         ga = [[jnp.zeros((1, BLOCK), F32)] * nb for _ in range(early)]
         w = [[w_ref[s, col(c), :] for c in chunks] for s in range(early)]
         for r in range(0, rows, tile):
@@ -552,27 +555,33 @@
     (ends,) = call(
         "end",
         end_body,
-        [shape((early * nb, grad_rows, BLOCK))],
+        [shape((early * nb + 1, grad_rows, BLOCK))],
         [flow[c][0] for c in chunks]
         + [flow[c][1] for c in chunks]
-        + [vectors, wb, trig],
+        + [vectors, wb, trig, late],
         scratch=[pltpu.VMEM((local_bits, rows, width), BF), pltpu.VMEM((early, rows, width), BF)],
         flops=6 * product,
     )
 
     if nrow == 2:
-        pairs = [(ends, swapped(ends, "row", 1)), (upper, swapped(upper, "row", 1))]
+        pairs = [(x, swapped(x, "row", 1)) for x in (ends, upper)]
     else:
-        pairs = [lax.psum(ends.astype(F32), "row"), lax.psum(upper.astype(F32), "row")]
+        pairs = [lax.psum(x.astype(F32), "row") for x in (ends, upper)]
         pairs = [(p, jnp.zeros_like(p)) for p in pairs]
 
     def final_body(place_ref, e0, e1, p0, p1, bs_ref, as_ref, step, new, step_a, new_a):
         def get(s, c):
             k = s * nb + c
-            a, b = (e0, e1) if s < early else (p0, p1)
-            k = k if s < early else k - early * nb
-            matrix = a[k, :BLOCK, :].astype(F32) + b[k, :BLOCK, :].astype(F32)
-            return matrix, a[k, BLOCK:, :].astype(F32) + b[k, BLOCK:, :].astype(F32)
+            if s < early:
+                a, b = e0.at[k], e1.at[k]
+            elif k - early * nb == late_at:
+                a, b = e0.at[early * nb], e1.at[early * nb]
+            else:
+                k -= early * nb
+                k -= k > late_at
+                a, b = p0.at[k], p1.at[k]
+            matrix = a[:BLOCK, :].astype(F32) + b[:BLOCK, :].astype(F32)
+            return matrix, a[BLOCK:, :].astype(F32) + b[BLOCK:, :].astype(F32)
 
         sign = signs(place_ref)
         for c in chunks:

time: 96.3 us -> 95.1 us (0.988)
  local copies, waits for them, and re-layouts: 2.52 us -> 0.82 us
  waiting for transfers between devices: 39.3 us -> 40.4 us
    unnamed x24 -> x18, local copies, waits for them, and re-layouts: 2.44 us -> 0.74 us
    ppermute x27, waiting for transfers between devices: 39.3 us -> 40.4 us  [swapped(): return lax.ppermute(value, axis, pairs)]
    pallas_call x16 -> x17, Pallas kernels: 18.1 us -> 17.7 us  [call(): pl.pallas_call(body, grid=(1,), in_specs=whole, out_specs=[pl.BlockSpec(o...]
  transfers between devices with their start and end apart: 27 -> 27, of which waited for: 14 -> 13; matrix products, arithmetic and copies ran while one was open for 0% -> 0% of each run, Pallas kernels for 13% -> 13%
where the time goes in v4:
time: 95.1 us; the launch traced here: 93.4 us
  waiting for transfers between devices  40.4 us (42%)
  starting transfers between devices  33.6 us (35%)
  Pallas kernels  17.7 us (19%)
    ppermute x27, waiting for transfers between devices, swapped(): return lax.ppermute(value, axis, pairs)  40.4 us
    ppermute x27, starting transfers between devices, swapped(): return lax.ppermute(value, axis, pairs)  33.6 us
    pallas_call x17, Pallas kernels, call(): pl.pallas_call(body, grid=(1,), in_specs=whole, out_specs=[pl.BlockSpec(o...  17.7 us
  transfers between devices with their start and end apart: 27, of which 13 were waited for; matrix products, arithmetic and copies ran while one was open for 0% of the time, Pallas kernels for 13%

profile of v4, /device:TPU:0, one launch (start us, length us, event | category | flops | bytes accessed | tf_op | source)
XLA Modules:
  0.0 93.4 jit_solution(3717395263868343825)
XLA Ops:
  0.7 2.6 %pack.1 = (bf16[560,256]{1,0:T(8,128)(2,1)}, bf16[560,256]{1,0:T(8,128)(2,1)}, bf16[560,256]{1,0:T(8,128)(2,1)}, bf16[432,256]{1,0:T(8,128)(2,1)}, f32[10,256]{1,0:T(8,128)}) custom-call(s32[1]{0:T(128)} %bitcast.place_ref, f32[5,256,128]{2,1,0:T(8,128)} %w_ref.3, s32[1664,256]{1,0:T(8,128)} %codes_hbm.1, f32[5,256]{1,0:T(8,128)} %angle_hbm.1), custom_call_target="tpu_custom_call" | custom-call | bytes 69120080 | tf_op jit(solution)/shard_map/pack/pallas_call | solution.py:52
  3.3 0.7 copy-done.6
  4.0 1.8 %first.1.v_ref = bf16[1664,256]{1,0:T(8,128)(2,1)S(1)} custom-call(bf16[1664,256]{1,0:T(8,128)(2,1)S(1)} %copy-done.4, f32[5,256,128]{2,1,0:T(8,128)S(1)} %copy-done, f32[10,256]{1,0:T(8,128)S(1)} %copy-done.6), custom_call_target="tpu_custom_call" | custom-call | flops 21810380800 | bytes 47390720 | tf_op jit(solution)/shard_map/first/pallas_call | solution.py:52
  6.3 4.7 %collective-permute-start.7 = (bf16[432,256]{1,0:T(8,128)(2,1)}, bf16[432,256]{1,0:T(8,128)(2,1)}, u32[]{:S(2)}, u32[]{:S(2)}) collective-permute-start(bf16[432,256]{1,0:T(8,128)(2,1)} %get-tuple-element.62), channel_id=1, source_target_pairs={{0,24},{2,26},{4,28},{6,30},{8,16},{10,18},{12,20},{14,22},{16,8},... | collective-permute-start | bytes 663560 | tf_op jit(solution)/shard_map/ppermute | solution.py:21
  11.7 0.8 scales.1
  12.9 1.7 %collective-permute-start.1 = (bf16[1664,128]{1,0:T(8,128)(2,1)S(1)}, bf16[1664,128]{1,0:T(8,128)(2,1)S(1)}, u32[]{:S(2)}, u32[]{:S(2)}) collective-permute-start(bf16[1664,128]{1,0:T(8,128)(2,1)S(1)} %forward2_chunk0.1.v_ref.refs_4_), channel_id=1, source_target_pairs={{0,4},{2,6},{4,0},{6,2},{8,12},{10,14},{12,8},{14,10},{16,20},{18,... | collective-permute-start | bytes 1277960 | tf_op jit(solution)/shard_map/ppermute | solution.py:21
  15.5 10.5 %collective-permute-done.2.refs_6_ = bf16[560,256]{1,0:T(8,128)(2,1)} collective-permute-done((bf16[560,256]{1,0:T(8,128)(2,1)}, bf16[560,256]{1,0:T(8,128)(2,1)}, u32[]{:S(2)}, u32[]{:S(2)}) %collective-permute-start.2) | collective-permute-done | bytes 286752 | tf_op jit(solution)/shard_map/ppermute | solution.py:21
  26.4 2.1 %collective-permute-start.3 = (bf16[416,128]{1,0:T(8,128)(2,1)S(1)}, bf16[416,128]{1,0:T(8,128)(2,1)S(1)}, u32[]{:S(2)}, u32[]{:S(2)}) collective-permute-start(bf16[416,128]{1,0:T(8,128)(2,1)S(1)} %get-tuple-element.57), channel_id=1, source_target_pairs={{0,16},{2,18},{4,20},{6,22},{8,24},{10,26},{12,28},{14,30},{16,0},... | collective-permute-start | bytes 319496 | tf_op jit(solution)/shard_map/ppermute | solution.py:21
  28.4 1.6 %collective-permute-start.4 = (bf16[416,128]{1,0:T(8,128)(2,1)S(1)}, bf16[416,128]{1,0:T(8,128)(2,1)S(1)}, u32[]{:S(2)}, u32[]{:S(2)}) collective-permute-start(bf16[416,128]{1,0:T(8,128)(2,1)S(1)} %get-tuple-element.58), channel_id=1, source_target_pairs={{0,24},{2,26},{4,28},{6,30},{8,16},{10,18},{12,20},{14,22},{16,8},... | collective-permute-start | bytes 319496 | tf_op jit(solution)/shard_map/ppermute | solution.py:21
  30.0 8.5 %collective-permute-done.5.p_ref.refs_4_ = bf16[560,256]{1,0:T(8,128)(2,1)S(1)} collective-permute-done((bf16[560,256]{1,0:T(8,128)(2,1)}, bf16[560,256]{1,0:T(8,128)(2,1)S(1)}, u32[]{:S(2)}, u32[]{:S(2)}) %collective-permute-start.5) | collective-permute-done | bytes 286752 | tf_op jit(solution)/shard_map/ppermute | solution.py:21
  39.0 3.1 %collective-permute-start.13 = (bf16[416,128]{1,0:T(8,128)(2,1)S(1)}, bf16[416,128]{1,0:T(8,128)(2,1)S(1)}, u32[]{:S(2)}, u32[]{:S(2)}) collective-permute-start(bf16[416,128]{1,0:T(8,128)(2,1)S(1)} %get-tuple-element.73), channel_id=1, source_target_pairs={{0,16},{2,18},{4,20},{6,22},{8,24},{10,26},{12,28},{14,30},{16,0},... | collective-permute-start | bytes 319496 | tf_op jit(solution)/shard_map/ppermute | solution.py:21
  42.1 1.4 %collective-permute-start.14 = (bf16[416,128]{1,0:T(8,128)(2,1)S(1)}, bf16[416,128]{1,0:T(8,128)(2,1)S(1)}, u32[]{:S(2)}, u32[]{:S(2)}) collective-permute-start(bf16[416,128]{1,0:T(8,128)(2,1)S(1)} %get-tuple-element.74), channel_id=1, source_target_pairs={{0,24},{2,26},{4,28},{6,30},{8,16},{10,18},{12,20},{14,22},{16,8},... | collective-permute-start | bytes 319496 | tf_op jit(solution)/shard_map/ppermute | solution.py:21
  43.4 5.0 %collective-permute-done.6.refs_2_.refs_9_ = bf16[672,128]{1,0:T(8,128)(2,1)S(1)} collective-permute-done((bf16[672,128]{1,0:T(8,128)(2,1)S(1)}, bf16[672,128]{1,0:T(8,128)(2,1)S(1)}, u32[]{:S(2)}, u32[]{:S(2)}) %collective-permute-start.6) | collective-permute-done | bytes 172064 | tf_op jit(solution)/shard_map/ppermute | solution.py:21
  48.4 2.5 %group_chunk0.1 = (bf16[416,128]{1,0:T(8,128)(2,1)S(1)}, bf16[416,128]{1,0:T(8,128)(2,1)S(1)}, bf16[416,128]{1,0:T(8,128)(2,1)S(1)}, bf16[416,128]{1,0:T(8,128)(2,1)S(1)}, bf16[4,144,128]{2,1,0:T(8,128)(2,1)S(1)}) custom-call(bf16[416,128]{1,0:T(8,128)(2,1)S(1)} %collective-permute-done.3.refs_0_, bf16[416,128]{1,0:T(8,128)(2,1)S(1)} %collective-permute-done.4.refs_1_, ...), custom_call_target="tpu_custom_call" | custom-call | flops 16357785600 | bytes 50626560 | tf_op jit(solution)/shard_map/group_chunk0/pallas_call | solution.py:52
  51.0 3.1 %collective-permute-start.9 = (bf16[416,128]{1,0:T(8,128)(2,1)S(1)}, bf16[416,128]{1,0:T(8,128)(2,1)S(1)}, u32[]{:S(2)}, u32[]{:S(2)}) collective-permute-start(bf16[416,128]{1,0:T(8,128)(2,1)S(1)} %get-tuple-element.67), channel_id=1, source_target_pairs={{0,24},{2,26},{4,28},{6,30},{8,16},{10,18},{12,20},{14,22},{16,8},... | collective-permute-start | bytes 319496 | tf_op jit(solution)/shard_map/ppermute | solution.py:21
  54.6 2.5 %group_chunk1.1 = (bf16[416,128]{1,0:T(8,128)(2,1)S(1)}, bf16[416,128]{1,0:T(8,128)(2,1)S(1)}, bf16[416,128]{1,0:T(8,128)(2,1)S(1)}, bf16[416,128]{1,0:T(8,128)(...) custom-call(bf16[416,128]{1,0:T(8,128)(2,1)S(1)} %collective-permute, ...), custom_call_target="tpu_custom_call" | custom-call | flops 16357785600 | bytes 54476800 | tf_op jit(solution)/shard_map/group_chunk1/pallas_call | solution.py:52
  57.1 1.6 %collective-permute-start.18 = (bf16[416,128]{1,0:T(8,128)(2,1)S(1)}, bf16[416,128]{1,0:T(8,128)(2,1)S(1)}, u32[]{:S(2)}, u32[]{:S(2)}) collective-permute-start(bf16[416,128]{1,0:T(8,128)(2,1)S(1)} %get-tuple-element.82), channel_id=1, source_target_pairs={{0,8},{2,10},{4,12},{6,14},{8,0},{10,2},{12,4},{14,6},{16,24},{18,... | collective-permute-start | bytes 319496 | tf_op jit(solution)/shard_map/ppermute | solution.py:21
  58.7 1.5 %collective-permute-done.8.refs_0_ = bf16[416,128]{1,0:T(8,128)(2,1)S(1)} collective-permute-done((bf16[416,128]{1,0:T(8,128)(2,1)S(1)}, bf16[416,128]{1,0:T(8,128)(2,1)S(1)}, u32[]{:S(2)}, u32[]{:S(2)}) %collective-permute-start.8) | collective-permute-done | bytes 106528 | tf_op jit(solution)/shard_map/ppermute | solution.py:21
  60.7 1.3 %collective-permute-start.17 = (bf16[416,128]{1,0:T(8,128)(2,1)S(1)}, bf16[416,128]{1,0:T(8,128)(2,1)S(1)}, u32[]{:S(2)}, u32[]{:S(2)}) collective-permute-start(bf16[416,128]{1,0:T(8,128)(2,1)S(1)} %get-tuple-element.81), channel_id=1, source_target_pairs={{0,24},{2,26},{4,28},{6,30},{8,16},{10,18},{12,20},{14,22},{16,8},... | collective-permute-start | bytes 319496 | tf_op jit(solution)/shard_map/ppermute | solution.py:21
  62.6 1.6 %collective-permute-start.11 = (bf16[1664,128]{1,0:T(8,128)(2,1)S(1)}, bf16[1664,128]{1,0:T(8,128)(2,1)S(1)}, u32[]{:S(2)}, u32[]{:S(2)}) collective-permute-start(bf16[1664,128]{1,0:T(8,128)(2,1)S(1)} %get-tuple-element.71), channel_id=1, source_target_pairs={{0,4},{2,6},{4,0},{6,2},{8,12},{10,14},{12,8},{14,10},{16,20},{18,... | collective-permute-start | bytes 1277960 | tf_op jit(solution)/shard_map/ppermute | solution.py:21
  64.3 4.6 %collective-permute-done.16.refs_0_ = bf16[416,128]{1,0:T(8,128)(2,1)S(1)} collective-permute-done((bf16[416,128]{1,0:T(8,128)(2,1)S(1)}, bf16[416,128]{1,0:T(8,128)(2,1)S(1)}, u32[]{:S(2)}, u32[]{:S(2)}) %collective-permute-start.16) | collective-permute-done | bytes 106528 | tf_op jit(solution)/shard_map/ppermute | solution.py:21
  69.5 1.6 %collective-permute-start.19 = (bf16[1664,128]{1,0:T(8,128)(2,1)S(1)}, bf16[1664,128]{1,0:T(8,128)(2,1)S(1)}, u32[]{:S(2)}, u32[]{:S(2)}) collective-permute-start(bf16[1664,128]{1,0:T(8,128)(2,1)S(1)} %get-tuple-element.85), channel_id=1, source_target_pairs={{0,4},{2,6},{4,0},{6,2},{8,12},{10,14},{12,8},{14,10},{16,20},{18,... | collective-permute-start | bytes 1277960 | tf_op jit(solution)/shard_map/ppermute | solution.py:21
  71.1 2.7 %collective-permute-start.20 = (bf16[2,144,128]{2,1,0:T(8,128)(2,1)S(1)}, bf16[2,144,128]{2,1,0:T(8,128)(2,1)S(1)}, u32[]{:S(2)}, u32[]{:S(2)}) collective-permute-start(bf16[2,144,128]{2,1,0:T(8,128)(2,1)S(1)} %get-tuple-element.90), channel_id=1, source_target_pairs={{0,16},{2,18},{4,20},{6,22},{8,24},{10,26},{12,28},{14,30},{16,0},... | collective-permute-start | bytes 221192 | tf_op jit(solution)/shard_map/ppermute | solution.py:21
  73.8 1.4 %collective-permute-start.21 = (bf16[2,144,128]{2,1,0:T(8,128)(2,1)S(1)}, bf16[2,144,128]{2,1,0:T(8,128)(2,1)S(1)}, u32[]{:S(2)}, u32[]{:S(2)}) collective-permute-start(bf16[2,144,128]{2,1,0:T(8,128)(2,1)S(1)} %get-tuple-element.91), channel_id=1, source_target_pairs={{0,24},{2,26},{4,28},{6,30},{8,16},{10,18},{12,20},{14,22},{16,8},... | collective-permute-start | bytes 221192 | tf_op jit(solution)/shard_map/ppermute | solution.py:21
  76.0 0.8 collective-permute-done.20.refs_2_
  76.8 3.2 %collective-permute-done.21.refs_3_ = bf16[2,144,128]{2,1,0:T(8,128)(2,1)S(1)} collective-permute-done((bf16[2,144,128]{2,1,0:T(8,128)(2,1)S(1)}, bf16[2,144,128]{2,1,0:T(8,128)(2,1)S(1)}, u32[]{:S(2)}, u32[]{:S(2)}) %collective-permute-start.21) | collective-permute-done | bytes 73760 | tf_op jit(solution)/shard_map/ppermute | solution.py:21
  81.2 1.5 %collective-permute-start.26 = (bf16[5,144,128]{2,1,0:T(8,128)(2,1)S(1)}, bf16[5,144,128]{2,1,0:T(8,128)(2,1)S(1)}, u32[]{:S(2)}, u32[]{:S(2)}) collective-permute-start(bf16[5,144,128]{2,1,0:T(8,128)(2,1)S(1)} %uppers.1.p0), channel_id=1, source_target_pairs={{0,1},{1,0},{2,3},{3,2},{4,5},{5,4},{6,7},{7,6},{8,9},{9,8},{10,11... | collective-permute-start | bytes 552968 | tf_op jit(solution)/shard_map/ppermute | solution.py:21
  82.9 2.1 %end.1.e0 = bf16[5,144,128]{2,1,0:T(8,128)(2,1)S(1)} custom-call(bf16[1664,128]{1,0:T(8,128)(2,1)S(1)} %get-tuple-element.72.refs_0_, bf16[1664,128]{1,0:T(8,128)(2,1)S(1)} %get-tuple-element.97.refs_1_, bf16[1664,128]{1,0:T(8,128)(2,1)S(1)} %collective-permute-done.23.refs_2_, bf16[1664,128]{1,0:T(8,128)(2,1)S(1)} %collective-permute-done.24.refs_3_, ...), custom_call_target="tpu_custom_call" | custom-call | flops 32715571200 | bytes 62300160 | tf_op jit(solution)/shard_map/end/pallas_call | solution.py:52
  85.0 1.5 %collective-permute-start.25 = (bf16[5,144,128]{2,1,0:T(8,128)(2,1)S(1)}, bf16[5,144,128]{2,1,0:T(8,128)(2,1)S(1)}, u32[]{:S(2)}, u32[]{:S(2)}) collective-permute-start(bf16[5,144,128]{2,1,0:T(8,128)(2,1)S(1)} %end.1.e0), channel_id=1, source_target_pairs={{0,1},{1,0},{2,3},{3,2},{4,5},{5,4},{6,7},{7,6},{8,9},{9,8},{10,11... | collective-permute-start | bytes 552968 | tf_op jit(solution)/shard_map/ppermute | solution.py:21
  86.6 1.9 %collective-permute-done.26.p1 = bf16[5,144,128]{2,1,0:T(8,128)(2,1)S(1)} collective-permute-done((bf16[5,144,128]{2,1,0:T(8,128)(2,1)S(1)}, bf16[5,144,128]{2,1,0:T(8,128)(2,1)S(1)}, u32[]{:S(2)}, u32[]{:S(2)}) %collective-permute-start.26) | collective-permute-done | bytes 184352 | tf_op jit(solution)/shard_map/ppermute | solution.py:21
  88.5 3.6 %collective-permute-done.25.e1 = bf16[5,144,128]{2,1,0:T(8,128)(2,1)S(1)} collective-permute-done((bf16[5,144,128]{2,1,0:T(8,128)(2,1)S(1)}, bf16[5,144,128]{2,1,0:T(8,128)(2,1)S(1)}, u32[]{:S(2)}, u32[]{:S(2)}) %collective-permute-start.25) | collective-permute-done | bytes 184352 | tf_op jit(solution)/shard_map/ppermute | solution.py:21
  92.2 1.2 %final.1 = (f32[5,256,128]{2,1,0:T(8,128)}, f32[5,256,128]{2,1,0:T(8,128)}, f32[5,256]{1,0:T(8,128)}, f32[5,256]{1,0:T(8,128)}) custom-call(s32[1]{0:T(128)} %bitcast.place_ref, bf16[5,144,128]{2,1,0:T(8,128)(2,1)S(1)} %end.1.e0, bf16[5,144,128]{2,1,0:T(8,128)(2,1)S(1)} %collective-permute-done.25.e1, bf16[5,144,128]{2,1,0:T(8,128)(2,1)S(1)} %uppers.1.p0, ...), custom_call_target="tpu_custom_call" | custom-call | bytes 54374480 | tf_op jit(solution)/shard_map/final/pallas_call | solution.py:52
  (58 shorter events, 7.8 us)
Async XLA Ops:
  4.0 7.7 %copy-start.3 = (f32[16]{0:T(128)S(1)}, f32[16]{0:T(128)}, u32[]{:S(2)}) copy-start(f32[16]{0:T(128)} %table_ref.1) | copy-start | bytes 196
  4.0 8.6 %copy-start.7 = (f32[10,256]{1,0:T(8,128)S(1)}, f32[10,256]{1,0:T(8,128)}, u32[]{:S(2)}) copy-start(f32[10,256]{1,0:T(8,128)} %get-tuple-element.53.trig_ref.refs_7_.refs_6_) | copy-start | bytes 30724
  5.8 6.7 %collective-permute-start = (bf16[1664,256]{1,0:T(8,128)(2,1)S(1)}, bf16[1664,256]{1,0:T(8,128)(2,1)S(1)}, u32[]{:S(2)}, u32[]{:S(2)}) collective-permute-start(bf16[1664,256]{1,0:T(8,128)(2,1)S(1)} %first.1.v_ref), channel_id=1, source_target_pairs={{0,2},{2,0},{4,6},{6,4},{8,10},{10,8},{12,14},{14,12},{16,18},{18,... | collective-permute-start | bytes 2555912 | tf_op jit(solution)/shard_map/ppermute | solution.py:21
  6.3 35.7 %collective-permute-start.7 = (bf16[432,256]{1,0:T(8,128)(2,1)}, bf16[432,256]{1,0:T(8,128)(2,1)}, u32[]{:S(2)}, u32[]{:S(2)}) collective-permute-start(bf16[432,256]{1,0:T(8,128)(2,1)} %get-tuple-element.62), channel_id=1, source_target_pairs={{0,24},{2,26},{4,28},{6,30},{8,16},{10,18},{12,20},{14,22},{16,8},... | collective-permute-start | bytes 663560 | tf_op jit(solution)/shard_map/ppermute | solution.py:21
  11.0 15.0 %collective-permute-start.2 = (bf16[560,256]{1,0:T(8,128)(2,1)}, bf16[560,256]{1,0:T(8,128)(2,1)}, u32[]{:S(2)}, u32[]{:S(2)}) collective-permute-start(bf16[560,256]{1,0:T(8,128)(2,1)} %get-tuple-element.55), channel_id=1, source_target_pairs={{0,8},{2,10},{4,12},{6,14},{8,0},{10,2},{12,4},{14,6},{16,24},{18,... | collective-permute-start | bytes 860168 | tf_op jit(solution)/shard_map/ppermute | solution.py:21
  11.0 27.5 %collective-permute-start.5 = (bf16[560,256]{1,0:T(8,128)(2,1)}, bf16[560,256]{1,0:T(8,128)(2,1)S(1)}, u32[]{:S(2)}, u32[]{:S(2)}) collective-permute-start(bf16[560,256]{1,0:T(8,128)(2,1)} %get-tuple-element.60), channel_id=1, source_target_pairs={{0,16},{2,18},{4,20},{6,22},{8,24},{10,26},{12,28},{14,30},{16,0},... | collective-permute-start | bytes 860168 | tf_op jit(solution)/shard_map/ppermute | solution.py:21
  12.9 13.0 %collective-permute-start.1 = (bf16[1664,128]{1,0:T(8,128)(2,1)S(1)}, bf16[1664,128]{1,0:T(8,128)(2,1)S(1)}, u32[]{:S(2)}, u32[]{:S(2)}) collective-permute-start(bf16[1664,128]{1,0:T(8,128)(2,1)S(1)} %forward2_chunk0.1.v_ref.refs_4_), channel_id=1, source_target_pairs={{0,4},{2,6},{4,0},{6,2},{8,12},{10,14},{12,8},{14,10},{16,20},{18,... | collective-permute-start | bytes 1277960 | tf_op jit(solution)/shard_map/ppermute | solution.py:21
  15.1 23.6 %collective-permute-start.12 = (bf16[1664,128]{1,0:T(8,128)(2,1)S(1)}, bf16[1664,128]{1,0:T(8,128)(2,1)S(1)}, u32[]{:S(2)}, u32[]{:S(2)}) collective-permute-start(bf16[1664,128]{1,0:T(8,128)(2,1)S(1)} %forward2_chunk1.1.v_ref.refs_4_), channel_id=1, source_target_pairs={{0,4},{2,6},{4,0},{6,2},{8,12},{10,14},{12,8},{14,10},{16,20},{18,... | collective-permute-start | bytes 1277960 | tf_op jit(solution)/shard_map/ppermute | solution.py:21
  26.4 17.1 %collective-permute-start.3 = (bf16[416,128]{1,0:T(8,128)(2,1)S(1)}, bf16[416,128]{1,0:T(8,128)(2,1)S(1)}, u32[]{:S(2)}, u32[]{:S(2)}) collective-permute-start(bf16[416,128]{1,0:T(8,128)(2,1)S(1)} %get-tuple-element.57), channel_id=1, source_target_pairs={{0,16},{2,18},{4,20},{6,22},{8,24},{10,26},{12,28},{14,30},{16,0},... | collective-permute-start | bytes 319496 | tf_op jit(solution)/shard_map/ppermute | solution.py:21
  28.4 15.0 %collective-permute-start.4 = (bf16[416,128]{1,0:T(8,128)(2,1)S(1)}, bf16[416,128]{1,0:T(8,128)(2,1)S(1)}, u32[]{:S(2)}, u32[]{:S(2)}) collective-permute-start(bf16[416,128]{1,0:T(8,128)(2,1)S(1)} %get-tuple-element.58), channel_id=1, source_target_pairs={{0,24},{2,26},{4,28},{6,30},{8,16},{10,18},{12,20},{14,22},{16,8},... | collective-permute-start | bytes 319496 | tf_op jit(solution)/shard_map/ppermute | solution.py:21
  38.5 9.9 %copy-start.5 = (bf16[560,256]{1,0:T(8,128)(2,1)S(1)}, bf16[560,256]{1,0:T(8,128)(2,1)}, u32[]{:S(2)}) copy-start(bf16[560,256]{1,0:T(8,128)(2,1)} %get-tuple-element.64.refs_7_) | copy-start | bytes 860164
  38.5 9.9 %collective-permute-start.6 = (bf16[672,128]{1,0:T(8,128)(2,1)S(1)}, bf16[672,128]{1,0:T(8,128)(2,1)S(1)}, u32[]{:S(2)}, u32[]{:S(2)}) collective-permute-start(bf16[672,128]{1,0:T(8,128)(2,1)S(1)} %near.1), channel_id=1, source_target_pairs={{0,8},{2,10},{4,12},{6,14},{8,0},{10,2},{12,4},{14,6},{16,24},{18,... | collective-permute-start | bytes 516104 | tf_op jit(solution)/shard_map/ppermute | solution.py:21
  39.0 15.1 %collective-permute-start.13 = (bf16[416,128]{1,0:T(8,128)(2,1)S(1)}, bf16[416,128]{1,0:T(8,128)(2,1)S(1)}, u32[]{:S(2)}, u32[]{:S(2)}) collective-permute-start(bf16[416,128]{1,0:T(8,128)(2,1)S(1)} %get-tuple-element.73), channel_id=1, source_target_pairs={{0,16},{2,18},{4,20},{6,22},{8,24},{10,26},{12,28},{14,30},{16,0},... | collective-permute-start | bytes 319496 | tf_op jit(solution)/shard_map/ppermute | solution.py:21
  42.1 12.5 %collective-permute-start.14 = (bf16[416,128]{1,0:T(8,128)(2,1)S(1)}, bf16[416,128]{1,0:T(8,128)(2,1)S(1)}, u32[]{:S(2)}, u32[]{:S(2)}) collective-permute-start(bf16[416,128]{1,0:T(8,128)(2,1)S(1)} %get-tuple-element.74), channel_id=1, source_target_pairs={{0,24},{2,26},{4,28},{6,30},{8,16},{10,18},{12,20},{14,22},{16,8},... | collective-permute-start | bytes 319496 | tf_op jit(solution)/shard_map/ppermute | solution.py:21
  43.4 11.2 %collective-permute-start.15 = (bf16[416,128]{1,0:T(8,128)(2,1)S(1)}, bf16[416,128]{1,0:T(8,128)(2,1)S(1)}, u32[]{:S(2)}, u32[]{:S(2)}) collective-permute-start(bf16[416,128]{1,0:T(8,128)(2,1)S(1)} %get-tuple-element.75), channel_id=1, source_target_pairs={{0,8},{2,10},{4,12},{6,14},{8,0},{10,2},{12,4},{14,6},{16,24},{18,... | collective-permute-start | bytes 319496 | tf_op jit(solution)/shard_map/ppermute | solution.py:21
  50.9 9.3 %collective-permute-start.8 = (bf16[416,128]{1,0:T(8,128)(2,1)S(1)}, bf16[416,128]{1,0:T(8,128)(2,1)S(1)}, u32[]{:S(2)}, u32[]{:S(2)}) collective-permute-start(bf16[416,128]{1,0:T(8,128)(2,1)S(1)} %get-tuple-element.66), channel_id=1, source_target_pairs={{0,16},{2,18},{4,20},{6,22},{8,24},{10,26},{12,28},{14,30},{16,0},... | collective-permute-start | bytes 319496 | tf_op jit(solution)/shard_map/ppermute | solution.py:21
  51.0 11.0 %collective-permute-start.9 = (bf16[416,128]{1,0:T(8,128)(2,1)S(1)}, bf16[416,128]{1,0:T(8,128)(2,1)S(1)}, u32[]{:S(2)}, u32[]{:S(2)}) collective-permute-start(bf16[416,128]{1,0:T(8,128)(2,1)S(1)} %get-tuple-element.67), channel_id=1, source_target_pairs={{0,24},{2,26},{4,28},{6,30},{8,16},{10,18},{12,20},{14,22},{16,8},... | collective-permute-start | bytes 319496 | tf_op jit(solution)/shard_map/ppermute | solution.py:21
  54.1 7.9 %collective-permute-start.10 = (bf16[416,128]{1,0:T(8,128)(2,1)S(1)}, bf16[416,128]{1,0:T(8,128)(2,1)S(1)}, u32[]{:S(2)}, u32[]{:S(2)}) collective-permute-start(bf16[416,128]{1,0:T(8,128)(2,1)S(1)} %get-tuple-element.68), channel_id=1, source_target_pairs={{0,8},{2,10},{4,12},{6,14},{8,0},{10,2},{12,4},{14,6},{16,24},{18,... | collective-permute-start | bytes 319496 | tf_op jit(solution)/shard_map/ppermute | solution.py:21
  57.1 7.2 %collective-permute-start.18 = (bf16[416,128]{1,0:T(8,128)(2,1)S(1)}, bf16[416,128]{1,0:T(8,128)(2,1)S(1)}, u32[]{:S(2)}, u32[]{:S(2)}) collective-permute-start(bf16[416,128]{1,0:T(8,128)(2,1)S(1)} %get-tuple-element.82), channel_id=1, source_target_pairs={{0,8},{2,10},{4,12},{6,14},{8,0},{10,2},{12,4},{14,6},{16,24},{18,... | collective-permute-start | bytes 319496 | tf_op jit(solution)/shard_map/ppermute | solution.py:21
  60.2 8.7 %collective-permute-start.16 = (bf16[416,128]{1,0:T(8,128)(2,1)S(1)}, bf16[416,128]{1,0:T(8,128)(2,1)S(1)}, u32[]{:S(2)}, u32[]{:S(2)}) collective-permute-start(bf16[416,128]{1,0:T(8,128)(2,1)S(1)} %get-tuple-element.80), channel_id=1, source_target_pairs={{0,16},{2,18},{4,20},{6,22},{8,24},{10,26},{12,28},{14,30},{16,0},... | collective-permute-start | bytes 319496 | tf_op jit(solution)/shard_map/ppermute | solution.py:21
  60.7 8.2 %collective-permute-start.17 = (bf16[416,128]{1,0:T(8,128)(2,1)S(1)}, bf16[416,128]{1,0:T(8,128)(2,1)S(1)}, u32[]{:S(2)}, u32[]{:S(2)}) collective-permute-start(bf16[416,128]{1,0:T(8,128)(2,1)S(1)} %get-tuple-element.81), channel_id=1, source_target_pairs={{0,24},{2,26},{4,28},{6,30},{8,16},{10,18},{12,20},{14,22},{16,8},... | collective-permute-start | bytes 319496 | tf_op jit(solution)/shard_map/ppermute | solution.py:21
  62.6 12.6 %collective-permute-start.11 = (bf16[1664,128]{1,0:T(8,128)(2,1)S(1)}, bf16[1664,128]{1,0:T(8,128)(2,1)S(1)}, u32[]{:S(2)}, u32[]{:S(2)}) collective-permute-start(bf16[1664,128]{1,0:T(8,128)(2,1)S(1)} %get-tuple-element.71), channel_id=1, source_target_pairs={{0,4},{2,6},{4,0},{6,2},{8,12},{10,14},{12,8},{14,10},{16,20},{18,... | collective-permute-start | bytes 1277960 | tf_op jit(solution)/shard_map/ppermute | solution.py:21
  69.5 10.9 %collective-permute-start.19 = (bf16[1664,128]{1,0:T(8,128)(2,1)S(1)}, bf16[1664,128]{1,0:T(8,128)(2,1)S(1)}, u32[]{:S(2)}, u32[]{:S(2)}) collective-permute-start(bf16[1664,128]{1,0:T(8,128)(2,1)S(1)} %get-tuple-element.85), channel_id=1, source_target_pairs={{0,4},{2,6},{4,0},{6,2},{8,12},{10,14},{12,8},{14,10},{16,20},{18,... | collective-permute-start | bytes 1277960 | tf_op jit(solution)/shard_map/ppermute | solution.py:21
  71.1 5.7 %collective-permute-start.20 = (bf16[2,144,128]{2,1,0:T(8,128)(2,1)S(1)}, bf16[2,144,128]{2,1,0:T(8,128)(2,1)S(1)}, u32[]{:S(2)}, u32[]{:S(2)}) collective-permute-start(bf16[2,144,128]{2,1,0:T(8,128)(2,1)S(1)} %get-tuple-element.90), channel_id=1, source_target_pairs={{0,16},{2,18},{4,20},{6,22},{8,24},{10,26},{12,28},{14,30},{16,0},... | collective-permute-start | bytes 221192 | tf_op jit(solution)/shard_map/ppermute | solution.py:21
  73.8 6.3 %collective-permute-start.21 = (bf16[2,144,128]{2,1,0:T(8,128)(2,1)S(1)}, bf16[2,144,128]{2,1,0:T(8,128)(2,1)S(1)}, u32[]{:S(2)}, u32[]{:S(2)}) collective-permute-start(bf16[2,144,128]{2,1,0:T(8,128)(2,1)S(1)} %get-tuple-element.91), channel_id=1, source_target_pairs={{0,24},{2,26},{4,28},{6,30},{8,16},{10,18},{12,20},{14,22},{16,8},... | collective-permute-start | bytes 221192 | tf_op jit(solution)/shard_map/ppermute | solution.py:21
  75.2 5.1 %collective-permute-start.22 = (bf16[2,144,128]{2,1,0:T(8,128)(2,1)S(1)}, bf16[2,144,128]{2,1,0:T(8,128)(2,1)S(1)}, u32[]{:S(2)}, u32[]{:S(2)}) collective-permute-start(bf16[2,144,128]{2,1,0:T(8,128)(2,1)S(1)} %get-tuple-element.92), channel_id=1, source_target_pairs={{0,8},{2,10},{4,12},{6,14},{8,0},{10,2},{12,4},{14,6},{16,24},{18,... | collective-permute-start | bytes 221192 | tf_op jit(solution)/shard_map/ppermute | solution.py:21
  75.9 6.8 %collective-permute-start.23 = (bf16[1664,128]{1,0:T(8,128)(2,1)S(1)}, bf16[1664,128]{1,0:T(8,128)(2,1)S(1)}, u32[]{:S(2)}, u32[]{:S(2)}) collective-permute-start(bf16[1664,128]{1,0:T(8,128)(2,1)S(1)} %get-tuple-element.98), channel_id=1, source_target_pairs={{0,2},{2,0},{4,6},{6,4},{8,10},{10,8},{12,14},{14,12},{16,18},{18,... | collective-permute-start | bytes 1277960 | tf_op jit(solution)/shard_map/ppermute | solution.py:21
  81.1 1.8 %collective-permute-start.24 = (bf16[1664,128]{1,0:T(8,128)(2,1)S(1)}, bf16[1664,128]{1,0:T(8,128)(2,1)S(1)}, u32[]{:S(2)}, u32[]{:S(2)}) collective-permute-start(bf16[1664,128]{1,0:T(8,128)(2,1)S(1)} %get-tuple-element.99), channel_id=1, source_target_pairs={{0,2},{2,0},{4,6},{6,4},{8,10},{10,8},{12,14},{14,12},{16,18},{18,... | collective-permute-start | bytes 1277960 | tf_op jit(solution)/shard_map/ppermute | solution.py:21
  81.2 7.4 %collective-permute-start.26 = (bf16[5,144,128]{2,1,0:T(8,128)(2,1)S(1)}, bf16[5,144,128]{2,1,0:T(8,128)(2,1)S(1)}, u32[]{:S(2)}, u32[]{:S(2)}) collective-permute-start(bf16[5,144,128]{2,1,0:T(8,128)(2,1)S(1)} %uppers.1.p0), channel_id=1, source_target_pairs={{0,1},{1,0},{2,3},{3,2},{4,5},{5,4},{6,7},{7,6},{8,9},{9,8},{10,11... | collective-permute-start | bytes 552968 | tf_op jit(solution)/shard_map/ppermute | solution.py:21
  82.9 9.2 %copy-start.1 = (f32[5,256,128]{2,1,0:T(8,128)S(1)}, f32[5,256,128]{2,1,0:T(8,128)}, u32[]{:S(2)}) copy-start(f32[5,256,128]{2,1,0:T(8,128)} %bs_ref.1) | copy-start | bytes 1966084
  82.9 9.3 %copy-start.2 = (f32[5,256]{1,0:T(8,128)S(1)}, f32[5,256]{1,0:T(8,128)}, u32[]{:S(2)}) copy-start(f32[5,256]{1,0:T(8,128)} %as_ref.1) | copy-start | bytes 15364
  85.0 7.1 %collective-permute-start.25 = (bf16[5,144,128]{2,1,0:T(8,128)(2,1)S(1)}, bf16[5,144,128]{2,1,0:T(8,128)(2,1)S(1)}, u32[]{:S(2)}, u32[]{:S(2)}) collective-permute-start(bf16[5,144,128]{2,1,0:T(8,128)(2,1)S(1)} %end.1.e0), channel_id=1, source_target_pairs={{0,1},{1,0},{2,3},{3,2},{4,5},{5,4},{6,7},{7,6},{8,9},{9,8},{10,11... | collective-permute-start | bytes 552968 | tf_op jit(solution)/shard_map/ppermute | solution.py:21
  (4 other events, 13.6 us)

commit v5 on v4

--- a/solution.py
+++ b/solution.py
@@ -210,7 +210,11 @@
     packs = {m: swapped(packed[m], "dim", m << shift) for m in order[:-1]}
     packs[0] = packed[0]
 
-    def first_body(u_ref, w_ref, trig_ref, v_out):
+    def first_body(place_ref, u_ref, w_ref, angle_ref, v_out, trig_ref):
+        angle = angle_ref[...]
+        trig_ref[...] = jnp.concatenate(
+            [jnp.cos(angle), signs(place_ref) * jnp.sin(angle)], axis=0
+        )
         weights = [[w_ref[s, col(c), :].astype(BF) for c in chunks] for s in range(early)]
         for r in range(0, rows, tile):
             at = pl.ds(r, tile)
@@ -222,7 +226,9 @@
         "first",
         first_body,
         [shape((rows, width))],
-        [vectors, blocks, trig],
+        [place_arr, vectors, blocks, lax.optimization_barrier((angles, trig))[0]],
+        specs={0: SMEM},
+        scratch=[pltpu.VMEM((2 * sections, width), F32)],
         flops=rows * width * BLOCK * 4,
     )
     other_first = swapped(v_first, "dim", 1)
@@ -388,7 +394,7 @@
     for c in chunks:
         out = group_stage(c, list(partial))
         if c > 0:
-            out[2], out[3], _ = lax.optimization_barrier((out[2], out[3], returned[c - 1][2]))
+            out[3], _ = lax.optimization_barrier((out[3], returned[c - 1][2]))
         returned[c] = {m: swapped(out[m], "dim", m << shift) for m in order[:-1]}
         returned[c][0] = out[0]
         partial.append(out[GROUP])

time: 95.1 us -> 93.8 us (0.986)
  transfers between devices with their start and end apart: 27 -> 27, of which waited for: 13 -> 11; matrix products, arithmetic and copies ran while one was open for 0% -> 0% of each run, Pallas kernels for 13% -> 13%
where the time goes in v5:
time: 93.8 us; the launch traced here: 92.7 us
  waiting for transfers between devices  39.5 us (42%)
  starting transfers between devices  34.5 us (37%)
  Pallas kernels  17.8 us (19%)
    ppermute x27, waiting for transfers between devices, swapped(): return lax.ppermute(value, axis, pairs)  39.5 us
    ppermute x27, starting transfers between devices, swapped(): return lax.ppermute(value, axis, pairs)  34.5 us
    pallas_call x17, Pallas kernels, call(): pl.pallas_call(body, grid=(1,), in_specs=whole, out_specs=[pl.BlockSpec(o...  17.8 us
  transfers between devices with their start and end apart: 27, of which 11 were waited for; matrix products, arithmetic and copies ran while one was open for 0% of the time, Pallas kernels for 13%

profile of v5, /device:TPU:0, one launch (start us, length us, event | category | flops | bytes accessed | tf_op | source)
XLA Modules:
  0.0 92.7 jit_solution(11196579857895954141)
XLA Ops:
  0.7 2.6 %pack.1 = (bf16[560,256]{1,0:T(8,128)(2,1)}, bf16[560,256]{1,0:T(8,128)(2,1)}, bf16[560,256]{1,0:T(8,128)(2,1)}, bf16[432,256]{1,0:T(8,128)(2,1)}, f32[10,256]{1,0:T(8,128)}) custom-call(s32[1]{0:T(128)} %bitcast.place_ref, f32[5,256,128]{2,1,0:T(8,128)} %w_ref.3, s32[1664,256]{1,0:T(8,128)} %codes_hbm.1, f32[5,256]{1,0:T(8,128)} %angle_ref), custom_call_target="tpu_custom_call" | custom-call | bytes 69120080 | tf_op jit(solution)/shard_map/pack/pallas_call | solution.py:52
  3.3 1.8 %first.1.v_ref = bf16[1664,256]{1,0:T(8,128)(2,1)S(1)} custom-call(s32[1]{0:T(128)} %bitcast.place_ref, bf16[1664,256]{1,0:T(8,128)(2,1)S(1)} %copy-done.5, f32[5,256,128]{2,1,0:T(8,128)S(1)} %copy-done, f32[5,256]{1,0:T(8,128)S(1)} %copy-done.3), custom_call_target="tpu_custom_call" | custom-call | flops 21810380800 | bytes 47288400 | tf_op jit(solution)/shard_map/first/pallas_call | solution.py:52
  5.7 4.7 %collective-permute-start.7 = (bf16[432,256]{1,0:T(8,128)(2,1)}, bf16[432,256]{1,0:T(8,128)(2,1)}, u32[]{:S(2)}, u32[]{:S(2)}) collective-permute-start(bf16[432,256]{1,0:T(8,128)(2,1)} %get-tuple-element.63), channel_id=1, source_target_pairs={{0,24},{2,26},{4,28},{6,30},{8,16},{10,18},{12,20},{14,22},{16,8},... | collective-permute-start | bytes 663560 | tf_op jit(solution)/shard_map/ppermute | solution.py:21
  11.1 0.8 scales.1
  12.3 1.7 %collective-permute-start.1 = (bf16[1664,128]{1,0:T(8,128)(2,1)S(1)}, bf16[1664,128]{1,0:T(8,128)(2,1)S(1)}, u32[]{:S(2)}, u32[]{:S(2)}) collective-permute-start(bf16[1664,128]{1,0:T(8,128)(2,1)S(1)} %forward2_chunk0.1.v_ref.refs_4_), channel_id=1, source_target_pairs={{0,4},{2,6},{4,0},{6,2},{8,12},{10,14},{12,8},{14,10},{16,20},{18,... | collective-permute-start | bytes 1277960 | tf_op jit(solution)/shard_map/ppermute | solution.py:21
  14.8 10.5 %collective-permute-done.2.refs_6_ = bf16[560,256]{1,0:T(8,128)(2,1)} collective-permute-done((bf16[560,256]{1,0:T(8,128)(2,1)}, bf16[560,256]{1,0:T(8,128)(2,1)}, u32[]{:S(2)}, u32[]{:S(2)}) %collective-permute-start.2) | collective-permute-done | bytes 286752 | tf_op jit(solution)/shard_map/ppermute | solution.py:21
  25.7 2.1 %collective-permute-start.3 = (bf16[416,128]{1,0:T(8,128)(2,1)S(1)}, bf16[416,128]{1,0:T(8,128)(2,1)S(1)}, u32[]{:S(2)}, u32[]{:S(2)}) collective-permute-start(bf16[416,128]{1,0:T(8,128)(2,1)S(1)} %get-tuple-element.58), channel_id=1, source_target_pairs={{0,16},{2,18},{4,20},{6,22},{8,24},{10,26},{12,28},{14,30},{16,0},... | collective-permute-start | bytes 319496 | tf_op jit(solution)/shard_map/ppermute | solution.py:21
  27.8 1.6 %collective-permute-start.4 = (bf16[416,128]{1,0:T(8,128)(2,1)S(1)}, bf16[416,128]{1,0:T(8,128)(2,1)S(1)}, u32[]{:S(2)}, u32[]{:S(2)}) collective-permute-start(bf16[416,128]{1,0:T(8,128)(2,1)S(1)} %get-tuple-element.59), channel_id=1, source_target_pairs={{0,24},{2,26},{4,28},{6,30},{8,16},{10,18},{12,20},{14,22},{16,8},... | collective-permute-start | bytes 319496 | tf_op jit(solution)/shard_map/ppermute | solution.py:21
  29.3 8.5 %collective-permute-done.5.p_ref.refs_4_ = bf16[560,256]{1,0:T(8,128)(2,1)S(1)} collective-permute-done((bf16[560,256]{1,0:T(8,128)(2,1)}, bf16[560,256]{1,0:T(8,128)(2,1)S(1)}, u32[]{:S(2)}, u32[]{:S(2)}) %collective-permute-start.5) | collective-permute-done | bytes 286752 | tf_op jit(solution)/shard_map/ppermute | solution.py:21
  38.3 3.1 %collective-permute-start.13 = (bf16[416,128]{1,0:T(8,128)(2,1)S(1)}, bf16[416,128]{1,0:T(8,128)(2,1)S(1)}, u32[]{:S(2)}, u32[]{:S(2)}) collective-permute-start(bf16[416,128]{1,0:T(8,128)(2,1)S(1)} %get-tuple-element.74), channel_id=1, source_target_pairs={{0,16},{2,18},{4,20},{6,22},{8,24},{10,26},{12,28},{14,30},{16,0},... | collective-permute-start | bytes 319496 | tf_op jit(solution)/shard_map/ppermute | solution.py:21
  41.4 1.3 %collective-permute-start.14 = (bf16[416,128]{1,0:T(8,128)(2,1)S(1)}, bf16[416,128]{1,0:T(8,128)(2,1)S(1)}, u32[]{:S(2)}, u32[]{:S(2)}) collective-permute-start(bf16[416,128]{1,0:T(8,128)(2,1)S(1)} %get-tuple-element.75), channel_id=1, source_target_pairs={{0,24},{2,26},{4,28},{6,30},{8,16},{10,18},{12,20},{14,22},{16,8},... | collective-permute-start | bytes 319496 | tf_op jit(solution)/shard_map/ppermute | solution.py:21
  42.8 5.0 %collective-permute-done.6.refs_2_.refs_9_ = bf16[672,128]{1,0:T(8,128)(2,1)S(1)} collective-permute-done((bf16[672,128]{1,0:T(8,128)(2,1)S(1)}, bf16[672,128]{1,0:T(8,128)(2,1)S(1)}, u32[]{:S(2)}, u32[]{:S(2)}) %collective-permute-start.6) | collective-permute-done | bytes 172064 | tf_op jit(solution)/shard_map/ppermute | solution.py:21
  47.8 2.5 %group_chunk0.1 = (bf16[416,128]{1,0:T(8,128)(2,1)S(1)}, bf16[416,128]{1,0:T(8,128)(2,1)S(1)}, bf16[416,128]{1,0:T(8,128)(2,1)S(1)}, bf16[416,128]{1,0:T(8,128)(2,1)S(1)}, bf16[4,144,128]{2,1,0:T(8,128)(2,1)S(1)}) custom-call(bf16[416,128]{1,0:T(8,128)(2,1)S(1)} %collective-permute-done.3.refs_0_, bf16[416,128]{1,0:T(8,128)(2,1)S(1)} %collective-permute-done.4.refs_1_, ...), custom_call_target="tpu_custom_call" | custom-call | flops 16357785600 | bytes 50626560 | tf_op jit(solution)/shard_map/group_chunk0/pallas_call | solution.py:52
  50.3 3.1 %collective-permute-start.9 = (bf16[416,128]{1,0:T(8,128)(2,1)S(1)}, bf16[416,128]{1,0:T(8,128)(2,1)S(1)}, u32[]{:S(2)}, u32[]{:S(2)}) collective-permute-start(bf16[416,128]{1,0:T(8,128)(2,1)S(1)} %get-tuple-element.68), channel_id=1, source_target_pairs={{0,24},{2,26},{4,28},{6,30},{8,16},{10,18},{12,20},{14,22},{16,8},... | collective-permute-start | bytes 319496 | tf_op jit(solution)/shard_map/ppermute | solution.py:21
  54.0 2.5 %group_chunk1.1 = (bf16[416,128]{1,0:T(8,128)(2,1)S(1)}, bf16[416,128]{1,0:T(8,128)(2,1)S(1)}, bf16[416,128]{1,0:T(8,128)(2,1)S(1)}, bf16[416,128]{1,0:T(8,128)(...) custom-call(bf16[416,128]{1,0:T(8,128)(2,1)S(1)} %collective-permute, ...), custom_call_target="tpu_custom_call" | custom-call | flops 16357785600 | bytes 54476800 | tf_op jit(solution)/shard_map/group_chunk1/pallas_call | solution.py:52
  56.5 2.9 %collective-permute-start.16 = (bf16[416,128]{1,0:T(8,128)(2,1)S(1)}, bf16[416,128]{1,0:T(8,128)(2,1)S(1)}, u32[]{:S(2)}, u32[]{:S(2)}) collective-permute-start(bf16[416,128]{1,0:T(8,128)(2,1)S(1)} %get-tuple-element.79), channel_id=1, source_target_pairs={{0,16},{2,18},{4,20},{6,22},{8,24},{10,26},{12,28},{14,30},{16,0},... | collective-permute-start | bytes 319496 | tf_op jit(solution)/shard_map/ppermute | solution.py:21
  59.4 0.7 collective-permute-start.18
  62.0 1.6 %collective-permute-start.11 = (bf16[1664,128]{1,0:T(8,128)(2,1)S(1)}, bf16[1664,128]{1,0:T(8,128)(2,1)S(1)}, u32[]{:S(2)}, u32[]{:S(2)}) collective-permute-start(bf16[1664,128]{1,0:T(8,128)(2,1)S(1)} %get-tuple-element.72), channel_id=1, source_target_pairs={{0,4},{2,6},{4,0},{6,2},{8,12},{10,14},{12,8},{14,10},{16,20},{18,... | collective-permute-start | bytes 1277960 | tf_op jit(solution)/shard_map/ppermute | solution.py:21
  63.5 4.7 %collective-permute-done.16.refs_0_ = bf16[416,128]{1,0:T(8,128)(2,1)S(1)} collective-permute-done((bf16[416,128]{1,0:T(8,128)(2,1)S(1)}, bf16[416,128]{1,0:T(8,128)(2,1)S(1)}, u32[]{:S(2)}, u32[]{:S(2)}) %collective-permute-start.16) | collective-permute-done | bytes 106528 | tf_op jit(solution)/shard_map/ppermute | solution.py:21
  68.8 1.6 %collective-permute-start.19 = (bf16[1664,128]{1,0:T(8,128)(2,1)S(1)}, bf16[1664,128]{1,0:T(8,128)(2,1)S(1)}, u32[]{:S(2)}, u32[]{:S(2)}) collective-permute-start(bf16[1664,128]{1,0:T(8,128)(2,1)S(1)} %get-tuple-element.85), channel_id=1, source_target_pairs={{0,4},{2,6},{4,0},{6,2},{8,12},{10,14},{12,8},{14,10},{16,20},{18,... | collective-permute-start | bytes 1277960 | tf_op jit(solution)/shard_map/ppermute | solution.py:21
  70.4 2.7 %collective-permute-start.20 = (bf16[2,144,128]{2,1,0:T(8,128)(2,1)S(1)}, bf16[2,144,128]{2,1,0:T(8,128)(2,1)S(1)}, u32[]{:S(2)}, u32[]{:S(2)}) collective-permute-start(bf16[2,144,128]{2,1,0:T(8,128)(2,1)S(1)} %get-tuple-element.90), channel_id=1, source_target_pairs={{0,16},{2,18},{4,20},{6,22},{8,24},{10,26},{12,28},{14,30},{16,0},... | collective-permute-start | bytes 221192 | tf_op jit(solution)/shard_map/ppermute | solution.py:21
  73.1 1.4 %collective-permute-start.21 = (bf16[2,144,128]{2,1,0:T(8,128)(2,1)S(1)}, bf16[2,144,128]{2,1,0:T(8,128)(2,1)S(1)}, u32[]{:S(2)}, u32[]{:S(2)}) collective-permute-start(bf16[2,144,128]{2,1,0:T(8,128)(2,1)S(1)} %get-tuple-element.91), channel_id=1, source_target_pairs={{0,24},{2,26},{4,28},{6,30},{8,16},{10,18},{12,20},{14,22},{16,8},... | collective-permute-start | bytes 221192 | tf_op jit(solution)/shard_map/ppermute | solution.py:21
  74.5 0.7 backward2_chunk0.1
  75.2 0.9 collective-permute-done.20.refs_2_
  76.1 3.3 %collective-permute-done.21.refs_3_ = bf16[2,144,128]{2,1,0:T(8,128)(2,1)S(1)} collective-permute-done((bf16[2,144,128]{2,1,0:T(8,128)(2,1)S(1)}, bf16[2,144,128]{2,1,0:T(8,128)(2,1)S(1)}, u32[]{:S(2)}, u32[]{:S(2)}) %collective-permute-start.21) | collective-permute-done | bytes 73760 | tf_op jit(solution)/shard_map/ppermute | solution.py:21
  79.7 0.7 backward2_chunk1.1
  80.5 1.6 %collective-permute-start.26 = (bf16[5,144,128]{2,1,0:T(8,128)(2,1)S(1)}, bf16[5,144,128]{2,1,0:T(8,128)(2,1)S(1)}, u32[]{:S(2)}, u32[]{:S(2)}) collective-permute-start(bf16[5,144,128]{2,1,0:T(8,128)(2,1)S(1)} %uppers.1.p0), channel_id=1, source_target_pairs={{0,1},{1,0},{2,3},{3,2},{4,5},{5,4},{6,7},{7,6},{8,9},{9,8},{10,11... | collective-permute-start | bytes 552968 | tf_op jit(solution)/shard_map/ppermute | solution.py:21
  82.2 2.1 %end.1.e0 = bf16[5,144,128]{2,1,0:T(8,128)(2,1)S(1)} custom-call(bf16[1664,128]{1,0:T(8,128)(2,1)S(1)} %get-tuple-element.73.refs_0_, bf16[1664,128]{1,0:T(8,128)(2,1)S(1)} %get-tuple-element.97.refs_1_, bf16[1664,128]{1,0:T(8,128)(2,1)S(1)} %collective-permute-done.23.refs_2_, bf16[1664,128]{1,0:T(8,128)(2,1)S(1)} %collective-permute-done.24.refs_3_, ...), custom_call_target="tpu_custom_call" | custom-call | flops 32715571200 | bytes 62300160 | tf_op jit(solution)/shard_map/end/pallas_call | solution.py:52
  84.4 1.6 %collective-permute-start.25 = (bf16[5,144,128]{2,1,0:T(8,128)(2,1)S(1)}, bf16[5,144,128]{2,1,0:T(8,128)(2,1)S(1)}, u32[]{:S(2)}, u32[]{:S(2)}) collective-permute-start(bf16[5,144,128]{2,1,0:T(8,128)(2,1)S(1)} %end.1.e0), channel_id=1, source_target_pairs={{0,1},{1,0},{2,3},{3,2},{4,5},{5,4},{6,7},{7,6},{8,9},{9,8},{10,11... | collective-permute-start | bytes 552968 | tf_op jit(solution)/shard_map/ppermute | solution.py:21
  85.9 1.9 %collective-permute-done.26.p1 = bf16[5,144,128]{2,1,0:T(8,128)(2,1)S(1)} collective-permute-done((bf16[5,144,128]{2,1,0:T(8,128)(2,1)S(1)}, bf16[5,144,128]{2,1,0:T(8,128)(2,1)S(1)}, u32[]{:S(2)}, u32[]{:S(2)}) %collective-permute-start.26) | collective-permute-done | bytes 184352 | tf_op jit(solution)/shard_map/ppermute | solution.py:21
  87.8 3.6 %collective-permute-done.25.e1 = bf16[5,144,128]{2,1,0:T(8,128)(2,1)S(1)} collective-permute-done((bf16[5,144,128]{2,1,0:T(8,128)(2,1)S(1)}, bf16[5,144,128]{2,1,0:T(8,128)(2,1)S(1)}, u32[]{:S(2)}, u32[]{:S(2)}) %collective-permute-start.25) | collective-permute-done | bytes 184352 | tf_op jit(solution)/shard_map/ppermute | solution.py:21
  91.5 1.2 %final.1 = (f32[5,256,128]{2,1,0:T(8,128)}, f32[5,256,128]{2,1,0:T(8,128)}, f32[5,256]{1,0:T(8,128)}, f32[5,256]{1,0:T(8,128)}) custom-call(s32[1]{0:T(128)} %bitcast.place_ref, bf16[5,144,128]{2,1,0:T(8,128)(2,1)S(1)} %end.1.e0, bf16[5,144,128]{2,1,0:T(8,128)(2,1)S(1)} %collective-permute-done.25.e1, bf16[5,144,128]{2,1,0:T(8,128)(2,1)S(1)} %uppers.1.p0, ...), custom_call_target="tpu_custom_call" | custom-call | bytes 54374480 | tf_op jit(solution)/shard_map/final/pallas_call | solution.py:52
  (58 shorter events, 7.1 us)
Async XLA Ops:
  3.3 7.8 %copy-start.4 = (f32[16]{0:T(128)S(1)}, f32[16]{0:T(128)}, u32[]{:S(2)}) copy-start(f32[16]{0:T(128)} %table_ref.1) | copy-start | bytes 196
  3.3 8.6 %copy-start.7 = (f32[10,256]{1,0:T(8,128)S(1)}, f32[10,256]{1,0:T(8,128)}, u32[]{:S(2)}) copy-start(f32[10,256]{1,0:T(8,128)} %get-tuple-element.53.trig_ref.refs_7_.refs_6_) | copy-start | bytes 30724
  5.2 6.7 %collective-permute-start = (bf16[1664,256]{1,0:T(8,128)(2,1)S(1)}, bf16[1664,256]{1,0:T(8,128)(2,1)S(1)}, u32[]{:S(2)}, u32[]{:S(2)}) collective-permute-start(bf16[1664,256]{1,0:T(8,128)(2,1)S(1)} %first.1.v_ref), channel_id=1, source_target_pairs={{0,2},{2,0},{4,6},{6,4},{8,10},{10,8},{12,14},{14,12},{16,18},{18,... | collective-permute-start | bytes 2555912 | tf_op jit(solution)/shard_map/ppermute | solution.py:21
  5.7 35.8 %collective-permute-start.7 = (bf16[432,256]{1,0:T(8,128)(2,1)}, bf16[432,256]{1,0:T(8,128)(2,1)}, u32[]{:S(2)}, u32[]{:S(2)}) collective-permute-start(bf16[432,256]{1,0:T(8,128)(2,1)} %get-tuple-element.63), channel_id=1, source_target_pairs={{0,24},{2,26},{4,28},{6,30},{8,16},{10,18},{12,20},{14,22},{16,8},... | collective-permute-start | bytes 663560 | tf_op jit(solution)/shard_map/ppermute | solution.py:21
  10.3 15.0 %collective-permute-start.2 = (bf16[560,256]{1,0:T(8,128)(2,1)}, bf16[560,256]{1,0:T(8,128)(2,1)}, u32[]{:S(2)}, u32[]{:S(2)}) collective-permute-start(bf16[560,256]{1,0:T(8,128)(2,1)} %get-tuple-element.56), channel_id=1, source_target_pairs={{0,8},{2,10},{4,12},{6,14},{8,0},{10,2},{12,4},{14,6},{16,24},{18,... | collective-permute-start | bytes 860168 | tf_op jit(solution)/shard_map/ppermute | solution.py:21
  10.4 27.5 %collective-permute-start.5 = (bf16[560,256]{1,0:T(8,128)(2,1)}, bf16[560,256]{1,0:T(8,128)(2,1)S(1)}, u32[]{:S(2)}, u32[]{:S(2)}) collective-permute-start(bf16[560,256]{1,0:T(8,128)(2,1)} %get-tuple-element.61), channel_id=1, source_target_pairs={{0,16},{2,18},{4,20},{6,22},{8,24},{10,26},{12,28},{14,30},{16,0},... | collective-permute-start | bytes 860168 | tf_op jit(solution)/shard_map/ppermute | solution.py:21
  12.3 13.0 %collective-permute-start.1 = (bf16[1664,128]{1,0:T(8,128)(2,1)S(1)}, bf16[1664,128]{1,0:T(8,128)(2,1)S(1)}, u32[]{:S(2)}, u32[]{:S(2)}) collective-permute-start(bf16[1664,128]{1,0:T(8,128)(2,1)S(1)} %forward2_chunk0.1.v_ref.refs_4_), channel_id=1, source_target_pairs={{0,4},{2,6},{4,0},{6,2},{8,12},{10,14},{12,8},{14,10},{16,20},{18,... | collective-permute-start | bytes 1277960 | tf_op jit(solution)/shard_map/ppermute | solution.py:21
  14.4 23.6 %collective-permute-start.12 = (bf16[1664,128]{1,0:T(8,128)(2,1)S(1)}, bf16[1664,128]{1,0:T(8,128)(2,1)S(1)}, u32[]{:S(2)}, u32[]{:S(2)}) collective-permute-start(bf16[1664,128]{1,0:T(8,128)(2,1)S(1)} %forward2_chunk1.1.v_ref.refs_4_), channel_id=1, source_target_pairs={{0,4},{2,6},{4,0},{6,2},{8,12},{10,14},{12,8},{14,10},{16,20},{18,... | collective-permute-start | bytes 1277960 | tf_op jit(solution)/shard_map/ppermute | solution.py:21
  25.7 17.1 %collective-permute-start.3 = (bf16[416,128]{1,0:T(8,128)(2,1)S(1)}, bf16[416,128]{1,0:T(8,128)(2,1)S(1)}, u32[]{:S(2)}, u32[]{:S(2)}) collective-permute-start(bf16[416,128]{1,0:T(8,128)(2,1)S(1)} %get-tuple-element.58), channel_id=1, source_target_pairs={{0,16},{2,18},{4,20},{6,22},{8,24},{10,26},{12,28},{14,30},{16,0},... | collective-permute-start | bytes 319496 | tf_op jit(solution)/shard_map/ppermute | solution.py:21
  27.8 15.0 %collective-permute-start.4 = (bf16[416,128]{1,0:T(8,128)(2,1)S(1)}, bf16[416,128]{1,0:T(8,128)(2,1)S(1)}, u32[]{:S(2)}, u32[]{:S(2)}) collective-permute-start(bf16[416,128]{1,0:T(8,128)(2,1)S(1)} %get-tuple-element.59), channel_id=1, source_target_pairs={{0,24},{2,26},{4,28},{6,30},{8,16},{10,18},{12,20},{14,22},{16,8},... | collective-permute-start | bytes 319496 | tf_op jit(solution)/shard_map/ppermute | solution.py:21
  37.9 9.9 %copy-start.6 = (bf16[560,256]{1,0:T(8,128)(2,1)S(1)}, bf16[560,256]{1,0:T(8,128)(2,1)}, u32[]{:S(2)}) copy-start(bf16[560,256]{1,0:T(8,128)(2,1)} %get-tuple-element.65.refs_7_) | copy-start | bytes 860164
  37.9 9.9 %collective-permute-start.6 = (bf16[672,128]{1,0:T(8,128)(2,1)S(1)}, bf16[672,128]{1,0:T(8,128)(2,1)S(1)}, u32[]{:S(2)}, u32[]{:S(2)}) collective-permute-start(bf16[672,128]{1,0:T(8,128)(2,1)S(1)} %near.1), channel_id=1, source_target_pairs={{0,8},{2,10},{4,12},{6,14},{8,0},{10,2},{12,4},{14,6},{16,24},{18,... | collective-permute-start | bytes 516104 | tf_op jit(solution)/shard_map/ppermute | solution.py:21
  38.3 15.1 %collective-permute-start.13 = (bf16[416,128]{1,0:T(8,128)(2,1)S(1)}, bf16[416,128]{1,0:T(8,128)(2,1)S(1)}, u32[]{:S(2)}, u32[]{:S(2)}) collective-permute-start(bf16[416,128]{1,0:T(8,128)(2,1)S(1)} %get-tuple-element.74), channel_id=1, source_target_pairs={{0,16},{2,18},{4,20},{6,22},{8,24},{10,26},{12,28},{14,30},{16,0},... | collective-permute-start | bytes 319496 | tf_op jit(solution)/shard_map/ppermute | solution.py:21
  41.4 12.5 %collective-permute-start.14 = (bf16[416,128]{1,0:T(8,128)(2,1)S(1)}, bf16[416,128]{1,0:T(8,128)(2,1)S(1)}, u32[]{:S(2)}, u32[]{:S(2)}) collective-permute-start(bf16[416,128]{1,0:T(8,128)(2,1)S(1)} %get-tuple-element.75), channel_id=1, source_target_pairs={{0,24},{2,26},{4,28},{6,30},{8,16},{10,18},{12,20},{14,22},{16,8},... | collective-permute-start | bytes 319496 | tf_op jit(solution)/shard_map/ppermute | solution.py:21
  42.8 11.2 %collective-permute-start.15 = (bf16[416,128]{1,0:T(8,128)(2,1)S(1)}, bf16[416,128]{1,0:T(8,128)(2,1)S(1)}, u32[]{:S(2)}, u32[]{:S(2)}) collective-permute-start(bf16[416,128]{1,0:T(8,128)(2,1)S(1)} %get-tuple-element.76), channel_id=1, source_target_pairs={{0,8},{2,10},{4,12},{6,14},{8,0},{10,2},{12,4},{14,6},{16,24},{18,... | collective-permute-start | bytes 319496 | tf_op jit(solution)/shard_map/ppermute | solution.py:21
  50.3 10.4 %collective-permute-start.8 = (bf16[416,128]{1,0:T(8,128)(2,1)S(1)}, bf16[416,128]{1,0:T(8,128)(2,1)S(1)}, u32[]{:S(2)}, u32[]{:S(2)}) collective-permute-start(bf16[416,128]{1,0:T(8,128)(2,1)S(1)} %get-tuple-element.67), channel_id=1, source_target_pairs={{0,16},{2,18},{4,20},{6,22},{8,24},{10,26},{12,28},{14,30},{16,0},... | collective-permute-start | bytes 319496 | tf_op jit(solution)/shard_map/ppermute | solution.py:21
  50.3 11.0 %collective-permute-start.9 = (bf16[416,128]{1,0:T(8,128)(2,1)S(1)}, bf16[416,128]{1,0:T(8,128)(2,1)S(1)}, u32[]{:S(2)}, u32[]{:S(2)}) collective-permute-start(bf16[416,128]{1,0:T(8,128)(2,1)S(1)} %get-tuple-element.68), channel_id=1, source_target_pairs={{0,24},{2,26},{4,28},{6,30},{8,16},{10,18},{12,20},{14,22},{16,8},... | collective-permute-start | bytes 319496 | tf_op jit(solution)/shard_map/ppermute | solution.py:21
  53.5 7.9 %collective-permute-start.10 = (bf16[416,128]{1,0:T(8,128)(2,1)S(1)}, bf16[416,128]{1,0:T(8,128)(2,1)S(1)}, u32[]{:S(2)}, u32[]{:S(2)}) collective-permute-start(bf16[416,128]{1,0:T(8,128)(2,1)S(1)} %get-tuple-element.69), channel_id=1, source_target_pairs={{0,8},{2,10},{4,12},{6,14},{8,0},{10,2},{12,4},{14,6},{16,24},{18,... | collective-permute-start | bytes 319496 | tf_op jit(solution)/shard_map/ppermute | solution.py:21
  56.5 11.7 %collective-permute-start.16 = (bf16[416,128]{1,0:T(8,128)(2,1)S(1)}, bf16[416,128]{1,0:T(8,128)(2,1)S(1)}, u32[]{:S(2)}, u32[]{:S(2)}) collective-permute-start(bf16[416,128]{1,0:T(8,128)(2,1)S(1)} %get-tuple-element.79), channel_id=1, source_target_pairs={{0,16},{2,18},{4,20},{6,22},{8,24},{10,26},{12,28},{14,30},{16,0},... | collective-permute-start | bytes 319496 | tf_op jit(solution)/shard_map/ppermute | solution.py:21
  59.4 8.8 %collective-permute-start.18 = (bf16[416,128]{1,0:T(8,128)(2,1)S(1)}, bf16[416,128]{1,0:T(8,128)(2,1)S(1)}, u32[]{:S(2)}, u32[]{:S(2)}) collective-permute-start(bf16[416,128]{1,0:T(8,128)(2,1)S(1)} %get-tuple-element.82), channel_id=1, source_target_pairs={{0,8},{2,10},{4,12},{6,14},{8,0},{10,2},{12,4},{14,6},{16,24},{18,... | collective-permute-start | bytes 319496 | tf_op jit(solution)/shard_map/ppermute | solution.py:21
  60.7 7.5 %collective-permute-start.17 = (bf16[416,128]{1,0:T(8,128)(2,1)S(1)}, bf16[416,128]{1,0:T(8,128)(2,1)S(1)}, u32[]{:S(2)}, u32[]{:S(2)}) collective-permute-start(bf16[416,128]{1,0:T(8,128)(2,1)S(1)} %get-tuple-element.81), channel_id=1, source_target_pairs={{0,24},{2,26},{4,28},{6,30},{8,16},{10,18},{12,20},{14,22},{16,8},... | collective-permute-start | bytes 319496 | tf_op jit(solution)/shard_map/ppermute | solution.py:21
  62.0 12.5 %collective-permute-start.11 = (bf16[1664,128]{1,0:T(8,128)(2,1)S(1)}, bf16[1664,128]{1,0:T(8,128)(2,1)S(1)}, u32[]{:S(2)}, u32[]{:S(2)}) collective-permute-start(bf16[1664,128]{1,0:T(8,128)(2,1)S(1)} %get-tuple-element.72), channel_id=1, source_target_pairs={{0,4},{2,6},{4,0},{6,2},{8,12},{10,14},{12,8},{14,10},{16,20},{18,... | collective-permute-start | bytes 1277960 | tf_op jit(solution)/shard_map/ppermute | solution.py:21
  68.8 10.9 %collective-permute-start.19 = (bf16[1664,128]{1,0:T(8,128)(2,1)S(1)}, bf16[1664,128]{1,0:T(8,128)(2,1)S(1)}, u32[]{:S(2)}, u32[]{:S(2)}) collective-permute-start(bf16[1664,128]{1,0:T(8,128)(2,1)S(1)} %get-tuple-element.85), channel_id=1, source_target_pairs={{0,4},{2,6},{4,0},{6,2},{8,12},{10,14},{12,8},{14,10},{16,20},{18,... | collective-permute-start | bytes 1277960 | tf_op jit(solution)/shard_map/ppermute | solution.py:21
  70.4 5.7 %collective-permute-start.20 = (bf16[2,144,128]{2,1,0:T(8,128)(2,1)S(1)}, bf16[2,144,128]{2,1,0:T(8,128)(2,1)S(1)}, u32[]{:S(2)}, u32[]{:S(2)}) collective-permute-start(bf16[2,144,128]{2,1,0:T(8,128)(2,1)S(1)} %get-tuple-element.90), channel_id=1, source_target_pairs={{0,16},{2,18},{4,20},{6,22},{8,24},{10,26},{12,28},{14,30},{16,0},... | collective-permute-start | bytes 221192 | tf_op jit(solution)/shard_map/ppermute | solution.py:21
  73.1 6.3 %collective-permute-start.21 = (bf16[2,144,128]{2,1,0:T(8,128)(2,1)S(1)}, bf16[2,144,128]{2,1,0:T(8,128)(2,1)S(1)}, u32[]{:S(2)}, u32[]{:S(2)}) collective-permute-start(bf16[2,144,128]{2,1,0:T(8,128)(2,1)S(1)} %get-tuple-element.91), channel_id=1, source_target_pairs={{0,24},{2,26},{4,28},{6,30},{8,16},{10,18},{12,20},{14,22},{16,8},... | collective-permute-start | bytes 221192 | tf_op jit(solution)/shard_map/ppermute | solution.py:21
  74.5 5.1 %collective-permute-start.22 = (bf16[2,144,128]{2,1,0:T(8,128)(2,1)S(1)}, bf16[2,144,128]{2,1,0:T(8,128)(2,1)S(1)}, u32[]{:S(2)}, u32[]{:S(2)}) collective-permute-start(bf16[2,144,128]{2,1,0:T(8,128)(2,1)S(1)} %get-tuple-element.92), channel_id=1, source_target_pairs={{0,8},{2,10},{4,12},{6,14},{8,0},{10,2},{12,4},{14,6},{16,24},{18,... | collective-permute-start | bytes 221192 | tf_op jit(solution)/shard_map/ppermute | solution.py:21
  75.1 6.9 %collective-permute-start.23 = (bf16[1664,128]{1,0:T(8,128)(2,1)S(1)}, bf16[1664,128]{1,0:T(8,128)(2,1)S(1)}, u32[]{:S(2)}, u32[]{:S(2)}) collective-permute-start(bf16[1664,128]{1,0:T(8,128)(2,1)S(1)} %get-tuple-element.98), channel_id=1, source_target_pairs={{0,2},{2,0},{4,6},{6,4},{8,10},{10,8},{12,14},{14,12},{16,18},{18,... | collective-permute-start | bytes 1277960 | tf_op jit(solution)/shard_map/ppermute | solution.py:21
  80.4 1.8 %collective-permute-start.24 = (bf16[1664,128]{1,0:T(8,128)(2,1)S(1)}, bf16[1664,128]{1,0:T(8,128)(2,1)S(1)}, u32[]{:S(2)}, u32[]{:S(2)}) collective-permute-start(bf16[1664,128]{1,0:T(8,128)(2,1)S(1)} %get-tuple-element.99), channel_id=1, source_target_pairs={{0,2},{2,0},{4,6},{6,4},{8,10},{10,8},{12,14},{14,12},{16,18},{18,... | collective-permute-start | bytes 1277960 | tf_op jit(solution)/shard_map/ppermute | solution.py:21
  80.5 7.4 %collective-permute-start.26 = (bf16[5,144,128]{2,1,0:T(8,128)(2,1)S(1)}, bf16[5,144,128]{2,1,0:T(8,128)(2,1)S(1)}, u32[]{:S(2)}, u32[]{:S(2)}) collective-permute-start(bf16[5,144,128]{2,1,0:T(8,128)(2,1)S(1)} %uppers.1.p0), channel_id=1, source_target_pairs={{0,1},{1,0},{2,3},{3,2},{4,5},{5,4},{6,7},{7,6},{8,9},{9,8},{10,11... | collective-permute-start | bytes 552968 | tf_op jit(solution)/shard_map/ppermute | solution.py:21
  82.2 9.2 %copy-start.1 = (f32[5,256,128]{2,1,0:T(8,128)S(1)}, f32[5,256,128]{2,1,0:T(8,128)}, u32[]{:S(2)}) copy-start(f32[5,256,128]{2,1,0:T(8,128)} %bs_ref.1) | copy-start | bytes 1966084
  82.2 9.3 %copy-start.2 = (f32[5,256]{1,0:T(8,128)S(1)}, f32[5,256]{1,0:T(8,128)}, u32[]{:S(2)}) copy-start(f32[5,256]{1,0:T(8,128)} %as_ref.1) | copy-start | bytes 15364
  84.4 7.1 %collective-permute-start.25 = (bf16[5,144,128]{2,1,0:T(8,128)(2,1)S(1)}, bf16[5,144,128]{2,1,0:T(8,128)(2,1)S(1)}, u32[]{:S(2)}, u32[]{:S(2)}) collective-permute-start(bf16[5,144,128]{2,1,0:T(8,128)(2,1)S(1)} %end.1.e0), channel_id=1, source_target_pairs={{0,1},{1,0},{2,3},{3,2},{4,5},{5,4},{6,7},{7,6},{8,9},{9,8},{10,11... | collective-permute-start | bytes 552968 | tf_op jit(solution)/shard_map/ppermute | solution.py:21
  (4 other events, 15.6 us)

commit v6 on v5

--- a/solution.py
+++ b/solution.py
@@ -136,7 +136,7 @@
     order = [2, 3, 1, 0]
     early = local_bits + 1
     base = quarter + TRIG
-    highs = [base + (0 if m == GROUP - 1 else BLOCK) for m in range(GROUP)]
+    highs = [base + BLOCK] * (GROUP - 1) + [quarter]
 
     def placed(refs):
         return [refs[order.index(m)] for m in range(GROUP)]
@@ -181,8 +181,8 @@
         lines = stack_lines(lines, TRIG).astype(BF)
         w_in.wait()
         for m in order:
-            p_out[m][quarter:base, :] = lines
             if highs[m] > base:
+                p_out[m][quarter:base, :] = lines
                 for c in chunks:
                     p_out[m][base:, col(c)] = w_held[col(c), :].astype(BF)
             c_in[m].wait()
@@ -284,16 +284,15 @@
             flops=product,
         )
 
-    def with_weights(mine):
+    def with_weights(c, mine):
         def body(m_ref, p_ref, out):
             for r in range(0, quarter, tile):
                 at = pl.ds(r, tile)
                 out[at, :] = m_ref[at, :]
-            for c in chunks:
-                out[quarter + c * BLOCK : quarter + (c + 1) * BLOCK, :] = p_ref[base:, col(c)]
+            out[quarter:, :] = p_ref[quarter:, col(c)]
 
         return call(
-            "near", body, [shape((quarter + nb * BLOCK, BLOCK))], [mine, packs[GROUP - 2]]
+            f"near_chunk{c}", body, [shape((base + BLOCK, BLOCK))], [mine, packs[GROUP - 2]]
         )[0]
 
     middles = list(range(local_bits, third))
@@ -308,30 +307,28 @@
             if s + 1 < third:
                 state[c] = (out[0], swapped(out[0], "dim", 1 << (s + 1 - local_bits)))
             else:
-                if c == chunks[0]:
-                    out[1] = with_weights(out[1])
+                out[1] = with_weights(c, out[1])
                 got = {m: swapped(out[m], "dim", m << shift) for m in order[:-1]}
                 got[0] = out[0]
                 state[c] = [got[m] for m in order]
-                if c == chunks[0]:
-                    relayed = got[1]
 
     def group_stage(c, earlier):
         final = c == chunks[-1]
 
         def body(*refs):
             a_refs, p_refs = placed(refs[:GROUP]), placed(refs[GROUP : 2 * GROUP])
-            f_ref, far_ref = refs[2 * GROUP], refs[2 * GROUP + 1]
-            e_refs = refs[2 * GROUP + 2 : 2 * GROUP + 2 + len(earlier)]
-            refs = refs[2 * GROUP + 2 + len(earlier) :]
+            f_ref = refs[2 * GROUP]
+            e_refs = refs[2 * GROUP + 1 : 2 * GROUP + 1 + len(earlier)]
+            refs = refs[2 * GROUP + 1 + len(earlier) :]
             outs, grad_refs = refs[:GROUP], refs[GROUP:]
             coef, w = [], []
             for m in range(GROUP):
-                t = p_refs[m][quarter:base, col(c)].astype(F32)
+                far = m == GROUP - 1
+                t = (a_refs[1][quarter:base, :] if far else p_refs[m][quarter:base, col(c)]).astype(F32)
                 coef.append(
                     [t[3 * k : 3 * k + 1] + t[3 * k + 1 : 3 * k + 2] + t[3 * k + 2 : 3 * k + 3] for k in range(4)]
                 )
-                w.append(p_refs[m][base:, col(c)] if highs[m] > base else far_ref[quarter + c * BLOCK : quarter + (c + 1) * BLOCK, :])
+                w.append(a_refs[1][base:, :] if far else p_refs[m][base:, col(c)])
             gw = [jnp.zeros((BLOCK, BLOCK), F32)] * GROUP
             ga = [[jnp.zeros((1, BLOCK), F32)] * GROUP for _ in range(2)]
             every = range(GROUP)
@@ -386,15 +383,13 @@
             f"group_chunk{c}",
             body,
             [shape((quarter, BLOCK))] * GROUP + grads,
-            state[c] + [packs[m] for m in order] + [factor, relayed] + earlier,
+            state[c] + [packs[m] for m in order] + [factor] + earlier,
             flops=3 * product,
         )
 
     returned, partial = {}, []
     for c in chunks:
         out = group_stage(c, list(partial))
-        if c > 0:
-            out[3], _ = lax.optimization_barrier((out[3], returned[c - 1][2]))
         returned[c] = {m: swapped(out[m], "dim", m << shift) for m in order[:-1]}
         returned[c][0] = out[0]
         partial.append(out[GROUP])

time: 93.8 us -> 92.6 us (0.987)
  waiting for transfers between devices: 39.5 us -> 36.1 us
  starting transfers between devices: 34.5 us -> 37.6 us
    ppermute x27, waiting for transfers between devices: 39.5 us -> 36.1 us  [swapped(): return lax.ppermute(value, axis, pairs)]
    ppermute x27, starting transfers between devices: 34.5 us -> 37.6 us  [swapped(): return lax.ppermute(value, axis, pairs)]
    pallas_call x17 -> x18, Pallas kernels: 17.8 us -> 17.7 us  [call(): pl.pallas_call(body, grid=(1,), in_specs=whole, out_specs=[pl.BlockSpec(o...]
  transfers between devices with their start and end apart: 27 -> 27, of which waited for: 11 -> 12; matrix products, arithmetic and copies ran while one was open for 0% -> 0% of each run, Pallas kernels for 13% -> 13%
where the time goes in v6:
time: 92.6 us; the launch traced here: 92.4 us
  starting transfers between devices  37.6 us (41%)
  waiting for transfers between devices  36.1 us (39%)
  Pallas kernels  17.7 us (19%)
    ppermute x27, starting transfers between devices, swapped(): return lax.ppermute(value, axis, pairs)  37.6 us
    ppermute x27, waiting for transfers between devices, swapped(): return lax.ppermute(value, axis, pairs)  36.1 us
    pallas_call x18, Pallas kernels, call(): pl.pallas_call(body, grid=(1,), in_specs=whole, out_specs=[pl.BlockSpec(o...  17.7 us
  transfers between devices with their start and end apart: 27, of which 12 were waited for; matrix products, arithmetic and copies ran while one was open for 0% of the time, Pallas kernels for 13%

profile of v6, /device:TPU:0, one launch (start us, length us, event | category | flops | bytes accessed | tf_op | source)
XLA Modules:
  0.0 92.4 jit_solution(15262817346502096105)
XLA Ops:
  0.7 2.6 %pack.1 = (bf16[560,256]{1,0:T(8,128)(2,1)}, bf16[560,256]{1,0:T(8,128)(2,1)}, bf16[560,256]{1,0:T(8,128)(2,1)}, bf16[416,256]{1,0:T(8,128)(2,1)}, f32[10,256]{1,0:T(8,128)}) custom-call(s32[1]{0:T(128)} %bitcast.place_ref, f32[5,256,128]{2,1,0:T(8,128)} %w_ref.3, s32[1664,256]{1,0:T(8,128)} %codes_hbm.1, f32[5,256]{1,0:T(8,128)} %angle_ref), custom_call_target="tpu_custom_call" | custom-call | bytes 68956240 | tf_op jit(solution)/shard_map/pack/pallas_call | solution.py:52
  3.3 1.8 %first.1.v_ref = bf16[1664,256]{1,0:T(8,128)(2,1)S(1)} custom-call(s32[1]{0:T(128)} %bitcast.place_ref, bf16[1664,256]{1,0:T(8,128)(2,1)S(1)} %copy-done.5, f32[5,256,128]{2,1,0:T(8,128)S(1)} %copy-done, f32[5,256]{1,0:T(8,128)S(1)} %copy-done.3), custom_call_target="tpu_custom_call" | custom-call | flops 21810380800 | bytes 47288400 | tf_op jit(solution)/shard_map/first/pallas_call | solution.py:52
  5.7 4.7 %collective-permute-start.7 = (bf16[416,256]{1,0:T(8,128)(2,1)}, bf16[416,256]{1,0:T(8,128)(2,1)}, u32[]{:S(2)}, u32[]{:S(2)}) collective-permute-start(bf16[416,256]{1,0:T(8,128)(2,1)} %get-tuple-element.62), channel_id=1, source_target_pairs={{0,24},{2,26},{4,28},{6,30},{8,16},{10,18},{12,20},{14,22},{16,8},... | collective-permute-start | bytes 638984 | tf_op jit(solution)/shard_map/ppermute | solution.py:21
  11.1 0.8 scales.1
  12.3 1.7 %collective-permute-start.1 = (bf16[1664,128]{1,0:T(8,128)(2,1)S(1)}, bf16[1664,128]{1,0:T(8,128)(2,1)S(1)}, u32[]{:S(2)}, u32[]{:S(2)}) collective-permute-start(bf16[1664,128]{1,0:T(8,128)(2,1)S(1)} %forward2_chunk0.1.v_ref.refs_4_), channel_id=1, source_target_pairs={{0,4},{2,6},{4,0},{6,2},{8,12},{10,14},{12,8},{14,10},{16,20},{18,... | collective-permute-start | bytes 1277960 | tf_op jit(solution)/shard_map/ppermute | solution.py:21
  14.8 10.5 %collective-permute-done.2.refs_6_ = bf16[560,256]{1,0:T(8,128)(2,1)} collective-permute-done((bf16[560,256]{1,0:T(8,128)(2,1)}, bf16[560,256]{1,0:T(8,128)(2,1)}, u32[]{:S(2)}, u32[]{:S(2)}) %collective-permute-start.2) | collective-permute-done | bytes 286752 | tf_op jit(solution)/shard_map/ppermute | solution.py:21
  25.7 2.1 %collective-permute-start.3 = (bf16[416,128]{1,0:T(8,128)(2,1)S(1)}, bf16[416,128]{1,0:T(8,128)(2,1)S(1)}, u32[]{:S(2)}, u32[]{:S(2)}) collective-permute-start(bf16[416,128]{1,0:T(8,128)(2,1)S(1)} %get-tuple-element.57), channel_id=1, source_target_pairs={{0,16},{2,18},{4,20},{6,22},{8,24},{10,26},{12,28},{14,30},{16,0},... | collective-permute-start | bytes 319496 | tf_op jit(solution)/shard_map/ppermute | solution.py:21
  27.8 1.6 %collective-permute-start.4 = (bf16[416,128]{1,0:T(8,128)(2,1)S(1)}, bf16[416,128]{1,0:T(8,128)(2,1)S(1)}, u32[]{:S(2)}, u32[]{:S(2)}) collective-permute-start(bf16[416,128]{1,0:T(8,128)(2,1)S(1)} %get-tuple-element.58), channel_id=1, source_target_pairs={{0,24},{2,26},{4,28},{6,30},{8,16},{10,18},{12,20},{14,22},{16,8},... | collective-permute-start | bytes 319496 | tf_op jit(solution)/shard_map/ppermute | solution.py:21
  29.3 8.1 %collective-permute-done.5.p_ref.refs_4_ = bf16[560,256]{1,0:T(8,128)(2,1)S(1)} collective-permute-done((bf16[560,256]{1,0:T(8,128)(2,1)}, bf16[560,256]{1,0:T(8,128)(2,1)S(1)}, u32[]{:S(2)}, u32[]{:S(2)}) %collective-permute-start.5) | collective-permute-done | bytes 286752 | tf_op jit(solution)/shard_map/ppermute | solution.py:21
  38.0 3.1 %collective-permute-start.13 = (bf16[416,128]{1,0:T(8,128)(2,1)S(1)}, bf16[416,128]{1,0:T(8,128)(2,1)S(1)}, u32[]{:S(2)}, u32[]{:S(2)}) collective-permute-start(bf16[416,128]{1,0:T(8,128)(2,1)S(1)} %get-tuple-element.73), channel_id=1, source_target_pairs={{0,16},{2,18},{4,20},{6,22},{8,24},{10,26},{12,28},{14,30},{16,0},... | collective-permute-start | bytes 319496 | tf_op jit(solution)/shard_map/ppermute | solution.py:21
  41.1 1.4 %collective-permute-start.14 = (bf16[416,128]{1,0:T(8,128)(2,1)S(1)}, bf16[416,128]{1,0:T(8,128)(2,1)S(1)}, u32[]{:S(2)}, u32[]{:S(2)}) collective-permute-start(bf16[416,128]{1,0:T(8,128)(2,1)S(1)} %get-tuple-element.74), channel_id=1, source_target_pairs={{0,24},{2,26},{4,28},{6,30},{8,16},{10,18},{12,20},{14,22},{16,8},... | collective-permute-start | bytes 319496 | tf_op jit(solution)/shard_map/ppermute | solution.py:21
  42.5 2.2 %collective-permute-done.6.refs_2_ = bf16[560,128]{1,0:T(8,128)(2,1)S(1)} collective-permute-done((bf16[560,128]{1,0:T(8,128)(2,1)S(1)}, bf16[560,128]{1,0:T(8,128)(2,1)S(1)}, u32[]{:S(2)}, u32[]{:S(2)}) %collective-permute-start.6) | collective-permute-done | bytes 143392 | tf_op jit(solution)/shard_map/ppermute | solution.py:21
  44.7 2.5 %group_chunk0.1 = (bf16[416,128]{1,0:T(8,128)(2,1)S(1)}, bf16[416,128]{1,0:T(8,128)(2,1)S(1)}, bf16[416,128]{1,0:T(8,128)(2,1)S(1)}, bf16[416,128]{1,0:T(8,128)(2,1)S(1)}, bf16[4,144,128]{2,1,0:T(8,128)(2,1)S(1)}) custom-call(bf16[416,128]{1,0:T(8,128)(2,1)S(1)} %collective-permute-done.3.refs_0_, bf16[416,128]{1,0:T(8,128)(2,1)S(1)} %collective-permute-done.4.refs_1_, ...), custom_call_target="tpu_custom_call" | custom-call | flops 16357785600 | bytes 46448640 | tf_op jit(solution)/shard_map/group_chunk0/pallas_call | solution.py:52
  47.2 0.9 collective-permute-start.8
  48.1 1.4 %collective-permute-start.9 = (bf16[416,128]{1,0:T(8,128)(2,1)S(1)}, bf16[416,128]{1,0:T(8,128)(2,1)S(1)}, u32[]{:S(2)}, u32[]{:S(2)}) collective-permute-start(bf16[416,128]{1,0:T(8,128)(2,1)S(1)} %get-tuple-element.67), channel_id=1, source_target_pairs={{0,24},{2,26},{4,28},{6,30},{8,16},{10,18},{12,20},{14,22},{16,8},... | collective-permute-start | bytes 319496 | tf_op jit(solution)/shard_map/ppermute | solution.py:21
  49.5 1.3 %collective-permute-start.10 = (bf16[416,128]{1,0:T(8,128)(2,1)S(1)}, bf16[416,128]{1,0:T(8,128)(2,1)S(1)}, u32[]{:S(2)}, u32[]{:S(2)}) collective-permute-start(bf16[416,128]{1,0:T(8,128)(2,1)S(1)} %get-tuple-element.68), channel_id=1, source_target_pairs={{0,8},{2,10},{4,12},{6,14},{8,0},{10,2},{12,4},{14,6},{16,24},{18,... | collective-permute-start | bytes 319496 | tf_op jit(solution)/shard_map/ppermute | solution.py:21
  51.2 2.5 %group_chunk1.1 = (bf16[416,128]{1,0:T(8,128)(2,1)S(1)}, bf16[416,128]{1,0:T(8,128)(2,1)S(1)}, bf16[416,128]{1,0:T(8,128)(2,1)S(1)}, bf16[416,128]{1,0:T(8,128)(...) custom-call(bf16[416,128]{1,0:T(8,128)(2,1)S(1)} %collective-permute, ...), custom_call_target="tpu_custom_call" | custom-call | flops 16357785600 | bytes 51609600 | tf_op jit(solution)/shard_map/group_chunk1/pallas_call | solution.py:52
  53.7 6.4 %collective-permute-start.16 = (bf16[416,128]{1,0:T(8,128)(2,1)S(1)}, bf16[416,128]{1,0:T(8,128)(2,1)S(1)}, u32[]{:S(2)}, u32[]{:S(2)}) collective-permute-start(bf16[416,128]{1,0:T(8,128)(2,1)S(1)} %get-tuple-element.78), channel_id=1, source_target_pairs={{0,16},{2,18},{4,20},{6,22},{8,24},{10,26},{12,28},{14,30},{16,0},... | collective-permute-start | bytes 319496 | tf_op jit(solution)/shard_map/ppermute | solution.py:21
  60.1 0.7 collective-permute-start.17
  61.5 1.6 %collective-permute-start.11 = (bf16[1664,128]{1,0:T(8,128)(2,1)S(1)}, bf16[1664,128]{1,0:T(8,128)(2,1)S(1)}, u32[]{:S(2)}, u32[]{:S(2)}) collective-permute-start(bf16[1664,128]{1,0:T(8,128)(2,1)S(1)} %get-tuple-element.71), channel_id=1, source_target_pairs={{0,4},{2,6},{4,0},{6,2},{8,12},{10,14},{12,8},{14,10},{16,20},{18,... | collective-permute-start | bytes 1277960 | tf_op jit(solution)/shard_map/ppermute | solution.py:21
  63.0 4.4 %collective-permute-done.16.refs_0_ = bf16[416,128]{1,0:T(8,128)(2,1)S(1)} collective-permute-done((bf16[416,128]{1,0:T(8,128)(2,1)S(1)}, bf16[416,128]{1,0:T(8,128)(2,1)S(1)}, u32[]{:S(2)}, u32[]{:S(2)}) %collective-permute-start.16) | collective-permute-done | bytes 106528 | tf_op jit(solution)/shard_map/ppermute | solution.py:21
  68.3 1.6 %collective-permute-start.19 = (bf16[1664,128]{1,0:T(8,128)(2,1)S(1)}, bf16[1664,128]{1,0:T(8,128)(2,1)S(1)}, u32[]{:S(2)}, u32[]{:S(2)}) collective-permute-start(bf16[1664,128]{1,0:T(8,128)(2,1)S(1)} %get-tuple-element.83), channel_id=1, source_target_pairs={{0,4},{2,6},{4,0},{6,2},{8,12},{10,14},{12,8},{14,10},{16,20},{18,... | collective-permute-start | bytes 1277960 | tf_op jit(solution)/shard_map/ppermute | solution.py:21
  69.9 2.8 %collective-permute-start.20 = (bf16[2,144,128]{2,1,0:T(8,128)(2,1)S(1)}, bf16[2,144,128]{2,1,0:T(8,128)(2,1)S(1)}, u32[]{:S(2)}, u32[]{:S(2)}) collective-permute-start(bf16[2,144,128]{2,1,0:T(8,128)(2,1)S(1)} %get-tuple-element.88), channel_id=1, source_target_pairs={{0,16},{2,18},{4,20},{6,22},{8,24},{10,26},{12,28},{14,30},{16,0},... | collective-permute-start | bytes 221192 | tf_op jit(solution)/shard_map/ppermute | solution.py:21
  72.8 1.4 %collective-permute-start.21 = (bf16[2,144,128]{2,1,0:T(8,128)(2,1)S(1)}, bf16[2,144,128]{2,1,0:T(8,128)(2,1)S(1)}, u32[]{:S(2)}, u32[]{:S(2)}) collective-permute-start(bf16[2,144,128]{2,1,0:T(8,128)(2,1)S(1)} %get-tuple-element.89), channel_id=1, source_target_pairs={{0,24},{2,26},{4,28},{6,30},{8,16},{10,18},{12,20},{14,22},{16,8},... | collective-permute-start | bytes 221192 | tf_op jit(solution)/shard_map/ppermute | solution.py:21
  74.9 2.7 %collective-permute-done.20.refs_2_ = bf16[2,144,128]{2,1,0:T(8,128)(2,1)S(1)} collective-permute-done((bf16[2,144,128]{2,1,0:T(8,128)(2,1)S(1)}, bf16[2,144,128]{2,1,0:T(8,128)(2,1)S(1)}, u32[]{:S(2)}, u32[]{:S(2)}) %collective-permute-start.20) | collective-permute-done | bytes 73760 | tf_op jit(solution)/shard_map/ppermute | solution.py:21
  77.6 1.5 %collective-permute-done.21.refs_3_ = bf16[2,144,128]{2,1,0:T(8,128)(2,1)S(1)} collective-permute-done((bf16[2,144,128]{2,1,0:T(8,128)(2,1)S(1)}, bf16[2,144,128]{2,1,0:T(8,128)(2,1)S(1)}, u32[]{:S(2)}, u32[]{:S(2)}) %collective-permute-start.21) | collective-permute-done | bytes 73760 | tf_op jit(solution)/shard_map/ppermute | solution.py:21
  80.1 1.6 %collective-permute-start.26 = (bf16[5,144,128]{2,1,0:T(8,128)(2,1)S(1)}, bf16[5,144,128]{2,1,0:T(8,128)(2,1)S(1)}, u32[]{:S(2)}, u32[]{:S(2)}) collective-permute-start(bf16[5,144,128]{2,1,0:T(8,128)(2,1)S(1)} %uppers.1.p0), channel_id=1, source_target_pairs={{0,1},{1,0},{2,3},{3,2},{4,5},{5,4},{6,7},{7,6},{8,9},{9,8},{10,11... | collective-permute-start | bytes 552968 | tf_op jit(solution)/shard_map/ppermute | solution.py:21
  81.9 2.1 %end.1.e0 = bf16[5,144,128]{2,1,0:T(8,128)(2,1)S(1)} custom-call(bf16[1664,128]{1,0:T(8,128)(2,1)S(1)} %get-tuple-element.72.refs_0_, bf16[1664,128]{1,0:T(8,128)(2,1)S(1)} %get-tuple-element.95.refs_1_, bf16[1664,128]{1,0:T(8,128)(2,1)S(1)} %collective-permute-done.23.refs_2_, bf16[1664,128]{1,0:T(8,128)(2,1)S(1)} %collective-permute-done.24.refs_3_, ...), custom_call_target="tpu_custom_call" | custom-call | flops 32715571200 | bytes 62300160 | tf_op jit(solution)/shard_map/end/pallas_call | solution.py:52
  84.0 1.6 %collective-permute-start.25 = (bf16[5,144,128]{2,1,0:T(8,128)(2,1)S(1)}, bf16[5,144,128]{2,1,0:T(8,128)(2,1)S(1)}, u32[]{:S(2)}, u32[]{:S(2)}) collective-permute-start(bf16[5,144,128]{2,1,0:T(8,128)(2,1)S(1)} %end.1.e0), channel_id=1, source_target_pairs={{0,1},{1,0},{2,3},{3,2},{4,5},{5,4},{6,7},{7,6},{8,9},{9,8},{10,11... | collective-permute-start | bytes 552968 | tf_op jit(solution)/shard_map/ppermute | solution.py:21
  85.6 1.9 %collective-permute-done.26.p1 = bf16[5,144,128]{2,1,0:T(8,128)(2,1)S(1)} collective-permute-done((bf16[5,144,128]{2,1,0:T(8,128)(2,1)S(1)}, bf16[5,144,128]{2,1,0:T(8,128)(2,1)S(1)}, u32[]{:S(2)}, u32[]{:S(2)}) %collective-permute-start.26) | collective-permute-done | bytes 184352 | tf_op jit(solution)/shard_map/ppermute | solution.py:21
  87.5 3.6 %collective-permute-done.25.e1 = bf16[5,144,128]{2,1,0:T(8,128)(2,1)S(1)} collective-permute-done((bf16[5,144,128]{2,1,0:T(8,128)(2,1)S(1)}, bf16[5,144,128]{2,1,0:T(8,128)(2,1)S(1)}, u32[]{:S(2)}, u32[]{:S(2)}) %collective-permute-start.25) | collective-permute-done | bytes 184352 | tf_op jit(solution)/shard_map/ppermute | solution.py:21
  91.1 1.2 %final.1 = (f32[5,256,128]{2,1,0:T(8,128)}, f32[5,256,128]{2,1,0:T(8,128)}, f32[5,256]{1,0:T(8,128)}, f32[5,256]{1,0:T(8,128)}) custom-call(s32[1]{0:T(128)} %bitcast.place_ref, bf16[5,144,128]{2,1,0:T(8,128)(2,1)S(1)} %end.1.e0, bf16[5,144,128]{2,1,0:T(8,128)(2,1)S(1)} %collective-permute-done.25.e1, bf16[5,144,128]{2,1,0:T(8,128)(2,1)S(1)} %uppers.1.p0, ...), custom_call_target="tpu_custom_call" | custom-call | bytes 54374480 | tf_op jit(solution)/shard_map/final/pallas_call | solution.py:52
  (59 shorter events, 7.2 us)
Async XLA Ops:
  3.3 7.7 %copy-start.8 = (s32[1664]{0:T(1024)S(1)}, s32[1664]{0:T(1024)}, u32[]{:S(2)}) copy-start(s32[1664]{0:T(1024)} %param.12) | copy-start | bytes 19972
  3.3 7.8 %copy-start.4 = (f32[16]{0:T(128)S(1)}, f32[16]{0:T(128)}, u32[]{:S(2)}) copy-start(f32[16]{0:T(128)} %table_ref.1) | copy-start | bytes 196
  3.3 8.6 %copy-start.7 = (f32[10,256]{1,0:T(8,128)S(1)}, f32[10,256]{1,0:T(8,128)}, u32[]{:S(2)}) copy-start(f32[10,256]{1,0:T(8,128)} %get-tuple-element.52.trig_ref.refs_7_.refs_6_) | copy-start | bytes 30724
  5.2 6.7 %collective-permute-start = (bf16[1664,256]{1,0:T(8,128)(2,1)S(1)}, bf16[1664,256]{1,0:T(8,128)(2,1)S(1)}, u32[]{:S(2)}, u32[]{:S(2)}) collective-permute-start(bf16[1664,256]{1,0:T(8,128)(2,1)S(1)} %first.1.v_ref), channel_id=1, source_target_pairs={{0,2},{2,0},{4,6},{6,4},{8,10},{10,8},{12,14},{14,12},{16,18},{18,... | collective-permute-start | bytes 2555912 | tf_op jit(solution)/shard_map/ppermute | solution.py:21
  5.7 35.4 %collective-permute-start.7 = (bf16[416,256]{1,0:T(8,128)(2,1)}, bf16[416,256]{1,0:T(8,128)(2,1)}, u32[]{:S(2)}, u32[]{:S(2)}) collective-permute-start(bf16[416,256]{1,0:T(8,128)(2,1)} %get-tuple-element.62), channel_id=1, source_target_pairs={{0,24},{2,26},{4,28},{6,30},{8,16},{10,18},{12,20},{14,22},{16,8},... | collective-permute-start | bytes 638984 | tf_op jit(solution)/shard_map/ppermute | solution.py:21
  10.3 15.0 %collective-permute-start.2 = (bf16[560,256]{1,0:T(8,128)(2,1)}, bf16[560,256]{1,0:T(8,128)(2,1)}, u32[]{:S(2)}, u32[]{:S(2)}) collective-permute-start(bf16[560,256]{1,0:T(8,128)(2,1)} %get-tuple-element.55), channel_id=1, source_target_pairs={{0,8},{2,10},{4,12},{6,14},{8,0},{10,2},{12,4},{14,6},{16,24},{18,... | collective-permute-start | bytes 860168 | tf_op jit(solution)/shard_map/ppermute | solution.py:21
  10.3 27.1 %collective-permute-start.5 = (bf16[560,256]{1,0:T(8,128)(2,1)}, bf16[560,256]{1,0:T(8,128)(2,1)S(1)}, u32[]{:S(2)}, u32[]{:S(2)}) collective-permute-start(bf16[560,256]{1,0:T(8,128)(2,1)} %get-tuple-element.60), channel_id=1, source_target_pairs={{0,16},{2,18},{4,20},{6,22},{8,24},{10,26},{12,28},{14,30},{16,0},... | collective-permute-start | bytes 860168 | tf_op jit(solution)/shard_map/ppermute | solution.py:21
  12.3 13.0 %collective-permute-start.1 = (bf16[1664,128]{1,0:T(8,128)(2,1)S(1)}, bf16[1664,128]{1,0:T(8,128)(2,1)S(1)}, u32[]{:S(2)}, u32[]{:S(2)}) collective-permute-start(bf16[1664,128]{1,0:T(8,128)(2,1)S(1)} %forward2_chunk0.1.v_ref.refs_4_), channel_id=1, source_target_pairs={{0,4},{2,6},{4,0},{6,2},{8,12},{10,14},{12,8},{14,10},{16,20},{18,... | collective-permute-start | bytes 1277960 | tf_op jit(solution)/shard_map/ppermute | solution.py:21
  14.4 23.2 %collective-permute-start.12 = (bf16[1664,128]{1,0:T(8,128)(2,1)S(1)}, bf16[1664,128]{1,0:T(8,128)(2,1)S(1)}, u32[]{:S(2)}, u32[]{:S(2)}) collective-permute-start(bf16[1664,128]{1,0:T(8,128)(2,1)S(1)} %forward2_chunk1.1.v_ref.refs_4_), channel_id=1, source_target_pairs={{0,4},{2,6},{4,0},{6,2},{8,12},{10,14},{12,8},{14,10},{16,20},{18,... | collective-permute-start | bytes 1277960 | tf_op jit(solution)/shard_map/ppermute | solution.py:21
  25.7 16.8 %collective-permute-start.3 = (bf16[416,128]{1,0:T(8,128)(2,1)S(1)}, bf16[416,128]{1,0:T(8,128)(2,1)S(1)}, u32[]{:S(2)}, u32[]{:S(2)}) collective-permute-start(bf16[416,128]{1,0:T(8,128)(2,1)S(1)} %get-tuple-element.57), channel_id=1, source_target_pairs={{0,16},{2,18},{4,20},{6,22},{8,24},{10,26},{12,28},{14,30},{16,0},... | collective-permute-start | bytes 319496 | tf_op jit(solution)/shard_map/ppermute | solution.py:21
  27.8 14.8 %collective-permute-start.4 = (bf16[416,128]{1,0:T(8,128)(2,1)S(1)}, bf16[416,128]{1,0:T(8,128)(2,1)S(1)}, u32[]{:S(2)}, u32[]{:S(2)}) collective-permute-start(bf16[416,128]{1,0:T(8,128)(2,1)S(1)} %get-tuple-element.58), channel_id=1, source_target_pairs={{0,24},{2,26},{4,28},{6,30},{8,16},{10,18},{12,20},{14,22},{16,8},... | collective-permute-start | bytes 319496 | tf_op jit(solution)/shard_map/ppermute | solution.py:21
  37.5 7.2 %collective-permute-start.6 = (bf16[560,128]{1,0:T(8,128)(2,1)S(1)}, bf16[560,128]{1,0:T(8,128)(2,1)S(1)}, u32[]{:S(2)}, u32[]{:S(2)}) collective-permute-start(bf16[560,128]{1,0:T(8,128)(2,1)S(1)} %near_chunk0.1), channel_id=1, source_target_pairs={{0,8},{2,10},{4,12},{6,14},{8,0},{10,2},{12,4},{14,6},{16,24},{18,... | collective-permute-start | bytes 430088 | tf_op jit(solution)/shard_map/ppermute | solution.py:21
  38.0 11.5 %collective-permute-start.13 = (bf16[416,128]{1,0:T(8,128)(2,1)S(1)}, bf16[416,128]{1,0:T(8,128)(2,1)S(1)}, u32[]{:S(2)}, u32[]{:S(2)}) collective-permute-start(bf16[416,128]{1,0:T(8,128)(2,1)S(1)} %get-tuple-element.73), channel_id=1, source_target_pairs={{0,16},{2,18},{4,20},{6,22},{8,24},{10,26},{12,28},{14,30},{16,0},... | collective-permute-start | bytes 319496 | tf_op jit(solution)/shard_map/ppermute | solution.py:21
  41.1 9.7 %collective-permute-start.14 = (bf16[416,128]{1,0:T(8,128)(2,1)S(1)}, bf16[416,128]{1,0:T(8,128)(2,1)S(1)}, u32[]{:S(2)}, u32[]{:S(2)}) collective-permute-start(bf16[416,128]{1,0:T(8,128)(2,1)S(1)} %get-tuple-element.74), channel_id=1, source_target_pairs={{0,24},{2,26},{4,28},{6,30},{8,16},{10,18},{12,20},{14,22},{16,8},... | collective-permute-start | bytes 319496 | tf_op jit(solution)/shard_map/ppermute | solution.py:21
  42.5 8.6 %collective-permute-start.15 = (bf16[560,128]{1,0:T(8,128)(2,1)S(1)}, bf16[560,128]{1,0:T(8,128)(2,1)S(1)}, u32[]{:S(2)}, u32[]{:S(2)}) collective-permute-start(bf16[560,128]{1,0:T(8,128)(2,1)S(1)} %near_chunk1.1), channel_id=1, source_target_pairs={{0,8},{2,10},{4,12},{6,14},{8,0},{10,2},{12,4},{14,6},{16,24},{18,... | collective-permute-start | bytes 430088 | tf_op jit(solution)/shard_map/ppermute | solution.py:21
  47.2 13.6 %collective-permute-start.8 = (bf16[416,128]{1,0:T(8,128)(2,1)S(1)}, bf16[416,128]{1,0:T(8,128)(2,1)S(1)}, u32[]{:S(2)}, u32[]{:S(2)}) collective-permute-start(bf16[416,128]{1,0:T(8,128)(2,1)S(1)} %get-tuple-element.66), channel_id=1, source_target_pairs={{0,16},{2,18},{4,20},{6,22},{8,24},{10,26},{12,28},{14,30},{16,0},... | collective-permute-start | bytes 319496 | tf_op jit(solution)/shard_map/ppermute | solution.py:21
  48.1 12.7 %collective-permute-start.9 = (bf16[416,128]{1,0:T(8,128)(2,1)S(1)}, bf16[416,128]{1,0:T(8,128)(2,1)S(1)}, u32[]{:S(2)}, u32[]{:S(2)}) collective-permute-start(bf16[416,128]{1,0:T(8,128)(2,1)S(1)} %get-tuple-element.67), channel_id=1, source_target_pairs={{0,24},{2,26},{4,28},{6,30},{8,16},{10,18},{12,20},{14,22},{16,8},... | collective-permute-start | bytes 319496 | tf_op jit(solution)/shard_map/ppermute | solution.py:21
  49.5 11.3 %collective-permute-start.10 = (bf16[416,128]{1,0:T(8,128)(2,1)S(1)}, bf16[416,128]{1,0:T(8,128)(2,1)S(1)}, u32[]{:S(2)}, u32[]{:S(2)}) collective-permute-start(bf16[416,128]{1,0:T(8,128)(2,1)S(1)} %get-tuple-element.68), channel_id=1, source_target_pairs={{0,8},{2,10},{4,12},{6,14},{8,0},{10,2},{12,4},{14,6},{16,24},{18,... | collective-permute-start | bytes 319496 | tf_op jit(solution)/shard_map/ppermute | solution.py:21
  53.7 13.8 %collective-permute-start.16 = (bf16[416,128]{1,0:T(8,128)(2,1)S(1)}, bf16[416,128]{1,0:T(8,128)(2,1)S(1)}, u32[]{:S(2)}, u32[]{:S(2)}) collective-permute-start(bf16[416,128]{1,0:T(8,128)(2,1)S(1)} %get-tuple-element.78), channel_id=1, source_target_pairs={{0,16},{2,18},{4,20},{6,22},{8,24},{10,26},{12,28},{14,30},{16,0},... | collective-permute-start | bytes 319496 | tf_op jit(solution)/shard_map/ppermute | solution.py:21
  60.1 7.3 %collective-permute-start.17 = (bf16[416,128]{1,0:T(8,128)(2,1)S(1)}, bf16[416,128]{1,0:T(8,128)(2,1)S(1)}, u32[]{:S(2)}, u32[]{:S(2)}) collective-permute-start(bf16[416,128]{1,0:T(8,128)(2,1)S(1)} %get-tuple-element.79), channel_id=1, source_target_pairs={{0,24},{2,26},{4,28},{6,30},{8,16},{10,18},{12,20},{14,22},{16,8},... | collective-permute-start | bytes 319496 | tf_op jit(solution)/shard_map/ppermute | solution.py:21
  60.8 6.9 %collective-permute-start.18 = (bf16[416,128]{1,0:T(8,128)(2,1)S(1)}, bf16[416,128]{1,0:T(8,128)(2,1)S(1)}, u32[]{:S(2)}, u32[]{:S(2)}) collective-permute-start(bf16[416,128]{1,0:T(8,128)(2,1)S(1)} %get-tuple-element.80), channel_id=1, source_target_pairs={{0,8},{2,10},{4,12},{6,14},{8,0},{10,2},{12,4},{14,6},{16,24},{18,... | collective-permute-start | bytes 319496 | tf_op jit(solution)/shard_map/ppermute | solution.py:21
  61.5 12.7 %collective-permute-start.11 = (bf16[1664,128]{1,0:T(8,128)(2,1)S(1)}, bf16[1664,128]{1,0:T(8,128)(2,1)S(1)}, u32[]{:S(2)}, u32[]{:S(2)}) collective-permute-start(bf16[1664,128]{1,0:T(8,128)(2,1)S(1)} %get-tuple-element.71), channel_id=1, source_target_pairs={{0,4},{2,6},{4,0},{6,2},{8,12},{10,14},{12,8},{14,10},{16,20},{18,... | collective-permute-start | bytes 1277960 | tf_op jit(solution)/shard_map/ppermute | solution.py:21
  68.3 11.0 %collective-permute-start.19 = (bf16[1664,128]{1,0:T(8,128)(2,1)S(1)}, bf16[1664,128]{1,0:T(8,128)(2,1)S(1)}, u32[]{:S(2)}, u32[]{:S(2)}) collective-permute-start(bf16[1664,128]{1,0:T(8,128)(2,1)S(1)} %get-tuple-element.83), channel_id=1, source_target_pairs={{0,4},{2,6},{4,0},{6,2},{8,12},{10,14},{12,8},{14,10},{16,20},{18,... | collective-permute-start | bytes 1277960 | tf_op jit(solution)/shard_map/ppermute | solution.py:21
  69.9 7.6 %collective-permute-start.20 = (bf16[2,144,128]{2,1,0:T(8,128)(2,1)S(1)}, bf16[2,144,128]{2,1,0:T(8,128)(2,1)S(1)}, u32[]{:S(2)}, u32[]{:S(2)}) collective-permute-start(bf16[2,144,128]{2,1,0:T(8,128)(2,1)S(1)} %get-tuple-element.88), channel_id=1, source_target_pairs={{0,16},{2,18},{4,20},{6,22},{8,24},{10,26},{12,28},{14,30},{16,0},... | collective-permute-start | bytes 221192 | tf_op jit(solution)/shard_map/ppermute | solution.py:21
  72.8 6.3 %collective-permute-start.21 = (bf16[2,144,128]{2,1,0:T(8,128)(2,1)S(1)}, bf16[2,144,128]{2,1,0:T(8,128)(2,1)S(1)}, u32[]{:S(2)}, u32[]{:S(2)}) collective-permute-start(bf16[2,144,128]{2,1,0:T(8,128)(2,1)S(1)} %get-tuple-element.89), channel_id=1, source_target_pairs={{0,24},{2,26},{4,28},{6,30},{8,16},{10,18},{12,20},{14,22},{16,8},... | collective-permute-start | bytes 221192 | tf_op jit(solution)/shard_map/ppermute | solution.py:21
  74.1 5.1 %collective-permute-start.22 = (bf16[2,144,128]{2,1,0:T(8,128)(2,1)S(1)}, bf16[2,144,128]{2,1,0:T(8,128)(2,1)S(1)}, u32[]{:S(2)}, u32[]{:S(2)}) collective-permute-start(bf16[2,144,128]{2,1,0:T(8,128)(2,1)S(1)} %get-tuple-element.90), channel_id=1, source_target_pairs={{0,8},{2,10},{4,12},{6,14},{8,0},{10,2},{12,4},{14,6},{16,24},{18,... | collective-permute-start | bytes 221192 | tf_op jit(solution)/shard_map/ppermute | solution.py:21
  74.8 6.9 %collective-permute-start.23 = (bf16[1664,128]{1,0:T(8,128)(2,1)S(1)}, bf16[1664,128]{1,0:T(8,128)(2,1)S(1)}, u32[]{:S(2)}, u32[]{:S(2)}) collective-permute-start(bf16[1664,128]{1,0:T(8,128)(2,1)S(1)} %get-tuple-element.96), channel_id=1, source_target_pairs={{0,2},{2,0},{4,6},{6,4},{8,10},{10,8},{12,14},{14,12},{16,18},{18,... | collective-permute-start | bytes 1277960 | tf_op jit(solution)/shard_map/ppermute | solution.py:21
  80.0 1.8 %collective-permute-start.24 = (bf16[1664,128]{1,0:T(8,128)(2,1)S(1)}, bf16[1664,128]{1,0:T(8,128)(2,1)S(1)}, u32[]{:S(2)}, u32[]{:S(2)}) collective-permute-start(bf16[1664,128]{1,0:T(8,128)(2,1)S(1)} %get-tuple-element.97), channel_id=1, source_target_pairs={{0,2},{2,0},{4,6},{6,4},{8,10},{10,8},{12,14},{14,12},{16,18},{18,... | collective-permute-start | bytes 1277960 | tf_op jit(solution)/shard_map/ppermute | solution.py:21
  80.1 7.4 %collective-permute-start.26 = (bf16[5,144,128]{2,1,0:T(8,128)(2,1)S(1)}, bf16[5,144,128]{2,1,0:T(8,128)(2,1)S(1)}, u32[]{:S(2)}, u32[]{:S(2)}) collective-permute-start(bf16[5,144,128]{2,1,0:T(8,128)(2,1)S(1)} %uppers.1.p0), channel_id=1, source_target_pairs={{0,1},{1,0},{2,3},{3,2},{4,5},{5,4},{6,7},{7,6},{8,9},{9,8},{10,11... | collective-permute-start | bytes 552968 | tf_op jit(solution)/shard_map/ppermute | solution.py:21
  81.9 9.2 %copy-start.1 = (f32[5,256,128]{2,1,0:T(8,128)S(1)}, f32[5,256,128]{2,1,0:T(8,128)}, u32[]{:S(2)}) copy-start(f32[5,256,128]{2,1,0:T(8,128)} %bs_ref.1) | copy-start | bytes 1966084
  81.9 9.3 %copy-start.2 = (f32[5,256]{1,0:T(8,128)S(1)}, f32[5,256]{1,0:T(8,128)}, u32[]{:S(2)}) copy-start(f32[5,256]{1,0:T(8,128)} %as_ref.1) | copy-start | bytes 15364
  84.0 7.1 %collective-permute-start.25 = (bf16[5,144,128]{2,1,0:T(8,128)(2,1)S(1)}, bf16[5,144,128]{2,1,0:T(8,128)(2,1)S(1)}, u32[]{:S(2)}, u32[]{:S(2)}) collective-permute-start(bf16[5,144,128]{2,1,0:T(8,128)(2,1)S(1)} %end.1.e0), channel_id=1, source_target_pairs={{0,1},{1,0},{2,3},{3,2},{4,5},{5,4},{6,7},{7,6},{8,9},{9,8},{10,11... | collective-permute-start | bytes 552968 | tf_op jit(solution)/shard_map/ppermute | solution.py:21
  (4 other events, 15.1 us)

commit v7 on v6

--- a/solution.py
+++ b/solution.py
@@ -446,14 +446,13 @@
         )
 
     uppers = [(s, c) for s in range(early, third + 1) for c in chunks]
-    upper_shape = shape(((sections - early) * nb - 1, grad_rows, BLOCK))
+    upper_shape = shape((((sections - early) * nb - 1) * BLOCK + EXTRA, BLOCK))
 
     def gather_uppers(owns, others, given, out):
+        parts = []
         for k, grad in enumerate(given):
-            matrix, lines = pack_grad(grad[:BLOCK, :], [grad[BLOCK : BLOCK + 1, :]])
-            out[k, :BLOCK, :] = matrix
-            out[k, BLOCK:, :] = lines
-        base_at = len(uppers) - 1
+            out[k * BLOCK : (k + 1) * BLOCK, :] = grad[:BLOCK, :].astype(BF)
+            parts += split3(grad[BLOCK : BLOCK + 1, :])[:2]
         for c in chunks:
             own = owns[c] if c == chunks[-1] else owns[c].at[0]
             total = own[:BLOCK, :].astype(F32)
@@ -461,9 +460,10 @@
             for other in others:
                 total = total + other[c, :BLOCK, :].astype(F32)
                 tail = tail + other[c, BLOCK:, :].astype(F32)
-            matrix, lines = pack_grad(total, [unpack_line(tail, 0), unpack_line(tail, 1)])
-            out[base_at + c, :BLOCK, :] = matrix
-            out[base_at + c, BLOCK:, :] = lines
+            k = len(given) + c
+            out[k * BLOCK : (k + 1) * BLOCK, :] = total.astype(BF)
+            parts += split3(unpack_line(tail, 0))[:2] + split3(unpack_line(tail, 1))[:2]
+        out[-EXTRA:, :] = stack_lines(parts, EXTRA).astype(BF)
 
     def upper_body(*refs):
         owns, others = refs[:nb], refs[nb : nb + GROUP - 1]
@@ -513,7 +513,6 @@
     def end_body(*refs):
         g_refs, i_refs = refs[:nb], refs[nb : 2 * nb]
         u_ref, w_ref, trig_ref, late_ref, grad, u_held, d_held = refs[2 * nb :]
-        grad[early * nb] = late_ref[...]
         ga = [[jnp.zeros((1, BLOCK), F32)] * nb for _ in range(early)]
         w = [[w_ref[s, col(c), :] for c in chunks] for s in range(early)]
         for r in range(0, rows, tile):
@@ -546,17 +545,23 @@
                 d = [
                     (cs(trig_ref, t, c)[0] * g[c] + q[c ^ (1 << t)]).astype(BF) for c in chunks
                 ]
+        parts = []
         for s in range(early):
             for c in chunks:
                 left = u_held[s - 1, :, col(c)] if s else u_ref[:, col(c)]
-                matrix, lines = pack_grad(t_dot(left, d_held[s, :, col(c)]), [ga[s][c]])
-                grad[s * nb + c, :BLOCK, :] = matrix
-                grad[s * nb + c, BLOCK:, :] = lines
+                k = s * nb + c
+                matrix = t_dot(left, d_held[s, :, col(c)])
+                grad[k * BLOCK : (k + 1) * BLOCK, :] = matrix.astype(BF)
+                parts += split3(ga[s][c])[:2]
+        grad[early * nb * BLOCK : (early * nb + 1) * BLOCK, :] = late_ref[:BLOCK, :]
+        tail = late_ref[BLOCK:, :].astype(F32)
+        parts += [tail[0:1], tail[1:2]]
+        grad[-EXTRA:, :] = stack_lines(parts, EXTRA).astype(BF)
 
     (ends,) = call(
         "end",
         end_body,
-        [shape((early * nb + 1, grad_rows, BLOCK))],
+        [shape(((early * nb + 1) * BLOCK + EXTRA, BLOCK))],
         [flow[c][0] for c in chunks]
         + [flow[c][1] for c in chunks]
         + [vectors, wb, trig, late],
@@ -571,18 +576,25 @@
         pairs = [(p, jnp.zeros_like(p)) for p in pairs]
 
     def final_body(place_ref, e0, e1, p0, p1, bs_ref, as_ref, step, new, step_a, new_a):
+        tails = {
+            at: a[-EXTRA:, :].astype(F32) + b[-EXTRA:, :].astype(F32)
+            for at, a, b in (("end", e0, e1), ("upper", p0, p1))
+        }
+
         def get(s, c):
             k = s * nb + c
-            if s < early:
-                a, b = e0.at[k], e1.at[k]
-            elif k - early * nb == late_at:
-                a, b = e0.at[early * nb], e1.at[early * nb]
-            else:
+            at, a, b = "end", e0, e1
+            if k - early * nb == late_at:
+                k = early * nb
+            elif s >= early:
+                at, a, b = "upper", p0, p1
                 k -= early * nb
                 k -= k > late_at
-                a, b = p0.at[k], p1.at[k]
-            matrix = a[:BLOCK, :].astype(F32) + b[:BLOCK, :].astype(F32)
-            return matrix, a[BLOCK:, :].astype(F32) + b[BLOCK:, :].astype(F32)
+            line = k + max(0, k - len(uppers) + 1) if at == "upper" else k
+            lines = [line, line + 1] if s == last else [line]
+            rows_of = slice(k * BLOCK, (k + 1) * BLOCK)
+            matrix = a[rows_of, :].astype(F32) + b[rows_of, :].astype(F32)
+            return matrix, [unpack_line(tails[at], line) for line in lines]
 
         sign = signs(place_ref)
         for c in chunks:
@@ -593,11 +605,11 @@
                 new[s, col(c), :] = state_new
                 step[s, col(c), :] = g * lax.rsqrt(state_new)
                 if s == last:
-                    angle[last], angle[third] = unpack_line(lines, 0), unpack_line(lines, 1)
+                    angle[last], angle[third] = lines[0], lines[1]
                 elif s >= early:
-                    angle[s - 1] = unpack_line(lines, 0)
+                    angle[s - 1] = lines[0]
                 elif s < local_bits:
-                    angle[s] = unpack_line(lines, 0)
+                    angle[s] = lines[0]
             g = jnp.concatenate(angle, axis=0) * sign[:, col(c)]
             state_new = 0.9 * as_ref[:, col(c)] + 0.1 * g * g
             new_a[:, col(c)] = state_new

time: 92.6 us -> 91.9 us (level)
  no operation moved by 1% of the time
where the time goes in v7:
time: 91.9 us; the launch traced here: 91.7 us
  starting transfers between devices  37.6 us (41%)
  waiting for transfers between devices  35.4 us (39%)
  Pallas kernels  17.7 us (19%)
    ppermute x27, starting transfers between devices, swapped(): return lax.ppermute(value, axis, pairs)  37.6 us
    ppermute x27, waiting for transfers between devices, swapped(): return lax.ppermute(value, axis, pairs)  35.4 us
    pallas_call x18, Pallas kernels, call(): pl.pallas_call(body, grid=(1,), in_specs=whole, out_specs=[pl.BlockSpec(o...  17.7 us
  transfers between devices with their start and end apart: 27, of which 12 were waited for; matrix products, arithmetic and copies ran while one was open for 0% of the time, Pallas kernels for 13%

profile of v7, /device:TPU:0, one launch (start us, length us, event | category | flops | bytes accessed | tf_op | source)
XLA Modules:
  0.0 91.7 jit_solution(646055995184536093)
XLA Ops:
  0.7 2.6 %pack.1 = (bf16[560,256]{1,0:T(8,128)(2,1)}, bf16[560,256]{1,0:T(8,128)(2,1)}, bf16[560,256]{1,0:T(8,128)(2,1)}, bf16[416,256]{1,0:T(8,128)(2,1)}, f32[10,256]{1,0:T(8,128)}) custom-call(s32[1]{0:T(128)} %bitcast.place_ref, f32[5,256,128]{2,1,0:T(8,128)} %w_ref.3, s32[1664,256]{1,0:T(8,128)} %codes_hbm.1, f32[5,256]{1,0:T(8,128)} %angle_ref), custom_call_target="tpu_custom_call" | custom-call | bytes 68956240 | tf_op jit(solution)/shard_map/pack/pallas_call | solution.py:52
  3.3 1.8 %first.1.v_ref = bf16[1664,256]{1,0:T(8,128)(2,1)S(1)} custom-call(s32[1]{0:T(128)} %bitcast.place_ref, bf16[1664,256]{1,0:T(8,128)(2,1)S(1)} %copy-done.5, f32[5,256,128]{2,1,0:T(8,128)S(1)} %copy-done, f32[5,256]{1,0:T(8,128)S(1)} %copy-done.3), custom_call_target="tpu_custom_call" | custom-call | flops 21810380800 | bytes 47288400 | tf_op jit(solution)/shard_map/first/pallas_call | solution.py:52
  5.7 4.7 %collective-permute-start.7 = (bf16[416,256]{1,0:T(8,128)(2,1)}, bf16[416,256]{1,0:T(8,128)(2,1)}, u32[]{:S(2)}, u32[]{:S(2)}) collective-permute-start(bf16[416,256]{1,0:T(8,128)(2,1)} %get-tuple-element.62), channel_id=1, source_target_pairs={{0,24},{2,26},{4,28},{6,30},{8,16},{10,18},{12,20},{14,22},{16,8},... | collective-permute-start | bytes 638984 | tf_op jit(solution)/shard_map/ppermute | solution.py:21
  11.1 0.8 scales.1
  12.3 1.7 %collective-permute-start.1 = (bf16[1664,128]{1,0:T(8,128)(2,1)S(1)}, bf16[1664,128]{1,0:T(8,128)(2,1)S(1)}, u32[]{:S(2)}, u32[]{:S(2)}) collective-permute-start(bf16[1664,128]{1,0:T(8,128)(2,1)S(1)} %forward2_chunk0.1.v_ref.refs_4_), channel_id=1, source_target_pairs={{0,4},{2,6},{4,0},{6,2},{8,12},{10,14},{12,8},{14,10},{16,20},{18,... | collective-permute-start | bytes 1277960 | tf_op jit(solution)/shard_map/ppermute | solution.py:21
  14.8 10.5 %collective-permute-done.2.refs_6_ = bf16[560,256]{1,0:T(8,128)(2,1)} collective-permute-done((bf16[560,256]{1,0:T(8,128)(2,1)}, bf16[560,256]{1,0:T(8,128)(2,1)}, u32[]{:S(2)}, u32[]{:S(2)}) %collective-permute-start.2) | collective-permute-done | bytes 286752 | tf_op jit(solution)/shard_map/ppermute | solution.py:21
  25.7 2.1 %collective-permute-start.3 = (bf16[416,128]{1,0:T(8,128)(2,1)S(1)}, bf16[416,128]{1,0:T(8,128)(2,1)S(1)}, u32[]{:S(2)}, u32[]{:S(2)}) collective-permute-start(bf16[416,128]{1,0:T(8,128)(2,1)S(1)} %get-tuple-element.57), channel_id=1, source_target_pairs={{0,16},{2,18},{4,20},{6,22},{8,24},{10,26},{12,28},{14,30},{16,0},... | collective-permute-start | bytes 319496 | tf_op jit(solution)/shard_map/ppermute | solution.py:21
  27.8 1.6 %collective-permute-start.4 = (bf16[416,128]{1,0:T(8,128)(2,1)S(1)}, bf16[416,128]{1,0:T(8,128)(2,1)S(1)}, u32[]{:S(2)}, u32[]{:S(2)}) collective-permute-start(bf16[416,128]{1,0:T(8,128)(2,1)S(1)} %get-tuple-element.58), channel_id=1, source_target_pairs={{0,24},{2,26},{4,28},{6,30},{8,16},{10,18},{12,20},{14,22},{16,8},... | collective-permute-start | bytes 319496 | tf_op jit(solution)/shard_map/ppermute | solution.py:21
  29.3 8.1 %collective-permute-done.5.p_ref.refs_4_ = bf16[560,256]{1,0:T(8,128)(2,1)S(1)} collective-permute-done((bf16[560,256]{1,0:T(8,128)(2,1)}, bf16[560,256]{1,0:T(8,128)(2,1)S(1)}, u32[]{:S(2)}, u32[]{:S(2)}) %collective-permute-start.5) | collective-permute-done | bytes 286752 | tf_op jit(solution)/shard_map/ppermute | solution.py:21
  38.0 3.1 %collective-permute-start.13 = (bf16[416,128]{1,0:T(8,128)(2,1)S(1)}, bf16[416,128]{1,0:T(8,128)(2,1)S(1)}, u32[]{:S(2)}, u32[]{:S(2)}) collective-permute-start(bf16[416,128]{1,0:T(8,128)(2,1)S(1)} %get-tuple-element.73), channel_id=1, source_target_pairs={{0,16},{2,18},{4,20},{6,22},{8,24},{10,26},{12,28},{14,30},{16,0},... | collective-permute-start | bytes 319496 | tf_op jit(solution)/shard_map/ppermute | solution.py:21
  41.1 1.4 %collective-permute-start.14 = (bf16[416,128]{1,0:T(8,128)(2,1)S(1)}, bf16[416,128]{1,0:T(8,128)(2,1)S(1)}, u32[]{:S(2)}, u32[]{:S(2)}) collective-permute-start(bf16[416,128]{1,0:T(8,128)(2,1)S(1)} %get-tuple-element.74), channel_id=1, source_target_pairs={{0,24},{2,26},{4,28},{6,30},{8,16},{10,18},{12,20},{14,22},{16,8},... | collective-permute-start | bytes 319496 | tf_op jit(solution)/shard_map/ppermute | solution.py:21
  42.5 2.2 %collective-permute-done.6.refs_2_ = bf16[560,128]{1,0:T(8,128)(2,1)S(1)} collective-permute-done((bf16[560,128]{1,0:T(8,128)(2,1)S(1)}, bf16[560,128]{1,0:T(8,128)(2,1)S(1)}, u32[]{:S(2)}, u32[]{:S(2)}) %collective-permute-start.6) | collective-permute-done | bytes 143392 | tf_op jit(solution)/shard_map/ppermute | solution.py:21
  44.7 2.5 %group_chunk0.1 = (bf16[416,128]{1,0:T(8,128)(2,1)S(1)}, bf16[416,128]{1,0:T(8,128)(2,1)S(1)}, bf16[416,128]{1,0:T(8,128)(2,1)S(1)}, bf16[416,128]{1,0:T(8,128)(2,1)S(1)}, bf16[4,144,128]{2,1,0:T(8,128)(2,1)S(1)}) custom-call(bf16[416,128]{1,0:T(8,128)(2,1)S(1)} %collective-permute-done.3.refs_0_, bf16[416,128]{1,0:T(8,128)(2,1)S(1)} %collective-permute-done.4.refs_1_, ...), custom_call_target="tpu_custom_call" | custom-call | flops 16357785600 | bytes 46448640 | tf_op jit(solution)/shard_map/group_chunk0/pallas_call | solution.py:52
  47.2 0.9 collective-permute-start.8
  48.1 1.4 %collective-permute-start.9 = (bf16[416,128]{1,0:T(8,128)(2,1)S(1)}, bf16[416,128]{1,0:T(8,128)(2,1)S(1)}, u32[]{:S(2)}, u32[]{:S(2)}) collective-permute-start(bf16[416,128]{1,0:T(8,128)(2,1)S(1)} %get-tuple-element.67), channel_id=1, source_target_pairs={{0,24},{2,26},{4,28},{6,30},{8,16},{10,18},{12,20},{14,22},{16,8},... | collective-permute-start | bytes 319496 | tf_op jit(solution)/shard_map/ppermute | solution.py:21
  49.5 1.3 %collective-permute-start.10 = (bf16[416,128]{1,0:T(8,128)(2,1)S(1)}, bf16[416,128]{1,0:T(8,128)(2,1)S(1)}, u32[]{:S(2)}, u32[]{:S(2)}) collective-permute-start(bf16[416,128]{1,0:T(8,128)(2,1)S(1)} %get-tuple-element.68), channel_id=1, source_target_pairs={{0,8},{2,10},{4,12},{6,14},{8,0},{10,2},{12,4},{14,6},{16,24},{18,... | collective-permute-start | bytes 319496 | tf_op jit(solution)/shard_map/ppermute | solution.py:21
  51.2 2.5 %group_chunk1.1 = (bf16[416,128]{1,0:T(8,128)(2,1)S(1)}, bf16[416,128]{1,0:T(8,128)(2,1)S(1)}, bf16[416,128]{1,0:T(8,128)(2,1)S(1)}, bf16[416,128]{1,0:T(8,128)(...) custom-call(bf16[416,128]{1,0:T(8,128)(2,1)S(1)} %collective-permute, ...), custom_call_target="tpu_custom_call" | custom-call | flops 16357785600 | bytes 51609600 | tf_op jit(solution)/shard_map/group_chunk1/pallas_call | solution.py:52
  53.7 6.4 %collective-permute-start.16 = (bf16[416,128]{1,0:T(8,128)(2,1)S(1)}, bf16[416,128]{1,0:T(8,128)(2,1)S(1)}, u32[]{:S(2)}, u32[]{:S(2)}) collective-permute-start(bf16[416,128]{1,0:T(8,128)(2,1)S(1)} %get-tuple-element.78), channel_id=1, source_target_pairs={{0,16},{2,18},{4,20},{6,22},{8,24},{10,26},{12,28},{14,30},{16,0},... | collective-permute-start | bytes 319496 | tf_op jit(solution)/shard_map/ppermute | solution.py:21
  60.1 0.7 collective-permute-start.17
  61.5 1.6 %collective-permute-start.11 = (bf16[1664,128]{1,0:T(8,128)(2,1)S(1)}, bf16[1664,128]{1,0:T(8,128)(2,1)S(1)}, u32[]{:S(2)}, u32[]{:S(2)}) collective-permute-start(bf16[1664,128]{1,0:T(8,128)(2,1)S(1)} %get-tuple-element.71), channel_id=1, source_target_pairs={{0,4},{2,6},{4,0},{6,2},{8,12},{10,14},{12,8},{14,10},{16,20},{18,... | collective-permute-start | bytes 1277960 | tf_op jit(solution)/shard_map/ppermute | solution.py:21
  63.0 4.4 %collective-permute-done.16.refs_0_ = bf16[416,128]{1,0:T(8,128)(2,1)S(1)} collective-permute-done((bf16[416,128]{1,0:T(8,128)(2,1)S(1)}, bf16[416,128]{1,0:T(8,128)(2,1)S(1)}, u32[]{:S(2)}, u32[]{:S(2)}) %collective-permute-start.16) | collective-permute-done | bytes 106528 | tf_op jit(solution)/shard_map/ppermute | solution.py:21
  68.3 1.6 %collective-permute-start.19 = (bf16[1664,128]{1,0:T(8,128)(2,1)S(1)}, bf16[1664,128]{1,0:T(8,128)(2,1)S(1)}, u32[]{:S(2)}, u32[]{:S(2)}) collective-permute-start(bf16[1664,128]{1,0:T(8,128)(2,1)S(1)} %get-tuple-element.83), channel_id=1, source_target_pairs={{0,4},{2,6},{4,0},{6,2},{8,12},{10,14},{12,8},{14,10},{16,20},{18,... | collective-permute-start | bytes 1277960 | tf_op jit(solution)/shard_map/ppermute | solution.py:21
  69.9 2.8 %collective-permute-start.20 = (bf16[2,144,128]{2,1,0:T(8,128)(2,1)S(1)}, bf16[2,144,128]{2,1,0:T(8,128)(2,1)S(1)}, u32[]{:S(2)}, u32[]{:S(2)}) collective-permute-start(bf16[2,144,128]{2,1,0:T(8,128)(2,1)S(1)} %get-tuple-element.88), channel_id=1, source_target_pairs={{0,16},{2,18},{4,20},{6,22},{8,24},{10,26},{12,28},{14,30},{16,0},... | collective-permute-start | bytes 221192 | tf_op jit(solution)/shard_map/ppermute | solution.py:21
  72.8 1.4 %collective-permute-start.21 = (bf16[2,144,128]{2,1,0:T(8,128)(2,1)S(1)}, bf16[2,144,128]{2,1,0:T(8,128)(2,1)S(1)}, u32[]{:S(2)}, u32[]{:S(2)}) collective-permute-start(bf16[2,144,128]{2,1,0:T(8,128)(2,1)S(1)} %get-tuple-element.89), channel_id=1, source_target_pairs={{0,24},{2,26},{4,28},{6,30},{8,16},{10,18},{12,20},{14,22},{16,8},... | collective-permute-start | bytes 221192 | tf_op jit(solution)/shard_map/ppermute | solution.py:21
  74.9 2.7 %collective-permute-done.20.refs_2_ = bf16[2,144,128]{2,1,0:T(8,128)(2,1)S(1)} collective-permute-done((bf16[2,144,128]{2,1,0:T(8,128)(2,1)S(1)}, bf16[2,144,128]{2,1,0:T(8,128)(2,1)S(1)}, u32[]{:S(2)}, u32[]{:S(2)}) %collective-permute-start.20) | collective-permute-done | bytes 73760 | tf_op jit(solution)/shard_map/ppermute | solution.py:21
  77.6 1.5 %collective-permute-done.21.refs_3_ = bf16[2,144,128]{2,1,0:T(8,128)(2,1)S(1)} collective-permute-done((bf16[2,144,128]{2,1,0:T(8,128)(2,1)S(1)}, bf16[2,144,128]{2,1,0:T(8,128)(2,1)S(1)}, u32[]{:S(2)}, u32[]{:S(2)}) %collective-permute-start.21) | collective-permute-done | bytes 73760 | tf_op jit(solution)/shard_map/ppermute | solution.py:21
  80.1 1.6 %collective-permute-start.26 = (bf16[656,128]{1,0:T(8,128)(2,1)S(1)}, bf16[656,128]{1,0:T(8,128)(2,1)S(1)}, u32[]{:S(2)}, u32[]{:S(2)}) collective-permute-start(bf16[656,128]{1,0:T(8,128)(2,1)S(1)} %uppers.1.p0), channel_id=1, source_target_pairs={{0,1},{1,0},{2,3},{3,2},{4,5},{5,4},{6,7},{7,6},{8,9},{9,8},{10,11... | collective-permute-start | bytes 503816 | tf_op jit(solution)/shard_map/ppermute | solution.py:21
  81.9 2.1 %end.1.e0 = bf16[656,128]{1,0:T(8,128)(2,1)S(1)} custom-call(bf16[1664,128]{1,0:T(8,128)(2,1)S(1)} %get-tuple-element.72.refs_0_, bf16[1664,128]{1,0:T(8,128)(2,1)S(1)} %get-tuple-element.95.refs_1_, bf16[1664,128]{1,0:T(8,128)(2,1)S(1)} %collective-permute-done.23.refs_2_, bf16[1664,128]{1,0:T(8,128)(2,1)S(1)} %collective-permute-done.24.refs_3_, ...), custom_call_target="tpu_custom_call" | custom-call | flops 32715571200 | bytes 61972480 | tf_op jit(solution)/shard_map/end/pallas_call | solution.py:52
  84.0 1.6 %collective-permute-start.25 = (bf16[656,128]{1,0:T(8,128)(2,1)S(1)}, bf16[656,128]{1,0:T(8,128)(2,1)S(1)}, u32[]{:S(2)}, u32[]{:S(2)}) collective-permute-start(bf16[656,128]{1,0:T(8,128)(2,1)S(1)} %end.1.e0), channel_id=1, source_target_pairs={{0,1},{1,0},{2,3},{3,2},{4,5},{5,4},{6,7},{7,6},{8,9},{9,8},{10,11... | collective-permute-start | bytes 503816 | tf_op jit(solution)/shard_map/ppermute | solution.py:21
  85.6 1.3 %collective-permute-done.26.p1 = bf16[656,128]{1,0:T(8,128)(2,1)S(1)} collective-permute-done((bf16[656,128]{1,0:T(8,128)(2,1)S(1)}, bf16[656,128]{1,0:T(8,128)(2,1)S(1)}, u32[]{:S(2)}, u32[]{:S(2)}) %collective-permute-start.26) | collective-permute-done | bytes 167968 | tf_op jit(solution)/shard_map/ppermute | solution.py:21
  86.8 3.6 %collective-permute-done.25.e1 = bf16[656,128]{1,0:T(8,128)(2,1)S(1)} collective-permute-done((bf16[656,128]{1,0:T(8,128)(2,1)S(1)}, bf16[656,128]{1,0:T(8,128)(2,1)S(1)}, u32[]{:S(2)}, u32[]{:S(2)}) %collective-permute-start.25) | collective-permute-done | bytes 167968 | tf_op jit(solution)/shard_map/ppermute | solution.py:21
  90.4 1.2 %final.1 = (f32[5,256,128]{2,1,0:T(8,128)}, f32[5,256,128]{2,1,0:T(8,128)}, f32[5,256]{1,0:T(8,128)}, f32[5,256]{1,0:T(8,128)}) custom-call(s32[1]{0:T(128)} %bitcast.place_ref, bf16[656,128]{1,0:T(8,128)(2,1)S(1)} %end.1.e0, bf16[656,128]{1,0:T(8,128)(2,1)S(1)} %collective-permute-done.25.e1, bf16[656,128]{1,0:T(8,128)(2,1)S(1)} %uppers.1.p0, ...), custom_call_target="tpu_custom_call" | custom-call | bytes 53063760 | tf_op jit(solution)/shard_map/final/pallas_call | solution.py:52
  (59 shorter events, 7.2 us)
Async XLA Ops:
  3.3 7.7 %copy-start.8 = (s32[1664]{0:T(1024)S(1)}, s32[1664]{0:T(1024)}, u32[]{:S(2)}) copy-start(s32[1664]{0:T(1024)} %param.12) | copy-start | bytes 19972
  3.3 7.8 %copy-start.4 = (f32[16]{0:T(128)S(1)}, f32[16]{0:T(128)}, u32[]{:S(2)}) copy-start(f32[16]{0:T(128)} %table_ref.1) | copy-start | bytes 196
  3.3 8.6 %copy-start.7 = (f32[10,256]{1,0:T(8,128)S(1)}, f32[10,256]{1,0:T(8,128)}, u32[]{:S(2)}) copy-start(f32[10,256]{1,0:T(8,128)} %get-tuple-element.52.trig_ref.refs_7_.refs_6_) | copy-start | bytes 30724
  5.2 6.7 %collective-permute-start = (bf16[1664,256]{1,0:T(8,128)(2,1)S(1)}, bf16[1664,256]{1,0:T(8,128)(2,1)S(1)}, u32[]{:S(2)}, u32[]{:S(2)}) collective-permute-start(bf16[1664,256]{1,0:T(8,128)(2,1)S(1)} %first.1.v_ref), channel_id=1, source_target_pairs={{0,2},{2,0},{4,6},{6,4},{8,10},{10,8},{12,14},{14,12},{16,18},{18,... | collective-permute-start | bytes 2555912 | tf_op jit(solution)/shard_map/ppermute | solution.py:21
  5.7 35.4 %collective-permute-start.7 = (bf16[416,256]{1,0:T(8,128)(2,1)}, bf16[416,256]{1,0:T(8,128)(2,1)}, u32[]{:S(2)}, u32[]{:S(2)}) collective-permute-start(bf16[416,256]{1,0:T(8,128)(2,1)} %get-tuple-element.62), channel_id=1, source_target_pairs={{0,24},{2,26},{4,28},{6,30},{8,16},{10,18},{12,20},{14,22},{16,8},... | collective-permute-start | bytes 638984 | tf_op jit(solution)/shard_map/ppermute | solution.py:21
  10.3 15.0 %collective-permute-start.2 = (bf16[560,256]{1,0:T(8,128)(2,1)}, bf16[560,256]{1,0:T(8,128)(2,1)}, u32[]{:S(2)}, u32[]{:S(2)}) collective-permute-start(bf16[560,256]{1,0:T(8,128)(2,1)} %get-tuple-element.55), channel_id=1, source_target_pairs={{0,8},{2,10},{4,12},{6,14},{8,0},{10,2},{12,4},{14,6},{16,24},{18,... | collective-permute-start | bytes 860168 | tf_op jit(solution)/shard_map/ppermute | solution.py:21
  10.3 27.1 %collective-permute-start.5 = (bf16[560,256]{1,0:T(8,128)(2,1)}, bf16[560,256]{1,0:T(8,128)(2,1)S(1)}, u32[]{:S(2)}, u32[]{:S(2)}) collective-permute-start(bf16[560,256]{1,0:T(8,128)(2,1)} %get-tuple-element.60), channel_id=1, source_target_pairs={{0,16},{2,18},{4,20},{6,22},{8,24},{10,26},{12,28},{14,30},{16,0},... | collective-permute-start | bytes 860168 | tf_op jit(solution)/shard_map/ppermute | solution.py:21
  12.3 13.0 %collective-permute-start.1 = (bf16[1664,128]{1,0:T(8,128)(2,1)S(1)}, bf16[1664,128]{1,0:T(8,128)(2,1)S(1)}, u32[]{:S(2)}, u32[]{:S(2)}) collective-permute-start(bf16[1664,128]{1,0:T(8,128)(2,1)S(1)} %forward2_chunk0.1.v_ref.refs_4_), channel_id=1, source_target_pairs={{0,4},{2,6},{4,0},{6,2},{8,12},{10,14},{12,8},{14,10},{16,20},{18,... | collective-permute-start | bytes 1277960 | tf_op jit(solution)/shard_map/ppermute | solution.py:21
  14.4 23.2 %collective-permute-start.12 = (bf16[1664,128]{1,0:T(8,128)(2,1)S(1)}, bf16[1664,128]{1,0:T(8,128)(2,1)S(1)}, u32[]{:S(2)}, u32[]{:S(2)}) collective-permute-start(bf16[1664,128]{1,0:T(8,128)(2,1)S(1)} %forward2_chunk1.1.v_ref.refs_4_), channel_id=1, source_target_pairs={{0,4},{2,6},{4,0},{6,2},{8,12},{10,14},{12,8},{14,10},{16,20},{18,... | collective-permute-start | bytes 1277960 | tf_op jit(solution)/shard_map/ppermute | solution.py:21
  25.7 16.8 %collective-permute-start.3 = (bf16[416,128]{1,0:T(8,128)(2,1)S(1)}, bf16[416,128]{1,0:T(8,128)(2,1)S(1)}, u32[]{:S(2)}, u32[]{:S(2)}) collective-permute-start(bf16[416,128]{1,0:T(8,128)(2,1)S(1)} %get-tuple-element.57), channel_id=1, source_target_pairs={{0,16},{2,18},{4,20},{6,22},{8,24},{10,26},{12,28},{14,30},{16,0},... | collective-permute-start | bytes 319496 | tf_op jit(solution)/shard_map/ppermute | solution.py:21
  27.8 14.8 %collective-permute-start.4 = (bf16[416,128]{1,0:T(8,128)(2,1)S(1)}, bf16[416,128]{1,0:T(8,128)(2,1)S(1)}, u32[]{:S(2)}, u32[]{:S(2)}) collective-permute-start(bf16[416,128]{1,0:T(8,128)(2,1)S(1)} %get-tuple-element.58), channel_id=1, source_target_pairs={{0,24},{2,26},{4,28},{6,30},{8,16},{10,18},{12,20},{14,22},{16,8},... | collective-permute-start | bytes 319496 | tf_op jit(solution)/shard_map/ppermute | solution.py:21
  37.5 7.2 %collective-permute-start.6 = (bf16[560,128]{1,0:T(8,128)(2,1)S(1)}, bf16[560,128]{1,0:T(8,128)(2,1)S(1)}, u32[]{:S(2)}, u32[]{:S(2)}) collective-permute-start(bf16[560,128]{1,0:T(8,128)(2,1)S(1)} %near_chunk0.1), channel_id=1, source_target_pairs={{0,8},{2,10},{4,12},{6,14},{8,0},{10,2},{12,4},{14,6},{16,24},{18,... | collective-permute-start | bytes 430088 | tf_op jit(solution)/shard_map/ppermute | solution.py:21
  38.0 11.5 %collective-permute-start.13 = (bf16[416,128]{1,0:T(8,128)(2,1)S(1)}, bf16[416,128]{1,0:T(8,128)(2,1)S(1)}, u32[]{:S(2)}, u32[]{:S(2)}) collective-permute-start(bf16[416,128]{1,0:T(8,128)(2,1)S(1)} %get-tuple-element.73), channel_id=1, source_target_pairs={{0,16},{2,18},{4,20},{6,22},{8,24},{10,26},{12,28},{14,30},{16,0},... | collective-permute-start | bytes 319496 | tf_op jit(solution)/shard_map/ppermute | solution.py:21
  41.1 9.7 %collective-permute-start.14 = (bf16[416,128]{1,0:T(8,128)(2,1)S(1)}, bf16[416,128]{1,0:T(8,128)(2,1)S(1)}, u32[]{:S(2)}, u32[]{:S(2)}) collective-permute-start(bf16[416,128]{1,0:T(8,128)(2,1)S(1)} %get-tuple-element.74), channel_id=1, source_target_pairs={{0,24},{2,26},{4,28},{6,30},{8,16},{10,18},{12,20},{14,22},{16,8},... | collective-permute-start | bytes 319496 | tf_op jit(solution)/shard_map/ppermute | solution.py:21
  42.5 8.6 %collective-permute-start.15 = (bf16[560,128]{1,0:T(8,128)(2,1)S(1)}, bf16[560,128]{1,0:T(8,128)(2,1)S(1)}, u32[]{:S(2)}, u32[]{:S(2)}) collective-permute-start(bf16[560,128]{1,0:T(8,128)(2,1)S(1)} %near_chunk1.1), channel_id=1, source_target_pairs={{0,8},{2,10},{4,12},{6,14},{8,0},{10,2},{12,4},{14,6},{16,24},{18,... | collective-permute-start | bytes 430088 | tf_op jit(solution)/shard_map/ppermute | solution.py:21
  47.2 13.6 %collective-permute-start.8 = (bf16[416,128]{1,0:T(8,128)(2,1)S(1)}, bf16[416,128]{1,0:T(8,128)(2,1)S(1)}, u32[]{:S(2)}, u32[]{:S(2)}) collective-permute-start(bf16[416,128]{1,0:T(8,128)(2,1)S(1)} %get-tuple-element.66), channel_id=1, source_target_pairs={{0,16},{2,18},{4,20},{6,22},{8,24},{10,26},{12,28},{14,30},{16,0},... | collective-permute-start | bytes 319496 | tf_op jit(solution)/shard_map/ppermute | solution.py:21
  48.1 12.7 %collective-permute-start.9 = (bf16[416,128]{1,0:T(8,128)(2,1)S(1)}, bf16[416,128]{1,0:T(8,128)(2,1)S(1)}, u32[]{:S(2)}, u32[]{:S(2)}) collective-permute-start(bf16[416,128]{1,0:T(8,128)(2,1)S(1)} %get-tuple-element.67), channel_id=1, source_target_pairs={{0,24},{2,26},{4,28},{6,30},{8,16},{10,18},{12,20},{14,22},{16,8},... | collective-permute-start | bytes 319496 | tf_op jit(solution)/shard_map/ppermute | solution.py:21
  49.5 11.3 %collective-permute-start.10 = (bf16[416,128]{1,0:T(8,128)(2,1)S(1)}, bf16[416,128]{1,0:T(8,128)(2,1)S(1)}, u32[]{:S(2)}, u32[]{:S(2)}) collective-permute-start(bf16[416,128]{1,0:T(8,128)(2,1)S(1)} %get-tuple-element.68), channel_id=1, source_target_pairs={{0,8},{2,10},{4,12},{6,14},{8,0},{10,2},{12,4},{14,6},{16,24},{18,... | collective-permute-start | bytes 319496 | tf_op jit(solution)/shard_map/ppermute | solution.py:21
  53.7 13.8 %collective-permute-start.16 = (bf16[416,128]{1,0:T(8,128)(2,1)S(1)}, bf16[416,128]{1,0:T(8,128)(2,1)S(1)}, u32[]{:S(2)}, u32[]{:S(2)}) collective-permute-start(bf16[416,128]{1,0:T(8,128)(2,1)S(1)} %get-tuple-element.78), channel_id=1, source_target_pairs={{0,16},{2,18},{4,20},{6,22},{8,24},{10,26},{12,28},{14,30},{16,0},... | collective-permute-start | bytes 319496 | tf_op jit(solution)/shard_map/ppermute | solution.py:21
  60.1 7.3 %collective-permute-start.17 = (bf16[416,128]{1,0:T(8,128)(2,1)S(1)}, bf16[416,128]{1,0:T(8,128)(2,1)S(1)}, u32[]{:S(2)}, u32[]{:S(2)}) collective-permute-start(bf16[416,128]{1,0:T(8,128)(2,1)S(1)} %get-tuple-element.79), channel_id=1, source_target_pairs={{0,24},{2,26},{4,28},{6,30},{8,16},{10,18},{12,20},{14,22},{16,8},... | collective-permute-start | bytes 319496 | tf_op jit(solution)/shard_map/ppermute | solution.py:21
  60.8 6.9 %collective-permute-start.18 = (bf16[416,128]{1,0:T(8,128)(2,1)S(1)}, bf16[416,128]{1,0:T(8,128)(2,1)S(1)}, u32[]{:S(2)}, u32[]{:S(2)}) collective-permute-start(bf16[416,128]{1,0:T(8,128)(2,1)S(1)} %get-tuple-element.80), channel_id=1, source_target_pairs={{0,8},{2,10},{4,12},{6,14},{8,0},{10,2},{12,4},{14,6},{16,24},{18,... | collective-permute-start | bytes 319496 | tf_op jit(solution)/shard_map/ppermute | solution.py:21
  61.5 12.7 %collective-permute-start.11 = (bf16[1664,128]{1,0:T(8,128)(2,1)S(1)}, bf16[1664,128]{1,0:T(8,128)(2,1)S(1)}, u32[]{:S(2)}, u32[]{:S(2)}) collective-permute-start(bf16[1664,128]{1,0:T(8,128)(2,1)S(1)} %get-tuple-element.71), channel_id=1, source_target_pairs={{0,4},{2,6},{4,0},{6,2},{8,12},{10,14},{12,8},{14,10},{16,20},{18,... | collective-permute-start | bytes 1277960 | tf_op jit(solution)/shard_map/ppermute | solution.py:21
  68.3 11.0 %collective-permute-start.19 = (bf16[1664,128]{1,0:T(8,128)(2,1)S(1)}, bf16[1664,128]{1,0:T(8,128)(2,1)S(1)}, u32[]{:S(2)}, u32[]{:S(2)}) collective-permute-start(bf16[1664,128]{1,0:T(8,128)(2,1)S(1)} %get-tuple-element.83), channel_id=1, source_target_pairs={{0,4},{2,6},{4,0},{6,2},{8,12},{10,14},{12,8},{14,10},{16,20},{18,... | collective-permute-start | bytes 1277960 | tf_op jit(solution)/shard_map/ppermute | solution.py:21
  69.9 7.6 %collective-permute-start.20 = (bf16[2,144,128]{2,1,0:T(8,128)(2,1)S(1)}, bf16[2,144,128]{2,1,0:T(8,128)(2,1)S(1)}, u32[]{:S(2)}, u32[]{:S(2)}) collective-permute-start(bf16[2,144,128]{2,1,0:T(8,128)(2,1)S(1)} %get-tuple-element.88), channel_id=1, source_target_pairs={{0,16},{2,18},{4,20},{6,22},{8,24},{10,26},{12,28},{14,30},{16,0},... | collective-permute-start | bytes 221192 | tf_op jit(solution)/shard_map/ppermute | solution.py:21
  72.8 6.3 %collective-permute-start.21 = (bf16[2,144,128]{2,1,0:T(8,128)(2,1)S(1)}, bf16[2,144,128]{2,1,0:T(8,128)(2,1)S(1)}, u32[]{:S(2)}, u32[]{:S(2)}) collective-permute-start(bf16[2,144,128]{2,1,0:T(8,128)(2,1)S(1)} %get-tuple-element.89), channel_id=1, source_target_pairs={{0,24},{2,26},{4,28},{6,30},{8,16},{10,18},{12,20},{14,22},{16,8},... | collective-permute-start | bytes 221192 | tf_op jit(solution)/shard_map/ppermute | solution.py:21
  74.1 5.1 %collective-permute-start.22 = (bf16[2,144,128]{2,1,0:T(8,128)(2,1)S(1)}, bf16[2,144,128]{2,1,0:T(8,128)(2,1)S(1)}, u32[]{:S(2)}, u32[]{:S(2)}) collective-permute-start(bf16[2,144,128]{2,1,0:T(8,128)(2,1)S(1)} %get-tuple-element.90), channel_id=1, source_target_pairs={{0,8},{2,10},{4,12},{6,14},{8,0},{10,2},{12,4},{14,6},{16,24},{18,... | collective-permute-start | bytes 221192 | tf_op jit(solution)/shard_map/ppermute | solution.py:21
  74.8 6.9 %collective-permute-start.23 = (bf16[1664,128]{1,0:T(8,128)(2,1)S(1)}, bf16[1664,128]{1,0:T(8,128)(2,1)S(1)}, u32[]{:S(2)}, u32[]{:S(2)}) collective-permute-start(bf16[1664,128]{1,0:T(8,128)(2,1)S(1)} %get-tuple-element.96), channel_id=1, source_target_pairs={{0,2},{2,0},{4,6},{6,4},{8,10},{10,8},{12,14},{14,12},{16,18},{18,... | collective-permute-start | bytes 1277960 | tf_op jit(solution)/shard_map/ppermute | solution.py:21
  80.0 1.8 %collective-permute-start.24 = (bf16[1664,128]{1,0:T(8,128)(2,1)S(1)}, bf16[1664,128]{1,0:T(8,128)(2,1)S(1)}, u32[]{:S(2)}, u32[]{:S(2)}) collective-permute-start(bf16[1664,128]{1,0:T(8,128)(2,1)S(1)} %get-tuple-element.97), channel_id=1, source_target_pairs={{0,2},{2,0},{4,6},{6,4},{8,10},{10,8},{12,14},{14,12},{16,18},{18,... | collective-permute-start | bytes 1277960 | tf_op jit(solution)/shard_map/ppermute | solution.py:21
  80.1 6.7 %collective-permute-start.26 = (bf16[656,128]{1,0:T(8,128)(2,1)S(1)}, bf16[656,128]{1,0:T(8,128)(2,1)S(1)}, u32[]{:S(2)}, u32[]{:S(2)}) collective-permute-start(bf16[656,128]{1,0:T(8,128)(2,1)S(1)} %uppers.1.p0), channel_id=1, source_target_pairs={{0,1},{1,0},{2,3},{3,2},{4,5},{5,4},{6,7},{7,6},{8,9},{9,8},{10,11... | collective-permute-start | bytes 503816 | tf_op jit(solution)/shard_map/ppermute | solution.py:21
  81.9 8.5 %copy-start.1 = (f32[5,256,128]{2,1,0:T(8,128)S(1)}, f32[5,256,128]{2,1,0:T(8,128)}, u32[]{:S(2)}) copy-start(f32[5,256,128]{2,1,0:T(8,128)} %bs_ref.1) | copy-start | bytes 1966084
  81.9 8.5 %copy-start.2 = (f32[5,256]{1,0:T(8,128)S(1)}, f32[5,256]{1,0:T(8,128)}, u32[]{:S(2)}) copy-start(f32[5,256]{1,0:T(8,128)} %as_ref.1) | copy-start | bytes 15364
  84.0 6.4 %collective-permute-start.25 = (bf16[656,128]{1,0:T(8,128)(2,1)S(1)}, bf16[656,128]{1,0:T(8,128)(2,1)S(1)}, u32[]{:S(2)}, u32[]{:S(2)}) collective-permute-start(bf16[656,128]{1,0:T(8,128)(2,1)S(1)} %end.1.e0), channel_id=1, source_target_pairs={{0,1},{1,0},{2,3},{3,2},{4,5},{5,4},{6,7},{7,6},{8,9},{9,8},{10,11... | collective-permute-start | bytes 503816 | tf_op jit(solution)/shard_map/ppermute | solution.py:21
  (4 other events, 15.1 us)

commit v8 on v7

--- a/solution.py
+++ b/solution.py
@@ -35,7 +35,7 @@
 
 def tile_of(rows):
     best = 16
-    for size in range(16, 257, 16):
+    for size in range(16, 417, 16):
         if rows % size == 0:
             best = size
     return best
@@ -216,8 +216,8 @@
             [jnp.cos(angle), signs(place_ref) * jnp.sin(angle)], axis=0
         )
         weights = [[w_ref[s, col(c), :].astype(BF) for c in chunks] for s in range(early)]
-        for r in range(0, rows, tile):
-            at = pl.ds(r, tile)
+        for r in range(0, rows, 2 * tile):
+            at = pl.ds(r, 2 * tile)
             u = forward([u_ref[at, col(c)] for c in chunks], weights, trig_ref)[1]
             for c in chunks:
                 v_out[at, col(c)] = dot(u[c], weights[local_bits][c]).astype(BF)
@@ -515,8 +515,8 @@
         u_ref, w_ref, trig_ref, late_ref, grad, u_held, d_held = refs[2 * nb :]
         ga = [[jnp.zeros((1, BLOCK), F32)] * nb for _ in range(early)]
         w = [[w_ref[s, col(c), :] for c in chunks] for s in range(early)]
-        for r in range(0, rows, tile):
-            at = pl.ds(r, tile)
+        for r in range(0, rows, 2 * tile):
+            at = pl.ds(r, 2 * tile)
             steps, u = forward([u_ref[at, col(c)] for c in chunks], w, trig_ref)
             inputs = [u for u, _ in steps] + [u]
             d = []

time: 91.9 us -> 90.8 us (0.988)
  Pallas kernels: 17.7 us -> 15.6 us
  waiting for transfers between devices: 35.4 us -> 36.7 us
    pallas_call x18, Pallas kernels: 17.7 us -> 15.6 us  [call(): pl.pallas_call(body, grid=(1,), in_specs=whole, out_specs=[pl.BlockSpec(o...]
    ppermute x27, waiting for transfers between devices: 35.4 us -> 36.7 us  [swapped(): return lax.ppermute(value, axis, pairs)]
  transfers between devices with their start and end apart: 27 -> 27, of which waited for: 12 -> 12; matrix products, arithmetic and copies ran while one was open for 0% -> 0% of each run, Pallas kernels for 13% -> 12%
where the time goes in v8:
time: 90.8 us; the launch traced here: 90.4 us
  starting transfers between devices  37.1 us (41%)
  waiting for transfers between devices  36.7 us (40%)
  Pallas kernels  15.6 us (17%)
    ppermute x27, starting transfers between devices, swapped(): return lax.ppermute(value, axis, pairs)  37.1 us
    ppermute x27, waiting for transfers between devices, swapped(): return lax.ppermute(value, axis, pairs)  36.7 us
    pallas_call x18, Pallas kernels, call(): pl.pallas_call(body, grid=(1,), in_specs=whole, out_specs=[pl.BlockSpec(o...  15.6 us
  transfers between devices with their start and end apart: 27, of which 12 were waited for; matrix products, arithmetic and copies ran while one was open for 0% of the time, Pallas kernels for 12%

profile of v8, /device:TPU:0, one launch (start us, length us, event | category | flops | bytes accessed | tf_op | source)
XLA Modules:
  0.0 90.4 jit_solution(16642690328946581112)
XLA Ops:
  0.7 2.6 %pack.1 = (bf16[560,256]{1,0:T(8,128)(2,1)}, bf16[560,256]{1,0:T(8,128)(2,1)}, bf16[560,256]{1,0:T(8,128)(2,1)}, bf16[416,256]{1,0:T(8,128)(2,1)}, f32[10,256]{1,0:T(8,128)}) custom-call(s32[1]{0:T(128)} %bitcast.place_ref, f32[5,256,128]{2,1,0:T(8,128)} %w_ref.3, s32[1664,256]{1,0:T(8,128)} %codes_hbm.1, f32[5,256]{1,0:T(8,128)} %angle_ref), custom_call_target="tpu_custom_call" | custom-call | bytes 68956240 | tf_op jit(solution)/shard_map/pack/pallas_call | solution.py:52
  3.3 0.8 first.1.v_ref
  4.6 4.7 %collective-permute-start.7 = (bf16[416,256]{1,0:T(8,128)(2,1)}, bf16[416,256]{1,0:T(8,128)(2,1)}, u32[]{:S(2)}, u32[]{:S(2)}) collective-permute-start(bf16[416,256]{1,0:T(8,128)(2,1)} %get-tuple-element.62), channel_id=1, source_target_pairs={{0,24},{2,26},{4,28},{6,30},{8,16},{10,18},{12,20},{14,22},{16,8},... | collective-permute-start | bytes 638984 | tf_op jit(solution)/shard_map/ppermute | solution.py:21
  10.0 0.8 scales.1
  11.1 1.7 %collective-permute-start.1 = (bf16[1664,128]{1,0:T(8,128)(2,1)S(1)}, bf16[1664,128]{1,0:T(8,128)(2,1)S(1)}, u32[]{:S(2)}, u32[]{:S(2)}) collective-permute-start(bf16[1664,128]{1,0:T(8,128)(2,1)S(1)} %forward2_chunk0.1.v_ref.refs_4_), channel_id=1, source_target_pairs={{0,4},{2,6},{4,0},{6,2},{8,12},{10,14},{12,8},{14,10},{16,20},{18,... | collective-permute-start | bytes 1277960 | tf_op jit(solution)/shard_map/ppermute | solution.py:21
  13.6 10.7 %collective-permute-done.2.refs_6_ = bf16[560,256]{1,0:T(8,128)(2,1)} collective-permute-done((bf16[560,256]{1,0:T(8,128)(2,1)}, bf16[560,256]{1,0:T(8,128)(2,1)}, u32[]{:S(2)}, u32[]{:S(2)}) %collective-permute-start.2) | collective-permute-done | bytes 286752 | tf_op jit(solution)/shard_map/ppermute | solution.py:21
  24.6 2.0 %collective-permute-start.3 = (bf16[416,128]{1,0:T(8,128)(2,1)S(1)}, bf16[416,128]{1,0:T(8,128)(2,1)S(1)}, u32[]{:S(2)}, u32[]{:S(2)}) collective-permute-start(bf16[416,128]{1,0:T(8,128)(2,1)S(1)} %get-tuple-element.57), channel_id=1, source_target_pairs={{0,16},{2,18},{4,20},{6,22},{8,24},{10,26},{12,28},{14,30},{16,0},... | collective-permute-start | bytes 319496 | tf_op jit(solution)/shard_map/ppermute | solution.py:21
  26.5 1.6 %collective-permute-start.4 = (bf16[416,128]{1,0:T(8,128)(2,1)S(1)}, bf16[416,128]{1,0:T(8,128)(2,1)S(1)}, u32[]{:S(2)}, u32[]{:S(2)}) collective-permute-start(bf16[416,128]{1,0:T(8,128)(2,1)S(1)} %get-tuple-element.58), channel_id=1, source_target_pairs={{0,24},{2,26},{4,28},{6,30},{8,16},{10,18},{12,20},{14,22},{16,8},... | collective-permute-start | bytes 319496 | tf_op jit(solution)/shard_map/ppermute | solution.py:21
  28.1 8.3 %collective-permute-done.5.p_ref.refs_4_ = bf16[560,256]{1,0:T(8,128)(2,1)S(1)} collective-permute-done((bf16[560,256]{1,0:T(8,128)(2,1)}, bf16[560,256]{1,0:T(8,128)(2,1)S(1)}, u32[]{:S(2)}, u32[]{:S(2)}) %collective-permute-start.5) | collective-permute-done | bytes 286752 | tf_op jit(solution)/shard_map/ppermute | solution.py:21
  36.8 3.1 %collective-permute-start.13 = (bf16[416,128]{1,0:T(8,128)(2,1)S(1)}, bf16[416,128]{1,0:T(8,128)(2,1)S(1)}, u32[]{:S(2)}, u32[]{:S(2)}) collective-permute-start(bf16[416,128]{1,0:T(8,128)(2,1)S(1)} %get-tuple-element.73), channel_id=1, source_target_pairs={{0,16},{2,18},{4,20},{6,22},{8,24},{10,26},{12,28},{14,30},{16,0},... | collective-permute-start | bytes 319496 | tf_op jit(solution)/shard_map/ppermute | solution.py:21
  39.9 1.4 %collective-permute-start.14 = (bf16[416,128]{1,0:T(8,128)(2,1)S(1)}, bf16[416,128]{1,0:T(8,128)(2,1)S(1)}, u32[]{:S(2)}, u32[]{:S(2)}) collective-permute-start(bf16[416,128]{1,0:T(8,128)(2,1)S(1)} %get-tuple-element.74), channel_id=1, source_target_pairs={{0,24},{2,26},{4,28},{6,30},{8,16},{10,18},{12,20},{14,22},{16,8},... | collective-permute-start | bytes 319496 | tf_op jit(solution)/shard_map/ppermute | solution.py:21
  41.4 2.4 %collective-permute-done.6.refs_2_ = bf16[560,128]{1,0:T(8,128)(2,1)S(1)} collective-permute-done((bf16[560,128]{1,0:T(8,128)(2,1)S(1)}, bf16[560,128]{1,0:T(8,128)(2,1)S(1)}, u32[]{:S(2)}, u32[]{:S(2)}) %collective-permute-start.6) | collective-permute-done | bytes 143392 | tf_op jit(solution)/shard_map/ppermute | solution.py:21
  43.8 2.3 %group_chunk0.1 = (bf16[416,128]{1,0:T(8,128)(2,1)S(1)}, bf16[416,128]{1,0:T(8,128)(2,1)S(1)}, bf16[416,128]{1,0:T(8,128)(2,1)S(1)}, bf16[416,128]{1,0:T(8,128)(2,1)S(1)}, bf16[4,144,128]{2,1,0:T(8,128)(2,1)S(1)}) custom-call(bf16[416,128]{1,0:T(8,128)(2,1)S(1)} %collective-permute-done.3.refs_0_, bf16[416,128]{1,0:T(8,128)(2,1)S(1)} %collective-permute-done.4.refs_1_, ...), custom_call_target="tpu_custom_call" | custom-call | flops 16357785600 | bytes 46448640 | tf_op jit(solution)/shard_map/group_chunk0/pallas_call | solution.py:52
  46.1 0.7 collective-permute-start.8
  46.8 1.3 %collective-permute-start.9 = (bf16[416,128]{1,0:T(8,128)(2,1)S(1)}, bf16[416,128]{1,0:T(8,128)(2,1)S(1)}, u32[]{:S(2)}, u32[]{:S(2)}) collective-permute-start(bf16[416,128]{1,0:T(8,128)(2,1)S(1)} %get-tuple-element.67), channel_id=1, source_target_pairs={{0,24},{2,26},{4,28},{6,30},{8,16},{10,18},{12,20},{14,22},{16,8},... | collective-permute-start | bytes 319496 | tf_op jit(solution)/shard_map/ppermute | solution.py:21
  48.1 1.5 %collective-permute-start.10 = (bf16[416,128]{1,0:T(8,128)(2,1)S(1)}, bf16[416,128]{1,0:T(8,128)(2,1)S(1)}, u32[]{:S(2)}, u32[]{:S(2)}) collective-permute-start(bf16[416,128]{1,0:T(8,128)(2,1)S(1)} %get-tuple-element.68), channel_id=1, source_target_pairs={{0,8},{2,10},{4,12},{6,14},{8,0},{10,2},{12,4},{14,6},{16,24},{18,... | collective-permute-start | bytes 319496 | tf_op jit(solution)/shard_map/ppermute | solution.py:21
  49.7 0.6 collective-permute-done.15.refs_2_
  50.3 2.3 %group_chunk1.1 = (bf16[416,128]{1,0:T(8,128)(2,1)S(1)}, bf16[416,128]{1,0:T(8,128)(2,1)S(1)}, bf16[416,128]{1,0:T(8,128)(2,1)S(1)}, bf16[416,128]{1,0:T(8,128)(...) custom-call(bf16[416,128]{1,0:T(8,128)(2,1)S(1)} %collective-permute, ...), custom_call_target="tpu_custom_call" | custom-call | flops 16357785600 | bytes 51609600 | tf_op jit(solution)/shard_map/group_chunk1/pallas_call | solution.py:52
  52.6 6.2 %collective-permute-start.16 = (bf16[416,128]{1,0:T(8,128)(2,1)S(1)}, bf16[416,128]{1,0:T(8,128)(2,1)S(1)}, u32[]{:S(2)}, u32[]{:S(2)}) collective-permute-start(bf16[416,128]{1,0:T(8,128)(2,1)S(1)} %get-tuple-element.78), channel_id=1, source_target_pairs={{0,16},{2,18},{4,20},{6,22},{8,24},{10,26},{12,28},{14,30},{16,0},... | collective-permute-start | bytes 319496 | tf_op jit(solution)/shard_map/ppermute | solution.py:21
  60.0 1.6 %collective-permute-start.11 = (bf16[1664,128]{1,0:T(8,128)(2,1)S(1)}, bf16[1664,128]{1,0:T(8,128)(2,1)S(1)}, u32[]{:S(2)}, u32[]{:S(2)}) collective-permute-start(bf16[1664,128]{1,0:T(8,128)(2,1)S(1)} %get-tuple-element.71), channel_id=1, source_target_pairs={{0,4},{2,6},{4,0},{6,2},{8,12},{10,14},{12,8},{14,10},{16,20},{18,... | collective-permute-start | bytes 1277960 | tf_op jit(solution)/shard_map/ppermute | solution.py:21
  61.6 4.7 %collective-permute-done.16.refs_0_ = bf16[416,128]{1,0:T(8,128)(2,1)S(1)} collective-permute-done((bf16[416,128]{1,0:T(8,128)(2,1)S(1)}, bf16[416,128]{1,0:T(8,128)(2,1)S(1)}, u32[]{:S(2)}, u32[]{:S(2)}) %collective-permute-start.16) | collective-permute-done | bytes 106528 | tf_op jit(solution)/shard_map/ppermute | solution.py:21
  67.2 1.6 %collective-permute-start.19 = (bf16[1664,128]{1,0:T(8,128)(2,1)S(1)}, bf16[1664,128]{1,0:T(8,128)(2,1)S(1)}, u32[]{:S(2)}, u32[]{:S(2)}) collective-permute-start(bf16[1664,128]{1,0:T(8,128)(2,1)S(1)} %get-tuple-element.83), channel_id=1, source_target_pairs={{0,4},{2,6},{4,0},{6,2},{8,12},{10,14},{12,8},{14,10},{16,20},{18,... | collective-permute-start | bytes 1277960 | tf_op jit(solution)/shard_map/ppermute | solution.py:21
  68.8 2.8 %collective-permute-start.20 = (bf16[2,144,128]{2,1,0:T(8,128)(2,1)S(1)}, bf16[2,144,128]{2,1,0:T(8,128)(2,1)S(1)}, u32[]{:S(2)}, u32[]{:S(2)}) collective-permute-start(bf16[2,144,128]{2,1,0:T(8,128)(2,1)S(1)} %get-tuple-element.88), channel_id=1, source_target_pairs={{0,16},{2,18},{4,20},{6,22},{8,24},{10,26},{12,28},{14,30},{16,0},... | collective-permute-start | bytes 221192 | tf_op jit(solution)/shard_map/ppermute | solution.py:21
  71.6 1.3 %collective-permute-start.21 = (bf16[2,144,128]{2,1,0:T(8,128)(2,1)S(1)}, bf16[2,144,128]{2,1,0:T(8,128)(2,1)S(1)}, u32[]{:S(2)}, u32[]{:S(2)}) collective-permute-start(bf16[2,144,128]{2,1,0:T(8,128)(2,1)S(1)} %get-tuple-element.89), channel_id=1, source_target_pairs={{0,24},{2,26},{4,28},{6,30},{8,16},{10,18},{12,20},{14,22},{16,8},... | collective-permute-start | bytes 221192 | tf_op jit(solution)/shard_map/ppermute | solution.py:21
  73.7 2.8 %collective-permute-done.20.refs_2_ = bf16[2,144,128]{2,1,0:T(8,128)(2,1)S(1)} collective-permute-done((bf16[2,144,128]{2,1,0:T(8,128)(2,1)S(1)}, bf16[2,144,128]{2,1,0:T(8,128)(2,1)S(1)}, u32[]{:S(2)}, u32[]{:S(2)}) %collective-permute-start.20) | collective-permute-done | bytes 73760 | tf_op jit(solution)/shard_map/ppermute | solution.py:21
  76.4 1.5 %collective-permute-done.21.refs_3_ = bf16[2,144,128]{2,1,0:T(8,128)(2,1)S(1)} collective-permute-done((bf16[2,144,128]{2,1,0:T(8,128)(2,1)S(1)}, bf16[2,144,128]{2,1,0:T(8,128)(2,1)S(1)}, u32[]{:S(2)}, u32[]{:S(2)}) %collective-permute-start.21) | collective-permute-done | bytes 73760 | tf_op jit(solution)/shard_map/ppermute | solution.py:21
  78.9 1.6 %collective-permute-start.26 = (bf16[656,128]{1,0:T(8,128)(2,1)S(1)}, bf16[656,128]{1,0:T(8,128)(2,1)S(1)}, u32[]{:S(2)}, u32[]{:S(2)}) collective-permute-start(bf16[656,128]{1,0:T(8,128)(2,1)S(1)} %uppers.1.p0), channel_id=1, source_target_pairs={{0,1},{1,0},{2,3},{3,2},{4,5},{5,4},{6,7},{7,6},{8,9},{9,8},{10,11... | collective-permute-start | bytes 503816 | tf_op jit(solution)/shard_map/ppermute | solution.py:21
  80.6 2.1 %end.1.e0 = bf16[656,128]{1,0:T(8,128)(2,1)S(1)} custom-call(bf16[1664,128]{1,0:T(8,128)(2,1)S(1)} %get-tuple-element.72.refs_0_, bf16[1664,128]{1,0:T(8,128)(2,1)S(1)} %get-tuple-element.95.refs_1_, bf16[1664,128]{1,0:T(8,128)(2,1)S(1)} %collective-permute-done.23.refs_2_, bf16[1664,128]{1,0:T(8,128)(2,1)S(1)} %collective-permute-done.24.refs_3_, ...), custom_call_target="tpu_custom_call" | custom-call | flops 32715571200 | bytes 61972480 | tf_op jit(solution)/shard_map/end/pallas_call | solution.py:52
  82.7 1.6 %collective-permute-start.25 = (bf16[656,128]{1,0:T(8,128)(2,1)S(1)}, bf16[656,128]{1,0:T(8,128)(2,1)S(1)}, u32[]{:S(2)}, u32[]{:S(2)}) collective-permute-start(bf16[656,128]{1,0:T(8,128)(2,1)S(1)} %end.1.e0), channel_id=1, source_target_pairs={{0,1},{1,0},{2,3},{3,2},{4,5},{5,4},{6,7},{7,6},{8,9},{9,8},{10,11... | collective-permute-start | bytes 503816 | tf_op jit(solution)/shard_map/ppermute | solution.py:21
  84.3 1.3 %collective-permute-done.26.p1 = bf16[656,128]{1,0:T(8,128)(2,1)S(1)} collective-permute-done((bf16[656,128]{1,0:T(8,128)(2,1)S(1)}, bf16[656,128]{1,0:T(8,128)(2,1)S(1)}, u32[]{:S(2)}, u32[]{:S(2)}) %collective-permute-start.26) | collective-permute-done | bytes 167968 | tf_op jit(solution)/shard_map/ppermute | solution.py:21
  85.6 3.6 %collective-permute-done.25.e1 = bf16[656,128]{1,0:T(8,128)(2,1)S(1)} collective-permute-done((bf16[656,128]{1,0:T(8,128)(2,1)S(1)}, bf16[656,128]{1,0:T(8,128)(2,1)S(1)}, u32[]{:S(2)}, u32[]{:S(2)}) %collective-permute-start.25) | collective-permute-done | bytes 167968 | tf_op jit(solution)/shard_map/ppermute | solution.py:21
  89.2 1.2 %final.1 = (f32[5,256,128]{2,1,0:T(8,128)}, f32[5,256,128]{2,1,0:T(8,128)}, f32[5,256]{1,0:T(8,128)}, f32[5,256]{1,0:T(8,128)}) custom-call(s32[1]{0:T(128)} %bitcast.place_ref, bf16[656,128]{1,0:T(8,128)(2,1)S(1)} %end.1.e0, bf16[656,128]{1,0:T(8,128)(2,1)S(1)} %collective-permute-done.25.e1, bf16[656,128]{1,0:T(8,128)(2,1)S(1)} %uppers.1.p0, ...), custom_call_target="tpu_custom_call" | custom-call | bytes 53063760 | tf_op jit(solution)/shard_map/final/pallas_call | solution.py:52
  (59 shorter events, 6.9 us)
Async XLA Ops:
  3.3 6.7 %copy-start.4 = (f32[16]{0:T(128)S(1)}, f32[16]{0:T(128)}, u32[]{:S(2)}) copy-start(f32[16]{0:T(128)} %table_ref.1) | copy-start | bytes 196
  3.3 7.5 %copy-start.7 = (f32[10,256]{1,0:T(8,128)S(1)}, f32[10,256]{1,0:T(8,128)}, u32[]{:S(2)}) copy-start(f32[10,256]{1,0:T(8,128)} %get-tuple-element.52.trig_ref.refs_7_.refs_6_) | copy-start | bytes 30724
  4.1 6.7 %collective-permute-start = (bf16[1664,256]{1,0:T(8,128)(2,1)S(1)}, bf16[1664,256]{1,0:T(8,128)(2,1)S(1)}, u32[]{:S(2)}, u32[]{:S(2)}) collective-permute-start(bf16[1664,256]{1,0:T(8,128)(2,1)S(1)} %first.1.v_ref), channel_id=1, source_target_pairs={{0,2},{2,0},{4,6},{6,4},{8,10},{10,8},{12,14},{14,12},{16,18},{18,... | collective-permute-start | bytes 2555912 | tf_op jit(solution)/shard_map/ppermute | solution.py:21
  4.6 35.3 %collective-permute-start.7 = (bf16[416,256]{1,0:T(8,128)(2,1)}, bf16[416,256]{1,0:T(8,128)(2,1)}, u32[]{:S(2)}, u32[]{:S(2)}) collective-permute-start(bf16[416,256]{1,0:T(8,128)(2,1)} %get-tuple-element.62), channel_id=1, source_target_pairs={{0,24},{2,26},{4,28},{6,30},{8,16},{10,18},{12,20},{14,22},{16,8},... | collective-permute-start | bytes 638984 | tf_op jit(solution)/shard_map/ppermute | solution.py:21
  9.3 15.0 %collective-permute-start.2 = (bf16[560,256]{1,0:T(8,128)(2,1)}, bf16[560,256]{1,0:T(8,128)(2,1)}, u32[]{:S(2)}, u32[]{:S(2)}) collective-permute-start(bf16[560,256]{1,0:T(8,128)(2,1)} %get-tuple-element.55), channel_id=1, source_target_pairs={{0,8},{2,10},{4,12},{6,14},{8,0},{10,2},{12,4},{14,6},{16,24},{18,... | collective-permute-start | bytes 860168 | tf_op jit(solution)/shard_map/ppermute | solution.py:21
  9.3 27.1 %collective-permute-start.5 = (bf16[560,256]{1,0:T(8,128)(2,1)}, bf16[560,256]{1,0:T(8,128)(2,1)S(1)}, u32[]{:S(2)}, u32[]{:S(2)}) collective-permute-start(bf16[560,256]{1,0:T(8,128)(2,1)} %get-tuple-element.60), channel_id=1, source_target_pairs={{0,16},{2,18},{4,20},{6,22},{8,24},{10,26},{12,28},{14,30},{16,0},... | collective-permute-start | bytes 860168 | tf_op jit(solution)/shard_map/ppermute | solution.py:21
  11.1 13.1 %collective-permute-start.1 = (bf16[1664,128]{1,0:T(8,128)(2,1)S(1)}, bf16[1664,128]{1,0:T(8,128)(2,1)S(1)}, u32[]{:S(2)}, u32[]{:S(2)}) collective-permute-start(bf16[1664,128]{1,0:T(8,128)(2,1)S(1)} %forward2_chunk0.1.v_ref.refs_4_), channel_id=1, source_target_pairs={{0,4},{2,6},{4,0},{6,2},{8,12},{10,14},{12,8},{14,10},{16,20},{18,... | collective-permute-start | bytes 1277960 | tf_op jit(solution)/shard_map/ppermute | solution.py:21
  13.1 23.4 %collective-permute-start.12 = (bf16[1664,128]{1,0:T(8,128)(2,1)S(1)}, bf16[1664,128]{1,0:T(8,128)(2,1)S(1)}, u32[]{:S(2)}, u32[]{:S(2)}) collective-permute-start(bf16[1664,128]{1,0:T(8,128)(2,1)S(1)} %forward2_chunk1.1.v_ref.refs_4_), channel_id=1, source_target_pairs={{0,4},{2,6},{4,0},{6,2},{8,12},{10,14},{12,8},{14,10},{16,20},{18,... | collective-permute-start | bytes 1277960 | tf_op jit(solution)/shard_map/ppermute | solution.py:21
  24.6 16.8 %collective-permute-start.3 = (bf16[416,128]{1,0:T(8,128)(2,1)S(1)}, bf16[416,128]{1,0:T(8,128)(2,1)S(1)}, u32[]{:S(2)}, u32[]{:S(2)}) collective-permute-start(bf16[416,128]{1,0:T(8,128)(2,1)S(1)} %get-tuple-element.57), channel_id=1, source_target_pairs={{0,16},{2,18},{4,20},{6,22},{8,24},{10,26},{12,28},{14,30},{16,0},... | collective-permute-start | bytes 319496 | tf_op jit(solution)/shard_map/ppermute | solution.py:21
  26.5 14.8 %collective-permute-start.4 = (bf16[416,128]{1,0:T(8,128)(2,1)S(1)}, bf16[416,128]{1,0:T(8,128)(2,1)S(1)}, u32[]{:S(2)}, u32[]{:S(2)}) collective-permute-start(bf16[416,128]{1,0:T(8,128)(2,1)S(1)} %get-tuple-element.58), channel_id=1, source_target_pairs={{0,24},{2,26},{4,28},{6,30},{8,16},{10,18},{12,20},{14,22},{16,8},... | collective-permute-start | bytes 319496 | tf_op jit(solution)/shard_map/ppermute | solution.py:21
  36.4 7.4 %copy-start.6 = (bf16[560,256]{1,0:T(8,128)(2,1)S(1)}, bf16[560,256]{1,0:T(8,128)(2,1)}, u32[]{:S(2)}) copy-start(bf16[560,256]{1,0:T(8,128)(2,1)} %get-tuple-element.64.refs_7_) | copy-start | bytes 860164
  36.4 7.4 %collective-permute-start.6 = (bf16[560,128]{1,0:T(8,128)(2,1)S(1)}, bf16[560,128]{1,0:T(8,128)(2,1)S(1)}, u32[]{:S(2)}, u32[]{:S(2)}) collective-permute-start(bf16[560,128]{1,0:T(8,128)(2,1)S(1)} %near_chunk0.1), channel_id=1, source_target_pairs={{0,8},{2,10},{4,12},{6,14},{8,0},{10,2},{12,4},{14,6},{16,24},{18,... | collective-permute-start | bytes 430088 | tf_op jit(solution)/shard_map/ppermute | solution.py:21
  36.8 11.3 %collective-permute-start.13 = (bf16[416,128]{1,0:T(8,128)(2,1)S(1)}, bf16[416,128]{1,0:T(8,128)(2,1)S(1)}, u32[]{:S(2)}, u32[]{:S(2)}) collective-permute-start(bf16[416,128]{1,0:T(8,128)(2,1)S(1)} %get-tuple-element.73), channel_id=1, source_target_pairs={{0,16},{2,18},{4,20},{6,22},{8,24},{10,26},{12,28},{14,30},{16,0},... | collective-permute-start | bytes 319496 | tf_op jit(solution)/shard_map/ppermute | solution.py:21
  39.9 9.7 %collective-permute-start.14 = (bf16[416,128]{1,0:T(8,128)(2,1)S(1)}, bf16[416,128]{1,0:T(8,128)(2,1)S(1)}, u32[]{:S(2)}, u32[]{:S(2)}) collective-permute-start(bf16[416,128]{1,0:T(8,128)(2,1)S(1)} %get-tuple-element.74), channel_id=1, source_target_pairs={{0,24},{2,26},{4,28},{6,30},{8,16},{10,18},{12,20},{14,22},{16,8},... | collective-permute-start | bytes 319496 | tf_op jit(solution)/shard_map/ppermute | solution.py:21
  41.4 8.9 %collective-permute-start.15 = (bf16[560,128]{1,0:T(8,128)(2,1)S(1)}, bf16[560,128]{1,0:T(8,128)(2,1)S(1)}, u32[]{:S(2)}, u32[]{:S(2)}) collective-permute-start(bf16[560,128]{1,0:T(8,128)(2,1)S(1)} %near_chunk1.1), channel_id=1, source_target_pairs={{0,8},{2,10},{4,12},{6,14},{8,0},{10,2},{12,4},{14,6},{16,24},{18,... | collective-permute-start | bytes 430088 | tf_op jit(solution)/shard_map/ppermute | solution.py:21
  46.1 13.2 %collective-permute-start.8 = (bf16[416,128]{1,0:T(8,128)(2,1)S(1)}, bf16[416,128]{1,0:T(8,128)(2,1)S(1)}, u32[]{:S(2)}, u32[]{:S(2)}) collective-permute-start(bf16[416,128]{1,0:T(8,128)(2,1)S(1)} %get-tuple-element.66), channel_id=1, source_target_pairs={{0,16},{2,18},{4,20},{6,22},{8,24},{10,26},{12,28},{14,30},{16,0},... | collective-permute-start | bytes 319496 | tf_op jit(solution)/shard_map/ppermute | solution.py:21
  46.8 12.7 %collective-permute-start.9 = (bf16[416,128]{1,0:T(8,128)(2,1)S(1)}, bf16[416,128]{1,0:T(8,128)(2,1)S(1)}, u32[]{:S(2)}, u32[]{:S(2)}) collective-permute-start(bf16[416,128]{1,0:T(8,128)(2,1)S(1)} %get-tuple-element.67), channel_id=1, source_target_pairs={{0,24},{2,26},{4,28},{6,30},{8,16},{10,18},{12,20},{14,22},{16,8},... | collective-permute-start | bytes 319496 | tf_op jit(solution)/shard_map/ppermute | solution.py:21
  48.1 11.3 %collective-permute-start.10 = (bf16[416,128]{1,0:T(8,128)(2,1)S(1)}, bf16[416,128]{1,0:T(8,128)(2,1)S(1)}, u32[]{:S(2)}, u32[]{:S(2)}) collective-permute-start(bf16[416,128]{1,0:T(8,128)(2,1)S(1)} %get-tuple-element.68), channel_id=1, source_target_pairs={{0,8},{2,10},{4,12},{6,14},{8,0},{10,2},{12,4},{14,6},{16,24},{18,... | collective-permute-start | bytes 319496 | tf_op jit(solution)/shard_map/ppermute | solution.py:21
  52.6 13.7 %collective-permute-start.16 = (bf16[416,128]{1,0:T(8,128)(2,1)S(1)}, bf16[416,128]{1,0:T(8,128)(2,1)S(1)}, u32[]{:S(2)}, u32[]{:S(2)}) collective-permute-start(bf16[416,128]{1,0:T(8,128)(2,1)S(1)} %get-tuple-element.78), channel_id=1, source_target_pairs={{0,16},{2,18},{4,20},{6,22},{8,24},{10,26},{12,28},{14,30},{16,0},... | collective-permute-start | bytes 319496 | tf_op jit(solution)/shard_map/ppermute | solution.py:21
  58.8 7.5 %collective-permute-start.17 = (bf16[416,128]{1,0:T(8,128)(2,1)S(1)}, bf16[416,128]{1,0:T(8,128)(2,1)S(1)}, u32[]{:S(2)}, u32[]{:S(2)}) collective-permute-start(bf16[416,128]{1,0:T(8,128)(2,1)S(1)} %get-tuple-element.79), channel_id=1, source_target_pairs={{0,24},{2,26},{4,28},{6,30},{8,16},{10,18},{12,20},{14,22},{16,8},... | collective-permute-start | bytes 319496 | tf_op jit(solution)/shard_map/ppermute | solution.py:21
  59.3 7.3 %collective-permute-start.18 = (bf16[416,128]{1,0:T(8,128)(2,1)S(1)}, bf16[416,128]{1,0:T(8,128)(2,1)S(1)}, u32[]{:S(2)}, u32[]{:S(2)}) collective-permute-start(bf16[416,128]{1,0:T(8,128)(2,1)S(1)} %get-tuple-element.80), channel_id=1, source_target_pairs={{0,8},{2,10},{4,12},{6,14},{8,0},{10,2},{12,4},{14,6},{16,24},{18,... | collective-permute-start | bytes 319496 | tf_op jit(solution)/shard_map/ppermute | solution.py:21
  60.0 13.0 %collective-permute-start.11 = (bf16[1664,128]{1,0:T(8,128)(2,1)S(1)}, bf16[1664,128]{1,0:T(8,128)(2,1)S(1)}, u32[]{:S(2)}, u32[]{:S(2)}) collective-permute-start(bf16[1664,128]{1,0:T(8,128)(2,1)S(1)} %get-tuple-element.71), channel_id=1, source_target_pairs={{0,4},{2,6},{4,0},{6,2},{8,12},{10,14},{12,8},{14,10},{16,20},{18,... | collective-permute-start | bytes 1277960 | tf_op jit(solution)/shard_map/ppermute | solution.py:21
  67.2 11.0 %collective-permute-start.19 = (bf16[1664,128]{1,0:T(8,128)(2,1)S(1)}, bf16[1664,128]{1,0:T(8,128)(2,1)S(1)}, u32[]{:S(2)}, u32[]{:S(2)}) collective-permute-start(bf16[1664,128]{1,0:T(8,128)(2,1)S(1)} %get-tuple-element.83), channel_id=1, source_target_pairs={{0,4},{2,6},{4,0},{6,2},{8,12},{10,14},{12,8},{14,10},{16,20},{18,... | collective-permute-start | bytes 1277960 | tf_op jit(solution)/shard_map/ppermute | solution.py:21
  68.8 7.6 %collective-permute-start.20 = (bf16[2,144,128]{2,1,0:T(8,128)(2,1)S(1)}, bf16[2,144,128]{2,1,0:T(8,128)(2,1)S(1)}, u32[]{:S(2)}, u32[]{:S(2)}) collective-permute-start(bf16[2,144,128]{2,1,0:T(8,128)(2,1)S(1)} %get-tuple-element.88), channel_id=1, source_target_pairs={{0,16},{2,18},{4,20},{6,22},{8,24},{10,26},{12,28},{14,30},{16,0},... | collective-permute-start | bytes 221192 | tf_op jit(solution)/shard_map/ppermute | solution.py:21
  71.6 6.3 %collective-permute-start.21 = (bf16[2,144,128]{2,1,0:T(8,128)(2,1)S(1)}, bf16[2,144,128]{2,1,0:T(8,128)(2,1)S(1)}, u32[]{:S(2)}, u32[]{:S(2)}) collective-permute-start(bf16[2,144,128]{2,1,0:T(8,128)(2,1)S(1)} %get-tuple-element.89), channel_id=1, source_target_pairs={{0,24},{2,26},{4,28},{6,30},{8,16},{10,18},{12,20},{14,22},{16,8},... | collective-permute-start | bytes 221192 | tf_op jit(solution)/shard_map/ppermute | solution.py:21
  73.0 5.1 %collective-permute-start.22 = (bf16[2,144,128]{2,1,0:T(8,128)(2,1)S(1)}, bf16[2,144,128]{2,1,0:T(8,128)(2,1)S(1)}, u32[]{:S(2)}, u32[]{:S(2)}) collective-permute-start(bf16[2,144,128]{2,1,0:T(8,128)(2,1)S(1)} %get-tuple-element.90), channel_id=1, source_target_pairs={{0,8},{2,10},{4,12},{6,14},{8,0},{10,2},{12,4},{14,6},{16,24},{18,... | collective-permute-start | bytes 221192 | tf_op jit(solution)/shard_map/ppermute | solution.py:21
  73.6 6.8 %collective-permute-start.23 = (bf16[1664,128]{1,0:T(8,128)(2,1)S(1)}, bf16[1664,128]{1,0:T(8,128)(2,1)S(1)}, u32[]{:S(2)}, u32[]{:S(2)}) collective-permute-start(bf16[1664,128]{1,0:T(8,128)(2,1)S(1)} %get-tuple-element.96), channel_id=1, source_target_pairs={{0,2},{2,0},{4,6},{6,4},{8,10},{10,8},{12,14},{14,12},{16,18},{18,... | collective-permute-start | bytes 1277960 | tf_op jit(solution)/shard_map/ppermute | solution.py:21
  78.8 1.8 %collective-permute-start.24 = (bf16[1664,128]{1,0:T(8,128)(2,1)S(1)}, bf16[1664,128]{1,0:T(8,128)(2,1)S(1)}, u32[]{:S(2)}, u32[]{:S(2)}) collective-permute-start(bf16[1664,128]{1,0:T(8,128)(2,1)S(1)} %get-tuple-element.97), channel_id=1, source_target_pairs={{0,2},{2,0},{4,6},{6,4},{8,10},{10,8},{12,14},{14,12},{16,18},{18,... | collective-permute-start | bytes 1277960 | tf_op jit(solution)/shard_map/ppermute | solution.py:21
  78.9 6.7 %collective-permute-start.26 = (bf16[656,128]{1,0:T(8,128)(2,1)S(1)}, bf16[656,128]{1,0:T(8,128)(2,1)S(1)}, u32[]{:S(2)}, u32[]{:S(2)}) collective-permute-start(bf16[656,128]{1,0:T(8,128)(2,1)S(1)} %uppers.1.p0), channel_id=1, source_target_pairs={{0,1},{1,0},{2,3},{3,2},{4,5},{5,4},{6,7},{7,6},{8,9},{9,8},{10,11... | collective-permute-start | bytes 503816 | tf_op jit(solution)/shard_map/ppermute | solution.py:21
  80.6 8.5 %copy-start.1 = (f32[5,256,128]{2,1,0:T(8,128)S(1)}, f32[5,256,128]{2,1,0:T(8,128)}, u32[]{:S(2)}) copy-start(f32[5,256,128]{2,1,0:T(8,128)} %bs_ref.1) | copy-start | bytes 1966084
  80.6 8.5 %copy-start.2 = (f32[5,256]{1,0:T(8,128)S(1)}, f32[5,256]{1,0:T(8,128)}, u32[]{:S(2)}) copy-start(f32[5,256]{1,0:T(8,128)} %as_ref.1) | copy-start | bytes 15364
  82.7 6.4 %collective-permute-start.25 = (bf16[656,128]{1,0:T(8,128)(2,1)S(1)}, bf16[656,128]{1,0:T(8,128)(2,1)S(1)}, u32[]{:S(2)}, u32[]{:S(2)}) collective-permute-start(bf16[656,128]{1,0:T(8,128)(2,1)S(1)} %end.1.e0), channel_id=1, source_target_pairs={{0,1},{1,0},{2,3},{3,2},{4,5},{5,4},{6,7},{7,6},{8,9},{9,8},{10,11... | collective-permute-start | bytes 503816 | tf_op jit(solution)/shard_map/ppermute | solution.py:21
  (4 other events, 14.5 us)
